TPU v7x, 32 devices: a whole 2x2x4 slice. The times are simulated.
32 devices in a mesh: gx: 4 (over y, x), gy: 2 (over core), gz: 4 (over z).
Axes of the slice: x: 2, y: 2, z: 4, core: 2. Of those that a mesh axis runs over, the one named last changes fastest.
Arguments:
- positions: float32 [4, 2, 4, 3, 64], P('gx', 'gy', 'gz'), may hold values from 0 to 5
- species: int32 [4, 2, 4, 64], P('gx', 'gy', 'gz'), may hold values from 0 to 7
- counts: int32 [4, 2, 4], P('gx', 'gy', 'gz'), may hold values from 4 to 64, as said below
- embed: bfloat16 [8, 128], replicated, may hold values from -6 to 6
- radial_one: float32 [2, 4, 128], replicated, may hold values from -6 to 6
- mix_one: bfloat16 [128, 256], replicated, may hold values from -0.375 to 0.375
- read_one: float32 [128], replicated, may hold values from -0.5 to 0.5
- radial_two: float32 [4, 128], replicated, may hold values from -6 to 6
- mix_two: bfloat16 [128, 128], replicated, may hold values from -0.5 to 0.5
- read_hidden: bfloat16 [16, 128], replicated, may hold values from -0.5 to 0.5
- read_out: float32 [16], replicated, may hold values from -1.5 to 1.5
Outputs:
- forces: float32 [4, 2, 4, 3, 64], P('gx', 'gy', 'gz')
- energies: float32 [4, 2, 4, 64], P('gx', 'gy', 'gz')
- features: bfloat16 [4, 2, 4, 128, 64], P('gx', 'gy', 'gz')
Inputs may be any that keep to these rules, and one draw needn't show every extreme that they name: `counts`: the first block of the grid holds exactly 64 live atoms.
All inputs are finite; a program needn't handle non-finite values.
Results may differ from a plain program's by a relative error of at most 0.018.
Values may be sent and summed in bfloat16 or wider, within the bound.
No kernel may reach another device: no remote copies, remote signals or barrier semaphores. Data moves between devices by JAX's collectives and lax.ppermute only.
A program may use at most 64 MiB of HBM per device.

v0:
```python
import itertools
import math

import jax
import jax.numpy as jnp
from jax import lax
from jax.experimental import pallas as pl
from jax.experimental.pallas import tpu as pltpu
from jax.sharding import PartitionSpec as P

CELL_SIDE = 5.0
CUT_SQUARE = 25.0
SOFTEN = 0.25
MSG_SCALE = 0.05
ROOT_THREE = math.sqrt(3.0)
FAR = 1.0e4
AXES = ("gx", "gy", "gz")
F32 = jnp.float32
BF16 = jnp.bfloat16
COS_TERMS = (
    0.9999999997799041,
    -4.934802137078749,
    4.058709159554242,
    -1.335212003029471,
    0.23493731372678894,
    -0.024396324214549327,
)
SIN_TERMS = (
    3.14159265353629,
    -5.167712764624453,
    2.550163318944743,
    -0.5992521977996564,
    0.08205040170151112,
    -0.007028386239784362,
)
VMEM_LIMIT = 48 * 1024 * 1024
NT = (((1,), (1,)), ((), ()))
NN = (((1,), (0,)), ((), ()))


def dot(a, b, dims=NN):
    return lax.dot_general(a, b, dims, preferred_element_type=F32)


def dot_exact(a, b, dims=NN):
    return lax.dot_general(
        a, b, dims, precision=lax.Precision.HIGHEST, preferred_element_type=F32
    )


def split_dot(a, b):
    high = a.astype(BF16)
    low = (a - high.astype(F32)).astype(BF16)
    return dot(high, b) + dot(low, b)


def offsets_of(count):
    return (0, 1) if count == 2 else (0, 1, -1)


def poly(terms, arg):
    total = arg * terms[-1] + terms[-2]
    for term in terms[-3::-1]:
        total = total * arg + term
    return total


class Plan:
    def __init__(self, mesh, slots, nbasis, nspec):
        self.sizes = {axis: mesh.shape[axis] for axis in AXES}
        self.ndev = math.prod(self.sizes.values())
        self.tiles = list(
            itertools.product(offsets_of(self.sizes["gx"]), offsets_of(self.sizes["gz"]))
        )
        self.sides = offsets_of(self.sizes["gy"])
        self.slots = slots
        self.width = len(self.sides) * slots
        self.far = len(self.tiles) * self.width
        self.nbasis = nbasis
        self.nspec = nspec
        self.wrapped = [self.sizes[axis] == 2 for axis in AXES]

    def neighbour_ids(self):
        index = {axis: lax.axis_index(axis) for axis in AXES}

        def moved(axis, step):
            return lax.rem(index[axis] + (step + self.sizes[axis]), self.sizes[axis])

        ids, plane = [], []
        for ox, oz in self.tiles:
            for oy in self.sides:
                place = (moved("gx", ox) * self.sizes["gy"] + moved("gy", oy)) * self.sizes["gz"]
                ids.append(place + moved("gz", oz))
            plane.append(moved("gx", ox) * self.sizes["gz"] + moved("gz", oz))
        return jnp.stack(ids + plane).astype(jnp.int32)

    def offset(self, tile, side):
        ox, oz = self.tiles[tile]
        return (ox, self.sides[side], oz)


def separations(plan, rows, cols):
    parts = []
    for axis in range(3):
        diff = rows[axis] - cols[axis]
        if plan.wrapped[axis]:
            diff = jnp.where(diff > CELL_SIDE, diff - 2.0 * CELL_SIDE, diff)
        parts.append(diff)
    return parts


def distance(plan, parts, tile):
    dist_sq = parts[0] * parts[0] + parts[1] * parts[1] + parts[2] * parts[2] + SOFTEN
    if tile == 0:
        row = lax.broadcasted_iota(jnp.int32, dist_sq.shape, 0)
        col = lax.broadcasted_iota(jnp.int32, dist_sq.shape, 1)
        dist_sq = jnp.where(row == col, FAR, dist_sq)
    return dist_sq, lax.rsqrt(dist_sq)


def waves(dist_sq, inverse):
    arg = jnp.minimum(dist_sq * inverse * (1.0 / CELL_SIDE) - 0.5, 0.5)
    square = arg * arg
    return poly(COS_TERMS, square), -(arg * poly(SIN_TERMS, square))


def first_kernel(plan, nrefs, ids_ref, *refs):
    far_refs, refs = refs[:nrefs], refs[nrefs:]
    (cols_ref, table_ref, embed_ref, mix_ref), refs = refs[:4], refs[4:]
    rows_ref, basis_ref, layer_ref, vector_ref, mixing_ref, pair_ref = refs
    slots, nbasis, nspec = plan.slots, plan.nbasis, plan.nspec
    cols = [cols_ref[:, axis : axis + 1] for axis in range(3)]
    species = lax.broadcasted_iota(jnp.int32, (nbasis * nspec, plan.width), 0) % nspec
    hot = []
    for tile in range(len(plan.tiles)):
        blocks = [fetch(plan, ids_ref, far_refs, tile, side) for side in range(len(plan.sides))]
        placed = side_by_side(plan, blocks) + tile_shift(plan, tile)
        rows_ref[tile] = placed
        rows = [placed[k : k + 1] for k in range(4)]
        hot.append((rows[3].astype(jnp.int32) == species).astype(F32).astype(BF16))
        parts = separations(plan, rows, cols)
        dist_sq, inverse = distance(plan, parts, tile)
        sine, cosine = waves(dist_sq, inverse)
        fade = jnp.maximum(1.0 - dist_sq * (1.0 / CUT_SQUARE), 0.0)
        radial = fade * fade * inverse
        units = [part * (inverse * ROOT_THREE) for part in parts]
        before, now = None, sine * radial
        lanes = slice(tile * plan.width, (tile + 1) * plan.width)
        for n in range(nbasis):
            if n == 1:
                before, now = now, 2.0 * cosine * now
            elif n > 1:
                before, now = now, 2.0 * cosine * now - before
            packed = now.astype(BF16)
            basis_ref[n, :, lanes] = packed
            pair_ref[n, :slots, lanes] = packed
            for k in range(3):
                pair_ref[n, (k + 1) * slots : (k + 2) * slots, lanes] = (units[k] * now).astype(BF16)
    hot = jnp.concatenate(hot, axis=1)
    gathered = dot(pair_ref[...].reshape(nbasis * 4 * slots, plan.far), hot, NT)
    gathered = gathered.reshape(nbasis, 4 * slots, nbasis * nspec)
    group = lax.broadcasted_iota(jnp.int32, gathered.shape[1:], 1) // nspec
    counted = jnp.zeros(gathered.shape[1:], F32)
    for n in range(nbasis):
        counted = jnp.where(group == n, gathered[n], counted)
    scalar = MSG_SCALE * split_dot(counted[:slots], table_ref[0])
    vector = MSG_SCALE * split_dot(counted[slots:], table_ref[1])
    vector_ref[...] = vector
    squares = vector * vector
    norm = squares[:slots] + squares[slots : 2 * slots] + squares[2 * slots :]
    invariants = jnp.concatenate([scalar.astype(BF16), norm.astype(BF16)], axis=1)
    mixing = dot(invariants, mix_ref[...], NT)
    mixing_ref[...] = mixing
    layer = (embed_ref[...] + mixing * sigmoid(mixing)).astype(BF16)
    for copy in range(layer_ref.shape[0]):
        layer_ref[copy] = layer


def sigmoid(value):
    return 1.0 / (1.0 + jnp.exp(-value))


def fetch(plan, ids_ref, far_refs, tile, side):
    if len(far_refs) == 1:
        return far_refs[0][ids_ref[tile * len(plan.sides) + side]]
    if far_refs[side].shape[0] == len(plan.tiles):
        return far_refs[side][tile]
    return far_refs[side][ids_ref[len(plan.tiles) * len(plan.sides) + tile]]


def side_by_side(plan, blocks):
    if len(blocks) == 2:
        lane = lax.broadcasted_iota(jnp.int32, blocks[0].shape, 1)
        return jnp.where(lane < plan.slots, blocks[0], blocks[1])
    return jnp.concatenate([block[:, : plan.slots] for block in blocks], axis=1)


def tile_shift(plan, tile):
    row = lax.broadcasted_iota(jnp.int32, (4, plan.width), 0)
    side = lax.broadcasted_iota(jnp.int32, (4, plan.width), 1) // plan.slots
    shift = jnp.zeros((4, plan.width), F32)
    for s in range(len(plan.sides)):
        for k, steps in enumerate(plan.offset(tile, s)):
            if steps:
                shift = jnp.where((row == k) & (side == s), CELL_SIDE * steps, shift)
    return shift


def gather_far(plan, ids_ref, far_refs, all_ref):
    slots = plan.slots
    for tile in range(len(plan.tiles)):
        for side in range(len(plan.sides)):
            start = tile * plan.width + side * slots
            all_ref[start : start + slots] = fetch(plan, ids_ref, far_refs, tile, side)


def second_kernel(plan, nrefs, ids_ref, *refs):
    far_refs, refs = refs[:nrefs], refs[nrefs:]
    (layer_ref, basis_ref, cols_ref, radial_ref, mix_ref), refs = refs[:5], refs[5:]
    (hidden_ref, out_ref, one_ref), refs = refs[:3], refs[3:]
    adjoint_ref, energy_ref, features_ref, own_ref, all_ref = refs
    slots, nbasis = plan.slots, plan.nbasis
    gather_far(plan, ids_ref, far_refs, all_ref)
    summed = dot(basis_ref[...].reshape(nbasis * slots, plan.far), all_ref[...])
    message = jnp.zeros((slots, summed.shape[1]), F32)
    for n in range(nbasis):
        message = message + summed[n * slots : (n + 1) * slots] * radial_ref[n : n + 1]
    rounded = (MSG_SCALE * message).astype(BF16)
    mixing = dot(rounded, mix_ref[...], NT)
    gate = sigmoid(mixing)
    layer = layer_ref[0].astype(F32)
    features = (layer + mixing * gate).astype(BF16)
    features_ref[...] = features
    before = dot(features, hidden_ref[...], NT)
    open_hidden = sigmoid(before)
    live = cols_ref[:, 3:4]
    energy = dot_exact(one_ref[...], layer, NT) + dot_exact(out_ref[...], before * open_hidden, NT)
    live_row = dot(jnp.ones((1, 8), BF16), jnp.where(
        lax.broadcasted_iota(jnp.int32, (slots, 8), 1) == 0, live, 0.0
    ).astype(BF16), NT)
    energy_ref[...] = energy * live_row
    slope = out_ref[...] * (open_hidden * (1.0 + before * (1.0 - open_hidden))) * live
    from_hidden = dot(slope.astype(BF16), hidden_ref[...])
    own_ref[...] = from_hidden + one_ref[...] * live
    back = from_hidden * (gate * (1.0 + mixing * (1.0 - gate)))
    adjoint = dot(back.astype(BF16), mix_ref[...]).astype(BF16)
    for copy in range(adjoint_ref.shape[0]):
        adjoint_ref[copy] = adjoint


def slope_kernel(plan, nrefs, ids_ref, *refs):
    far_refs, refs = refs[:nrefs], refs[nrefs:]
    adjoint_ref, rows_ref, cols_ref, radial_ref, slope_ref, pair_ref, all_ref = refs
    slots, nbasis = plan.slots, plan.nbasis
    gather_far(plan, ids_ref, far_refs, all_ref)
    cols = [cols_ref[:, axis : axis + 1] for axis in range(3)]
    adjoint = adjoint_ref[0].astype(F32) * MSG_SCALE
    weighted = jnp.concatenate(
        [(adjoint * radial_ref[n : n + 1]).astype(BF16) for n in range(nbasis)], axis=0
    )
    for tile in range(len(plan.tiles)):
        lanes = slice(tile * plan.width, (tile + 1) * plan.width)
        pulled = dot(weighted, all_ref[lanes], NT)
        parts = separations(plan, [rows_ref[tile, k : k + 1] for k in range(3)], cols)
        dist_sq, inverse = distance(plan, parts, tile)
        sine, cosine = waves(dist_sq, inverse)
        fade = jnp.maximum(1.0 - dist_sq * (1.0 / CUT_SQUARE), 0.0)
        radial = fade * fade * inverse
        on_sine = -inverse * ((4.0 / CUT_SQUARE) * fade + radial * inverse)
        on_cosine = (math.pi / CELL_SIDE) * (inverse * radial)
        double = 2.0 * cosine
        before_s, now_s, before_c, now_c = None, sine, None, cosine
        total = jnp.zeros_like(dist_sq)
        for n in range(nbasis):
            if n == 1:
                before_s, now_s = now_s, double * now_s
                before_c, now_c = now_c, double * now_c - 1.0
            elif n > 1:
                before_s, now_s = now_s, double * now_s - before_s
                before_c, now_c = now_c, double * now_c - before_c
            slope = on_sine * now_s + (n + 1.0) * on_cosine * now_c
            slope_ref[n, :, lanes] = slope.astype(BF16)
            total = total + slope * pulled[n * slots : (n + 1) * slots]
        pair_ref[:, lanes] = total


def force_kernel(plan, nrefs, ids_ref, *refs):
    far_refs, refs = refs[:nrefs], refs[nrefs:]
    (own_ref, basis_ref, slope_ref, pair_ref, rows_ref, cols_ref), refs = refs[:6], refs[6:]
    (radial_ref, mixing_ref, mix_ref, vector_ref, table_ref), refs = refs[:5], refs[5:]
    out_refs, all_ref = refs[:-1], refs[-1]
    slots, nbasis, nspec, width = plan.slots, plan.nbasis, plan.nspec, plan.width
    gather_far(plan, ids_ref, far_refs, all_ref)
    summed = dot(basis_ref[...].reshape(nbasis * slots, plan.far), all_ref[...])
    adjoint = jnp.zeros((slots, summed.shape[1]), F32)
    for n in range(nbasis):
        adjoint = adjoint + summed[n * slots : (n + 1) * slots] * radial_ref[n : n + 1]
    adjoint = own_ref[...] + MSG_SCALE * adjoint
    mixing = mixing_ref[...]
    gate = sigmoid(mixing)
    back = (adjoint * (gate * (1.0 + mixing * (1.0 - gate)))).astype(BF16)
    invariants = dot(back, mix_ref[...])
    channels = invariants.shape[1] // 2
    on_scalar = (MSG_SCALE * invariants[:, :channels]).astype(BF16)
    doubled = (2.0 * MSG_SCALE) * invariants[:, channels:]
    on_vector = (vector_ref[...] * jnp.concatenate([doubled] * 3, axis=0)).astype(BF16)
    weights = jnp.concatenate(
        [dot(on_scalar, table_ref[0], NT), dot(on_vector, table_ref[1], NT)], axis=0
    ).astype(BF16)
    group = lax.broadcasted_iota(jnp.int32, weights.shape, 1) // nspec
    weights = weights.astype(F32)
    weights = jnp.concatenate(
        [jnp.where(group == n, weights, 0.0).astype(BF16) for n in range(nbasis)], axis=0
    )
    cols = [cols_ref[:, axis : axis + 1] for axis in range(3)]
    species = lax.broadcasted_iota(jnp.int32, (nbasis * nspec, width), 0) % nspec
    own = [jnp.zeros((slots, width), F32) for _ in range(3)]
    pulls = []
    for tile in range(len(plan.tiles)):
        lanes = slice(tile * width, (tile + 1) * width)
        rows = [rows_ref[tile, k : k + 1] for k in range(4)]
        hot = (rows[3].astype(jnp.int32) == species).astype(F32).astype(BF16)
        spread = dot(weights, hot)
        parts = separations(plan, rows, cols)
        dist_sq, inverse = distance(plan, parts, tile)
        scale = ROOT_THREE * inverse
        total = pair_ref[:, lanes]
        along, sides = None, [None] * 3
        for n in range(nbasis):
            start = n * 4 * slots
            piece = [spread[start + m * slots : start + (m + 1) * slots] for m in range(4)]
            slope = slope_ref[n, :, lanes].astype(F32)
            basis = basis_ref[n, :, lanes].astype(F32)
            mixed = parts[0] * piece[1] + parts[1] * piece[2] + parts[2] * piece[3]
            total = total + slope * (piece[0] + scale * mixed)
            term = basis * mixed
            along = term if along is None else along + term
            for k in range(3):
                term = basis * piece[k + 1]
                sides[k] = term if sides[k] is None else sides[k] + term
        total = total - inverse * inverse * (scale * along)
        pulls.append([])
        for k in range(3):
            pull = parts[k] * total + scale * sides[k]
            own[k] = own[k] + pull
            pulls[-1].append(jnp.sum(pull, axis=0, keepdims=True))
    ones = jnp.ones((8, width), F32)
    mine = jnp.concatenate([dot_exact(ones, own[k], NT)[:1] for k in range(3)], axis=0)
    if len(out_refs) == 1:
        out_refs[0][...] = jnp.zeros_like(out_refs[0])
    side_of = lax.broadcasted_iota(jnp.int32, (3, width), 1) // slots
    for tile in range(len(plan.tiles)):
        pulled = jnp.concatenate(pulls[tile], axis=0)
        if tile == 0:
            pulled = pulled - jnp.concatenate([mine] + [jnp.zeros_like(mine)] * (len(plan.sides) - 1), axis=1)
        for side in range(len(plan.sides)):
            if len(out_refs) == 1:
                place = ids_ref[tile * len(plan.sides) + side]
                out_refs[0][place, :3] = jnp.where(side_of == side, pulled, 0.0)
            else:
                out_refs[side][tile] = pulled[:, side * slots : (side + 1) * slots]


def prepare_kernel(plan, counts_ref, place_ref, kind_ref, sent_ref):
    live = lax.broadcasted_iota(jnp.int32, (1, plan.slots), 1) < counts_ref[0]
    rows = [
        jnp.where(live, place_ref[0], FAR),
        place_ref[1],
        place_ref[2],
        jnp.where(live, kind_ref[...], -1).astype(F32),
    ]
    rows = jnp.concatenate(rows, axis=0)
    rows = jnp.concatenate([rows, rows], axis=1)
    for copy in range(sent_ref.shape[0]):
        sent_ref[copy] = rows


def own_kernel(plan, sent_ref, embed_ref, radial_ref, cols_ref, table_ref, own_ref):
    slots, nspec = plan.slots, plan.nspec
    rows = sent_ref[0]
    cols = jnp.concatenate([rows, rows], axis=0).T[:slots]
    kind = cols[:, 3:4]
    lane = lax.broadcasted_iota(jnp.int32, cols.shape, 1)
    live = kind >= 0.0
    cols = jnp.where((lane == 0) & ~live, -FAR, cols)
    cols_ref[...] = jnp.where(lane == 3, live.astype(F32), cols)
    species = lax.broadcasted_iota(jnp.int32, (slots, nspec), 1)
    hot = (kind.astype(jnp.int32) == species).astype(F32).astype(BF16)
    embed = embed_ref[...]
    own_ref[...] = dot(hot, embed)
    embed = embed.astype(F32)
    for g in range(2):
        for n in range(plan.nbasis):
            row = radial_ref[g, n : n + 1]
            table_ref[g, n * nspec : (n + 1) * nspec] = (row * embed).astype(BF16)


def sum_kernel(plan, parts_ref, force_ref):
    total = parts_ref[0]
    for part in range(1, parts_ref.shape[0]):
        total = total + parts_ref[part]
    total = total[:, : plan.slots] + total[:, plan.slots :]
    for k in range(3):
        force_ref[k] = -total[k : k + 1]


VMEM_SPEC = pl.BlockSpec(memory_space=pltpu.VMEM)
SMEM_SPEC = pl.BlockSpec(memory_space=pltpu.SMEM)


def simple_call(kernel, plan, operands, outs, scalars=0, scratch=(), flops=2**20):
    single = not isinstance(outs, list)
    shapes = [jax.ShapeDtypeStruct(*out) for out in ([outs] if single else outs)]

    def body(*refs):
        kernel(plan, *refs)

    got = pl.pallas_call(
        body,
        out_shape=shapes,
        in_specs=[SMEM_SPEC] * scalars + [VMEM_SPEC] * (len(operands) - scalars),
        out_specs=[VMEM_SPEC] * len(shapes),
        scratch_shapes=[pltpu.VMEM(*buffer) for buffer in scratch],
        compiler_params=pltpu.CompilerParams(vmem_limit_bytes=VMEM_LIMIT),
        cost_estimate=pl.CostEstimate(flops=flops, bytes_accessed=2**20, transcendentals=0),
    )(*operands)
    return got[0] if single else got


def call(kernel, plan, far, ids, operands, outs, scratch, flops):
    def body(plan, *refs):
        kernel(plan, len(far), *refs)

    return simple_call(body, plan, [ids, *far, *operands], outs, 1, scratch, flops)


def shifted(value, axis, steps):
    count = lax.axis_size(axis)
    return lax.ppermute(value, axis, [(i, (i + steps) % count) for i in range(count)])


def neighbours_staged(plan, block):
    for axis in ("gz", "gx"):
        parts = [block] + [shifted(block, axis, -o) for o in offsets_of(plan.sizes[axis])[1:]]
        block = jnp.stack(parts)
    block = block.reshape((len(plan.tiles),) + block.shape[2:])
    return [block] + [shifted(block, "gy", -o) for o in plan.sides[1:]]


def everywhere(copies, axes):
    return lax.all_to_all(copies, axes, 0, 0, tiled=True)


def neighbours_lines(plan, copies):
    block = everywhere(copies, "gz")
    block = jnp.broadcast_to(block[None], (plan.sizes["gx"],) + block.shape)
    block = everywhere(block, "gx")
    block = block.reshape((-1,) + block.shape[2:])
    return [block, shifted(block, "gy", -1)]


def neighbours_plane(plan, copies):
    block = everywhere(copies, ("gx", "gz"))
    return [block, shifted(block, "gy", -1)]


def fold_staged(plan, parts):
    def folded(pieces, axis):
        total = pieces[0]
        for offset, piece in zip(offsets_of(plan.sizes[axis])[1:], pieces[1:]):
            total = total + shifted(piece, axis, offset)
        return total

    total = folded(parts, "gy")
    total = total.reshape((len(offsets_of(plan.sizes["gx"])), -1) + total.shape[1:])
    total = folded([total[m] for m in range(total.shape[0])], "gx")
    return folded([total[m] for m in range(total.shape[0])], "gz")


def local_program(mesh):
    def local(
        positions,
        species,
        counts,
        embed,
        radial_one,
        mix_one,
        read_one,
        radial_two,
        mix_two,
        read_hidden,
        read_out,
    ):
        slots, channels = positions.shape[-1], embed.shape[1]
        nbasis, nspec = radial_two.shape[0], embed.shape[0]
        plan = Plan(mesh, slots, nbasis, nspec)
        small = plan.ndev <= 64 and len(plan.sides) == 2
        place = positions[0, 0, 0].reshape(3, 1, slots)
        sent = simple_call(
            prepare_kernel,
            plan,
            [counts.reshape(1), place, species.reshape(1, slots)],
            ((plan.ndev if small else 1, 4, 2 * slots), F32),
            1,
        )
        ids = plan.neighbour_ids()
        far_sent = [everywhere(sent, AXES)] if small else neighbours_staged(plan, sent[0])
        cols, table, own_embed = simple_call(
            own_kernel,
            plan,
            [sent, embed, radial_one],
            [
                ((slots, 8), F32),
                ((2, nbasis * nspec, channels), BF16),
                ((slots, channels), F32),
            ],
        )
        pair_flops = 100 * slots * plan.far
        rows, basis, layer, vector, mixing = call(
            first_kernel,
            plan,
            far_sent,
            ids,
            [cols, table, own_embed, mix_one],
            [
                ((len(plan.tiles), 4, plan.width), F32),
                ((nbasis, slots, plan.far), BF16),
                ((plan.sizes["gz"] if small else 1, slots, channels), BF16),
                ((3 * slots, channels), F32),
                ((slots, channels), F32),
            ],
            [((nbasis, 4 * slots, plan.far), BF16)],
            pair_flops,
        )
        far_layer = neighbours_lines(plan, layer) if small else neighbours_staged(plan, layer[0])
        far_scratch = ((plan.far, channels), BF16)
        one_row, out_row = read_one[None], read_out[None]
        adjoint, energy, features, own_adjoint = call(
            second_kernel,
            plan,
            far_layer,
            ids,
            [layer, basis, cols, radial_two, mix_two, read_hidden, out_row, one_row],
            [
                ((plan.sizes["gx"] * plan.sizes["gz"] if small else 1, slots, channels), BF16),
                ((1, slots), F32),
                ((slots, channels), BF16),
                ((slots, channels), F32),
            ],
            [far_scratch],
            pair_flops,
        )
        if small:
            far_adjoint = neighbours_plane(plan, adjoint)
        else:
            far_adjoint = neighbours_staged(plan, adjoint[0])
        slope, pair = call(
            slope_kernel,
            plan,
            far_layer,
            ids,
            [adjoint, rows, cols, radial_two],
            [((nbasis, slots, plan.far), BF16), ((slots, plan.far), F32)],
            [far_scratch],
            pair_flops,
        )
        if small:
            pull_outs = [((plan.ndev, 4, plan.width), F32)]
        else:
            pull_outs = [((len(plan.tiles), 3, slots), F32)] * len(plan.sides)
        pulls = call(
            force_kernel,
            plan,
            far_adjoint,
            ids,
            [own_adjoint, basis, slope, pair, rows, cols, radial_two, mixing, mix_one, vector, table],
            pull_outs,
            [far_scratch],
            pair_flops,
        )
        if small:
            forces = simple_call(sum_kernel, plan, [everywhere(pulls[0], AXES)], ((3, 1, slots), F32))
        else:
            forces = -fold_staged(plan, pulls)
        return (
            forces.reshape(1, 1, 1, 3, slots),
            energy[None, None],
            features.T[None, None, None],
        )

    return local


def solution(mesh):
    split = [P(*AXES, None, None), P(*AXES, None), P(*AXES)]
    out_specs = (P(*AXES, None, None), P(*AXES, None), P(*AXES, None, None))
    return jax.shard_map(
        local_program(mesh),
        mesh=mesh,
        in_specs=tuple(split + [P()] * 8),
        out_specs=out_specs,
        check_vma=False,
    )
```

profile of v0, /device:TPU:0, one launch (start us, length us, event | category | flops | bytes accessed | tf_op | source)
XLA Modules:
  0.0 68.7 jit_solution(5829669402499157679)
XLA Ops:
  1.3 0.0 copy-start.6
  1.3 0.0 copy-start.7
  1.3 0.7 copy-done.6
  2.0 0.0 copy-done.7
  2.0 0.7 %shard_map.130.refs_0_ = f32[32,4,128]{2,1,0:T(4,128)} custom-call(s32[1]{0:T(128)} %bitcast.40.refs_0_, f32[3,1,64]{2,1,0:T(1,128)S(1)} %bitcast.44, s32[1,64]{1,0:T(1,128)S(1)} %bitcast.45), custom_call_target="tpu_custom_call" | custom-call | flops 1048576 | bytes 1048576 | tf_op jit(solution)/shard_map/pallas_call | solution.py:418
  2.7 7.3 %all-to-all-start = ((f32[32,4,128]{2,1,0:T(4,128)}), f32[32,4,128]{2,1,0:T(4,128)S(1)}, u32[]{:S(2)}, u32[]{:S(2)}) async-start(f32[32,4,128]{2,1,0:T(4,128)} %shard_map.130.refs_0_), calls=%async_computation | async-start | bytes 131072 | tf_op jit(solution)/shard_map/all_to_all | solution.py:451
  10.0 0.0 copy-start.4
  10.0 0.0 copy-start.5
  10.0 0.0 copy-start
  10.1 0.1 stack.111.refs_0_
  10.2 0.5 copy-done.4
  10.7 0.0 copy-done.5
  10.7 1.1 %shard_map.131 = (f32[64,8]{1,0:T(8,128)S(1)}, bf16[2,32,128]{2,1,0:T(8,128)(2,1)S(1)}, f32[64,128]{1,0:T(8,128)S(1)}) custom-call(f32[32,4,128]{2,1,0:T(4,128)} %shard_map.130.refs_0_, bf16[8,128]{1,0:T(8,128)(2,1)S(1)} %copy-done.5, f32[2,4,128]{2,1,0:T(4,128)S(1)} %copy-done.4), custom_call_target="tpu_custom_call" | custom-call | flops 1048576 | bytes 1048576 | tf_op jit(solution)/shard_map/pallas_call | solution.py:418
  11.8 5.7 %all-to-all-done.refs_1_ = f32[32,4,128]{2,1,0:T(4,128)S(1)} async-done(((f32[32,4,128]{2,1,0:T(4,128)}), f32[32,4,128]{2,1,0:T(4,128)S(1)}, u32[]{:S(2)}, u32[]{:S(2)}) %all-to-all-start) | async-done | bytes 65568 | tf_op jit(solution)/shard_map/all_to_all | solution.py:451
  17.5 0.0 copy-done
  17.5 2.4 %shard_map.132 = (f32[9,4,128]{2,1,0:T(4,128)S(1)}, bf16[4,64,1152]{2,1,0:T(8,128)(2,1)S(1)}, bf16[4,64,128]{2,1,0:T(8,128)(2,1)S(1)}, f32[192,128]{1,0:T(8,128)S(1)}, f32[64,128]{1,0:T(8,128)S(1)}) custom-call(s32[27]{0:T(128)S(1)} %stack.111.refs_0_, f32[32,4,128]{2,1,0:T(4,128)S(1)} %all-to-all-done.refs_1_, ...), custom_call_target="tpu_custom_call" | custom-call | flops 7372800 | bytes 1048576 | tf_op jit(solution)/shard_map/pallas_call | solution.py:418
  19.9 8.1 %all_to_all.25 = bf16[4,64,128]{2,1,0:T(8,128)(2,1)S(1)} all-to-all(bf16[4,64,128]{2,1,0:T(8,128)(2,1)S(1)} %get-tuple-element.20.refs_3_), channel_id=1, replica_groups=mesh['gx'=4,'gy'=2,'gz'=4] {'gz'}, dimensions={0} | all-to-all | bytes 131072 | tf_op jit(solution)/shard_map/all_to_all | solution.py:451
  28.1 0.0 copy-start.1
  28.1 8.1 %all_to_all.26 = bf16[4,4,64,128]{3,2,1,0:T(8,128)(2,1)S(1)} all-to-all(bf16[4,4,64,128]{3,2,1,0:T(8,128)(2,1)S(1)} %broadcast_in_dim.18), channel_id=1, replica_groups=mesh['gx'=4,'gy'=2,'gz'=4] {'gx'}, dimensions={0} | all-to-all | bytes 524288 | tf_op jit(solution)/shard_map/all_to_all | solution.py:451
  36.2 0.0 copy-start.3
  36.2 0.0 collective-permute-start
  36.2 1.5 %collective-permute-done.refs_2_ = bf16[16,64,128]{2,1,0:T(8,128)(2,1)S(1)} collective-permute-done((bf16[16,64,128]{2,1,0:T(8,128)(2,1)S(1)}, bf16[16,64,128]{2,1,0:T(8,128)(2,1)S(1)}, u32[]{:S(2)}, u32[]{:S(2)}) %collective-permute-start) | collective-permute-done | bytes 262176 | tf_op jit(solution)/shard_map/ppermute | solution.py:439
  37.7 0.0 copy-start.2
  37.7 0.0 copy-start.8
  37.7 0.0 copy-start.9
  37.7 0.0 copy-done.1
  37.7 0.0 copy-done.3
  37.8 0.7 copy-done.2
  38.4 0.0 copy-done.8
  38.4 0.0 copy-done.9
  38.4 2.0 %shard_map.133 = (bf16[16,64,128]{2,1,0:T(8,128)(2,1)S(1)}, f32[1,64]{1,0:T(1,128)}, bf16[64,128]{1,0:T(8,128)(2,1)}, f32[64,128]{1,0:T(8,128)S(1)}) custom-call(s32[27]{0:T(128)S(1)} %stack.111.refs_0_, bf16[16,64,128]{2,1,0:T(8,128)(2,1)S(1)} %bitcast.42, bf16[16,64,128]{2,1,0:T(8,128)(2,1)S(1)} %collective-permute-done.refs_2_, ...), custom_call_target="tpu_custom_call" | custom-call | flops 7372800 | bytes 1048576 | tf_op jit(solution)/shard_map/pallas_call | solution.py:418
  40.5 13.7 %all_to_all.27.refs_1_ = bf16[16,64,128]{2,1,0:T(8,128)(2,1)S(1)} all-to-all(bf16[16,64,128]{2,1,0:T(8,128)(2,1)S(1)} %get-tuple-element.22.refs_3_), channel_id=1, replica_groups=mesh['gx'=4,'gy'=2,'gz'=4] {'gx','gz'}, dimensions={0} | all-to-all | bytes 524288 | tf_op jit(solution)/shard_map/all_to_all | solution.py:451
  54.2 0.0 collective-permute-start.1
  54.2 1.6 %shard_map.134 = (bf16[4,64,1152]{2,1,0:T(8,128)(2,1)S(1)}, f32[64,1152]{1,0:T(8,128)S(1)}) custom-call(s32[27]{0:T(128)S(1)} %stack.111.refs_0_, bf16[16,64,128]{2,1,0:T(8,128)(2,1)S(1)} %bitcast.43, bf16[16,64,128]{2,1,0:T(8,128)(2,1)S(1)} %collective-permute-done.refs_2_, bf16[16,64,128]{2,1,0:T(8,128)(2,1)S(1)} %get-tuple-element.22.refs_3_, ...), custom_call_target="tpu_custom_call" | custom-call | flops 7372800 | bytes 1048576 | tf_op jit(solution)/shard_map/pallas_call | solution.py:418
  55.9 0.0 collective-permute-done.1.refs_2_
  55.9 2.9 %shard_map.135 = f32[32,4,128]{2,1,0:T(4,128)S(1)} custom-call(s32[27]{0:T(128)S(1)} %stack.111.refs_0_, bf16[16,64,128]{2,1,0:T(8,128)(2,1)S(1)} %all_to_all.27.refs_1_, bf16[16,64,128]{2,1,0:T(8,128)(2,1)S(1)} %collective-permute-done.1.refs_2_, f32[64,128]{1,0:T(8,128)S(1)} %get-tuple-element.23.refs_3_, ...), custom_call_target="tpu_custom_call" | custom-call | flops 7372800 | bytes 1048576 | tf_op jit(solution)/shard_map/pallas_call | solution.py:418
  58.8 9.2 %all_to_all.28.refs_0_ = f32[32,4,128]{2,1,0:T(4,128)S(1)} all-to-all(f32[32,4,128]{2,1,0:T(4,128)S(1)} %shard_map.135), channel_id=1, replica_groups=mesh['gx'=4,'gy'=2,'gz'=4] {'gx','gy','gz'}, dimensions={0} | all-to-all | bytes 131072 | tf_op jit(solution)/shard_map/all_to_all | solution.py:451
  68.0 0.7 shard_map.136
  (1 shorter events, 0.0 us)
Async XLA Ops:
  1.3 0.7 copy-start.6
  1.3 0.7 copy-start.7
  2.7 14.8 %all-to-all-start = ((f32[32,4,128]{2,1,0:T(4,128)}), f32[32,4,128]{2,1,0:T(4,128)S(1)}, u32[]{:S(2)}, u32[]{:S(2)}) async-start(f32[32,4,128]{2,1,0:T(4,128)} %shard_map.130.refs_0_), calls=%async_computation | async-start | bytes 131072 | tf_op jit(solution)/shard_map/all_to_all | solution.py:451
  10.0 0.7 %copy-start.4 = (f32[2,4,128]{2,1,0:T(4,128)S(1)}, f32[2,4,128]{2,1,0:T(4,128)}, u32[]{:S(2)}) copy-start(f32[2,4,128]{2,1,0:T(4,128)} %refs_2_.1) | copy-start | bytes 12292
  10.0 0.7 %copy-start.5 = (bf16[8,128]{1,0:T(8,128)(2,1)S(1)}, bf16[8,128]{1,0:T(8,128)(2,1)}, u32[]{:S(2)}) copy-start(bf16[8,128]{1,0:T(8,128)(2,1)} %refs_1_.1) | copy-start | bytes 6148
  10.0 7.4 %copy-start = (bf16[128,256]{1,0:T(8,128)(2,1)S(1)}, bf16[128,256]{1,0:T(8,128)(2,1)}, u32[]{:S(2)}) copy-start(bf16[128,256]{1,0:T(8,128)(2,1)} %refs_11_.1) | copy-start | bytes 196612
  28.1 9.7 %copy-start.1 = (bf16[128,128]{1,0:T(8,128)(2,1)S(1)}, bf16[128,128]{1,0:T(8,128)(2,1)}, u32[]{:S(2)}) copy-start(bf16[128,128]{1,0:T(8,128)(2,1)} %refs_7_.1) | copy-start | bytes 98308
  36.2 1.6 %copy-start.3 = (bf16[16,128]{1,0:T(8,128)(2,1)S(1)}, bf16[16,128]{1,0:T(8,128)(2,1)}, u32[]{:S(2)}) copy-start(bf16[16,128]{1,0:T(8,128)(2,1)} %refs_8_.1) | copy-start | bytes 12292
  36.2 1.5 %collective-permute-start = (bf16[16,64,128]{2,1,0:T(8,128)(2,1)S(1)}, bf16[16,64,128]{2,1,0:T(8,128)(2,1)S(1)}, u32[]{:S(2)}, u32[]{:S(2)}) collective-permute-start(bf16[16,64,128]{2,1,0:T(8,128)(2,1)S(1)} %bitcast.41), channel_id=1, source_target_pairs={{0,4},{4,0},{1,5},{5,1},{2,6},{6,2},{3,7},{7,3},{8,12},{12,8},{9,1... | collective-permute-start | bytes 786440 | tf_op jit(solution)/shard_map/ppermute | solution.py:439
  37.7 0.7 copy-start.2
  37.7 0.7 copy-start.8
  37.7 0.7 copy-start.9
  54.2 1.7 %collective-permute-start.1 = (bf16[16,64,128]{2,1,0:T(8,128)(2,1)S(1)}, bf16[16,64,128]{2,1,0:T(8,128)(2,1)S(1)}, u32[]{:S(2)}, u32[]{:S(2)}) collective-permute-start(bf16[16,64,128]{2,1,0:T(8,128)(2,1)S(1)} %all_to_all.27.refs_1_), channel_id=1, source_target_pairs={{0,4},{4,0},{1,5},{5,1},{2,6},{6,2},{3,7},{7,3},{8,12},{12,8},{9,1... | collective-permute-start | bytes 786440 | tf_op jit(solution)/shard_map/ppermute | solution.py:439
where the time goes:
time: 69.2 us; the launch traced here: 68.7 us
  blocking collectives  39.2 us (57%)
  Pallas kernels  11.5 us (17%)
  starting transfers between devices  7.3 us (11%)
  waiting for transfers between devices  7.19 us (10%)
  local copies, waits for them, and re-layouts  2.06 us (3%)
  between operations  1.43 us (2%)
    all_to_all x4, blocking collectives, everywhere(): return lax.all_to_all(copies, axes, 0, 0, tiled=True)  39.2 us
    pallas_call x7, Pallas kernels, simple_call(): pl.pallas_call(body, out_shape=shapes, in_specs=[SMEM_SPEC] * scalars + [...  11.5 us
    all_to_all x1, starting transfers between devices, everywhere(): return lax.all_to_all(copies, axes, 0, 0, tiled=True)  7.3 us
    all_to_all x1, waiting for transfers between devices, everywhere(): return lax.all_to_all(copies, axes, 0, 0, tiled=True)  5.65 us
    unnamed x20, local copies, waits for them, and re-layouts  1.91 us
    ppermute x2, waiting for transfers between devices, shifted(): lax.ppermute(value, axis, [(i, (i + steps) % count) for i in range(count)])  1.54 us
  transfers between devices with their start and end apart: 3, of which 2 were waited for; matrix products, arithmetic and copies ran while one was open for 0% of the time, Pallas kernels for 4%

commit v1 on v0

--- a/solution.py
+++ b/solution.py
@@ -58,6 +58,10 @@
     return (0, 1) if count == 2 else (0, 1, -1)
 
 
+def paired(count):
+    return count > 2 and count % 2 == 0
+
+
 def poly(terms, arg):
     total = arg * terms[-1] + terms[-2]
     for term in terms[-3::-1]:
@@ -80,19 +84,18 @@
         self.nspec = nspec
         self.wrapped = [self.sizes[axis] == 2 for axis in AXES]
 
-    def neighbour_ids(self):
-        index = {axis: lax.axis_index(axis) for axis in AXES}
-
-        def moved(axis, step):
-            return lax.rem(index[axis] + (step + self.sizes[axis]), self.sizes[axis])
-
-        ids, plane = [], []
-        for ox, oz in self.tiles:
-            for oy in self.sides:
-                place = (moved("gx", ox) * self.sizes["gy"] + moved("gy", oy)) * self.sizes["gz"]
-                ids.append(place + moved("gz", oz))
-            plane.append(moved("gx", ox) * self.sizes["gz"] + moved("gz", oz))
-        return jnp.stack(ids + plane).astype(jnp.int32)
+    def tile_places(self):
+        def place(axis, offset):
+            count = self.sizes[axis]
+            order = offsets_of(count).index(offset)
+            if order == 0 or not paired(count):
+                return jnp.int32(order)
+            parity = lax.rem(lax.axis_index(axis), 2)
+            return 1 + parity if offset == 1 else 2 - parity
+
+        depth = len(offsets_of(self.sizes["gz"]))
+        places = [place("gx", ox) * depth + place("gz", oz) for ox, oz in self.tiles]
+        return jnp.stack(places).astype(jnp.int32)
 
     def offset(self, tile, side):
         ox, oz = self.tiles[tile]
@@ -124,7 +127,7 @@
     return poly(COS_TERMS, square), -(arg * poly(SIN_TERMS, square))
 
 
-def first_kernel(plan, nrefs, ids_ref, *refs):
+def first_kernel(plan, nrefs, places_ref, *refs):
     far_refs, refs = refs[:nrefs], refs[nrefs:]
     (cols_ref, table_ref, embed_ref, mix_ref), refs = refs[:4], refs[4:]
     rows_ref, basis_ref, layer_ref, vector_ref, mixing_ref, pair_ref = refs
@@ -133,7 +136,7 @@
     species = lax.broadcasted_iota(jnp.int32, (nbasis * nspec, plan.width), 0) % nspec
     hot = []
     for tile in range(len(plan.tiles)):
-        blocks = [fetch(plan, ids_ref, far_refs, tile, side) for side in range(len(plan.sides))]
+        blocks = [fetch(places_ref, far_refs, tile, side) for side in range(len(plan.sides))]
         placed = side_by_side(plan, blocks) + tile_shift(plan, tile)
         rows_ref[tile] = placed
         rows = [placed[k : k + 1] for k in range(4)]
@@ -172,20 +175,15 @@
     mixing = dot(invariants, mix_ref[...], NT)
     mixing_ref[...] = mixing
     layer = (embed_ref[...] + mixing * sigmoid(mixing)).astype(BF16)
-    for copy in range(layer_ref.shape[0]):
-        layer_ref[copy] = layer
+    layer_ref[...] = layer
 
 
 def sigmoid(value):
     return 1.0 / (1.0 + jnp.exp(-value))
 
 
-def fetch(plan, ids_ref, far_refs, tile, side):
-    if len(far_refs) == 1:
-        return far_refs[0][ids_ref[tile * len(plan.sides) + side]]
-    if far_refs[side].shape[0] == len(plan.tiles):
-        return far_refs[side][tile]
-    return far_refs[side][ids_ref[len(plan.tiles) * len(plan.sides) + tile]]
+def fetch(places_ref, far_refs, tile, side):
+    return far_refs[side][places_ref[tile]]
 
 
 def side_by_side(plan, blocks):
@@ -206,21 +204,21 @@
     return shift
 
 
-def gather_far(plan, ids_ref, far_refs, all_ref):
+def gather_far(plan, places_ref, far_refs, all_ref):
     slots = plan.slots
     for tile in range(len(plan.tiles)):
         for side in range(len(plan.sides)):
             start = tile * plan.width + side * slots
-            all_ref[start : start + slots] = fetch(plan, ids_ref, far_refs, tile, side)
-
-
-def second_kernel(plan, nrefs, ids_ref, *refs):
+            all_ref[start : start + slots] = fetch(places_ref, far_refs, tile, side)
+
+
+def second_kernel(plan, nrefs, places_ref, *refs):
     far_refs, refs = refs[:nrefs], refs[nrefs:]
     (layer_ref, basis_ref, cols_ref, radial_ref, mix_ref), refs = refs[:5], refs[5:]
     (hidden_ref, out_ref, one_ref), refs = refs[:3], refs[3:]
     adjoint_ref, energy_ref, features_ref, own_ref, all_ref = refs
     slots, nbasis = plan.slots, plan.nbasis
-    gather_far(plan, ids_ref, far_refs, all_ref)
+    gather_far(plan, places_ref, far_refs, all_ref)
     summed = dot(basis_ref[...].reshape(nbasis * slots, plan.far), all_ref[...])
     message = jnp.zeros((slots, summed.shape[1]), F32)
     for n in range(nbasis):
@@ -228,7 +226,7 @@
     rounded = (MSG_SCALE * message).astype(BF16)
     mixing = dot(rounded, mix_ref[...], NT)
     gate = sigmoid(mixing)
-    layer = layer_ref[0].astype(F32)
+    layer = layer_ref[...].astype(F32)
     features = (layer + mixing * gate).astype(BF16)
     features_ref[...] = features
     before = dot(features, hidden_ref[...], NT)
@@ -243,18 +241,16 @@
     from_hidden = dot(slope.astype(BF16), hidden_ref[...])
     own_ref[...] = from_hidden + one_ref[...] * live
     back = from_hidden * (gate * (1.0 + mixing * (1.0 - gate)))
-    adjoint = dot(back.astype(BF16), mix_ref[...]).astype(BF16)
-    for copy in range(adjoint_ref.shape[0]):
-        adjoint_ref[copy] = adjoint
-
-
-def slope_kernel(plan, nrefs, ids_ref, *refs):
+    adjoint_ref[...] = dot(back.astype(BF16), mix_ref[...]).astype(BF16)
+
+
+def slope_kernel(plan, nrefs, places_ref, *refs):
     far_refs, refs = refs[:nrefs], refs[nrefs:]
     adjoint_ref, rows_ref, cols_ref, radial_ref, slope_ref, pair_ref, all_ref = refs
     slots, nbasis = plan.slots, plan.nbasis
-    gather_far(plan, ids_ref, far_refs, all_ref)
+    gather_far(plan, places_ref, far_refs, all_ref)
     cols = [cols_ref[:, axis : axis + 1] for axis in range(3)]
-    adjoint = adjoint_ref[0].astype(F32) * MSG_SCALE
+    adjoint = adjoint_ref[...].astype(F32) * MSG_SCALE
     weighted = jnp.concatenate(
         [(adjoint * radial_ref[n : n + 1]).astype(BF16) for n in range(nbasis)], axis=0
     )
@@ -284,13 +280,13 @@
         pair_ref[:, lanes] = total
 
 
-def force_kernel(plan, nrefs, ids_ref, *refs):
+def force_kernel(plan, nrefs, places_ref, *refs):
     far_refs, refs = refs[:nrefs], refs[nrefs:]
     (own_ref, basis_ref, slope_ref, pair_ref, rows_ref, cols_ref), refs = refs[:6], refs[6:]
     (radial_ref, mixing_ref, mix_ref, vector_ref, table_ref), refs = refs[:5], refs[5:]
-    out_refs, all_ref = refs[:-1], refs[-1]
+    out_ref, all_ref = refs
     slots, nbasis, nspec, width = plan.slots, plan.nbasis, plan.nspec, plan.width
-    gather_far(plan, ids_ref, far_refs, all_ref)
+    gather_far(plan, places_ref, far_refs, all_ref)
     summed = dot(basis_ref[...].reshape(nbasis * slots, plan.far), all_ref[...])
     adjoint = jnp.zeros((slots, summed.shape[1]), F32)
     for n in range(nbasis):
@@ -346,19 +342,12 @@
             pulls[-1].append(jnp.sum(pull, axis=0, keepdims=True))
     ones = jnp.ones((8, width), F32)
     mine = jnp.concatenate([dot_exact(ones, own[k], NT)[:1] for k in range(3)], axis=0)
-    if len(out_refs) == 1:
-        out_refs[0][...] = jnp.zeros_like(out_refs[0])
-    side_of = lax.broadcasted_iota(jnp.int32, (3, width), 1) // slots
     for tile in range(len(plan.tiles)):
         pulled = jnp.concatenate(pulls[tile], axis=0)
         if tile == 0:
-            pulled = pulled - jnp.concatenate([mine] + [jnp.zeros_like(mine)] * (len(plan.sides) - 1), axis=1)
-        for side in range(len(plan.sides)):
-            if len(out_refs) == 1:
-                place = ids_ref[tile * len(plan.sides) + side]
-                out_refs[0][place, :3] = jnp.where(side_of == side, pulled, 0.0)
-            else:
-                out_refs[side][tile] = pulled[:, side * slots : (side + 1) * slots]
+            others = [jnp.zeros_like(mine)] * (len(plan.sides) - 1)
+            pulled = pulled - jnp.concatenate([mine] + others, axis=1)
+        out_ref[places_ref[tile]] = pulled
 
 
 def prepare_kernel(plan, counts_ref, place_ref, kind_ref, sent_ref):
@@ -371,13 +360,12 @@
     ]
     rows = jnp.concatenate(rows, axis=0)
     rows = jnp.concatenate([rows, rows], axis=1)
-    for copy in range(sent_ref.shape[0]):
-        sent_ref[copy] = rows
+    sent_ref[...] = rows
 
 
 def own_kernel(plan, sent_ref, embed_ref, radial_ref, cols_ref, table_ref, own_ref):
     slots, nspec = plan.slots, plan.nspec
-    rows = sent_ref[0]
+    rows = sent_ref[...]
     cols = jnp.concatenate([rows, rows], axis=0).T[:slots]
     kind = cols[:, 3:4]
     lane = lax.broadcasted_iota(jnp.int32, cols.shape, 1)
@@ -395,15 +383,6 @@
             table_ref[g, n * nspec : (n + 1) * nspec] = (row * embed).astype(BF16)
 
 
-def sum_kernel(plan, parts_ref, force_ref):
-    total = parts_ref[0]
-    for part in range(1, parts_ref.shape[0]):
-        total = total + parts_ref[part]
-    total = total[:, : plan.slots] + total[:, plan.slots :]
-    for k in range(3):
-        force_ref[k] = -total[k : k + 1]
-
-
 VMEM_SPEC = pl.BlockSpec(memory_space=pltpu.VMEM)
 SMEM_SPEC = pl.BlockSpec(memory_space=pltpu.SMEM)
 
@@ -427,54 +406,54 @@
     return got[0] if single else got
 
 
-def call(kernel, plan, far, ids, operands, outs, scratch, flops):
+def call(kernel, plan, far, places, operands, outs, scratch, flops):
     def body(plan, *refs):
         kernel(plan, len(far), *refs)
 
-    return simple_call(body, plan, [ids, *far, *operands], outs, 1, scratch, flops)
-
-
-def shifted(value, axis, steps):
+    return simple_call(body, plan, [places, *far, *operands], outs, 1, scratch, flops)
+
+
+def swaps(axis):
     count = lax.axis_size(axis)
-    return lax.ppermute(value, axis, [(i, (i + steps) % count) for i in range(count)])
-
-
-def neighbours_staged(plan, block):
-    for axis in ("gz", "gx"):
-        parts = [block] + [shifted(block, axis, -o) for o in offsets_of(plan.sizes[axis])[1:]]
-        block = jnp.stack(parts)
-    block = block.reshape((len(plan.tiles),) + block.shape[2:])
-    return [block] + [shifted(block, "gy", -o) for o in plan.sides[1:]]
-
-
-def everywhere(copies, axes):
-    return lax.all_to_all(copies, axes, 0, 0, tiled=True)
-
-
-def neighbours_lines(plan, copies):
-    block = everywhere(copies, "gz")
-    block = jnp.broadcast_to(block[None], (plan.sizes["gx"],) + block.shape)
-    block = everywhere(block, "gx")
-    block = block.reshape((-1,) + block.shape[2:])
-    return [block, shifted(block, "gy", -1)]
-
-
-def neighbours_plane(plan, copies):
-    block = everywhere(copies, ("gx", "gz"))
-    return [block, shifted(block, "gy", -1)]
-
-
-def fold_staged(plan, parts):
-    def folded(pieces, axis):
-        total = pieces[0]
-        for offset, piece in zip(offsets_of(plan.sizes[axis])[1:], pieces[1:]):
-            total = total + shifted(piece, axis, offset)
-        return total
-
-    total = folded(parts, "gy")
-    total = total.reshape((len(offsets_of(plan.sizes["gx"])), -1) + total.shape[1:])
-    total = folded([total[m] for m in range(total.shape[0])], "gx")
-    return folded([total[m] for m in range(total.shape[0])], "gz")
+    if count == 2:
+        return [[(0, 1), (1, 0)]]
+    if paired(count):
+        near = [(i, i ^ 1) for i in range(count)]
+        far = [(i, (i - 1 + 2 * (i % 2)) % count) for i in range(count)]
+        return [near, far]
+    return [[((i + o) % count, i) for i in range(count)] for o in offsets_of(count)[1:]]
+
+
+def brought(block, axis):
+    got = [lax.ppermute(block, axis, pairs) for pairs in swaps(axis)[::-1]]
+    return [block] + got[::-1]
+
+
+def neighbours(plan, block):
+    stacked = jnp.stack(brought(block, "gz"))
+    stacked = jnp.concatenate(brought(stacked, "gx"))
+    return brought(stacked, "gy")
+
+
+def folded(pieces, axis):
+    got = [
+        lax.ppermute(piece, axis, [(to, source) for source, to in pairs])
+        for piece, pairs in list(zip(pieces[1:], swaps(axis)))[::-1]
+    ]
+    total = pieces[0]
+    for piece in got:
+        total = total + piece
+    return total
+
+
+def fold(plan, pulls):
+    for axis in ("gx", "gz"):
+        parts = len(offsets_of(plan.sizes[axis]))
+        pulls = pulls.reshape((parts, -1) + pulls.shape[1:])
+        pulls = folded([pulls[m] for m in range(parts)], axis)
+    pulls = pulls[0]
+    sides = [pulls[:, m * plan.slots : (m + 1) * plan.slots] for m in range(len(plan.sides))]
+    return folded(sides, "gy")
 
 
 def local_program(mesh):
@@ -494,17 +473,16 @@
         slots, channels = positions.shape[-1], embed.shape[1]
         nbasis, nspec = radial_two.shape[0], embed.shape[0]
         plan = Plan(mesh, slots, nbasis, nspec)
-        small = plan.ndev <= 64 and len(plan.sides) == 2
         place = positions[0, 0, 0].reshape(3, 1, slots)
         sent = simple_call(
             prepare_kernel,
             plan,
             [counts.reshape(1), place, species.reshape(1, slots)],
-            ((plan.ndev if small else 1, 4, 2 * slots), F32),
+            ((4, 2 * slots), F32),
             1,
         )
-        ids = plan.neighbour_ids()
-        far_sent = [everywhere(sent, AXES)] if small else neighbours_staged(plan, sent[0])
+        places = plan.tile_places()
+        far_sent = neighbours(plan, sent)
         cols, table, own_embed = simple_call(
             own_kernel,
             plan,
@@ -520,29 +498,29 @@
             first_kernel,
             plan,
             far_sent,
-            ids,
+            places,
             [cols, table, own_embed, mix_one],
             [
                 ((len(plan.tiles), 4, plan.width), F32),
                 ((nbasis, slots, plan.far), BF16),
-                ((plan.sizes["gz"] if small else 1, slots, channels), BF16),
+                ((slots, channels), BF16),
                 ((3 * slots, channels), F32),
                 ((slots, channels), F32),
             ],
             [((nbasis, 4 * slots, plan.far), BF16)],
             pair_flops,
         )
-        far_layer = neighbours_lines(plan, layer) if small else neighbours_staged(plan, layer[0])
+        far_layer = neighbours(plan, layer)
         far_scratch = ((plan.far, channels), BF16)
         one_row, out_row = read_one[None], read_out[None]
         adjoint, energy, features, own_adjoint = call(
             second_kernel,
             plan,
             far_layer,
-            ids,
+            places,
             [layer, basis, cols, radial_two, mix_two, read_hidden, out_row, one_row],
             [
-                ((plan.sizes["gx"] * plan.sizes["gz"] if small else 1, slots, channels), BF16),
+                ((slots, channels), BF16),
                 ((1, slots), F32),
                 ((slots, channels), BF16),
                 ((slots, channels), F32),
@@ -550,38 +528,28 @@
             [far_scratch],
             pair_flops,
         )
-        if small:
-            far_adjoint = neighbours_plane(plan, adjoint)
-        else:
-            far_adjoint = neighbours_staged(plan, adjoint[0])
+        far_adjoint = neighbours(plan, adjoint)
         slope, pair = call(
             slope_kernel,
             plan,
             far_layer,
-            ids,
+            places,
             [adjoint, rows, cols, radial_two],
             [((nbasis, slots, plan.far), BF16), ((slots, plan.far), F32)],
             [far_scratch],
             pair_flops,
         )
-        if small:
-            pull_outs = [((plan.ndev, 4, plan.width), F32)]
-        else:
-            pull_outs = [((len(plan.tiles), 3, slots), F32)] * len(plan.sides)
         pulls = call(
             force_kernel,
             plan,
             far_adjoint,
-            ids,
+            places,
             [own_adjoint, basis, slope, pair, rows, cols, radial_two, mixing, mix_one, vector, table],
-            pull_outs,
+            [((len(plan.tiles), 3, plan.width), F32)],
             [far_scratch],
             pair_flops,
         )
-        if small:
-            forces = simple_call(sum_kernel, plan, [everywhere(pulls[0], AXES)], ((3, 1, slots), F32))
-        else:
-            forces = -fold_staged(plan, pulls)
+        forces = -fold(plan, pulls[0])
         return (
             forces.reshape(1, 1, 1, 3, slots),
             energy[None, None],

time: 69.2 us -> 65.8 us (0.951)
  blocking collectives: 39.2 us -> 0 us
  waiting for transfers between devices: 7.19 us -> 26.5 us
  starting transfers between devices: 7.3 us -> 25.5 us
  Pallas kernels: 11.5 us -> 9.32 us
  local copies, waits for them, and re-layouts: 2.06 us -> 2.8 us
    all_to_all x4 -> x0, blocking collectives: 39.2 us -> none  [everywhere(): return lax.all_to_all(copies, axes, 0, 0, tiled=True)]
    ppermute x2 -> x20, starting transfers between devices: 0.01 us -> 25.5 us  [the longest x15 20 us: brought(): got = [lax.ppermute(block, axis, pairs) for pairs in swaps(axis)[::-1]]]
    ppermute x2 -> x20, waiting for transfers between devices: 1.54 us -> 26.5 us  [the longest x15 19.6 us: brought(): got = [lax.ppermute(block, axis, pairs) for pairs in swaps(axis)[::-1]]]
    all_to_all x1 -> x0, starting transfers between devices: 7.3 us -> none  [everywhere(): return lax.all_to_all(copies, axes, 0, 0, tiled=True)]
    all_to_all x1 -> x0, waiting for transfers between devices: 5.65 us -> none  [everywhere(): return lax.all_to_all(copies, axes, 0, 0, tiled=True)]
    pallas_call x7 -> x6, Pallas kernels: 11.5 us -> 9.32 us  [simple_call(): pl.pallas_call(body, out_shape=shapes, in_specs=[SMEM_SPEC] * scalars + [...]
    unnamed x20 -> x33, local copies, waits for them, and re-layouts: 1.91 us -> 2.6 us
  transfers between devices with their start and end apart: 3 -> 20, of which waited for: 2 -> 18; matrix products, arithmetic and copies ran while one was open for 0% -> 0% of each run, Pallas kernels for 4% -> 3%
where the time goes in v1:
time: 65.8 us; the launch traced here: 65.6 us
  waiting for transfers between devices  26.5 us (40%)
  starting transfers between devices  25.5 us (39%)
  Pallas kernels  9.32 us (14%)
  local copies, waits for them, and re-layouts  2.8 us (4%)
  between operations  1.43 us (2%)
    ppermute x15, starting transfers between devices, brought(): got = [lax.ppermute(block, axis, pairs) for pairs in swaps(axis)[::-1]]  20 us
    ppermute x15, waiting for transfers between devices, brought(): got = [lax.ppermute(block, axis, pairs) for pairs in swaps(axis)[::-1]]  19.6 us
    pallas_call x6, Pallas kernels, simple_call(): pl.pallas_call(body, out_shape=shapes, in_specs=[SMEM_SPEC] * scalars + [...  9.32 us
    ppermute x5, waiting for transfers between devices, folded(): lax.ppermute(piece, axis, [(to, source) for source, to in pairs])  6.87 us
    ppermute x5, starting transfers between devices, folded(): lax.ppermute(piece, axis, [(to, source) for source, to in pairs])  5.52 us
    unnamed x33, local copies, waits for them, and re-layouts  2.6 us
  transfers between devices with their start and end apart: 20, of which 18 were waited for; matrix products, arithmetic and copies ran while one was open for 0% of the time, Pallas kernels for 3%

profile of v1, /device:TPU:0, one launch (start us, length us, event | category | flops | bytes accessed | tf_op | source)
XLA Modules:
  0.0 65.6 jit_solution(2296188351094073341)
XLA Ops:
  1.3 0.7 %copy-done.6 = f32[1,1,1,3,64]{4,2,3,1,0:T(1,128)S(1)} copy-done((f32[1,1,1,3,64]{4,2,3,1,0:T(1,128)S(1)}, f32[1,1,1,3,64]{4,2,3,1,0:T(1,128)}, u32[]{:S(2)}) %copy-start.6) | copy-done | bytes 792
  2.0 0.1 shard_map.130.refs_0_
  2.0 3.0 %collective-permute-start = (f32[4,128]{1,0:T(4,128)S(1)}, f32[4,128]{1,0:T(4,128)S(1)}, u32[]{:S(2)}, u32[]{:S(2)}) collective-permute-start(f32[4,128]{1,0:T(4,128)S(1)} %shard_map.130.refs_0_), channel_id=1, source_target_pairs={{0,1},{1,0},{2,3},{3,2},{4,5},{5,4},{6,7},{7,6},{8,9},{9,8},{10,11... | collective-permute-start | bytes 6152 | tf_op jit(solution)/shard_map/ppermute | solution.py:428
  5.1 2.5 %collective-permute-start.1 = (f32[4,128]{1,0:T(4,128)S(1)}, f32[4,128]{1,0:T(4,128)S(1)}, u32[]{:S(2)}, u32[]{:S(2)}) collective-permute-start(f32[4,128]{1,0:T(4,128)S(1)} %shard_map.130.refs_0_), channel_id=1, source_target_pairs={{0,3},{1,2},{2,1},{3,0},{4,7},{5,6},{6,5},{7,4},{8,11},{9,10},{10,... | collective-permute-start | bytes 6152 | tf_op jit(solution)/shard_map/ppermute | solution.py:428
  7.5 2.9 %collective-permute-done.1 = f32[4,128]{1,0:T(4,128)S(1)} collective-permute-done((f32[4,128]{1,0:T(4,128)S(1)}, f32[4,128]{1,0:T(4,128)S(1)}, u32[]{:S(2)}, u32[]{:S(2)}) %collective-permute-start.1) | collective-permute-done | bytes 2080 | tf_op jit(solution)/shard_map/ppermute | solution.py:428
  10.5 1.6 %collective-permute-start.2 = (f32[3,4,128]{2,1,0:T(4,128)S(1)}, f32[3,4,128]{2,1,0:T(4,128)S(1)}, u32[]{:S(2)}, u32[]{:S(2)}) collective-permute-start(f32[3,4,128]{2,1,0:T(4,128)S(1)} %pad_maximum_fusion.2), channel_id=1, source_target_pairs={{0,8},{8,0},{16,24},{24,16},{1,9},{9,1},{17,25},{25,17},{2,10},{10... | collective-permute-start | bytes 18440 | tf_op jit(solution)/shard_map/ppermute | solution.py:428
  12.0 1.5 %collective-permute-start.3 = (f32[3,4,128]{2,1,0:T(4,128)S(1)}, f32[3,4,128]{2,1,0:T(4,128)S(1)}, u32[]{:S(2)}, u32[]{:S(2)}) collective-permute-start(f32[3,4,128]{2,1,0:T(4,128)S(1)} %pad_maximum_fusion.2), channel_id=1, source_target_pairs={{0,24},{8,16},{16,8},{24,0},{1,25},{9,17},{17,9},{25,1},{2,26},{10... | collective-permute-start | bytes 18440 | tf_op jit(solution)/shard_map/ppermute | solution.py:428
  13.5 0.6 collective-permute-done.2
  14.2 2.4 %collective-permute-done.3 = f32[3,4,128]{2,1,0:T(4,128)S(1)} collective-permute-done((f32[3,4,128]{2,1,0:T(4,128)S(1)}, f32[3,4,128]{2,1,0:T(4,128)S(1)}, u32[]{:S(2)}, u32[]{:S(2)}) %collective-permute-start.3) | collective-permute-done | bytes 6176 | tf_op jit(solution)/shard_map/ppermute | solution.py:428
  16.6 0.1 stack.71.refs_0_
  16.6 0.6 copy-done.4
  17.2 0.0 copy-done.5
  17.2 0.3 shard_map.131
  17.5 0.2 collective-permute-done.4.refs_2_
  17.7 2.4 %shard_map.132 = (f32[9,4,128]{2,1,0:T(4,128)S(1)}, bf16[4,64,1152]{2,1,0:T(8,128)(2,1)S(1)}, bf16[64,128]{1,0:T(8,128)(2,1)S(1)}, f32[192,128]{1,0:T(8,128)S(1)}, f32[64,128]{1,0:T(8,128)S(1)}) custom-call(s32[9]{0:T(128)S(1)} %stack.71.refs_0_, f32[9,4,128]{2,1,0:T(4,128)S(1)} %constant_dynamic-update-slice_fusion.refs_1_, ...), custom_call_target="tpu_custom_call" | custom-call | flops 7372800 | bytes 1048576 | tf_op jit(solution)/shard_map/pallas_call | solution.py:397
  20.2 0.1 collective-permute-start.5
  20.3 2.5 %collective-permute-start.6 = (bf16[64,128]{1,0:T(8,128)(2,1)S(1)}, bf16[64,128]{1,0:T(8,128)(2,1)S(1)}, u32[]{:S(2)}, u32[]{:S(2)}) collective-permute-start(bf16[64,128]{1,0:T(8,128)(2,1)S(1)} %get-tuple-element.20.refs_3_), channel_id=1, source_target_pairs={{0,3},{1,2},{2,1},{3,0},{4,7},{5,6},{6,5},{7,4},{8,11},{9,10},{10,... | collective-permute-start | bytes 49160 | tf_op jit(solution)/shard_map/ppermute | solution.py:428
  22.8 1.2 %collective-permute-done.5 = bf16[64,128]{1,0:T(8,128)(2,1)S(1)} collective-permute-done((bf16[64,128]{1,0:T(8,128)(2,1)S(1)}, bf16[64,128]{1,0:T(8,128)(2,1)S(1)}, u32[]{:S(2)}, u32[]{:S(2)}) %collective-permute-start.5) | collective-permute-done | bytes 16416 | tf_op jit(solution)/shard_map/ppermute | solution.py:428
  24.0 1.9 %collective-permute-done.6 = bf16[64,128]{1,0:T(8,128)(2,1)S(1)} collective-permute-done((bf16[64,128]{1,0:T(8,128)(2,1)S(1)}, bf16[64,128]{1,0:T(8,128)(2,1)S(1)}, u32[]{:S(2)}, u32[]{:S(2)}) %collective-permute-start.6) | collective-permute-done | bytes 16416 | tf_op jit(solution)/shard_map/ppermute | solution.py:428
  25.9 0.6 collective-permute-start.7
  26.5 2.4 %collective-permute-start.8 = (bf16[3,64,128]{2,1,0:T(8,128)(2,1)S(1)}, bf16[3,64,128]{2,1,0:T(8,128)(2,1)S(1)}, u32[]{:S(2)}, u32[]{:S(2)}) collective-permute-start(bf16[3,64,128]{2,1,0:T(8,128)(2,1)S(1)} %pad_maximum_fusion), channel_id=1, source_target_pairs={{0,24},{8,16},{16,8},{24,0},{1,25},{9,17},{17,9},{25,1},{2,26},{10... | collective-permute-start | bytes 147464 | tf_op jit(solution)/shard_map/ppermute | solution.py:428
  28.9 1.1 %collective-permute-done.7 = bf16[3,64,128]{2,1,0:T(8,128)(2,1)S(1)} collective-permute-done((bf16[3,64,128]{2,1,0:T(8,128)(2,1)S(1)}, bf16[3,64,128]{2,1,0:T(8,128)(2,1)S(1)}, u32[]{:S(2)}, u32[]{:S(2)}) %collective-permute-start.7) | collective-permute-done | bytes 49184 | tf_op jit(solution)/shard_map/ppermute | solution.py:428
  30.0 1.5 %collective-permute-done.8 = bf16[3,64,128]{2,1,0:T(8,128)(2,1)S(1)} collective-permute-done((bf16[3,64,128]{2,1,0:T(8,128)(2,1)S(1)}, bf16[3,64,128]{2,1,0:T(8,128)(2,1)S(1)}, u32[]{:S(2)}, u32[]{:S(2)}) %collective-permute-start.8) | collective-permute-done | bytes 49184 | tf_op jit(solution)/shard_map/ppermute | solution.py:428
  31.5 0.1 collective-permute-start.9
  31.6 1.4 %collective-permute-done.9.refs_2_ = bf16[9,64,128]{2,1,0:T(8,128)(2,1)S(1)} collective-permute-done((bf16[9,64,128]{2,1,0:T(8,128)(2,1)S(1)}, bf16[9,64,128]{2,1,0:T(8,128)(2,1)S(1)}, u32[]{:S(2)}, u32[]{:S(2)}) %collective-permute-start.9) | collective-permute-done | bytes 147488 | tf_op jit(solution)/shard_map/ppermute | solution.py:428
  33.0 0.7 %copy-done.2 = f32[4,128]{1,0:T(4,128)S(1)} copy-done((f32[4,128]{1,0:T(4,128)S(1)}, f32[4,128]{1,0:T(4,128)}, u32[]{:S(2)}) %copy-start.2) | copy-done | bytes 2072
  33.6 2.0 %shard_map.133 = (bf16[64,128]{1,0:T(8,128)(2,1)S(1)}, f32[1,64]{1,0:T(1,128)}, bf16[64,128]{1,0:T(8,128)(2,1)}, f32[64,128]{1,0:T(8,128)S(1)}) custom-call(s32[9]{0:T(128)S(1)} %stack.71.refs_0_, bf16[9,64,128]{2,1,0:T(8,128)(2,1)S(1)} %constant_dynamic-update-slice_fusion.5.refs_1_, bf16[9,64,128]{2,1,0:T(8,128)(2,1)S(1)} %collective-permute-done.9.refs_2_, ...), custom_call_target="tpu_custom_call" | custom-call | flops 7372800 | bytes 1048576 | tf_op jit(solution)/shard_map/pallas_call | solution.py:397
  35.7 0.1 collective-permute-start.10
  35.8 2.5 %collective-permute-start.11 = (bf16[64,128]{1,0:T(8,128)(2,1)S(1)}, bf16[64,128]{1,0:T(8,128)(2,1)S(1)}, u32[]{:S(2)}, u32[]{:S(2)}) collective-permute-start(bf16[64,128]{1,0:T(8,128)(2,1)S(1)} %get-tuple-element.22.refs_3_), channel_id=1, source_target_pairs={{0,3},{1,2},{2,1},{3,0},{4,7},{5,6},{6,5},{7,4},{8,11},{9,10},{10,... | collective-permute-start | bytes 49160 | tf_op jit(solution)/shard_map/ppermute | solution.py:428
  38.3 1.1 %collective-permute-done.10 = bf16[64,128]{1,0:T(8,128)(2,1)S(1)} collective-permute-done((bf16[64,128]{1,0:T(8,128)(2,1)S(1)}, bf16[64,128]{1,0:T(8,128)(2,1)S(1)}, u32[]{:S(2)}, u32[]{:S(2)}) %collective-permute-start.10) | collective-permute-done | bytes 16416 | tf_op jit(solution)/shard_map/ppermute | solution.py:428
  39.4 1.9 %collective-permute-done.11 = bf16[64,128]{1,0:T(8,128)(2,1)S(1)} collective-permute-done((bf16[64,128]{1,0:T(8,128)(2,1)S(1)}, bf16[64,128]{1,0:T(8,128)(2,1)S(1)}, u32[]{:S(2)}, u32[]{:S(2)}) %collective-permute-start.11) | collective-permute-done | bytes 16416 | tf_op jit(solution)/shard_map/ppermute | solution.py:428
  41.4 1.5 %collective-permute-start.12 = (bf16[3,64,128]{2,1,0:T(8,128)(2,1)S(1)}, bf16[3,64,128]{2,1,0:T(8,128)(2,1)S(1)}, u32[]{:S(2)}, u32[]{:S(2)}) collective-permute-start(bf16[3,64,128]{2,1,0:T(8,128)(2,1)S(1)} %pad_maximum_fusion.1), channel_id=1, source_target_pairs={{0,8},{8,0},{16,24},{24,16},{1,9},{9,1},{17,25},{25,17},{2,10},{10... | collective-permute-start | bytes 147464 | tf_op jit(solution)/shard_map/ppermute | solution.py:428
  42.9 1.5 %collective-permute-start.13 = (bf16[3,64,128]{2,1,0:T(8,128)(2,1)S(1)}, bf16[3,64,128]{2,1,0:T(8,128)(2,1)S(1)}, u32[]{:S(2)}, u32[]{:S(2)}) collective-permute-start(bf16[3,64,128]{2,1,0:T(8,128)(2,1)S(1)} %pad_maximum_fusion.1), channel_id=1, source_target_pairs={{0,24},{8,16},{16,8},{24,0},{1,25},{9,17},{17,9},{25,1},{2,26},{10... | collective-permute-start | bytes 147464 | tf_op jit(solution)/shard_map/ppermute | solution.py:428
  44.4 1.7 %collective-permute-done.12 = bf16[3,64,128]{2,1,0:T(8,128)(2,1)S(1)} collective-permute-done((bf16[3,64,128]{2,1,0:T(8,128)(2,1)S(1)}, bf16[3,64,128]{2,1,0:T(8,128)(2,1)S(1)}, u32[]{:S(2)}, u32[]{:S(2)}) %collective-permute-start.12) | collective-permute-done | bytes 49184 | tf_op jit(solution)/shard_map/ppermute | solution.py:428
  46.1 1.8 %collective-permute-done.13 = bf16[3,64,128]{2,1,0:T(8,128)(2,1)S(1)} collective-permute-done((bf16[3,64,128]{2,1,0:T(8,128)(2,1)S(1)}, bf16[3,64,128]{2,1,0:T(8,128)(2,1)S(1)}, u32[]{:S(2)}, u32[]{:S(2)}) %collective-permute-start.13) | collective-permute-done | bytes 49184 | tf_op jit(solution)/shard_map/ppermute | solution.py:428
  47.9 0.1 collective-permute-start.14
  48.0 1.7 %shard_map.134 = (bf16[4,64,1152]{2,1,0:T(8,128)(2,1)S(1)}, f32[64,1152]{1,0:T(8,128)S(1)}) custom-call(s32[9]{0:T(128)S(1)} %stack.71.refs_0_, bf16[9,64,128]{2,1,0:T(8,128)(2,1)S(1)} %constant_dynamic-update-slice_fusion.5.refs_1_, bf16[9,64,128]{2,1,0:T(8,128)(2,1)S(1)} %collective-permute-done.9.refs_2_, bf16[64,128]{1,0:T(8,128)(2,1)S(1)} %get-tuple-element.22.refs_3_, ...), custom_call_target="tpu_custom_call" | custom-call | flops 7372800 | bytes 1048576 | tf_op jit(solution)/shard_map/pallas_call | solution.py:397
  49.6 2.8 %shard_map.135 = f32[9,3,128]{2,1,0:T(4,128)S(1)} custom-call(s32[9]{0:T(128)S(1)} %stack.71.refs_0_, bf16[9,64,128]{2,1,0:T(8,128)(2,1)S(1)} %constant_dynamic-update-slice_fusion.10.refs_1_, bf16[9,64,128]{2,1,0:T(8,128)(2,1)S(1)} %collective-permute-done.14.refs_2_, f32[64,128]{1,0:T(8,128)S(1)} %get-tuple-element.23.refs_3_, ...), custom_call_target="tpu_custom_call" | custom-call | flops 7372800 | bytes 1048576 | tf_op jit(solution)/shard_map/pallas_call | solution.py:397
  52.5 1.6 %collective-permute-start.15 = (f32[3,3,128]{2,1,0:T(4,128)S(1)}, f32[3,3,128]{2,1,0:T(4,128)S(1)}, u32[]{:S(2)}, u32[]{:S(2)}) collective-permute-start(f32[3,3,128]{2,1,0:T(4,128)S(1)} %get-tuple-element.34), channel_id=1, source_target_pairs={{24,0},{16,8},{8,16},{0,24},{25,1},{17,9},{9,17},{1,25},{26,2},{18... | collective-permute-start | bytes 13832 | tf_op jit(solution)/shard_map/ppermute | solution.py:440
  54.1 1.5 %collective-permute-start.16 = (f32[3,3,128]{2,1,0:T(4,128)S(1)}, f32[3,3,128]{2,1,0:T(4,128)S(1)}, u32[]{:S(2)}, u32[]{:S(2)}) collective-permute-start(f32[3,3,128]{2,1,0:T(4,128)S(1)} %get-tuple-element.35), channel_id=1, source_target_pairs={{8,0},{0,8},{24,16},{16,24},{9,1},{1,9},{25,17},{17,25},{10,2},{2,... | collective-permute-start | bytes 13832 | tf_op jit(solution)/shard_map/ppermute | solution.py:440
  55.5 1.5 %collective-permute-done.15 = f32[3,3,128]{2,1,0:T(4,128)S(1)} collective-permute-done((f32[3,3,128]{2,1,0:T(4,128)S(1)}, f32[3,3,128]{2,1,0:T(4,128)S(1)}, u32[]{:S(2)}, u32[]{:S(2)}) %collective-permute-start.15) | collective-permute-done | bytes 4640 | tf_op jit(solution)/shard_map/ppermute | solution.py:440
  57.1 0.6 collective-permute-done.16
  57.7 2.5 %collective-permute-start.17 = (f32[1,3,128]{2,1,0:T(4,128)S(1)}, f32[1,3,128]{2,1,0:T(4,128)S(1)}, u32[]{:S(2)}, u32[]{:S(2)}) collective-permute-start(f32[1,3,128]{2,1,0:T(4,128)S(1)} %get-tuple-element.36), channel_id=1, source_target_pairs={{3,0},{2,1},{1,2},{0,3},{7,4},{6,5},{5,6},{4,7},{11,8},{10,9},{9,1... | collective-permute-start | bytes 4616 | tf_op jit(solution)/shard_map/ppermute | solution.py:440
  60.2 2.9 %collective-permute-done.17 = f32[1,3,128]{2,1,0:T(4,128)S(1)} collective-permute-done((f32[1,3,128]{2,1,0:T(4,128)S(1)}, f32[1,3,128]{2,1,0:T(4,128)S(1)}, u32[]{:S(2)}, u32[]{:S(2)}) %collective-permute-start.17) | collective-permute-done | bytes 1568 | tf_op jit(solution)/shard_map/ppermute | solution.py:440
  63.1 0.7 %collective-permute-done.18 = f32[1,3,128]{2,1,0:T(4,128)S(1)} collective-permute-done((f32[1,3,128]{2,1,0:T(4,128)S(1)}, f32[1,3,128]{2,1,0:T(4,128)S(1)}, u32[]{:S(2)}, u32[]{:S(2)}) %collective-permute-start.18) | collective-permute-done | bytes 1568 | tf_op jit(solution)/shard_map/ppermute | solution.py:440
  63.8 0.1 slice.37
  63.8 1.1 %collective-permute-done.19 = f32[3,64]{1,0:T(4,128)S(1)} collective-permute-done((f32[3,64]{1,0:T(4,128)S(1)}, f32[3,64]{1,0:T(4,128)S(1)}, u32[]{:S(2)}, u32[]{:S(2)}) %collective-permute-start.19) | collective-permute-done | bytes 800 | tf_op jit(solution)/shard_map/ppermute | solution.py:440
  65.0 0.6 copy.14
  (44 shorter events, 0.2 us)
Async XLA Ops:
  1.3 0.7 %copy-start.6 = (f32[1,1,1,3,64]{4,2,3,1,0:T(1,128)S(1)}, f32[1,1,1,3,64]{4,2,3,1,0:T(1,128)}, u32[]{:S(2)}) copy-start(f32[1,1,1,3,64]{4,2,3,1,0:T(1,128)} %param.11) | copy-start | bytes 2308
  1.3 0.7 %copy-start.9 = (s32[1,1,1,64]{3,2,1,0:T(1,128)S(1)}, s32[1,1,1,64]{3,2,1,0:T(1,128)}, u32[]{:S(2)}) copy-start(s32[1,1,1,64]{3,2,1,0:T(1,128)} %param.12) | copy-start | bytes 772
  2.0 5.5 %collective-permute-start = (f32[4,128]{1,0:T(4,128)S(1)}, f32[4,128]{1,0:T(4,128)S(1)}, u32[]{:S(2)}, u32[]{:S(2)}) collective-permute-start(f32[4,128]{1,0:T(4,128)S(1)} %shard_map.130.refs_0_), channel_id=1, source_target_pairs={{0,1},{1,0},{2,3},{3,2},{4,5},{5,4},{6,7},{7,6},{8,9},{9,8},{10,11... | collective-permute-start | bytes 6152 | tf_op jit(solution)/shard_map/ppermute | solution.py:428
  5.1 5.4 %collective-permute-start.1 = (f32[4,128]{1,0:T(4,128)S(1)}, f32[4,128]{1,0:T(4,128)S(1)}, u32[]{:S(2)}, u32[]{:S(2)}) collective-permute-start(f32[4,128]{1,0:T(4,128)S(1)} %shard_map.130.refs_0_), channel_id=1, source_target_pairs={{0,3},{1,2},{2,1},{3,0},{4,7},{5,6},{6,5},{7,4},{8,11},{9,10},{10,... | collective-permute-start | bytes 6152 | tf_op jit(solution)/shard_map/ppermute | solution.py:428
  10.4 7.3 %copy-start = (bf16[128,256]{1,0:T(8,128)(2,1)S(1)}, bf16[128,256]{1,0:T(8,128)(2,1)}, u32[]{:S(2)}) copy-start(bf16[128,256]{1,0:T(8,128)(2,1)} %refs_11_.1) | copy-start | bytes 196612
  10.5 3.7 %collective-permute-start.2 = (f32[3,4,128]{2,1,0:T(4,128)S(1)}, f32[3,4,128]{2,1,0:T(4,128)S(1)}, u32[]{:S(2)}, u32[]{:S(2)}) collective-permute-start(f32[3,4,128]{2,1,0:T(4,128)S(1)} %pad_maximum_fusion.2), channel_id=1, source_target_pairs={{0,8},{8,0},{16,24},{24,16},{1,9},{9,1},{17,25},{25,17},{2,10},{10... | collective-permute-start | bytes 18440 | tf_op jit(solution)/shard_map/ppermute | solution.py:428
  12.0 4.5 %collective-permute-start.3 = (f32[3,4,128]{2,1,0:T(4,128)S(1)}, f32[3,4,128]{2,1,0:T(4,128)S(1)}, u32[]{:S(2)}, u32[]{:S(2)}) collective-permute-start(f32[3,4,128]{2,1,0:T(4,128)S(1)} %pad_maximum_fusion.2), channel_id=1, source_target_pairs={{0,24},{8,16},{16,8},{24,0},{1,25},{9,17},{17,9},{25,1},{2,26},{10... | collective-permute-start | bytes 18440 | tf_op jit(solution)/shard_map/ppermute | solution.py:428
  16.5 1.2 %collective-permute-start.4 = (f32[9,4,128]{2,1,0:T(4,128)S(1)}, f32[9,4,128]{2,1,0:T(4,128)S(1)}, u32[]{:S(2)}, u32[]{:S(2)}) collective-permute-start(f32[9,4,128]{2,1,0:T(4,128)S(1)} %constant_dynamic-update-slice_fusion.refs_1_), channel_id=1, source_target_pairs={{0,4},{4,0},{1,5},{5,1},{2,6},{6,2},{3,7},{7,3},{8,12},{12,8},{9,1... | collective-permute-start | bytes 55304 | tf_op jit(solution)/shard_map/ppermute | solution.py:428
  16.5 0.7 %copy-start.4 = (f32[2,4,128]{2,1,0:T(4,128)S(1)}, f32[2,4,128]{2,1,0:T(4,128)}, u32[]{:S(2)}) copy-start(f32[2,4,128]{2,1,0:T(4,128)} %refs_2_.1) | copy-start | bytes 12292
  16.5 0.7 %copy-start.5 = (bf16[8,128]{1,0:T(8,128)(2,1)S(1)}, bf16[8,128]{1,0:T(8,128)(2,1)}, u32[]{:S(2)}) copy-start(bf16[8,128]{1,0:T(8,128)(2,1)} %refs_1_.1) | copy-start | bytes 6148
  20.2 3.8 %collective-permute-start.5 = (bf16[64,128]{1,0:T(8,128)(2,1)S(1)}, bf16[64,128]{1,0:T(8,128)(2,1)S(1)}, u32[]{:S(2)}, u32[]{:S(2)}) collective-permute-start(bf16[64,128]{1,0:T(8,128)(2,1)S(1)} %get-tuple-element.20.refs_3_), channel_id=1, source_target_pairs={{0,1},{1,0},{2,3},{3,2},{4,5},{5,4},{6,7},{7,6},{8,9},{9,8},{10,11... | collective-permute-start | bytes 49160 | tf_op jit(solution)/shard_map/ppermute | solution.py:428
  20.3 5.6 %collective-permute-start.6 = (bf16[64,128]{1,0:T(8,128)(2,1)S(1)}, bf16[64,128]{1,0:T(8,128)(2,1)S(1)}, u32[]{:S(2)}, u32[]{:S(2)}) collective-permute-start(bf16[64,128]{1,0:T(8,128)(2,1)S(1)} %get-tuple-element.20.refs_3_), channel_id=1, source_target_pairs={{0,3},{1,2},{2,1},{3,0},{4,7},{5,6},{6,5},{7,4},{8,11},{9,10},{10,... | collective-permute-start | bytes 49160 | tf_op jit(solution)/shard_map/ppermute | solution.py:428
  25.9 4.2 %collective-permute-start.7 = (bf16[3,64,128]{2,1,0:T(8,128)(2,1)S(1)}, bf16[3,64,128]{2,1,0:T(8,128)(2,1)S(1)}, u32[]{:S(2)}, u32[]{:S(2)}) collective-permute-start(bf16[3,64,128]{2,1,0:T(8,128)(2,1)S(1)} %pad_maximum_fusion), channel_id=1, source_target_pairs={{0,8},{8,0},{16,24},{24,16},{1,9},{9,1},{17,25},{25,17},{2,10},{10... | collective-permute-start | bytes 147464 | tf_op jit(solution)/shard_map/ppermute | solution.py:428
  26.5 5.0 %collective-permute-start.8 = (bf16[3,64,128]{2,1,0:T(8,128)(2,1)S(1)}, bf16[3,64,128]{2,1,0:T(8,128)(2,1)S(1)}, u32[]{:S(2)}, u32[]{:S(2)}) collective-permute-start(bf16[3,64,128]{2,1,0:T(8,128)(2,1)S(1)} %pad_maximum_fusion), channel_id=1, source_target_pairs={{0,24},{8,16},{16,8},{24,0},{1,25},{9,17},{17,9},{25,1},{2,26},{10... | collective-permute-start | bytes 147464 | tf_op jit(solution)/shard_map/ppermute | solution.py:428
  30.0 2.9 %copy-start.1 = (bf16[128,128]{1,0:T(8,128)(2,1)S(1)}, bf16[128,128]{1,0:T(8,128)(2,1)}, u32[]{:S(2)}) copy-start(bf16[128,128]{1,0:T(8,128)(2,1)} %refs_7_.1) | copy-start | bytes 98308
  31.5 1.5 %copy-start.3 = (bf16[16,128]{1,0:T(8,128)(2,1)S(1)}, bf16[16,128]{1,0:T(8,128)(2,1)}, u32[]{:S(2)}) copy-start(bf16[16,128]{1,0:T(8,128)(2,1)} %refs_8_.1) | copy-start | bytes 12292
  31.5 1.4 %collective-permute-start.9 = (bf16[9,64,128]{2,1,0:T(8,128)(2,1)S(1)}, bf16[9,64,128]{2,1,0:T(8,128)(2,1)S(1)}, u32[]{:S(2)}, u32[]{:S(2)}) collective-permute-start(bf16[9,64,128]{2,1,0:T(8,128)(2,1)S(1)} %constant_dynamic-update-slice_fusion.5.refs_1_), channel_id=1, source_target_pairs={{0,4},{4,0},{1,5},{5,1},{2,6},{6,2},{3,7},{7,3},{8,12},{12,8},{9,1... | collective-permute-start | bytes 442376 | tf_op jit(solution)/shard_map/ppermute | solution.py:428
  33.0 0.7 %copy-start.2 = (f32[4,128]{1,0:T(4,128)S(1)}, f32[4,128]{1,0:T(4,128)}, u32[]{:S(2)}) copy-start(f32[4,128]{1,0:T(4,128)} %refs_9_.1) | copy-start | bytes 6148
  33.0 0.7 %copy-start.7 = (f32[16]{0:T(128)S(1)}, f32[16]{0:T(128)}, u32[]{:S(2)}) copy-start(f32[16]{0:T(128)} %param.21) | copy-start | bytes 196
  33.0 0.7 %copy-start.8 = (f32[128]{0:T(128)S(1)}, f32[128]{0:T(128)}, u32[]{:S(2)}) copy-start(f32[128]{0:T(128)} %param.17) | copy-start | bytes 1540
  35.7 3.7 %collective-permute-start.10 = (bf16[64,128]{1,0:T(8,128)(2,1)S(1)}, bf16[64,128]{1,0:T(8,128)(2,1)S(1)}, u32[]{:S(2)}, u32[]{:S(2)}) collective-permute-start(bf16[64,128]{1,0:T(8,128)(2,1)S(1)} %get-tuple-element.22.refs_3_), channel_id=1, source_target_pairs={{0,1},{1,0},{2,3},{3,2},{4,5},{5,4},{6,7},{7,6},{8,9},{9,8},{10,11... | collective-permute-start | bytes 49160 | tf_op jit(solution)/shard_map/ppermute | solution.py:428
  35.8 5.5 %collective-permute-start.11 = (bf16[64,128]{1,0:T(8,128)(2,1)S(1)}, bf16[64,128]{1,0:T(8,128)(2,1)S(1)}, u32[]{:S(2)}, u32[]{:S(2)}) collective-permute-start(bf16[64,128]{1,0:T(8,128)(2,1)S(1)} %get-tuple-element.22.refs_3_), channel_id=1, source_target_pairs={{0,3},{1,2},{2,1},{3,0},{4,7},{5,6},{6,5},{7,4},{8,11},{9,10},{10,... | collective-permute-start | bytes 49160 | tf_op jit(solution)/shard_map/ppermute | solution.py:428
  41.4 4.7 %collective-permute-start.12 = (bf16[3,64,128]{2,1,0:T(8,128)(2,1)S(1)}, bf16[3,64,128]{2,1,0:T(8,128)(2,1)S(1)}, u32[]{:S(2)}, u32[]{:S(2)}) collective-permute-start(bf16[3,64,128]{2,1,0:T(8,128)(2,1)S(1)} %pad_maximum_fusion.1), channel_id=1, source_target_pairs={{0,8},{8,0},{16,24},{24,16},{1,9},{9,1},{17,25},{25,17},{2,10},{10... | collective-permute-start | bytes 147464 | tf_op jit(solution)/shard_map/ppermute | solution.py:428
  42.9 5.0 %collective-permute-start.13 = (bf16[3,64,128]{2,1,0:T(8,128)(2,1)S(1)}, bf16[3,64,128]{2,1,0:T(8,128)(2,1)S(1)}, u32[]{:S(2)}, u32[]{:S(2)}) collective-permute-start(bf16[3,64,128]{2,1,0:T(8,128)(2,1)S(1)} %pad_maximum_fusion.1), channel_id=1, source_target_pairs={{0,24},{8,16},{16,8},{24,0},{1,25},{9,17},{17,9},{25,1},{2,26},{10... | collective-permute-start | bytes 147464 | tf_op jit(solution)/shard_map/ppermute | solution.py:428
  47.9 1.7 %collective-permute-start.14 = (bf16[9,64,128]{2,1,0:T(8,128)(2,1)S(1)}, bf16[9,64,128]{2,1,0:T(8,128)(2,1)S(1)}, u32[]{:S(2)}, u32[]{:S(2)}) collective-permute-start(bf16[9,64,128]{2,1,0:T(8,128)(2,1)S(1)} %constant_dynamic-update-slice_fusion.10.refs_1_), channel_id=1, source_target_pairs={{0,4},{4,0},{1,5},{5,1},{2,6},{6,2},{3,7},{7,3},{8,12},{12,8},{9,1... | collective-permute-start | bytes 442376 | tf_op jit(solution)/shard_map/ppermute | solution.py:428
  52.5 4.6 %collective-permute-start.15 = (f32[3,3,128]{2,1,0:T(4,128)S(1)}, f32[3,3,128]{2,1,0:T(4,128)S(1)}, u32[]{:S(2)}, u32[]{:S(2)}) collective-permute-start(f32[3,3,128]{2,1,0:T(4,128)S(1)} %get-tuple-element.34), channel_id=1, source_target_pairs={{24,0},{16,8},{8,16},{0,24},{25,1},{17,9},{9,17},{1,25},{26,2},{18... | collective-permute-start | bytes 13832 | tf_op jit(solution)/shard_map/ppermute | solution.py:440
  54.1 3.6 %collective-permute-start.16 = (f32[3,3,128]{2,1,0:T(4,128)S(1)}, f32[3,3,128]{2,1,0:T(4,128)S(1)}, u32[]{:S(2)}, u32[]{:S(2)}) collective-permute-start(f32[3,3,128]{2,1,0:T(4,128)S(1)} %get-tuple-element.35), channel_id=1, source_target_pairs={{8,0},{0,8},{24,16},{16,24},{9,1},{1,9},{25,17},{17,25},{10,2},{2,... | collective-permute-start | bytes 13832 | tf_op jit(solution)/shard_map/ppermute | solution.py:440
  57.7 5.4 %collective-permute-start.17 = (f32[1,3,128]{2,1,0:T(4,128)S(1)}, f32[1,3,128]{2,1,0:T(4,128)S(1)}, u32[]{:S(2)}, u32[]{:S(2)}) collective-permute-start(f32[1,3,128]{2,1,0:T(4,128)S(1)} %get-tuple-element.36), channel_id=1, source_target_pairs={{3,0},{2,1},{1,2},{0,3},{7,4},{6,5},{5,6},{4,7},{11,8},{10,9},{9,1... | collective-permute-start | bytes 4616 | tf_op jit(solution)/shard_map/ppermute | solution.py:440
  60.2 3.6 %collective-permute-start.18 = (f32[1,3,128]{2,1,0:T(4,128)S(1)}, f32[1,3,128]{2,1,0:T(4,128)S(1)}, u32[]{:S(2)}, u32[]{:S(2)}) collective-permute-start(f32[1,3,128]{2,1,0:T(4,128)S(1)} %get-tuple-element.37), channel_id=1, source_target_pairs={{1,0},{0,1},{3,2},{2,3},{5,4},{4,5},{7,6},{6,7},{9,8},{8,9},{11,10... | collective-permute-start | bytes 4616 | tf_op jit(solution)/shard_map/ppermute | solution.py:440
  63.8 1.2 %collective-permute-start.19 = (f32[3,64]{1,0:T(4,128)S(1)}, f32[3,64]{1,0:T(4,128)S(1)}, u32[]{:S(2)}, u32[]{:S(2)}) collective-permute-start(f32[3,64]{1,0:T(4,128)S(1)} %slice.37), channel_id=1, source_target_pairs={{4,0},{0,4},{5,1},{1,5},{6,2},{2,6},{7,3},{3,7},{12,8},{8,12},{13,... | collective-permute-start | bytes 2312 | tf_op jit(solution)/shard_map/ppermute | solution.py:440

commit v2 on v1

--- a/solution.py
+++ b/solution.py
@@ -82,20 +82,36 @@
         self.far = len(self.tiles) * self.width
         self.nbasis = nbasis
         self.nspec = nspec
+        self.depth = len(offsets_of(self.sizes["gz"]))
+        self.wide = len(offsets_of(self.sizes["gx"]))
+        self.small = self.ndev <= 64 and len(self.sides) == 2
         self.wrapped = [self.sizes[axis] == 2 for axis in AXES]
 
-    def tile_places(self):
-        def place(axis, offset):
-            count = self.sizes[axis]
-            order = offsets_of(count).index(offset)
-            if order == 0 or not paired(count):
-                return jnp.int32(order)
-            parity = lax.rem(lax.axis_index(axis), 2)
-            return 1 + parity if offset == 1 else 2 - parity
+    def places(self):
+        index = {axis: lax.axis_index(axis) for axis in AXES}
+
+        def parity(axis):
+            return 1 - lax.rem(index[axis], 2) if paired(self.sizes[axis]) else jnp.int32(0)
+
+        def moved(axis, step):
+            return lax.rem(index[axis] + (step + self.sizes[axis]), self.sizes[axis])
 
         depth = len(offsets_of(self.sizes["gz"]))
-        places = [place("gx", ox) * depth + place("gz", oz) for ox, oz in self.tiles]
-        return jnp.stack(places).astype(jnp.int32)
+        turn = parity("gz")
+        found = [jnp.int32(0), 1 + turn, 2 - turn][:depth] + [parity("gx")]
+        for ox, oz in self.tiles:
+            for oy in self.sides:
+                place = (moved("gx", ox) * self.sizes["gy"] + moved("gy", oy)) * self.sizes["gz"]
+                found.append(place + moved("gz", oz))
+        return jnp.stack(found).astype(jnp.int32)
+
+    def global_place(self, places_ref, tile, side):
+        return places_ref[self.depth + 1 + tile * len(self.sides) + side]
+
+    def staged_place(self, places_ref, tile):
+        x, z = divmod(tile, self.depth)
+        flip = places_ref[self.depth]
+        return (0, 1 + flip, 2 - flip)[x] * self.depth + places_ref[z]
 
     def offset(self, tile, side):
         ox, oz = self.tiles[tile]
@@ -136,7 +152,7 @@
     species = lax.broadcasted_iota(jnp.int32, (nbasis * nspec, plan.width), 0) % nspec
     hot = []
     for tile in range(len(plan.tiles)):
-        blocks = [fetch(places_ref, far_refs, tile, side) for side in range(len(plan.sides))]
+        blocks = [fetch(plan, places_ref, far_refs, tile, side) for side in range(len(plan.sides))]
         placed = side_by_side(plan, blocks) + tile_shift(plan, tile)
         rows_ref[tile] = placed
         rows = [placed[k : k + 1] for k in range(4)]
@@ -182,8 +198,16 @@
     return 1.0 / (1.0 + jnp.exp(-value))
 
 
-def fetch(places_ref, far_refs, tile, side):
-    return far_refs[side][places_ref[tile]]
+def fetch(plan, places_ref, far_refs, tile, side):
+    if len(far_refs) == 1:
+        return far_refs[0][plan.global_place(places_ref, tile, side)]
+    x, z = divmod(tile, plan.depth)
+    place = places_ref[z]
+    columns = far_refs[side * plan.wide : (side + 1) * plan.wide]
+    if x == 0 or plan.wide == 2:
+        return columns[x][place]
+    kept, other = columns[x][place], columns[3 - x][place]
+    return jnp.where(places_ref[plan.depth] == 0, kept, other)
 
 
 def side_by_side(plan, blocks):
@@ -209,7 +233,7 @@
     for tile in range(len(plan.tiles)):
         for side in range(len(plan.sides)):
             start = tile * plan.width + side * slots
-            all_ref[start : start + slots] = fetch(places_ref, far_refs, tile, side)
+            all_ref[start : start + slots] = fetch(plan, places_ref, far_refs, tile, side)
 
 
 def second_kernel(plan, nrefs, places_ref, *refs):
@@ -342,12 +366,20 @@
             pulls[-1].append(jnp.sum(pull, axis=0, keepdims=True))
     ones = jnp.ones((8, width), F32)
     mine = jnp.concatenate([dot_exact(ones, own[k], NT)[:1] for k in range(3)], axis=0)
+    if plan.small:
+        out_ref[...] = jnp.zeros_like(out_ref)
+    side_of = lax.broadcasted_iota(jnp.int32, (3, width), 1) // slots
     for tile in range(len(plan.tiles)):
         pulled = jnp.concatenate(pulls[tile], axis=0)
         if tile == 0:
             others = [jnp.zeros_like(mine)] * (len(plan.sides) - 1)
             pulled = pulled - jnp.concatenate([mine] + others, axis=1)
-        out_ref[places_ref[tile]] = pulled
+        if not plan.small:
+            out_ref[plan.staged_place(places_ref, tile)] = pulled
+            continue
+        for side in range(len(plan.sides)):
+            place = plan.global_place(places_ref, tile, side)
+            out_ref[place, :3] = jnp.where(side_of == side, pulled, 0.0)
 
 
 def prepare_kernel(plan, counts_ref, place_ref, kind_ref, sent_ref):
@@ -360,12 +392,25 @@
     ]
     rows = jnp.concatenate(rows, axis=0)
     rows = jnp.concatenate([rows, rows], axis=1)
-    sent_ref[...] = rows
-
-
-def own_kernel(plan, sent_ref, embed_ref, radial_ref, cols_ref, table_ref, own_ref):
+    for copy in range(sent_ref.shape[0]):
+        sent_ref[copy] = rows
+
+
+def sum_kernel(plan, parts_ref, force_ref):
+    total = parts_ref[0]
+    for part in range(1, parts_ref.shape[0]):
+        total = total + parts_ref[part]
+    total = total[:, : plan.slots] + total[:, plan.slots :]
+    for k in range(3):
+        force_ref[k] = -total[k : k + 1]
+
+
+def own_kernel(plan, sent_ref, embed_ref, radial_ref, *refs):
+    weight_refs, (cols_ref, table_ref, own_ref), kept_refs = refs[:3], refs[3:6], refs[6:]
+    for weight_ref, kept_ref in zip(weight_refs, kept_refs):
+        kept_ref[...] = weight_ref[...]
     slots, nspec = plan.slots, plan.nspec
-    rows = sent_ref[...]
+    rows = sent_ref[0]
     cols = jnp.concatenate([rows, rows], axis=0).T[:slots]
     kind = cols[:, 3:4]
     lane = lax.broadcasted_iota(jnp.int32, cols.shape, 1)
@@ -420,19 +465,22 @@
     if paired(count):
         near = [(i, i ^ 1) for i in range(count)]
         far = [(i, (i - 1 + 2 * (i % 2)) % count) for i in range(count)]
-        return [near, far]
+        return [far, near]
     return [[((i + o) % count, i) for i in range(count)] for o in offsets_of(count)[1:]]
 
 
 def brought(block, axis):
-    got = [lax.ppermute(block, axis, pairs) for pairs in swaps(axis)[::-1]]
-    return [block] + got[::-1]
+    return [block] + [lax.ppermute(block, axis, pairs) for pairs in swaps(axis)]
 
 
 def neighbours(plan, block):
-    stacked = jnp.stack(brought(block, "gz"))
-    stacked = jnp.concatenate(brought(stacked, "gx"))
-    return brought(stacked, "gy")
+    columns = brought(jnp.stack(brought(block, "gz")), "gx")
+    swapped = [brought(column, "gy") for column in columns]
+    return [column[side] for side in range(len(plan.sides)) for column in swapped]
+
+
+def everywhere(copies):
+    return lax.all_to_all(copies, AXES, 0, 0, tiled=True)
 
 
 def folded(pieces, axis):
@@ -478,20 +526,22 @@
             prepare_kernel,
             plan,
             [counts.reshape(1), place, species.reshape(1, slots)],
-            ((4, 2 * slots), F32),
+            ((plan.ndev if plan.small else 1, 4, 2 * slots), F32),
             1,
         )
-        places = plan.tile_places()
-        far_sent = neighbours(plan, sent)
-        cols, table, own_embed = simple_call(
+        places = plan.places()
+        far_sent = [everywhere(sent)] if plan.small else neighbours(plan, sent[0])
+        weights = [radial_two, read_out[None], read_one[None]]
+        cols, table, own_embed, radial_two, out_row, one_row = simple_call(
             own_kernel,
             plan,
-            [sent, embed, radial_one],
+            [sent, embed, radial_one] + weights,
             [
                 ((slots, 8), F32),
                 ((2, nbasis * nspec, channels), BF16),
                 ((slots, channels), F32),
-            ],
+            ]
+            + [(weight.shape, weight.dtype) for weight in weights],
         )
         pair_flops = 100 * slots * plan.far
         rows, basis, layer, vector, mixing = call(
@@ -512,7 +562,6 @@
         )
         far_layer = neighbours(plan, layer)
         far_scratch = ((plan.far, channels), BF16)
-        one_row, out_row = read_one[None], read_out[None]
         adjoint, energy, features, own_adjoint = call(
             second_kernel,
             plan,
@@ -545,11 +594,14 @@
             far_adjoint,
             places,
             [own_adjoint, basis, slope, pair, rows, cols, radial_two, mixing, mix_one, vector, table],
-            [((len(plan.tiles), 3, plan.width), F32)],
+            [((plan.ndev, 4, plan.width) if plan.small else (len(plan.tiles), 3, plan.width), F32)],
             [far_scratch],
             pair_flops,
         )
-        forces = -fold(plan, pulls[0])
+        if plan.small:
+            forces = simple_call(sum_kernel, plan, [everywhere(pulls[0])], ((3, 1, slots), F32))
+        else:
+            forces = -fold(plan, pulls[0])
         return (
             forces.reshape(1, 1, 1, 3, slots),
             energy[None, None],

time: 65.8 us -> 61.9 us (0.941)
  blocking collectives: 0 us -> 10.5 us
  starting transfers between devices: 25.5 us -> 15.7 us
  waiting for transfers between devices: 26.5 us -> 21.1 us
  Pallas kernels: 9.32 us -> 11.5 us
  local copies, waits for them, and re-layouts: 2.8 us -> 1.35 us
    ppermute x20 -> x14, starting transfers between devices: 25.5 us -> 8.41 us  [brought(): return [block] + [lax.ppermute(block, axis, pairs) for pairs in swaps(axis)]]
    ppermute x20 -> x14, waiting for transfers between devices: 26.5 us -> 15.4 us  [brought(): return [block] + [lax.ppermute(block, axis, pairs) for pairs in swaps(axis)]]
    all_to_all x0 -> x1, blocking collectives: none -> 10.5 us  [everywhere(): return lax.all_to_all(copies, AXES, 0, 0, tiled=True)]
    all_to_all x0 -> x1, starting transfers between devices: none -> 7.3 us  [everywhere(): return lax.all_to_all(copies, AXES, 0, 0, tiled=True)]
    all_to_all x0 -> x1, waiting for transfers between devices: none -> 5.63 us  [everywhere(): return lax.all_to_all(copies, AXES, 0, 0, tiled=True)]
    pallas_call x6 -> x7, Pallas kernels: 9.32 us -> 11.5 us  [simple_call(): pl.pallas_call(body, out_shape=shapes, in_specs=[SMEM_SPEC] * scalars + [...]
    unnamed x33 -> x20, local copies, waits for them, and re-layouts: 2.6 us -> 1.25 us
  transfers between devices with their start and end apart: 20 -> 15, of which waited for: 18 -> 9; matrix products, arithmetic and copies ran while one was open for 0% -> 0% of each run, Pallas kernels for 3% -> 5%
where the time goes in v2:
time: 61.9 us; the launch traced here: 61.6 us
  waiting for transfers between devices  21.1 us (34%)
  starting transfers between devices  15.7 us (25%)
  Pallas kernels  11.5 us (19%)
  blocking collectives  10.5 us (17%)
  between operations  1.46 us (2%)
  local copies, waits for them, and re-layouts  1.35 us (2%)
    ppermute x14, waiting for transfers between devices, brought(): return [block] + [lax.ppermute(block, axis, pairs) for pairs in swaps(axis)]  15.4 us
    pallas_call x7, Pallas kernels, simple_call(): pl.pallas_call(body, out_shape=shapes, in_specs=[SMEM_SPEC] * scalars + [...  11.5 us
    all_to_all x1, blocking collectives, everywhere(): return lax.all_to_all(copies, AXES, 0, 0, tiled=True)  10.5 us
    ppermute x14, starting transfers between devices, brought(): return [block] + [lax.ppermute(block, axis, pairs) for pairs in swaps(axis)]  8.41 us
    all_to_all x1, starting transfers between devices, everywhere(): return lax.all_to_all(copies, AXES, 0, 0, tiled=True)  7.3 us
    all_to_all x1, waiting for transfers between devices, everywhere(): return lax.all_to_all(copies, AXES, 0, 0, tiled=True)  5.63 us
    unnamed x20, local copies, waits for them, and re-layouts  1.25 us
  transfers between devices with their start and end apart: 15, of which 9 were waited for; matrix products, arithmetic and copies ran while one was open for 0% of the time, Pallas kernels for 5%

profile of v2, /device:TPU:0, one launch (start us, length us, event | category | flops | bytes accessed | tf_op | source)
XLA Modules:
  0.0 61.6 jit_solution(7875223258977807669)
XLA Ops:
  1.3 0.7 %copy-done.6 = f32[1,1,1,3,64]{4,2,3,1,0:T(1,128)S(1)} copy-done((f32[1,1,1,3,64]{4,2,3,1,0:T(1,128)S(1)}, f32[1,1,1,3,64]{4,2,3,1,0:T(1,128)}, u32[]{:S(2)}) %copy-start.6) | copy-done | bytes 792
  2.0 0.7 %shard_map.130.refs_0_ = f32[32,4,128]{2,1,0:T(4,128)} custom-call(s32[1]{0:T(128)} %bitcast.39.refs_0_, f32[3,1,64]{2,1,0:T(1,128)S(1)} %bitcast.42, s32[1,64]{1,0:T(1,128)S(1)} %bitcast.43), custom_call_target="tpu_custom_call" | custom-call | flops 1048576 | bytes 1048576 | tf_op jit(solution)/shard_map/pallas_call | solution.py:442
  2.7 7.3 %all-to-all-start = ((f32[32,4,128]{2,1,0:T(4,128)}), f32[32,4,128]{2,1,0:T(4,128)S(1)}, u32[]{:S(2)}, u32[]{:S(2)}) async-start(f32[32,4,128]{2,1,0:T(4,128)} %shard_map.130.refs_0_), calls=%async_computation | async-start | bytes 131072 | tf_op jit(solution)/shard_map/all_to_all | solution.py:483
  10.0 0.0 copy-start.3
  10.0 0.0 copy-start.4
  10.0 0.0 copy-start.5
  10.0 0.0 copy-start.8
  10.0 0.0 copy-start.9
  10.1 0.0 copy-start
  10.1 0.1 stack.111.refs_0_
  10.2 0.5 copy-done.3
  10.7 0.0 copy-done.4
  10.7 0.0 copy-done.5
  10.7 1.1 %shard_map.131 = (f32[64,8]{1,0:T(8,128)S(1)}, bf16[2,32,128]{2,1,0:T(8,128)(2,1)S(1)}, f32[64,128]{1,0:T(8,128)S(1)}, f32[4,128]{1,0:T(4,128)S(1)}, f32[1,16]{1,0:T(1,128)S(1)}, /*index=5*/f32[1,128]{1,0:T(1,128)S(1)}) custom-call(f32[32,4,128]{2,1,0:T(4,128)} %shard_map.130.refs_0_, bf16[8,128]{1,0:T(8,128)(2,1)S(1)} %copy-done.4, ...), custom_call_target="tpu_custom_call" | custom-call | flops 1048576 | bytes 1048576 | tf_op jit(solution)/shard_map/pallas_call | solution.py:442
  11.8 5.6 %all-to-all-done.refs_1_ = f32[32,4,128]{2,1,0:T(4,128)S(1)} async-done(((f32[32,4,128]{2,1,0:T(4,128)}), f32[32,4,128]{2,1,0:T(4,128)S(1)}, u32[]{:S(2)}, u32[]{:S(2)}) %all-to-all-start) | async-done | bytes 65568 | tf_op jit(solution)/shard_map/all_to_all | solution.py:483
  17.5 2.4 %shard_map.132 = (f32[9,4,128]{2,1,0:T(4,128)S(1)}, bf16[4,64,1152]{2,1,0:T(8,128)(2,1)S(1)}, bf16[64,128]{1,0:T(8,128)(2,1)S(1)}, f32[192,128]{1,0:T(8,128)S(1)}, f32[64,128]{1,0:T(8,128)S(1)}) custom-call(s32[22]{0:T(128)S(1)} %stack.111.refs_0_, f32[32,4,128]{2,1,0:T(4,128)S(1)} %all-to-all-done.refs_1_, ...), custom_call_target="tpu_custom_call" | custom-call | flops 7372800 | bytes 1048576 | tf_op jit(solution)/shard_map/pallas_call | solution.py:442
  19.9 0.9 %collective-permute-start = (bf16[64,128]{1,0:T(8,128)(2,1)S(1)}, bf16[64,128]{1,0:T(8,128)(2,1)S(1)}, u32[]{:S(2)}, u32[]{:S(2)}) collective-permute-start(bf16[64,128]{1,0:T(8,128)(2,1)S(1)} %get-tuple-element.23.refs_7_), channel_id=1, source_target_pairs={{0,3},{1,2},{2,1},{3,0},{4,7},{5,6},{6,5},{7,4},{8,11},{9,10},{10,... | collective-permute-start | bytes 49160 | tf_op jit(solution)/shard_map/ppermute | solution.py:473
  20.8 0.2 collective-permute-start.1
  21.0 4.5 %collective-permute-done = bf16[64,128]{1,0:T(8,128)(2,1)S(1)} collective-permute-done((bf16[64,128]{1,0:T(8,128)(2,1)S(1)}, bf16[64,128]{1,0:T(8,128)(2,1)S(1)}, u32[]{:S(2)}, u32[]{:S(2)}) %collective-permute-start) | collective-permute-done | bytes 16416 | tf_op jit(solution)/shard_map/ppermute | solution.py:473
  25.5 0.0 collective-permute-done.1
  25.5 0.0 copy-start.2
  25.5 0.7 %collective-permute-start.2 = (bf16[3,64,128]{2,1,0:T(8,128)(2,1)S(1)}, bf16[3,64,128]{2,1,0:T(8,128)(2,1)S(1)}, u32[]{:S(2)}, u32[]{:S(2)}) collective-permute-start(bf16[3,64,128]{2,1,0:T(8,128)(2,1)S(1)} %pad_maximum_fusion.refs_1_), channel_id=1, source_target_pairs={{0,24},{8,16},{16,8},{24,0},{1,25},{9,17},{17,9},{25,1},{2,26},{10... | collective-permute-start | bytes 147464 | tf_op jit(solution)/shard_map/ppermute | solution.py:473
  26.2 1.5 %collective-permute-start.3 = (bf16[3,64,128]{2,1,0:T(8,128)(2,1)S(1)}, bf16[3,64,128]{2,1,0:T(8,128)(2,1)S(1)}, u32[]{:S(2)}, u32[]{:S(2)}) collective-permute-start(bf16[3,64,128]{2,1,0:T(8,128)(2,1)S(1)} %pad_maximum_fusion.refs_1_), channel_id=1, source_target_pairs={{0,8},{8,0},{16,24},{24,16},{1,9},{9,1},{17,25},{25,17},{2,10},{10... | collective-permute-start | bytes 147464 | tf_op jit(solution)/shard_map/ppermute | solution.py:473
  27.7 0.0 collective-permute-start.4
  27.7 2.8 %collective-permute-done.2.refs_2_ = bf16[3,64,128]{2,1,0:T(8,128)(2,1)S(1)} collective-permute-done((bf16[3,64,128]{2,1,0:T(8,128)(2,1)S(1)}, bf16[3,64,128]{2,1,0:T(8,128)(2,1)S(1)}, u32[]{:S(2)}, u32[]{:S(2)}) %collective-permute-start.2) | collective-permute-done | bytes 49184 | tf_op jit(solution)/shard_map/ppermute | solution.py:473
  30.6 0.0 collective-permute-start.5
  30.6 0.0 collective-permute-done.3.refs_3_
  30.6 0.5 collective-permute-start.6
  31.1 0.0 collective-permute-done.4.refs_4_
  31.1 0.7 %collective-permute-done.5.refs_5_ = bf16[3,64,128]{2,1,0:T(8,128)(2,1)S(1)} collective-permute-done((bf16[3,64,128]{2,1,0:T(8,128)(2,1)S(1)}, bf16[3,64,128]{2,1,0:T(8,128)(2,1)S(1)}, u32[]{:S(2)}, u32[]{:S(2)}) %collective-permute-start.5) | collective-permute-done | bytes 49184 | tf_op jit(solution)/shard_map/ppermute | solution.py:473
  31.8 0.2 collective-permute-done.6.refs_6_
  32.0 2.1 %shard_map.133 = (bf16[64,128]{1,0:T(8,128)(2,1)S(1)}, f32[1,64]{1,0:T(1,128)}, bf16[64,128]{1,0:T(8,128)(2,1)}, f32[64,128]{1,0:T(8,128)S(1)}) custom-call(s32[22]{0:T(128)S(1)} %stack.111.refs_0_, bf16[3,64,128]{2,1,0:T(8,128)(2,1)S(1)} %pad_maximum_fusion.refs_1_, bf16[3,64,128]{2,1,0:T(8,128)(2,1)S(1)} %collective-permute-done.2.refs_2_, ...), custom_call_target="tpu_custom_call" | custom-call | flops 7372800 | bytes 1048576 | tf_op jit(solution)/shard_map/pallas_call | solution.py:442
  34.0 2.0 %collective-permute-start.7 = (bf16[64,128]{1,0:T(8,128)(2,1)S(1)}, bf16[64,128]{1,0:T(8,128)(2,1)S(1)}, u32[]{:S(2)}, u32[]{:S(2)}) collective-permute-start(bf16[64,128]{1,0:T(8,128)(2,1)S(1)} %get-tuple-element.28.refs_7_), channel_id=1, source_target_pairs={{0,3},{1,2},{2,1},{3,0},{4,7},{5,6},{6,5},{7,4},{8,11},{9,10},{10,... | collective-permute-start | bytes 49160 | tf_op jit(solution)/shard_map/ppermute | solution.py:473
  36.1 0.0 collective-permute-start.8
  36.1 3.5 %collective-permute-done.7 = bf16[64,128]{1,0:T(8,128)(2,1)S(1)} collective-permute-done((bf16[64,128]{1,0:T(8,128)(2,1)S(1)}, bf16[64,128]{1,0:T(8,128)(2,1)S(1)}, u32[]{:S(2)}, u32[]{:S(2)}) %collective-permute-start.7) | collective-permute-done | bytes 16416 | tf_op jit(solution)/shard_map/ppermute | solution.py:473
  39.6 0.2 collective-permute-done.8
  39.8 1.9 %collective-permute-start.9 = (bf16[3,64,128]{2,1,0:T(8,128)(2,1)S(1)}, bf16[3,64,128]{2,1,0:T(8,128)(2,1)S(1)}, u32[]{:S(2)}, u32[]{:S(2)}) collective-permute-start(bf16[3,64,128]{2,1,0:T(8,128)(2,1)S(1)} %pad_maximum_fusion.1.refs_1_), channel_id=1, source_target_pairs={{0,24},{8,16},{16,8},{24,0},{1,25},{9,17},{17,9},{25,1},{2,26},{10... | collective-permute-start | bytes 147464 | tf_op jit(solution)/shard_map/ppermute | solution.py:473
  41.7 0.7 %collective-permute-start.10 = (bf16[3,64,128]{2,1,0:T(8,128)(2,1)S(1)}, bf16[3,64,128]{2,1,0:T(8,128)(2,1)S(1)}, u32[]{:S(2)}, u32[]{:S(2)}) collective-permute-start(bf16[3,64,128]{2,1,0:T(8,128)(2,1)S(1)} %pad_maximum_fusion.1.refs_1_), channel_id=1, source_target_pairs={{0,8},{8,0},{16,24},{24,16},{1,9},{9,1},{17,25},{25,17},{2,10},{10... | collective-permute-start | bytes 147464 | tf_op jit(solution)/shard_map/ppermute | solution.py:473
  42.4 0.0 collective-permute-start.11
  42.4 2.5 %collective-permute-done.9.refs_2_ = bf16[3,64,128]{2,1,0:T(8,128)(2,1)S(1)} collective-permute-done((bf16[3,64,128]{2,1,0:T(8,128)(2,1)S(1)}, bf16[3,64,128]{2,1,0:T(8,128)(2,1)S(1)}, u32[]{:S(2)}, u32[]{:S(2)}) %collective-permute-start.9) | collective-permute-done | bytes 49184 | tf_op jit(solution)/shard_map/ppermute | solution.py:473
  44.9 0.0 collective-permute-start.12
  44.9 1.0 %collective-permute-done.10.refs_3_ = bf16[3,64,128]{2,1,0:T(8,128)(2,1)S(1)} collective-permute-done((bf16[3,64,128]{2,1,0:T(8,128)(2,1)S(1)}, bf16[3,64,128]{2,1,0:T(8,128)(2,1)S(1)}, u32[]{:S(2)}, u32[]{:S(2)}) %collective-permute-start.10) | collective-permute-done | bytes 49184 | tf_op jit(solution)/shard_map/ppermute | solution.py:473
  45.8 1.7 %shard_map.134 = (bf16[4,64,1152]{2,1,0:T(8,128)(2,1)S(1)}, f32[64,1152]{1,0:T(8,128)S(1)}) custom-call(s32[22]{0:T(128)S(1)} %stack.111.refs_0_, bf16[3,64,128]{2,1,0:T(8,128)(2,1)S(1)} %pad_maximum_fusion.refs_1_, bf16[3,64,128]{2,1,0:T(8,128)(2,1)S(1)} %collective-permute-done.2.refs_2_, bf16[3,64,128]{2,1,0:T(8,128)(2,1)S(1)} %collective-permute-done.3.refs_3_, ...), custom_call_target="tpu_custom_call" | custom-call | flops 7372800 | bytes 1048576 | tf_op jit(solution)/shard_map/pallas_call | solution.py:442
  47.5 0.0 collective-permute-done.11.refs_4_
  47.5 0.0 collective-permute-done.12.refs_5_
  47.5 2.9 %shard_map.135 = f32[32,4,128]{2,1,0:T(4,128)S(1)} custom-call(s32[22]{0:T(128)S(1)} %stack.111.refs_0_, bf16[3,64,128]{2,1,0:T(8,128)(2,1)S(1)} %pad_maximum_fusion.1.refs_1_, bf16[3,64,128]{2,1,0:T(8,128)(2,1)S(1)} %collective-permute-done.9.refs_2_, bf16[3,64,128]{2,1,0:T(8,128)(2,1)S(1)} %collective-permute-done.10.refs_3_, ...), custom_call_target="tpu_custom_call" | custom-call | flops 7372800 | bytes 1048576 | tf_op jit(solution)/shard_map/pallas_call | solution.py:442
  50.4 10.5 %all_to_all.10.refs_0_ = f32[32,4,128]{2,1,0:T(4,128)S(1)} all-to-all(f32[32,4,128]{2,1,0:T(4,128)S(1)} %shard_map.135), channel_id=1, replica_groups=mesh['gx'=4,'gy'=2,'gz'=4] {'gx','gy','gz'}, dimensions={0} | all-to-all | bytes 131072 | tf_op jit(solution)/shard_map/all_to_all | solution.py:483
  60.9 0.7 %shard_map.136 = f32[3,1,64]{2,1,0:T(1,128)} custom-call(f32[32,4,128]{2,1,0:T(4,128)S(1)} %all_to_all.10.refs_0_), custom_call_target="tpu_custom_call" | custom-call | flops 1048576 | bytes 1048576 | tf_op jit(solution)/shard_map/pallas_call | solution.py:442
  (13 shorter events, 0.0 us)
Async XLA Ops:
  1.3 0.7 %copy-start.6 = (f32[1,1,1,3,64]{4,2,3,1,0:T(1,128)S(1)}, f32[1,1,1,3,64]{4,2,3,1,0:T(1,128)}, u32[]{:S(2)}) copy-start(f32[1,1,1,3,64]{4,2,3,1,0:T(1,128)} %param.11) | copy-start | bytes 2308
  1.3 0.7 %copy-start.7 = (s32[1,1,1,64]{3,2,1,0:T(1,128)S(1)}, s32[1,1,1,64]{3,2,1,0:T(1,128)}, u32[]{:S(2)}) copy-start(s32[1,1,1,64]{3,2,1,0:T(1,128)} %param.12) | copy-start | bytes 772
  2.7 14.8 %all-to-all-start = ((f32[32,4,128]{2,1,0:T(4,128)}), f32[32,4,128]{2,1,0:T(4,128)S(1)}, u32[]{:S(2)}, u32[]{:S(2)}) async-start(f32[32,4,128]{2,1,0:T(4,128)} %shard_map.130.refs_0_), calls=%async_computation | async-start | bytes 131072 | tf_op jit(solution)/shard_map/all_to_all | solution.py:483
  10.0 0.7 %copy-start.3 = (f32[2,4,128]{2,1,0:T(4,128)S(1)}, f32[2,4,128]{2,1,0:T(4,128)}, u32[]{:S(2)}) copy-start(f32[2,4,128]{2,1,0:T(4,128)} %refs_2_.1) | copy-start | bytes 12292
  10.0 0.7 %copy-start.4 = (bf16[8,128]{1,0:T(8,128)(2,1)S(1)}, bf16[8,128]{1,0:T(8,128)(2,1)}, u32[]{:S(2)}) copy-start(bf16[8,128]{1,0:T(8,128)(2,1)} %refs_1_.1) | copy-start | bytes 6148
  10.0 0.7 %copy-start.5 = (f32[4,128]{1,0:T(4,128)S(1)}, f32[4,128]{1,0:T(4,128)}, u32[]{:S(2)}) copy-start(f32[4,128]{1,0:T(4,128)} %refs_3_.1) | copy-start | bytes 6148
  10.0 0.7 %copy-start.8 = (f32[16]{0:T(128)S(1)}, f32[16]{0:T(128)}, u32[]{:S(2)}) copy-start(f32[16]{0:T(128)} %param.21) | copy-start | bytes 196
  10.0 0.7 %copy-start.9 = (f32[128]{0:T(128)S(1)}, f32[128]{0:T(128)}, u32[]{:S(2)}) copy-start(f32[128]{0:T(128)} %param.17) | copy-start | bytes 1540
  10.1 7.4 %copy-start = (bf16[128,256]{1,0:T(8,128)(2,1)S(1)}, bf16[128,256]{1,0:T(8,128)(2,1)}, u32[]{:S(2)}) copy-start(bf16[128,256]{1,0:T(8,128)(2,1)} %refs_15_.1) | copy-start | bytes 196612
  19.9 5.6 %collective-permute-start = (bf16[64,128]{1,0:T(8,128)(2,1)S(1)}, bf16[64,128]{1,0:T(8,128)(2,1)S(1)}, u32[]{:S(2)}, u32[]{:S(2)}) collective-permute-start(bf16[64,128]{1,0:T(8,128)(2,1)S(1)} %get-tuple-element.23.refs_7_), channel_id=1, source_target_pairs={{0,3},{1,2},{2,1},{3,0},{4,7},{5,6},{6,5},{7,4},{8,11},{9,10},{10,... | collective-permute-start | bytes 49160 | tf_op jit(solution)/shard_map/ppermute | solution.py:473
  20.8 4.7 %collective-permute-start.1 = (bf16[64,128]{1,0:T(8,128)(2,1)S(1)}, bf16[64,128]{1,0:T(8,128)(2,1)S(1)}, u32[]{:S(2)}, u32[]{:S(2)}) collective-permute-start(bf16[64,128]{1,0:T(8,128)(2,1)S(1)} %get-tuple-element.23.refs_7_), channel_id=1, source_target_pairs={{0,1},{1,0},{2,3},{3,2},{4,5},{5,4},{6,7},{7,6},{8,9},{9,8},{10,11... | collective-permute-start | bytes 49160 | tf_op jit(solution)/shard_map/ppermute | solution.py:473
  25.5 6.5 %copy-start.1 = (bf16[128,128]{1,0:T(8,128)(2,1)S(1)}, bf16[128,128]{1,0:T(8,128)(2,1)}, u32[]{:S(2)}) copy-start(bf16[128,128]{1,0:T(8,128)(2,1)} %refs_11_.1) | copy-start | bytes 98308
  25.5 6.5 %copy-start.2 = (bf16[16,128]{1,0:T(8,128)(2,1)S(1)}, bf16[16,128]{1,0:T(8,128)(2,1)}, u32[]{:S(2)}) copy-start(bf16[16,128]{1,0:T(8,128)(2,1)} %refs_12_.1) | copy-start | bytes 12292
  25.5 5.1 %collective-permute-start.2 = (bf16[3,64,128]{2,1,0:T(8,128)(2,1)S(1)}, bf16[3,64,128]{2,1,0:T(8,128)(2,1)S(1)}, u32[]{:S(2)}, u32[]{:S(2)}) collective-permute-start(bf16[3,64,128]{2,1,0:T(8,128)(2,1)S(1)} %pad_maximum_fusion.refs_1_), channel_id=1, source_target_pairs={{0,24},{8,16},{16,8},{24,0},{1,25},{9,17},{17,9},{25,1},{2,26},{10... | collective-permute-start | bytes 147464 | tf_op jit(solution)/shard_map/ppermute | solution.py:473
  26.2 4.4 %collective-permute-start.3 = (bf16[3,64,128]{2,1,0:T(8,128)(2,1)S(1)}, bf16[3,64,128]{2,1,0:T(8,128)(2,1)S(1)}, u32[]{:S(2)}, u32[]{:S(2)}) collective-permute-start(bf16[3,64,128]{2,1,0:T(8,128)(2,1)S(1)} %pad_maximum_fusion.refs_1_), channel_id=1, source_target_pairs={{0,8},{8,0},{16,24},{24,16},{1,9},{9,1},{17,25},{25,17},{2,10},{10... | collective-permute-start | bytes 147464 | tf_op jit(solution)/shard_map/ppermute | solution.py:473
  27.7 3.4 %collective-permute-start.4 = (bf16[3,64,128]{2,1,0:T(8,128)(2,1)S(1)}, bf16[3,64,128]{2,1,0:T(8,128)(2,1)S(1)}, u32[]{:S(2)}, u32[]{:S(2)}) collective-permute-start(bf16[3,64,128]{2,1,0:T(8,128)(2,1)S(1)} %pad_maximum_fusion.refs_1_), channel_id=1, source_target_pairs={{0,4},{4,0},{1,5},{5,1},{2,6},{6,2},{3,7},{7,3},{8,12},{12,8},{9,1... | collective-permute-start | bytes 147464 | tf_op jit(solution)/shard_map/ppermute | solution.py:473
  30.6 1.2 %collective-permute-start.5 = (bf16[3,64,128]{2,1,0:T(8,128)(2,1)S(1)}, bf16[3,64,128]{2,1,0:T(8,128)(2,1)S(1)}, u32[]{:S(2)}, u32[]{:S(2)}) collective-permute-start(bf16[3,64,128]{2,1,0:T(8,128)(2,1)S(1)} %collective-permute-done.2.refs_2_), channel_id=1, source_target_pairs={{0,4},{4,0},{1,5},{5,1},{2,6},{6,2},{3,7},{7,3},{8,12},{12,8},{9,1... | collective-permute-start | bytes 147464 | tf_op jit(solution)/shard_map/ppermute | solution.py:473
  30.6 1.4 %collective-permute-start.6 = (bf16[3,64,128]{2,1,0:T(8,128)(2,1)S(1)}, bf16[3,64,128]{2,1,0:T(8,128)(2,1)S(1)}, u32[]{:S(2)}, u32[]{:S(2)}) collective-permute-start(bf16[3,64,128]{2,1,0:T(8,128)(2,1)S(1)} %collective-permute-done.3.refs_3_), channel_id=1, source_target_pairs={{0,4},{4,0},{1,5},{5,1},{2,6},{6,2},{3,7},{7,3},{8,12},{12,8},{9,1... | collective-permute-start | bytes 147464 | tf_op jit(solution)/shard_map/ppermute | solution.py:473
  34.0 5.5 %collective-permute-start.7 = (bf16[64,128]{1,0:T(8,128)(2,1)S(1)}, bf16[64,128]{1,0:T(8,128)(2,1)S(1)}, u32[]{:S(2)}, u32[]{:S(2)}) collective-permute-start(bf16[64,128]{1,0:T(8,128)(2,1)S(1)} %get-tuple-element.28.refs_7_), channel_id=1, source_target_pairs={{0,3},{1,2},{2,1},{3,0},{4,7},{5,6},{6,5},{7,4},{8,11},{9,10},{10,... | collective-permute-start | bytes 49160 | tf_op jit(solution)/shard_map/ppermute | solution.py:473
  36.1 3.7 %collective-permute-start.8 = (bf16[64,128]{1,0:T(8,128)(2,1)S(1)}, bf16[64,128]{1,0:T(8,128)(2,1)S(1)}, u32[]{:S(2)}, u32[]{:S(2)}) collective-permute-start(bf16[64,128]{1,0:T(8,128)(2,1)S(1)} %get-tuple-element.28.refs_7_), channel_id=1, source_target_pairs={{0,1},{1,0},{2,3},{3,2},{4,5},{5,4},{6,7},{7,6},{8,9},{9,8},{10,11... | collective-permute-start | bytes 49160 | tf_op jit(solution)/shard_map/ppermute | solution.py:473
  39.8 5.1 %collective-permute-start.9 = (bf16[3,64,128]{2,1,0:T(8,128)(2,1)S(1)}, bf16[3,64,128]{2,1,0:T(8,128)(2,1)S(1)}, u32[]{:S(2)}, u32[]{:S(2)}) collective-permute-start(bf16[3,64,128]{2,1,0:T(8,128)(2,1)S(1)} %pad_maximum_fusion.1.refs_1_), channel_id=1, source_target_pairs={{0,24},{8,16},{16,8},{24,0},{1,25},{9,17},{17,9},{25,1},{2,26},{10... | collective-permute-start | bytes 147464 | tf_op jit(solution)/shard_map/ppermute | solution.py:473
  41.7 4.1 %collective-permute-start.10 = (bf16[3,64,128]{2,1,0:T(8,128)(2,1)S(1)}, bf16[3,64,128]{2,1,0:T(8,128)(2,1)S(1)}, u32[]{:S(2)}, u32[]{:S(2)}) collective-permute-start(bf16[3,64,128]{2,1,0:T(8,128)(2,1)S(1)} %pad_maximum_fusion.1.refs_1_), channel_id=1, source_target_pairs={{0,8},{8,0},{16,24},{24,16},{1,9},{9,1},{17,25},{25,17},{2,10},{10... | collective-permute-start | bytes 147464 | tf_op jit(solution)/shard_map/ppermute | solution.py:473
  42.4 5.1 %collective-permute-start.11 = (bf16[3,64,128]{2,1,0:T(8,128)(2,1)S(1)}, bf16[3,64,128]{2,1,0:T(8,128)(2,1)S(1)}, u32[]{:S(2)}, u32[]{:S(2)}) collective-permute-start(bf16[3,64,128]{2,1,0:T(8,128)(2,1)S(1)} %pad_maximum_fusion.1.refs_1_), channel_id=1, source_target_pairs={{0,4},{4,0},{1,5},{5,1},{2,6},{6,2},{3,7},{7,3},{8,12},{12,8},{9,1... | collective-permute-start | bytes 147464 | tf_op jit(solution)/shard_map/ppermute | solution.py:473
  44.9 2.7 %collective-permute-start.12 = (bf16[3,64,128]{2,1,0:T(8,128)(2,1)S(1)}, bf16[3,64,128]{2,1,0:T(8,128)(2,1)S(1)}, u32[]{:S(2)}, u32[]{:S(2)}) collective-permute-start(bf16[3,64,128]{2,1,0:T(8,128)(2,1)S(1)} %collective-permute-done.9.refs_2_), channel_id=1, source_target_pairs={{0,4},{4,0},{1,5},{5,1},{2,6},{6,2},{3,7},{7,3},{8,12},{12,8},{9,1... | collective-permute-start | bytes 147464 | tf_op jit(solution)/shard_map/ppermute | solution.py:473
  45.8 1.7 %collective-permute-start.13 = (bf16[3,64,128]{2,1,0:T(8,128)(2,1)S(1)}, bf16[3,64,128]{2,1,0:T(8,128)(2,1)S(1)}, u32[]{:S(2)}, u32[]{:S(2)}) collective-permute-start(bf16[3,64,128]{2,1,0:T(8,128)(2,1)S(1)} %collective-permute-done.10.refs_3_), channel_id=1, source_target_pairs={{0,4},{4,0},{1,5},{5,1},{2,6},{6,2},{3,7},{7,3},{8,12},{12,8},{9,1... | collective-permute-start | bytes 147464 | tf_op jit(solution)/shard_map/ppermute | solution.py:473

commit v3 on v2

--- a/solution.py
+++ b/solution.py
@@ -33,7 +33,8 @@
     0.08205040170151112,
     -0.007028386239784362,
 )
-VMEM_LIMIT = 48 * 1024 * 1024
+VMEM_LIMIT = 24 * 1024 * 1024
+FETCH_LIMIT = 60 * 1024 * 1024
 NT = (((1,), (1,)), ((), ()))
 NN = (((1,), (0,)), ((), ()))
 
@@ -91,7 +92,7 @@
         index = {axis: lax.axis_index(axis) for axis in AXES}
 
         def parity(axis):
-            return 1 - lax.rem(index[axis], 2) if paired(self.sizes[axis]) else jnp.int32(0)
+            return lax.rem(index[axis], 2) if paired(self.sizes[axis]) else jnp.int32(0)
 
         def moved(axis, step):
             return lax.rem(index[axis] + (step + self.sizes[axis]), self.sizes[axis])
@@ -162,7 +163,7 @@
         sine, cosine = waves(dist_sq, inverse)
         fade = jnp.maximum(1.0 - dist_sq * (1.0 / CUT_SQUARE), 0.0)
         radial = fade * fade * inverse
-        units = [part * (inverse * ROOT_THREE) for part in parts]
+        units = [(part * (inverse * ROOT_THREE)).astype(BF16) for part in parts]
         before, now = None, sine * radial
         lanes = slice(tile * plan.width, (tile + 1) * plan.width)
         for n in range(nbasis):
@@ -174,7 +175,7 @@
             basis_ref[n, :, lanes] = packed
             pair_ref[n, :slots, lanes] = packed
             for k in range(3):
-                pair_ref[n, (k + 1) * slots : (k + 2) * slots, lanes] = (units[k] * now).astype(BF16)
+                pair_ref[n, (k + 1) * slots : (k + 2) * slots, lanes] = units[k] * packed
     hot = jnp.concatenate(hot, axis=1)
     gathered = dot(pair_ref[...].reshape(nbasis * 4 * slots, plan.far), hot, NT)
     gathered = gathered.reshape(nbasis, 4 * slots, nbasis * nspec)
@@ -240,7 +241,7 @@
     far_refs, refs = refs[:nrefs], refs[nrefs:]
     (layer_ref, basis_ref, cols_ref, radial_ref, mix_ref), refs = refs[:5], refs[5:]
     (hidden_ref, out_ref, one_ref), refs = refs[:3], refs[3:]
-    adjoint_ref, energy_ref, features_ref, own_ref, all_ref = refs
+    adjoint_ref, features_ref, before_ref, own_ref, all_ref = refs
     slots, nbasis = plan.slots, plan.nbasis
     gather_far(plan, places_ref, far_refs, all_ref)
     summed = dot(basis_ref[...].reshape(nbasis * slots, plan.far), all_ref[...])
@@ -256,11 +257,7 @@
     before = dot(features, hidden_ref[...], NT)
     open_hidden = sigmoid(before)
     live = cols_ref[:, 3:4]
-    energy = dot_exact(one_ref[...], layer, NT) + dot_exact(out_ref[...], before * open_hidden, NT)
-    live_row = dot(jnp.ones((1, 8), BF16), jnp.where(
-        lax.broadcasted_iota(jnp.int32, (slots, 8), 1) == 0, live, 0.0
-    ).astype(BF16), NT)
-    energy_ref[...] = energy * live_row
+    before_ref[...] = before
     slope = out_ref[...] * (open_hidden * (1.0 + before * (1.0 - open_hidden))) * live
     from_hidden = dot(slope.astype(BF16), hidden_ref[...])
     own_ref[...] = from_hidden + one_ref[...] * live
@@ -268,12 +265,54 @@
     adjoint_ref[...] = dot(back.astype(BF16), mix_ref[...]).astype(BF16)
 
 
-def slope_kernel(plan, nrefs, places_ref, *refs):
+def slope_kernel(plan, rows_ref, cols_ref, layer_ref, again_ref, apart_ref, slope_ref, radial_ref, turned_ref):
+    again_ref[...] = layer_ref[...]
+    cols = [cols_ref[:, axis : axis + 1] for axis in range(3)]
+    for tile in range(len(plan.tiles)):
+        lanes = slice(tile * plan.width, (tile + 1) * plan.width)
+        parts = separations(plan, [rows_ref[tile, k : k + 1] for k in range(3)], cols)
+        for k in range(3):
+            apart_ref[k, :, lanes] = parts[k]
+        dist_sq, inverse = distance(plan, parts, tile)
+        sine, cosine = waves(dist_sq, inverse)
+        fade = jnp.maximum(1.0 - dist_sq * (1.0 / CUT_SQUARE), 0.0)
+        radial = fade * fade * inverse
+        on_sine = -inverse * ((4.0 / CUT_SQUARE) * fade + radial * inverse)
+        on_cosine = (math.pi / CELL_SIDE) * (inverse * radial)
+        scale = ROOT_THREE * inverse
+        scaled = scale * radial
+        square = inverse * inverse
+        double = 2.0 * cosine
+        before_s, now_s, before_c, now_c = None, sine, None, cosine
+        for n in range(plan.nbasis):
+            if n == 1:
+                before_s, now_s = now_s, double * now_s
+                before_c, now_c = now_c, double * now_c - 1.0
+            elif n > 1:
+                before_s, now_s = now_s, double * now_s - before_s
+                before_c, now_c = now_c, double * now_c - before_c
+            slope = on_sine * now_s + (n + 1.0) * on_cosine * now_c
+            factor = scaled * now_s
+            slope_ref[n, :, lanes] = slope
+            radial_ref[n, :, lanes] = factor
+            turned_ref[n, :, lanes] = scale * slope - square * factor
+
+
+def energy_kernel(plan, nrefs, places_ref, *refs):
     far_refs, refs = refs[:nrefs], refs[nrefs:]
-    adjoint_ref, rows_ref, cols_ref, radial_ref, slope_ref, pair_ref, all_ref = refs
+    (adjoint_ref, slope_ref, radial_ref, cols_ref, layer_ref), refs = refs[:5], refs[5:]
+    (before_ref, out_ref, one_ref, kept_ref), refs = refs[:4], refs[4:]
+    again_ref, pair_ref, energy_ref, features_ref, all_ref = refs
     slots, nbasis = plan.slots, plan.nbasis
+    again_ref[...] = adjoint_ref[...]
+    features_ref[...] = kept_ref[...]
+    before = before_ref[...]
+    live = jnp.where(lax.broadcasted_iota(jnp.int32, (slots, 8), 1) == 0, cols_ref[:, 3:4], 0.0)
+    live_row = dot(jnp.ones((1, 8), BF16), live.astype(BF16), NT)
+    energy = dot_exact(one_ref[...], layer_ref[...].astype(F32), NT)
+    energy = energy + dot_exact(out_ref[...], before * sigmoid(before), NT)
+    energy_ref[...] = energy * live_row
     gather_far(plan, places_ref, far_refs, all_ref)
-    cols = [cols_ref[:, axis : axis + 1] for axis in range(3)]
     adjoint = adjoint_ref[...].astype(F32) * MSG_SCALE
     weighted = jnp.concatenate(
         [(adjoint * radial_ref[n : n + 1]).astype(BF16) for n in range(nbasis)], axis=0
@@ -281,32 +320,16 @@
     for tile in range(len(plan.tiles)):
         lanes = slice(tile * plan.width, (tile + 1) * plan.width)
         pulled = dot(weighted, all_ref[lanes], NT)
-        parts = separations(plan, [rows_ref[tile, k : k + 1] for k in range(3)], cols)
-        dist_sq, inverse = distance(plan, parts, tile)
-        sine, cosine = waves(dist_sq, inverse)
-        fade = jnp.maximum(1.0 - dist_sq * (1.0 / CUT_SQUARE), 0.0)
-        radial = fade * fade * inverse
-        on_sine = -inverse * ((4.0 / CUT_SQUARE) * fade + radial * inverse)
-        on_cosine = (math.pi / CELL_SIDE) * (inverse * radial)
-        double = 2.0 * cosine
-        before_s, now_s, before_c, now_c = None, sine, None, cosine
-        total = jnp.zeros_like(dist_sq)
-        for n in range(nbasis):
-            if n == 1:
-                before_s, now_s = now_s, double * now_s
-                before_c, now_c = now_c, double * now_c - 1.0
-            elif n > 1:
-                before_s, now_s = now_s, double * now_s - before_s
-                before_c, now_c = now_c, double * now_c - before_c
-            slope = on_sine * now_s + (n + 1.0) * on_cosine * now_c
-            slope_ref[n, :, lanes] = slope.astype(BF16)
-            total = total + slope * pulled[n * slots : (n + 1) * slots]
+        total = slope_ref[0, :, lanes] * pulled[:slots]
+        for n in range(1, nbasis):
+            total = total + slope_ref[n, :, lanes] * pulled[n * slots : (n + 1) * slots]
         pair_ref[:, lanes] = total
 
 
 def force_kernel(plan, nrefs, places_ref, *refs):
     far_refs, refs = refs[:nrefs], refs[nrefs:]
-    (own_ref, basis_ref, slope_ref, pair_ref, rows_ref, cols_ref), refs = refs[:6], refs[6:]
+    (own_ref, basis_ref, pair_ref, rows_ref), refs = refs[:4], refs[4:]
+    (apart_ref, slope_ref, factor_ref, turned_ref), refs = refs[:4], refs[4:]
     (radial_ref, mixing_ref, mix_ref, vector_ref, table_ref), refs = refs[:5], refs[5:]
     out_ref, all_ref = refs
     slots, nbasis, nspec, width = plan.slots, plan.nbasis, plan.nspec, plan.width
@@ -332,40 +355,37 @@
     weights = jnp.concatenate(
         [jnp.where(group == n, weights, 0.0).astype(BF16) for n in range(nbasis)], axis=0
     )
-    cols = [cols_ref[:, axis : axis + 1] for axis in range(3)]
     species = lax.broadcasted_iota(jnp.int32, (nbasis * nspec, width), 0) % nspec
     own = [jnp.zeros((slots, width), F32) for _ in range(3)]
     pulls = []
     for tile in range(len(plan.tiles)):
         lanes = slice(tile * width, (tile + 1) * width)
-        rows = [rows_ref[tile, k : k + 1] for k in range(4)]
-        hot = (rows[3].astype(jnp.int32) == species).astype(F32).astype(BF16)
+        hot = (rows_ref[tile, 3:4].astype(jnp.int32) == species).astype(F32).astype(BF16)
         spread = dot(weights, hot)
-        parts = separations(plan, rows, cols)
-        dist_sq, inverse = distance(plan, parts, tile)
-        scale = ROOT_THREE * inverse
         total = pair_ref[:, lanes]
-        along, sides = None, [None] * 3
+        sides, turns = [None] * 3, [None] * 3
         for n in range(nbasis):
             start = n * 4 * slots
-            piece = [spread[start + m * slots : start + (m + 1) * slots] for m in range(4)]
-            slope = slope_ref[n, :, lanes].astype(F32)
-            basis = basis_ref[n, :, lanes].astype(F32)
-            mixed = parts[0] * piece[1] + parts[1] * piece[2] + parts[2] * piece[3]
-            total = total + slope * (piece[0] + scale * mixed)
-            term = basis * mixed
-            along = term if along is None else along + term
+            total = total + slope_ref[n, :, lanes] * spread[start : start + slots]
             for k in range(3):
-                term = basis * piece[k + 1]
-                sides[k] = term if sides[k] is None else sides[k] + term
-        total = total - inverse * inverse * (scale * along)
+                piece = spread[start + (k + 1) * slots : start + (k + 2) * slots]
+                side = factor_ref[n, :, lanes] * piece
+                turn = turned_ref[n, :, lanes] * piece
+                sides[k] = side if n == 0 else sides[k] + side
+                turns[k] = turn if n == 0 else turns[k] + turn
+        for k in range(3):
+            total = total + apart_ref[k, :, lanes] * turns[k]
         pulls.append([])
         for k in range(3):
-            pull = parts[k] * total + scale * sides[k]
+            pull = apart_ref[k, :, lanes] * total + sides[k]
             own[k] = own[k] + pull
             pulls[-1].append(jnp.sum(pull, axis=0, keepdims=True))
-    ones = jnp.ones((8, width), F32)
-    mine = jnp.concatenate([dot_exact(ones, own[k], NT)[:1] for k in range(3)], axis=0)
+    own = jnp.concatenate(own, axis=0)
+    high = own.astype(BF16)
+    low = (own - high.astype(F32)).astype(BF16)
+    ones = jnp.ones((8, width), BF16)
+    mine = (dot(ones, high, NT) + dot(ones, low, NT))[:1]
+    mine = jnp.concatenate([mine[:, k * slots : (k + 1) * slots] for k in range(3)], axis=0)
     if plan.small:
         out_ref[...] = jnp.zeros_like(out_ref)
     side_of = lax.broadcasted_iota(jnp.int32, (3, width), 1) // slots
@@ -382,7 +402,15 @@
             out_ref[place, :3] = jnp.where(side_of == side, pulled, 0.0)
 
 
-def prepare_kernel(plan, counts_ref, place_ref, kind_ref, sent_ref):
+def brought_in(pairs, sems):
+    copies = [pltpu.make_async_copy(*pair, sems.at[m]) for m, pair in enumerate(pairs)]
+    for copy in copies:
+        copy.start()
+    for copy in copies:
+        copy.wait()
+
+
+def live_rows(plan, counts_ref, place_ref, kind_ref):
     live = lax.broadcasted_iota(jnp.int32, (1, plan.slots), 1) < counts_ref[0]
     rows = [
         jnp.where(live, place_ref[0], FAR),
@@ -391,7 +419,12 @@
         jnp.where(live, kind_ref[...], -1).astype(F32),
     ]
     rows = jnp.concatenate(rows, axis=0)
-    rows = jnp.concatenate([rows, rows], axis=1)
+    return jnp.concatenate([rows, rows], axis=1)
+
+
+def prepare_kernel(plan, counts_ref, place_hbm, kind_hbm, sent_ref, place_ref, kind_ref, sems):
+    brought_in([(place_hbm, place_ref), (kind_hbm, kind_ref)], sems)
+    rows = live_rows(plan, counts_ref, place_ref, kind_ref)
     for copy in range(sent_ref.shape[0]):
         sent_ref[copy] = rows
 
@@ -405,12 +438,13 @@
         force_ref[k] = -total[k : k + 1]
 
 
-def own_kernel(plan, sent_ref, embed_ref, radial_ref, *refs):
-    weight_refs, (cols_ref, table_ref, own_ref), kept_refs = refs[:3], refs[3:6], refs[6:]
-    for weight_ref, kept_ref in zip(weight_refs, kept_refs):
-        kept_ref[...] = weight_ref[...]
+def own_kernel(plan, counts_ref, *refs):
+    fetched, weights, (cols_ref, table_ref, own_ref) = refs[:4], refs[4:10], refs[10:13]
+    kept, local_refs, sems = refs[13:19], refs[19:-1], refs[-1]
     slots, nspec = plan.slots, plan.nspec
-    rows = sent_ref[0]
+    brought_in([*zip(fetched, local_refs), *zip(weights, kept)], sems)
+    place_ref, kind_ref, embed_ref, radial_ref = local_refs
+    rows = live_rows(plan, counts_ref, place_ref, kind_ref)
     cols = jnp.concatenate([rows, rows], axis=0).T[:slots]
     kind = cols[:, 3:4]
     lane = lax.broadcasted_iota(jnp.int32, cols.shape, 1)
@@ -430,11 +464,13 @@
 
 VMEM_SPEC = pl.BlockSpec(memory_space=pltpu.VMEM)
 SMEM_SPEC = pl.BlockSpec(memory_space=pltpu.SMEM)
-
-
-def simple_call(kernel, plan, operands, outs, scalars=0, scratch=(), flops=2**20):
+HBM_SPEC = pl.BlockSpec(memory_space=pltpu.HBM)
+
+
+def simple_call(kernel, plan, operands, outs, scalars=0, scratch=(), flops=2**20, near=False, fetched=0):
     single = not isinstance(outs, list)
-    shapes = [jax.ShapeDtypeStruct(*out) for out in ([outs] if single else outs)]
+    kind = pltpu.VMEM if near else jax.ShapeDtypeStruct
+    shapes = [kind(*out) for out in ([outs] if single else outs)]
 
     def body(*refs):
         kernel(plan, *refs)
@@ -442,10 +478,13 @@
     got = pl.pallas_call(
         body,
         out_shape=shapes,
-        in_specs=[SMEM_SPEC] * scalars + [VMEM_SPEC] * (len(operands) - scalars),
+        in_specs=[SMEM_SPEC] * scalars
+        + [VMEM_SPEC] * (len(operands) - scalars - fetched)
+        + [HBM_SPEC] * fetched,
         out_specs=[VMEM_SPEC] * len(shapes),
-        scratch_shapes=[pltpu.VMEM(*buffer) for buffer in scratch],
-        compiler_params=pltpu.CompilerParams(vmem_limit_bytes=VMEM_LIMIT),
+        scratch_shapes=[pltpu.VMEM(*buffer) for buffer in scratch]
+        + [pltpu.SemaphoreType.DMA((fetched,))] * (fetched > 0),
+        compiler_params=pltpu.CompilerParams(vmem_limit_bytes=FETCH_LIMIT if fetched else VMEM_LIMIT),
         cost_estimate=pl.CostEstimate(flops=flops, bytes_accessed=2**20, transcendentals=0),
     )(*operands)
     return got[0] if single else got
@@ -465,7 +504,7 @@
     if paired(count):
         near = [(i, i ^ 1) for i in range(count)]
         far = [(i, (i - 1 + 2 * (i % 2)) % count) for i in range(count)]
-        return [far, near]
+        return [near, far]
     return [[((i + o) % count, i) for i in range(count)] for o in offsets_of(count)[1:]]
 
 
@@ -473,8 +512,10 @@
     return [block] + [lax.ppermute(block, axis, pairs) for pairs in swaps(axis)]
 
 
-def neighbours(plan, block):
-    columns = brought(jnp.stack(brought(block, "gz")), "gx")
+def neighbours(plan, block, again=None):
+    column = brought(block, "gz")
+    column = jnp.stack([block if again is None else again] + column[1:])
+    columns = brought(column, "gx")
     swapped = [brought(column, "gy") for column in columns]
     return [column[side] for side in range(len(plan.sides)) for column in swapped]
 
@@ -521,27 +562,36 @@
         slots, channels = positions.shape[-1], embed.shape[1]
         nbasis, nspec = radial_two.shape[0], embed.shape[0]
         plan = Plan(mesh, slots, nbasis, nspec)
-        place = positions[0, 0, 0].reshape(3, 1, slots)
+        count = counts.reshape(1)
+        given = [positions[0, 0, 0].reshape(3, 1, slots), species.reshape(1, slots)]
         sent = simple_call(
             prepare_kernel,
             plan,
-            [counts.reshape(1), place, species.reshape(1, slots)],
+            [count, *given],
             ((plan.ndev if plan.small else 1, 4, 2 * slots), F32),
             1,
+            [(array.shape, array.dtype) for array in given],
+            near=True,
+            fetched=len(given),
         )
         places = plan.places()
         far_sent = [everywhere(sent)] if plan.small else neighbours(plan, sent[0])
-        weights = [radial_two, read_out[None], read_one[None]]
-        cols, table, own_embed, radial_two, out_row, one_row = simple_call(
+        weights = [radial_two, read_out[None], read_one[None], mix_one, mix_two, read_hidden]
+        given = given + [embed, radial_one]
+        cols, table, own_embed, radial_two, out_row, one_row, mix_one, mix_two, read_hidden = simple_call(
             own_kernel,
             plan,
-            [sent, embed, radial_one] + weights,
+            [count, *given, *weights],
             [
                 ((slots, 8), F32),
                 ((2, nbasis * nspec, channels), BF16),
                 ((slots, channels), F32),
             ]
             + [(weight.shape, weight.dtype) for weight in weights],
+            1,
+            [(array.shape, array.dtype) for array in given],
+            near=True,
+            fetched=len(given) + len(weights),
         )
         pair_flops = 100 * slots * plan.far
         rows, basis, layer, vector, mixing = call(
@@ -560,9 +610,17 @@
             [((nbasis, 4 * slots, plan.far), BF16)],
             pair_flops,
         )
-        far_layer = neighbours(plan, layer)
+        again, apart, slope, factor, turned = simple_call(
+            slope_kernel,
+            plan,
+            [rows, cols, layer],
+            [(layer.shape, BF16)]
+            + [((count, slots, plan.far), F32) for count in (3, nbasis, nbasis, nbasis)],
+            flops=pair_flops,
+        )
+        far_layer = neighbours(plan, layer, again)
         far_scratch = ((plan.far, channels), BF16)
-        adjoint, energy, features, own_adjoint = call(
+        adjoint, kept, before, own_adjoint = call(
             second_kernel,
             plan,
             far_layer,
@@ -570,30 +628,36 @@
             [layer, basis, cols, radial_two, mix_two, read_hidden, out_row, one_row],
             [
                 ((slots, channels), BF16),
-                ((1, slots), F32),
                 ((slots, channels), BF16),
+                ((slots, read_hidden.shape[0]), F32),
                 ((slots, channels), F32),
             ],
             [far_scratch],
             pair_flops,
         )
-        far_adjoint = neighbours(plan, adjoint)
-        slope, pair = call(
-            slope_kernel,
+        again, pair, energy, features = call(
+            energy_kernel,
             plan,
             far_layer,
             places,
-            [adjoint, rows, cols, radial_two],
-            [((nbasis, slots, plan.far), BF16), ((slots, plan.far), F32)],
+            [adjoint, slope, radial_two, cols, layer, before, out_row, one_row, kept],
+            [
+                ((slots, channels), BF16),
+                ((slots, plan.far), F32),
+                ((1, slots), F32),
+                ((slots, channels), BF16),
+            ],
             [far_scratch],
             pair_flops,
         )
+        far_adjoint = neighbours(plan, adjoint, again)
         pulls = call(
             force_kernel,
             plan,
             far_adjoint,
             places,
-            [own_adjoint, basis, slope, pair, rows, cols, radial_two, mixing, mix_one, vector, table],
+            [own_adjoint, basis, pair, rows, apart, slope, factor, turned]
+            + [radial_two, mixing, mix_one, vector, table],
             [((plan.ndev, 4, plan.width) if plan.small else (len(plan.tiles), 3, plan.width), F32)],
             [far_scratch],
             pair_flops,

time: 61.9 us -> 60.1 us (0.971)
  waiting for transfers between devices: 21.1 us -> 19.8 us
  local copies, waits for them, and re-layouts: 1.35 us -> 0.1 us
  Pallas kernels: 11.5 us -> 12.7 us
    ppermute x14, waiting for transfers between devices: 15.4 us -> 13.9 us  [brought(): return [block] + [lax.ppermute(block, axis, pairs) for pairs in swaps(axis)]]
    unnamed x20 -> x0, local copies, waits for them, and re-layouts: 1.25 us -> none
    pallas_call x7 -> x8, Pallas kernels: 11.5 us -> 12.7 us  [simple_call(): pl.pallas_call(body, out_shape=shapes, in_specs=[SMEM_SPEC] * scalars + [...]
  transfers between devices with their start and end apart: 15 -> 15, of which waited for: 9 -> 11; matrix products, arithmetic and copies ran while one was open for 0% -> 0% of each run, Pallas kernels for 5% -> 7%
where the time goes in v3:
time: 60.1 us; the launch traced here: 59.9 us
  waiting for transfers between devices  19.8 us (33%)
  starting transfers between devices  15.7 us (26%)
  Pallas kernels  12.7 us (21%)
  blocking collectives  10.1 us (17%)
  between operations  1.39 us (2%)
    ppermute x14, waiting for transfers between devices, brought(): return [block] + [lax.ppermute(block, axis, pairs) for pairs in swaps(axis)]  13.9 us
    pallas_call x8, Pallas kernels, simple_call(): pl.pallas_call(body, out_shape=shapes, in_specs=[SMEM_SPEC] * scalars + [...  12.7 us
    all_to_all x1, blocking collectives, everywhere(): return lax.all_to_all(copies, AXES, 0, 0, tiled=True)  10.1 us
    ppermute x14, starting transfers between devices, brought(): return [block] + [lax.ppermute(block, axis, pairs) for pairs in swaps(axis)]  8.42 us
    all_to_all x1, starting transfers between devices, everywhere(): return lax.all_to_all(copies, AXES, 0, 0, tiled=True)  7.3 us
    all_to_all x1, waiting for transfers between devices, everywhere(): return lax.all_to_all(copies, AXES, 0, 0, tiled=True)  5.95 us
  transfers between devices with their start and end apart: 15, of which 11 were waited for; matrix products, arithmetic and copies ran while one was open for 0% of the time, Pallas kernels for 7%

profile of v3, /device:TPU:0, one launch (start us, length us, event | category | flops | bytes accessed | tf_op | source)
XLA Modules:
  0.0 59.9 jit_solution(17420582453121535025)
XLA Ops:
  1.3 1.4 %shard_map.130 = f32[32,4,128]{2,1,0:T(4,128)} custom-call(s32[1]{0:T(128)} %bitcast.39.refs_0_, f32[3,1,64]{2,1,0:T(1,128)} %bitcast.47, s32[1,64]{1,0:T(1,128)} %bitcast.49), custom_call_target="tpu_custom_call" | custom-call | flops 1048576 | bytes 1048576 | tf_op jit(solution)/shard_map/pallas_call | solution.py:478
  2.7 7.3 %all-to-all-start = ((f32[32,4,128]{2,1,0:T(4,128)}), f32[32,4,128]{2,1,0:T(4,128)S(1)}, u32[]{:S(2)}, u32[]{:S(2)}) async-start(f32[32,4,128]{2,1,0:T(4,128)} %shard_map.130), calls=%async_computation | async-start | bytes 131072 | tf_op jit(solution)/shard_map/all_to_all | solution.py:524
  10.0 0.1 stack.111.refs_0_
  10.1 1.4 %shard_map.131 = (f32[64,8]{1,0:T(8,128)S(1)}, bf16[2,32,128]{2,1,0:T(8,128)(2,1)S(1)}, f32[64,128]{1,0:T(8,128)S(1)}, f32[4,128]{1,0:T(4,128)S(1)}, f32[1,16]{1...) custom-call(s32[1]{0:T(128)} %bitcast.40.refs_0_, ...), custom_call_target="tpu_custom_call" | custom-call | flops 1048576 | bytes 1048576 | tf_op jit(solution)/shard_map/pallas_call | solution.py:478
  11.5 5.9 %all-to-all-done.refs_1_ = f32[32,4,128]{2,1,0:T(4,128)S(1)} async-done(((f32[32,4,128]{2,1,0:T(4,128)}), f32[32,4,128]{2,1,0:T(4,128)S(1)}, u32[]{:S(2)}, u32[]{:S(2)}) %all-to-all-start) | async-done | bytes 65568 | tf_op jit(solution)/shard_map/all_to_all | solution.py:524
  17.5 2.4 %shard_map.132 = (f32[9,4,128]{2,1,0:T(4,128)S(1)}, bf16[4,64,1152]{2,1,0:T(8,128)(2,1)S(1)}, bf16[64,128]{1,0:T(8,128)(2,1)S(1)}, f32[192,128]{1,0:T(8,128)S(1)}, f32[64,128]{1,0:T(8,128)S(1)}) custom-call(s32[22]{0:T(128)S(1)} %stack.111.refs_0_, f32[32,4,128]{2,1,0:T(4,128)S(1)} %all-to-all-done.refs_1_, ...), custom_call_target="tpu_custom_call" | custom-call | flops 7372800 | bytes 1048576 | tf_op jit(solution)/shard_map/pallas_call | solution.py:478
  19.9 0.9 %collective-permute-start.1 = (bf16[64,128]{1,0:T(8,128)(2,1)S(1)}, bf16[64,128]{1,0:T(8,128)(2,1)S(1)}, u32[]{:S(2)}, u32[]{:S(2)}) collective-permute-start(bf16[64,128]{1,0:T(8,128)(2,1)S(1)} %get-tuple-element.35.refs_2_.refs_7_.refs_11_), channel_id=1, source_target_pairs={{0,3},{1,2},{2,1},{3,0},{4,7},{5,6},{6,5},{7,4},{8,11},{9,10},{10,... | collective-permute-start | bytes 49160 | tf_op jit(solution)/shard_map/ppermute | solution.py:512
  20.8 0.2 collective-permute-start
  21.0 1.2 %shard_map.133 = (bf16[64,128]{1,0:T(8,128)(2,1)S(1)}, f32[3,64,1152]{2,1,0:T(8,128)S(1)}, f32[4,64,1152]{2,1,0:T(8,128)S(1)}, f32[4,64,1152]{2,1,0:T(8,128)S(1)}, f32[4,64,1152]{2,1,0:T(8,128)S(1)}) custom-call(f32[9,4,128]{2,1,0:T(4,128)S(1)} %get-tuple-element.34.refs_0_.refs_10_, f32[64,8]{1,0:T(8,128)S(1)} %get-tuple-element.30.refs_2_.refs_1_.refs_9_.refs_10_, ...), custom_call_target="tpu_custom_call" | custom-call | flops 7372800 | bytes 1048576 | tf_op jit(solution)/shard_map/pallas_call | solution.py:478
  22.2 3.3 %collective-permute-done.1 = bf16[64,128]{1,0:T(8,128)(2,1)S(1)} collective-permute-done((bf16[64,128]{1,0:T(8,128)(2,1)S(1)}, bf16[64,128]{1,0:T(8,128)(2,1)S(1)}, u32[]{:S(2)}, u32[]{:S(2)}) %collective-permute-start.1) | collective-permute-done | bytes 16416 | tf_op jit(solution)/shard_map/ppermute | solution.py:512
  25.5 0.0 collective-permute-done
  25.5 0.7 %collective-permute-start.3 = (bf16[3,64,128]{2,1,0:T(8,128)(2,1)S(1)}, bf16[3,64,128]{2,1,0:T(8,128)(2,1)S(1)}, u32[]{:S(2)}, u32[]{:S(2)}) collective-permute-start(bf16[3,64,128]{2,1,0:T(8,128)(2,1)S(1)} %pad_maximum_fusion.refs_1_), channel_id=1, source_target_pairs={{0,24},{8,16},{16,8},{24,0},{1,25},{9,17},{17,9},{25,1},{2,26},{10... | collective-permute-start | bytes 147464 | tf_op jit(solution)/shard_map/ppermute | solution.py:512
  26.2 1.5 %collective-permute-start.2 = (bf16[3,64,128]{2,1,0:T(8,128)(2,1)S(1)}, bf16[3,64,128]{2,1,0:T(8,128)(2,1)S(1)}, u32[]{:S(2)}, u32[]{:S(2)}) collective-permute-start(bf16[3,64,128]{2,1,0:T(8,128)(2,1)S(1)} %pad_maximum_fusion.refs_1_), channel_id=1, source_target_pairs={{0,8},{8,0},{16,24},{24,16},{1,9},{9,1},{17,25},{25,17},{2,10},{10... | collective-permute-start | bytes 147464 | tf_op jit(solution)/shard_map/ppermute | solution.py:512
  27.7 0.0 collective-permute-start.4
  27.7 2.9 %collective-permute-done.3.refs_3_ = bf16[3,64,128]{2,1,0:T(8,128)(2,1)S(1)} collective-permute-done((bf16[3,64,128]{2,1,0:T(8,128)(2,1)S(1)}, bf16[3,64,128]{2,1,0:T(8,128)(2,1)S(1)}, u32[]{:S(2)}, u32[]{:S(2)}) %collective-permute-start.3) | collective-permute-done | bytes 49184 | tf_op jit(solution)/shard_map/ppermute | solution.py:512
  30.6 0.0 collective-permute-start.6
  30.6 0.0 collective-permute-done.2.refs_2_
  30.6 0.5 collective-permute-start.5
  31.1 0.0 collective-permute-done.4.refs_4_
  31.1 0.7 %collective-permute-done.6.refs_6_ = bf16[3,64,128]{2,1,0:T(8,128)(2,1)S(1)} collective-permute-done((bf16[3,64,128]{2,1,0:T(8,128)(2,1)S(1)}, bf16[3,64,128]{2,1,0:T(8,128)(2,1)S(1)}, u32[]{:S(2)}, u32[]{:S(2)}) %collective-permute-start.6) | collective-permute-done | bytes 49184 | tf_op jit(solution)/shard_map/ppermute | solution.py:512
  31.8 0.2 collective-permute-done.5.refs_5_
  32.0 1.4 %shard_map.134 = (bf16[64,128]{1,0:T(8,128)(2,1)S(1)}, bf16[64,128]{1,0:T(8,128)(2,1)S(1)}, f32[64,16]{1,0:T(8,128)S(1)}, f32[64,128]{1,0:T(8,128)S(1)}) custom-call(s32[22]{0:T(128)S(1)} %stack.111.refs_0_, bf16[3,64,128]{2,1,0:T(8,128)(2,1)S(1)} %pad_maximum_fusion.refs_1_, bf16[3,64,128]{2,1,0:T(8,128)(2,1)S(1)} %collective-permute-done.2.refs_2_, ...), custom_call_target="tpu_custom_call" | custom-call | flops 7372800 | bytes 1048576 | tf_op jit(solution)/shard_map/pallas_call | solution.py:478
  33.4 2.0 %collective-permute-start.8 = (bf16[64,128]{1,0:T(8,128)(2,1)S(1)}, bf16[64,128]{1,0:T(8,128)(2,1)S(1)}, u32[]{:S(2)}, u32[]{:S(2)}) collective-permute-start(bf16[64,128]{1,0:T(8,128)(2,1)S(1)} %get-tuple-element.43.refs_7_), channel_id=1, source_target_pairs={{0,3},{1,2},{2,1},{3,0},{4,7},{5,6},{6,5},{7,4},{8,11},{9,10},{10,... | collective-permute-start | bytes 49160 | tf_op jit(solution)/shard_map/ppermute | solution.py:512
  35.4 0.0 collective-permute-start.7
  35.4 1.6 %shard_map.135 = (bf16[64,128]{1,0:T(8,128)(2,1)S(1)}, f32[64,1152]{1,0:T(8,128)S(1)}, f32[1,64]{1,0:T(1,128)}, bf16[64,128]{1,0:T(8,128)(2,1)}) custom-call(s32[22]{0:T(128)S(1)} %stack.111.refs_0_, bf16[3,64,128]{2,1,0:T(8,128)(2,1)S(1)} %pad_maximum_fusion.refs_1_, bf16[3,64,128]{2,1,0:T(8,128)(2,1)S(1)} %collective-permute-done.2.refs_2_, ...), custom_call_target="tpu_custom_call" | custom-call | flops 7372800 | bytes 1048576 | tf_op jit(solution)/shard_map/pallas_call | solution.py:478
  37.0 1.9 %collective-permute-done.8 = bf16[64,128]{1,0:T(8,128)(2,1)S(1)} collective-permute-done((bf16[64,128]{1,0:T(8,128)(2,1)S(1)}, bf16[64,128]{1,0:T(8,128)(2,1)S(1)}, u32[]{:S(2)}, u32[]{:S(2)}) %collective-permute-start.8) | collective-permute-done | bytes 16416 | tf_op jit(solution)/shard_map/ppermute | solution.py:512
  38.9 0.2 collective-permute-done.7
  39.2 1.9 %collective-permute-start.10 = (bf16[3,64,128]{2,1,0:T(8,128)(2,1)S(1)}, bf16[3,64,128]{2,1,0:T(8,128)(2,1)S(1)}, u32[]{:S(2)}, u32[]{:S(2)}) collective-permute-start(bf16[3,64,128]{2,1,0:T(8,128)(2,1)S(1)} %pad_maximum_fusion.1.refs_1_), channel_id=1, source_target_pairs={{0,24},{8,16},{16,8},{24,0},{1,25},{9,17},{17,9},{25,1},{2,26},{10... | collective-permute-start | bytes 147464 | tf_op jit(solution)/shard_map/ppermute | solution.py:512
  41.1 0.7 %collective-permute-start.9 = (bf16[3,64,128]{2,1,0:T(8,128)(2,1)S(1)}, bf16[3,64,128]{2,1,0:T(8,128)(2,1)S(1)}, u32[]{:S(2)}, u32[]{:S(2)}) collective-permute-start(bf16[3,64,128]{2,1,0:T(8,128)(2,1)S(1)} %pad_maximum_fusion.1.refs_1_), channel_id=1, source_target_pairs={{0,8},{8,0},{16,24},{24,16},{1,9},{9,1},{17,25},{25,17},{2,10},{10... | collective-permute-start | bytes 147464 | tf_op jit(solution)/shard_map/ppermute | solution.py:512
  41.8 0.0 collective-permute-start.11
  41.8 2.5 %collective-permute-done.10.refs_3_ = bf16[3,64,128]{2,1,0:T(8,128)(2,1)S(1)} collective-permute-done((bf16[3,64,128]{2,1,0:T(8,128)(2,1)S(1)}, bf16[3,64,128]{2,1,0:T(8,128)(2,1)S(1)}, u32[]{:S(2)}, u32[]{:S(2)}) %collective-permute-start.10) | collective-permute-done | bytes 49184 | tf_op jit(solution)/shard_map/ppermute | solution.py:512
  44.2 0.0 collective-permute-start.13
  44.2 1.0 %collective-permute-done.9.refs_2_ = bf16[3,64,128]{2,1,0:T(8,128)(2,1)S(1)} collective-permute-done((bf16[3,64,128]{2,1,0:T(8,128)(2,1)S(1)}, bf16[3,64,128]{2,1,0:T(8,128)(2,1)S(1)}, u32[]{:S(2)}, u32[]{:S(2)}) %collective-permute-start.9) | collective-permute-done | bytes 49184 | tf_op jit(solution)/shard_map/ppermute | solution.py:512
  45.2 0.0 collective-permute-start.12
  45.2 0.0 collective-permute-done.11.refs_4_
  45.2 0.3 collective-permute-done.13.refs_6_
  45.5 1.0 %collective-permute-done.12.refs_5_ = bf16[3,64,128]{2,1,0:T(8,128)(2,1)S(1)} collective-permute-done((bf16[3,64,128]{2,1,0:T(8,128)(2,1)S(1)}, bf16[3,64,128]{2,1,0:T(8,128)(2,1)S(1)}, u32[]{:S(2)}, u32[]{:S(2)}) %collective-permute-start.12) | collective-permute-done | bytes 49184 | tf_op jit(solution)/shard_map/ppermute | solution.py:512
  46.4 2.6 %shard_map.136 = f32[32,4,128]{2,1,0:T(4,128)S(1)} custom-call(s32[22]{0:T(128)S(1)} %stack.111.refs_0_, bf16[3,64,128]{2,1,0:T(8,128)(2,1)S(1)} %pad_maximum_fusion.1.refs_1_, bf16[3,64,128]{2,1,0:T(8,128)(2,1)S(1)} %collective-permute-done.9.refs_2_, bf16[3,64,128]{2,1,0:T(8,128)(2,1)S(1)} %collective-permute-done.10.refs_3_, ...), custom_call_target="tpu_custom_call" | custom-call | flops 7372800 | bytes 1048576 | tf_op jit(solution)/shard_map/pallas_call | solution.py:478
  49.0 10.1 %all_to_all.10.refs_0_ = f32[32,4,128]{2,1,0:T(4,128)S(1)} all-to-all(f32[32,4,128]{2,1,0:T(4,128)S(1)} %shard_map.136), channel_id=1, replica_groups=mesh['gx'=4,'gy'=2,'gz'=4] {'gx','gy','gz'}, dimensions={0} | all-to-all | bytes 131072 | tf_op jit(solution)/shard_map/all_to_all | solution.py:524
  59.2 0.7 %shard_map.137 = f32[3,1,64]{2,1,0:T(1,128)} custom-call(f32[32,4,128]{2,1,0:T(4,128)S(1)} %all_to_all.10.refs_0_), custom_call_target="tpu_custom_call" | custom-call | flops 1048576 | bytes 1048576 | tf_op jit(solution)/shard_map/pallas_call | solution.py:478
  (2 shorter events, 0.0 us)
Async XLA Ops:
  2.7 14.8 %all-to-all-start = ((f32[32,4,128]{2,1,0:T(4,128)}), f32[32,4,128]{2,1,0:T(4,128)S(1)}, u32[]{:S(2)}, u32[]{:S(2)}) async-start(f32[32,4,128]{2,1,0:T(4,128)} %shard_map.130), calls=%async_computation | async-start | bytes 131072 | tf_op jit(solution)/shard_map/all_to_all | solution.py:524
  19.9 5.6 %collective-permute-start.1 = (bf16[64,128]{1,0:T(8,128)(2,1)S(1)}, bf16[64,128]{1,0:T(8,128)(2,1)S(1)}, u32[]{:S(2)}, u32[]{:S(2)}) collective-permute-start(bf16[64,128]{1,0:T(8,128)(2,1)S(1)} %get-tuple-element.35.refs_2_.refs_7_.refs_11_), channel_id=1, source_target_pairs={{0,3},{1,2},{2,1},{3,0},{4,7},{5,6},{6,5},{7,4},{8,11},{9,10},{10,... | collective-permute-start | bytes 49160 | tf_op jit(solution)/shard_map/ppermute | solution.py:512
  20.8 4.7 %collective-permute-start = (bf16[64,128]{1,0:T(8,128)(2,1)S(1)}, bf16[64,128]{1,0:T(8,128)(2,1)S(1)}, u32[]{:S(2)}, u32[]{:S(2)}) collective-permute-start(bf16[64,128]{1,0:T(8,128)(2,1)S(1)} %get-tuple-element.35.refs_2_.refs_7_.refs_11_), channel_id=1, source_target_pairs={{0,1},{1,0},{2,3},{3,2},{4,5},{5,4},{6,7},{7,6},{8,9},{9,8},{10,11... | collective-permute-start | bytes 49160 | tf_op jit(solution)/shard_map/ppermute | solution.py:512
  25.5 5.1 %collective-permute-start.3 = (bf16[3,64,128]{2,1,0:T(8,128)(2,1)S(1)}, bf16[3,64,128]{2,1,0:T(8,128)(2,1)S(1)}, u32[]{:S(2)}, u32[]{:S(2)}) collective-permute-start(bf16[3,64,128]{2,1,0:T(8,128)(2,1)S(1)} %pad_maximum_fusion.refs_1_), channel_id=1, source_target_pairs={{0,24},{8,16},{16,8},{24,0},{1,25},{9,17},{17,9},{25,1},{2,26},{10... | collective-permute-start | bytes 147464 | tf_op jit(solution)/shard_map/ppermute | solution.py:512
  26.2 4.4 %collective-permute-start.2 = (bf16[3,64,128]{2,1,0:T(8,128)(2,1)S(1)}, bf16[3,64,128]{2,1,0:T(8,128)(2,1)S(1)}, u32[]{:S(2)}, u32[]{:S(2)}) collective-permute-start(bf16[3,64,128]{2,1,0:T(8,128)(2,1)S(1)} %pad_maximum_fusion.refs_1_), channel_id=1, source_target_pairs={{0,8},{8,0},{16,24},{24,16},{1,9},{9,1},{17,25},{25,17},{2,10},{10... | collective-permute-start | bytes 147464 | tf_op jit(solution)/shard_map/ppermute | solution.py:512
  27.7 3.4 %collective-permute-start.4 = (bf16[3,64,128]{2,1,0:T(8,128)(2,1)S(1)}, bf16[3,64,128]{2,1,0:T(8,128)(2,1)S(1)}, u32[]{:S(2)}, u32[]{:S(2)}) collective-permute-start(bf16[3,64,128]{2,1,0:T(8,128)(2,1)S(1)} %pad_maximum_fusion.refs_1_), channel_id=1, source_target_pairs={{0,4},{4,0},{1,5},{5,1},{2,6},{6,2},{3,7},{7,3},{8,12},{12,8},{9,1... | collective-permute-start | bytes 147464 | tf_op jit(solution)/shard_map/ppermute | solution.py:512
  30.6 1.2 %collective-permute-start.6 = (bf16[3,64,128]{2,1,0:T(8,128)(2,1)S(1)}, bf16[3,64,128]{2,1,0:T(8,128)(2,1)S(1)}, u32[]{:S(2)}, u32[]{:S(2)}) collective-permute-start(bf16[3,64,128]{2,1,0:T(8,128)(2,1)S(1)} %collective-permute-done.3.refs_3_), channel_id=1, source_target_pairs={{0,4},{4,0},{1,5},{5,1},{2,6},{6,2},{3,7},{7,3},{8,12},{12,8},{9,1... | collective-permute-start | bytes 147464 | tf_op jit(solution)/shard_map/ppermute | solution.py:512
  30.6 1.4 %collective-permute-start.5 = (bf16[3,64,128]{2,1,0:T(8,128)(2,1)S(1)}, bf16[3,64,128]{2,1,0:T(8,128)(2,1)S(1)}, u32[]{:S(2)}, u32[]{:S(2)}) collective-permute-start(bf16[3,64,128]{2,1,0:T(8,128)(2,1)S(1)} %collective-permute-done.2.refs_2_), channel_id=1, source_target_pairs={{0,4},{4,0},{1,5},{5,1},{2,6},{6,2},{3,7},{7,3},{8,12},{12,8},{9,1... | collective-permute-start | bytes 147464 | tf_op jit(solution)/shard_map/ppermute | solution.py:512
  33.4 5.5 %collective-permute-start.8 = (bf16[64,128]{1,0:T(8,128)(2,1)S(1)}, bf16[64,128]{1,0:T(8,128)(2,1)S(1)}, u32[]{:S(2)}, u32[]{:S(2)}) collective-permute-start(bf16[64,128]{1,0:T(8,128)(2,1)S(1)} %get-tuple-element.43.refs_7_), channel_id=1, source_target_pairs={{0,3},{1,2},{2,1},{3,0},{4,7},{5,6},{6,5},{7,4},{8,11},{9,10},{10,... | collective-permute-start | bytes 49160 | tf_op jit(solution)/shard_map/ppermute | solution.py:512
  35.4 3.7 %collective-permute-start.7 = (bf16[64,128]{1,0:T(8,128)(2,1)S(1)}, bf16[64,128]{1,0:T(8,128)(2,1)S(1)}, u32[]{:S(2)}, u32[]{:S(2)}) collective-permute-start(bf16[64,128]{1,0:T(8,128)(2,1)S(1)} %get-tuple-element.43.refs_7_), channel_id=1, source_target_pairs={{0,1},{1,0},{2,3},{3,2},{4,5},{5,4},{6,7},{7,6},{8,9},{9,8},{10,11... | collective-permute-start | bytes 49160 | tf_op jit(solution)/shard_map/ppermute | solution.py:512
  39.2 5.1 %collective-permute-start.10 = (bf16[3,64,128]{2,1,0:T(8,128)(2,1)S(1)}, bf16[3,64,128]{2,1,0:T(8,128)(2,1)S(1)}, u32[]{:S(2)}, u32[]{:S(2)}) collective-permute-start(bf16[3,64,128]{2,1,0:T(8,128)(2,1)S(1)} %pad_maximum_fusion.1.refs_1_), channel_id=1, source_target_pairs={{0,24},{8,16},{16,8},{24,0},{1,25},{9,17},{17,9},{25,1},{2,26},{10... | collective-permute-start | bytes 147464 | tf_op jit(solution)/shard_map/ppermute | solution.py:512
  41.1 4.1 %collective-permute-start.9 = (bf16[3,64,128]{2,1,0:T(8,128)(2,1)S(1)}, bf16[3,64,128]{2,1,0:T(8,128)(2,1)S(1)}, u32[]{:S(2)}, u32[]{:S(2)}) collective-permute-start(bf16[3,64,128]{2,1,0:T(8,128)(2,1)S(1)} %pad_maximum_fusion.1.refs_1_), channel_id=1, source_target_pairs={{0,8},{8,0},{16,24},{24,16},{1,9},{9,1},{17,25},{25,17},{2,10},{10... | collective-permute-start | bytes 147464 | tf_op jit(solution)/shard_map/ppermute | solution.py:512
  41.8 3.4 %collective-permute-start.11 = (bf16[3,64,128]{2,1,0:T(8,128)(2,1)S(1)}, bf16[3,64,128]{2,1,0:T(8,128)(2,1)S(1)}, u32[]{:S(2)}, u32[]{:S(2)}) collective-permute-start(bf16[3,64,128]{2,1,0:T(8,128)(2,1)S(1)} %pad_maximum_fusion.1.refs_1_), channel_id=1, source_target_pairs={{0,4},{4,0},{1,5},{5,1},{2,6},{6,2},{3,7},{7,3},{8,12},{12,8},{9,1... | collective-permute-start | bytes 147464 | tf_op jit(solution)/shard_map/ppermute | solution.py:512
  44.2 1.2 %collective-permute-start.13 = (bf16[3,64,128]{2,1,0:T(8,128)(2,1)S(1)}, bf16[3,64,128]{2,1,0:T(8,128)(2,1)S(1)}, u32[]{:S(2)}, u32[]{:S(2)}) collective-permute-start(bf16[3,64,128]{2,1,0:T(8,128)(2,1)S(1)} %collective-permute-done.10.refs_3_), channel_id=1, source_target_pairs={{0,4},{4,0},{1,5},{5,1},{2,6},{6,2},{3,7},{7,3},{8,12},{12,8},{9,1... | collective-permute-start | bytes 147464 | tf_op jit(solution)/shard_map/ppermute | solution.py:512
  45.2 1.2 %collective-permute-start.12 = (bf16[3,64,128]{2,1,0:T(8,128)(2,1)S(1)}, bf16[3,64,128]{2,1,0:T(8,128)(2,1)S(1)}, u32[]{:S(2)}, u32[]{:S(2)}) collective-permute-start(bf16[3,64,128]{2,1,0:T(8,128)(2,1)S(1)} %collective-permute-done.9.refs_2_), channel_id=1, source_target_pairs={{0,4},{4,0},{1,5},{5,1},{2,6},{6,2},{3,7},{7,3},{8,12},{12,8},{9,1... | collective-permute-start | bytes 147464 | tf_op jit(solution)/shard_map/ppermute | solution.py:512

commit v4 on v3

--- a/solution.py
+++ b/solution.py
@@ -63,6 +63,10 @@
     return count > 2 and count % 2 == 0
 
 
+def matched(which, parity):
+    return jnp.int32(0) if which == 0 else 1 + (parity if which == 1 else 1 - parity)
+
+
 def poly(terms, arg):
     total = arg * terms[-1] + terms[-2]
     for term in terms[-3::-1]:
@@ -85,6 +89,8 @@
         self.nspec = nspec
         self.depth = len(offsets_of(self.sizes["gz"]))
         self.wide = len(offsets_of(self.sizes["gx"]))
+        self.brought = list(itertools.product(range(self.wide), range(self.depth)))
+        self.mixed = self.depth == self.wide and self.sizes["gy"] % 2 == 0
         self.small = self.ndev <= 64 and len(self.sides) == 2
         self.wrapped = [self.sizes[axis] == 2 for axis in AXES]
 
@@ -97,22 +103,34 @@
         def moved(axis, step):
             return lax.rem(index[axis] + (step + self.sizes[axis]), self.sizes[axis])
 
-        depth = len(offsets_of(self.sizes["gz"]))
-        turn = parity("gz")
-        found = [jnp.int32(0), 1 + turn, 2 - turn][:depth] + [parity("gx")]
+        turns = parity("gx"), parity("gz")
+        core = lax.rem(index["gy"], 2) if self.mixed else jnp.int32(0)
+        found = []
+        for side in range(len(self.sides)):
+            x_first = core if side == 0 or not self.mixed else 1 - core
+            for second, first in self.brought:
+                plain = matched(second, turns[0]) * self.depth + matched(first, turns[1])
+                crossed = matched(first, turns[0]) * self.depth + matched(second, turns[1])
+                tile = jnp.where(x_first == 1, crossed, plain) if self.mixed else plain
+                found.append(tile * len(self.sides) + side)
+        found += turns
         for ox, oz in self.tiles:
             for oy in self.sides:
                 place = (moved("gx", ox) * self.sizes["gy"] + moved("gy", oy)) * self.sizes["gz"]
                 found.append(place + moved("gz", oz))
         return jnp.stack(found).astype(jnp.int32)
 
+    def brought_place(self, places_ref, side, pair):
+        return places_ref[side * len(self.brought) + pair]
+
     def global_place(self, places_ref, tile, side):
-        return places_ref[self.depth + 1 + tile * len(self.sides) + side]
+        start = len(self.sides) * len(self.brought) + 2
+        return places_ref[start + tile * len(self.sides) + side]
 
     def staged_place(self, places_ref, tile):
+        start = len(self.sides) * len(self.brought)
         x, z = divmod(tile, self.depth)
-        flip = places_ref[self.depth]
-        return (0, 1 + flip, 2 - flip)[x] * self.depth + places_ref[z]
+        return matched(x, places_ref[start]) * self.depth + matched(z, places_ref[start + 1])
 
     def offset(self, tile, side):
         ox, oz = self.tiles[tile]
@@ -147,13 +165,22 @@
 def first_kernel(plan, nrefs, places_ref, *refs):
     far_refs, refs = refs[:nrefs], refs[nrefs:]
     (cols_ref, table_ref, embed_ref, mix_ref), refs = refs[:4], refs[4:]
-    rows_ref, basis_ref, layer_ref, vector_ref, mixing_ref, pair_ref = refs
+    rows_ref, basis_ref, layer_ref, vector_ref, mixing_ref, pair_ref, block_ref = refs
     slots, nbasis, nspec = plan.slots, plan.nbasis, plan.nspec
     cols = [cols_ref[:, axis : axis + 1] for axis in range(3)]
     species = lax.broadcasted_iota(jnp.int32, (nbasis * nspec, plan.width), 0) % nspec
     hot = []
+
+    def put(place, block):
+        block_ref[place] = block
+
+    if not plan.small:
+        scatter(plan, places_ref, far_refs, put)
     for tile in range(len(plan.tiles)):
-        blocks = [fetch(plan, places_ref, far_refs, tile, side) for side in range(len(plan.sides))]
+        if plan.small:
+            blocks = [far_refs[0][plan.global_place(places_ref, tile, s)] for s in range(len(plan.sides))]
+        else:
+            blocks = [block_ref[tile * len(plan.sides) + s] for s in range(len(plan.sides))]
         placed = side_by_side(plan, blocks) + tile_shift(plan, tile)
         rows_ref[tile] = placed
         rows = [placed[k : k + 1] for k in range(4)]
@@ -199,16 +226,11 @@
     return 1.0 / (1.0 + jnp.exp(-value))
 
 
-def fetch(plan, places_ref, far_refs, tile, side):
-    if len(far_refs) == 1:
-        return far_refs[0][plan.global_place(places_ref, tile, side)]
-    x, z = divmod(tile, plan.depth)
-    place = places_ref[z]
-    columns = far_refs[side * plan.wide : (side + 1) * plan.wide]
-    if x == 0 or plan.wide == 2:
-        return columns[x][place]
-    kept, other = columns[x][place], columns[3 - x][place]
-    return jnp.where(places_ref[plan.depth] == 0, kept, other)
+def scatter(plan, places_ref, far_refs, put):
+    for side in range(len(plan.sides)):
+        for pair, (second, first) in enumerate(plan.brought):
+            block = far_refs[side * plan.wide + second][first]
+            put(plan.brought_place(places_ref, side, pair), block)
 
 
 def side_by_side(plan, blocks):
@@ -230,11 +252,11 @@
 
 
 def gather_far(plan, places_ref, far_refs, all_ref):
-    slots = plan.slots
-    for tile in range(len(plan.tiles)):
-        for side in range(len(plan.sides)):
-            start = tile * plan.width + side * slots
-            all_ref[start : start + slots] = fetch(plan, places_ref, far_refs, tile, side)
+    def put(place, block):
+        start = pl.multiple_of(place * plan.slots, plan.slots)
+        all_ref[pl.ds(start, plan.slots)] = block
+
+    scatter(plan, places_ref, far_refs, put)
 
 
 def second_kernel(plan, nrefs, places_ref, *refs):
@@ -497,26 +519,44 @@
     return simple_call(body, plan, [places, *far, *operands], outs, 1, scratch, flops)
 
 
-def swaps(axis):
-    count = lax.axis_size(axis)
+def swaps(count):
     if count == 2:
-        return [[(0, 1), (1, 0)]]
+        return [[1, 0]]
     if paired(count):
-        near = [(i, i ^ 1) for i in range(count)]
-        far = [(i, (i - 1 + 2 * (i % 2)) % count) for i in range(count)]
+        near = [i ^ 1 for i in range(count)]
+        far = [(i - 1 + 2 * (i % 2)) % count for i in range(count)]
         return [near, far]
-    return [[((i + o) % count, i) for i in range(count)] for o in offsets_of(count)[1:]]
-
-
-def brought(block, axis):
-    return [block] + [lax.ppermute(block, axis, pairs) for pairs in swaps(axis)]
+    return [[(i + o) % count for i in range(count)] for o in offsets_of(count)[1:]]
+
+
+def brought(plan, block, second):
+    sizes, sources = plan.sizes, {axis: swaps(plan.sizes[axis]) for axis in AXES}
+    got = []
+    for m in range(len(sources["gx" if second else "gz"])):
+        pairs = []
+        for x, y, z in itertools.product(*(range(sizes[axis]) for axis in AXES)):
+            along_x = second != (plan.mixed and y % 2 == 1)
+            source = (sources["gx"][m][x], y, z) if along_x else (x, y, sources["gz"][m][z])
+            pairs.append((flat(sizes, *source), flat(sizes, x, y, z)))
+        got.append(lax.ppermute(block, AXES, pairs))
+    return got
+
+
+def flat(sizes, x, y, z):
+    return (x * sizes["gy"] + y) * sizes["gz"] + z
+
+
+def along(block, axis):
+    return [
+        lax.ppermute(block, axis, [(source, i) for i, source in enumerate(sources)])
+        for sources in swaps(lax.axis_size(axis))
+    ]
 
 
 def neighbours(plan, block, again=None):
-    column = brought(block, "gz")
-    column = jnp.stack([block if again is None else again] + column[1:])
-    columns = brought(column, "gx")
-    swapped = [brought(column, "gy") for column in columns]
+    column = jnp.stack([block if again is None else again] + brought(plan, block, False))
+    columns = [column] + brought(plan, column, True)
+    swapped = [[column] + along(column, "gy") for column in columns]
     return [column[side] for side in range(len(plan.sides)) for column in swapped]
 
 
@@ -525,13 +565,9 @@
 
 
 def folded(pieces, axis):
-    got = [
-        lax.ppermute(piece, axis, [(to, source) for source, to in pairs])
-        for piece, pairs in list(zip(pieces[1:], swaps(axis)))[::-1]
-    ]
     total = pieces[0]
-    for piece in got:
-        total = total + piece
+    for piece, sources in zip(pieces[1:], swaps(lax.axis_size(axis))):
+        total = total + lax.ppermute(piece, axis, list(enumerate(sources)))
     return total
 
 
@@ -607,7 +643,10 @@
                 ((3 * slots, channels), F32),
                 ((slots, channels), F32),
             ],
-            [((nbasis, 4 * slots, plan.far), BF16)],
+            [
+                ((nbasis, 4 * slots, plan.far), BF16),
+                ((len(plan.tiles) * len(plan.sides), 4, 2 * slots), F32),
+            ],
             pair_flops,
         )
         again, apart, slope, factor, turned = simple_call(

time: 60.1 us -> 60.1 us (level)
  no operation moved by 1% of the time
where the time goes in v4:
time: 60.1 us; the launch traced here: 59.8 us
  waiting for transfers between devices  19.8 us (33%)
  starting transfers between devices  15.7 us (26%)
  Pallas kernels  12.7 us (21%)
  blocking collectives  10.1 us (17%)
  between operations  1.41 us (2%)
    pallas_call x8, Pallas kernels, simple_call(): pl.pallas_call(body, out_shape=shapes, in_specs=[SMEM_SPEC] * scalars + [...  12.7 us
    ppermute x8, waiting for transfers between devices, brought(): got.append(lax.ppermute(block, AXES, pairs))  11.8 us
    all_to_all x1, blocking collectives, everywhere(): return lax.all_to_all(copies, AXES, 0, 0, tiled=True)  10.1 us
    ppermute x8, starting transfers between devices, brought(): got.append(lax.ppermute(block, AXES, pairs))  7.9 us
    all_to_all x1, starting transfers between devices, everywhere(): return lax.all_to_all(copies, AXES, 0, 0, tiled=True)  7.3 us
    all_to_all x1, waiting for transfers between devices, everywhere(): return lax.all_to_all(copies, AXES, 0, 0, tiled=True)  5.91 us
    ppermute x6, waiting for transfers between devices, along(): lax.ppermute(block, axis, [(source, i) for i, source in enumerate(sources)])  2.11 us
  transfers between devices with their start and end apart: 15, of which 11 were waited for; matrix products, arithmetic and copies ran while one was open for 0% of the time, Pallas kernels for 7%

profile of v4, /device:TPU:0, one launch (start us, length us, event | category | flops | bytes accessed | tf_op | source)
XLA Modules:
  0.0 59.8 jit_solution(5779441909716902783)
XLA Ops:
  1.3 1.4 %shard_map.130 = f32[32,4,128]{2,1,0:T(4,128)} custom-call(s32[1]{0:T(128)} %bitcast.54.refs_0_, f32[3,1,64]{2,1,0:T(1,128)} %bitcast.62, s32[1,64]{1,0:T(1,128)} %bitcast.64), custom_call_target="tpu_custom_call" | custom-call | flops 1048576 | bytes 1048576 | tf_op jit(solution)/shard_map/pallas_call | solution.py:500
  2.7 7.3 %all-to-all-start = ((f32[32,4,128]{2,1,0:T(4,128)}), f32[32,4,128]{2,1,0:T(4,128)S(1)}, u32[]{:S(2)}, u32[]{:S(2)}) async-start(f32[32,4,128]{2,1,0:T(4,128)} %shard_map.130), calls=%async_computation | async-start | bytes 131072 | tf_op jit(solution)/shard_map/all_to_all | solution.py:564
  10.1 0.1 stack.173.refs_0_
  10.2 1.4 %shard_map.131 = (f32[64,8]{1,0:T(8,128)S(1)}, bf16[2,32,128]{2,1,0:T(8,128)(2,1)S(1)}, f32[64,128]{1,0:T(8,128)S(1)}, f32[4,128]{1,0:T(4,128)S(1)}, f32[1,16]{1...) custom-call(s32[1]{0:T(128)} %bitcast.55.refs_0_, ...), custom_call_target="tpu_custom_call" | custom-call | flops 1048576 | bytes 1048576 | tf_op jit(solution)/shard_map/pallas_call | solution.py:500
  11.6 5.9 %all-to-all-done.refs_1_ = f32[32,4,128]{2,1,0:T(4,128)S(1)} async-done(((f32[32,4,128]{2,1,0:T(4,128)}), f32[32,4,128]{2,1,0:T(4,128)S(1)}, u32[]{:S(2)}, u32[]{:S(2)}) %all-to-all-start) | async-done | bytes 65568 | tf_op jit(solution)/shard_map/all_to_all | solution.py:564
  17.5 2.4 %shard_map.132 = (f32[9,4,128]{2,1,0:T(4,128)S(1)}, bf16[4,64,1152]{2,1,0:T(8,128)(2,1)S(1)}, bf16[64,128]{1,0:T(8,128)(2,1)S(1)}, f32[192,128]{1,0:T(8,128)S(1)}, f32[64,128]{1,0:T(8,128)S(1)}) custom-call(s32[38]{0:T(128)S(1)} %stack.173.refs_0_, f32[32,4,128]{2,1,0:T(4,128)S(1)} %all-to-all-done.refs_1_, ...), custom_call_target="tpu_custom_call" | custom-call | flops 7372800 | bytes 1048576 | tf_op jit(solution)/shard_map/pallas_call | solution.py:500
  19.9 0.9 %collective-permute-start.1 = (bf16[64,128]{1,0:T(8,128)(2,1)S(1)}, bf16[64,128]{1,0:T(8,128)(2,1)S(1)}, u32[]{:S(2)}, u32[]{:S(2)}) collective-permute-start(bf16[64,128]{1,0:T(8,128)(2,1)S(1)} %get-tuple-element.35.refs_2_.refs_7_.refs_11_), channel_id=1, source_target_pairs={{3,0},{2,1},{1,2},{0,3},{28,4},{29,5},{30,6},{31,7},{11,8},{10,9},... | collective-permute-start | bytes 49160 | tf_op jit(solution)/shard_map/ppermute | solution.py:541
  20.8 0.2 collective-permute-start
  21.0 1.2 %shard_map.133 = (bf16[64,128]{1,0:T(8,128)(2,1)S(1)}, f32[3,64,1152]{2,1,0:T(8,128)S(1)}, f32[4,64,1152]{2,1,0:T(8,128)S(1)}, f32[4,64,1152]{2,1,0:T(8,128)S(1)}, f32[4,64,1152]{2,1,0:T(8,128)S(1)}) custom-call(f32[9,4,128]{2,1,0:T(4,128)S(1)} %get-tuple-element.34.refs_0_.refs_10_, f32[64,8]{1,0:T(8,128)S(1)} %get-tuple-element.30.refs_2_.refs_1_.refs_9_.refs_10_, ...), custom_call_target="tpu_custom_call" | custom-call | flops 7372800 | bytes 1048576 | tf_op jit(solution)/shard_map/pallas_call | solution.py:500
  22.2 3.3 %collective-permute-done.1 = bf16[64,128]{1,0:T(8,128)(2,1)S(1)} collective-permute-done((bf16[64,128]{1,0:T(8,128)(2,1)S(1)}, bf16[64,128]{1,0:T(8,128)(2,1)S(1)}, u32[]{:S(2)}, u32[]{:S(2)}) %collective-permute-start.1) | collective-permute-done | bytes 16416 | tf_op jit(solution)/shard_map/ppermute | solution.py:541
  25.5 0.0 collective-permute-done
  25.5 0.7 %collective-permute-start.3 = (bf16[3,64,128]{2,1,0:T(8,128)(2,1)S(1)}, bf16[3,64,128]{2,1,0:T(8,128)(2,1)S(1)}, u32[]{:S(2)}, u32[]{:S(2)}) collective-permute-start(bf16[3,64,128]{2,1,0:T(8,128)(2,1)S(1)} %pad_maximum_fusion.refs_1_), channel_id=1, source_target_pairs={{24,0},{25,1},{26,2},{27,3},{7,4},{6,5},{5,6},{4,7},{16,8},{17,9},... | collective-permute-start | bytes 147464 | tf_op jit(solution)/shard_map/ppermute | solution.py:541
  26.2 1.5 %collective-permute-start.2 = (bf16[3,64,128]{2,1,0:T(8,128)(2,1)S(1)}, bf16[3,64,128]{2,1,0:T(8,128)(2,1)S(1)}, u32[]{:S(2)}, u32[]{:S(2)}) collective-permute-start(bf16[3,64,128]{2,1,0:T(8,128)(2,1)S(1)} %pad_maximum_fusion.refs_1_), channel_id=1, source_target_pairs={{8,0},{9,1},{10,2},{11,3},{5,4},{4,5},{7,6},{6,7},{0,8},{1,9},{2,1... | collective-permute-start | bytes 147464 | tf_op jit(solution)/shard_map/ppermute | solution.py:541
  27.7 0.0 collective-permute-start.4
  27.7 2.9 %collective-permute-done.3.refs_3_ = bf16[3,64,128]{2,1,0:T(8,128)(2,1)S(1)} collective-permute-done((bf16[3,64,128]{2,1,0:T(8,128)(2,1)S(1)}, bf16[3,64,128]{2,1,0:T(8,128)(2,1)S(1)}, u32[]{:S(2)}, u32[]{:S(2)}) %collective-permute-start.3) | collective-permute-done | bytes 49184 | tf_op jit(solution)/shard_map/ppermute | solution.py:541
  30.6 0.0 collective-permute-start.6
  30.6 0.0 collective-permute-done.2.refs_2_
  30.6 0.5 collective-permute-start.5
  31.1 0.0 collective-permute-done.4.refs_4_
  31.1 0.7 %collective-permute-done.6.refs_6_ = bf16[3,64,128]{2,1,0:T(8,128)(2,1)S(1)} collective-permute-done((bf16[3,64,128]{2,1,0:T(8,128)(2,1)S(1)}, bf16[3,64,128]{2,1,0:T(8,128)(2,1)S(1)}, u32[]{:S(2)}, u32[]{:S(2)}) %collective-permute-start.6) | collective-permute-done | bytes 49184 | tf_op jit(solution)/shard_map/ppermute | solution.py:551
  31.8 0.2 collective-permute-done.5.refs_5_
  32.0 1.4 %shard_map.134 = (bf16[64,128]{1,0:T(8,128)(2,1)S(1)}, bf16[64,128]{1,0:T(8,128)(2,1)S(1)}, f32[64,16]{1,0:T(8,128)S(1)}, f32[64,128]{1,0:T(8,128)S(1)}) custom-call(s32[38]{0:T(128)S(1)} %stack.173.refs_0_, bf16[3,64,128]{2,1,0:T(8,128)(2,1)S(1)} %pad_maximum_fusion.refs_1_, bf16[3,64,128]{2,1,0:T(8,128)(2,1)S(1)} %collective-permute-done.2.refs_2_, ...), custom_call_target="tpu_custom_call" | custom-call | flops 7372800 | bytes 1048576 | tf_op jit(solution)/shard_map/pallas_call | solution.py:500
  33.4 2.0 %collective-permute-start.8 = (bf16[64,128]{1,0:T(8,128)(2,1)S(1)}, bf16[64,128]{1,0:T(8,128)(2,1)S(1)}, u32[]{:S(2)}, u32[]{:S(2)}) collective-permute-start(bf16[64,128]{1,0:T(8,128)(2,1)S(1)} %get-tuple-element.43.refs_7_), channel_id=1, source_target_pairs={{3,0},{2,1},{1,2},{0,3},{28,4},{29,5},{30,6},{31,7},{11,8},{10,9},... | collective-permute-start | bytes 49160 | tf_op jit(solution)/shard_map/ppermute | solution.py:541
  35.4 0.0 collective-permute-start.7
  35.4 1.6 %shard_map.135 = (bf16[64,128]{1,0:T(8,128)(2,1)S(1)}, f32[64,1152]{1,0:T(8,128)S(1)}, f32[1,64]{1,0:T(1,128)}, bf16[64,128]{1,0:T(8,128)(2,1)}) custom-call(s32[38]{0:T(128)S(1)} %stack.173.refs_0_, bf16[3,64,128]{2,1,0:T(8,128)(2,1)S(1)} %pad_maximum_fusion.refs_1_, bf16[3,64,128]{2,1,0:T(8,128)(2,1)S(1)} %collective-permute-done.2.refs_2_, ...), custom_call_target="tpu_custom_call" | custom-call | flops 7372800 | bytes 1048576 | tf_op jit(solution)/shard_map/pallas_call | solution.py:500
  37.0 2.0 %collective-permute-done.8 = bf16[64,128]{1,0:T(8,128)(2,1)S(1)} collective-permute-done((bf16[64,128]{1,0:T(8,128)(2,1)S(1)}, bf16[64,128]{1,0:T(8,128)(2,1)S(1)}, u32[]{:S(2)}, u32[]{:S(2)}) %collective-permute-start.8) | collective-permute-done | bytes 16416 | tf_op jit(solution)/shard_map/ppermute | solution.py:541
  38.9 0.2 collective-permute-done.7
  39.2 1.9 %collective-permute-start.10 = (bf16[3,64,128]{2,1,0:T(8,128)(2,1)S(1)}, bf16[3,64,128]{2,1,0:T(8,128)(2,1)S(1)}, u32[]{:S(2)}, u32[]{:S(2)}) collective-permute-start(bf16[3,64,128]{2,1,0:T(8,128)(2,1)S(1)} %pad_maximum_fusion.1.refs_1_), channel_id=1, source_target_pairs={{24,0},{25,1},{26,2},{27,3},{7,4},{6,5},{5,6},{4,7},{16,8},{17,9},... | collective-permute-start | bytes 147464 | tf_op jit(solution)/shard_map/ppermute | solution.py:541
  41.1 0.7 %collective-permute-start.9 = (bf16[3,64,128]{2,1,0:T(8,128)(2,1)S(1)}, bf16[3,64,128]{2,1,0:T(8,128)(2,1)S(1)}, u32[]{:S(2)}, u32[]{:S(2)}) collective-permute-start(bf16[3,64,128]{2,1,0:T(8,128)(2,1)S(1)} %pad_maximum_fusion.1.refs_1_), channel_id=1, source_target_pairs={{8,0},{9,1},{10,2},{11,3},{5,4},{4,5},{7,6},{6,7},{0,8},{1,9},{2,1... | collective-permute-start | bytes 147464 | tf_op jit(solution)/shard_map/ppermute | solution.py:541
  41.8 0.0 collective-permute-start.11
  41.8 2.5 %collective-permute-done.10.refs_3_ = bf16[3,64,128]{2,1,0:T(8,128)(2,1)S(1)} collective-permute-done((bf16[3,64,128]{2,1,0:T(8,128)(2,1)S(1)}, bf16[3,64,128]{2,1,0:T(8,128)(2,1)S(1)}, u32[]{:S(2)}, u32[]{:S(2)}) %collective-permute-start.10) | collective-permute-done | bytes 49184 | tf_op jit(solution)/shard_map/ppermute | solution.py:541
  44.2 0.0 collective-permute-start.13
  44.2 1.0 %collective-permute-done.9.refs_2_ = bf16[3,64,128]{2,1,0:T(8,128)(2,1)S(1)} collective-permute-done((bf16[3,64,128]{2,1,0:T(8,128)(2,1)S(1)}, bf16[3,64,128]{2,1,0:T(8,128)(2,1)S(1)}, u32[]{:S(2)}, u32[]{:S(2)}) %collective-permute-start.9) | collective-permute-done | bytes 49184 | tf_op jit(solution)/shard_map/ppermute | solution.py:541
  45.2 0.0 collective-permute-start.12
  45.2 0.0 collective-permute-done.11.refs_4_
  45.2 0.3 collective-permute-done.13.refs_6_
  45.5 1.0 %collective-permute-done.12.refs_5_ = bf16[3,64,128]{2,1,0:T(8,128)(2,1)S(1)} collective-permute-done((bf16[3,64,128]{2,1,0:T(8,128)(2,1)S(1)}, bf16[3,64,128]{2,1,0:T(8,128)(2,1)S(1)}, u32[]{:S(2)}, u32[]{:S(2)}) %collective-permute-start.12) | collective-permute-done | bytes 49184 | tf_op jit(solution)/shard_map/ppermute | solution.py:551
  46.4 2.6 %shard_map.136 = f32[32,4,128]{2,1,0:T(4,128)S(1)} custom-call(s32[38]{0:T(128)S(1)} %stack.173.refs_0_, bf16[3,64,128]{2,1,0:T(8,128)(2,1)S(1)} %pad_maximum_fusion.1.refs_1_, bf16[3,64,128]{2,1,0:T(8,128)(2,1)S(1)} %collective-permute-done.9.refs_2_, bf16[3,64,128]{2,1,0:T(8,128)(2,1)S(1)} %collective-permute-done.10.refs_3_, ...), custom_call_target="tpu_custom_call" | custom-call | flops 7372800 | bytes 1048576 | tf_op jit(solution)/shard_map/pallas_call | solution.py:500
  49.0 10.1 %all_to_all.10.refs_0_ = f32[32,4,128]{2,1,0:T(4,128)S(1)} all-to-all(f32[32,4,128]{2,1,0:T(4,128)S(1)} %shard_map.136), channel_id=1, replica_groups=mesh['gx'=4,'gy'=2,'gz'=4] {'gx','gy','gz'}, dimensions={0} | all-to-all | bytes 131072 | tf_op jit(solution)/shard_map/all_to_all | solution.py:564
  59.2 0.7 %shard_map.137 = f32[3,1,64]{2,1,0:T(1,128)} custom-call(f32[32,4,128]{2,1,0:T(4,128)S(1)} %all_to_all.10.refs_0_), custom_call_target="tpu_custom_call" | custom-call | flops 1048576 | bytes 1048576 | tf_op jit(solution)/shard_map/pallas_call | solution.py:500
  (2 shorter events, 0.0 us)
Async XLA Ops:
  2.7 14.8 %all-to-all-start = ((f32[32,4,128]{2,1,0:T(4,128)}), f32[32,4,128]{2,1,0:T(4,128)S(1)}, u32[]{:S(2)}, u32[]{:S(2)}) async-start(f32[32,4,128]{2,1,0:T(4,128)} %shard_map.130), calls=%async_computation | async-start | bytes 131072 | tf_op jit(solution)/shard_map/all_to_all | solution.py:564
  19.9 5.6 %collective-permute-start.1 = (bf16[64,128]{1,0:T(8,128)(2,1)S(1)}, bf16[64,128]{1,0:T(8,128)(2,1)S(1)}, u32[]{:S(2)}, u32[]{:S(2)}) collective-permute-start(bf16[64,128]{1,0:T(8,128)(2,1)S(1)} %get-tuple-element.35.refs_2_.refs_7_.refs_11_), channel_id=1, source_target_pairs={{3,0},{2,1},{1,2},{0,3},{28,4},{29,5},{30,6},{31,7},{11,8},{10,9},... | collective-permute-start | bytes 49160 | tf_op jit(solution)/shard_map/ppermute | solution.py:541
  20.8 4.7 %collective-permute-start = (bf16[64,128]{1,0:T(8,128)(2,1)S(1)}, bf16[64,128]{1,0:T(8,128)(2,1)S(1)}, u32[]{:S(2)}, u32[]{:S(2)}) collective-permute-start(bf16[64,128]{1,0:T(8,128)(2,1)S(1)} %get-tuple-element.35.refs_2_.refs_7_.refs_11_), channel_id=1, source_target_pairs={{1,0},{0,1},{3,2},{2,3},{12,4},{13,5},{14,6},{15,7},{9,8},{8,9},{1... | collective-permute-start | bytes 49160 | tf_op jit(solution)/shard_map/ppermute | solution.py:541
  25.5 5.1 %collective-permute-start.3 = (bf16[3,64,128]{2,1,0:T(8,128)(2,1)S(1)}, bf16[3,64,128]{2,1,0:T(8,128)(2,1)S(1)}, u32[]{:S(2)}, u32[]{:S(2)}) collective-permute-start(bf16[3,64,128]{2,1,0:T(8,128)(2,1)S(1)} %pad_maximum_fusion.refs_1_), channel_id=1, source_target_pairs={{24,0},{25,1},{26,2},{27,3},{7,4},{6,5},{5,6},{4,7},{16,8},{17,9},... | collective-permute-start | bytes 147464 | tf_op jit(solution)/shard_map/ppermute | solution.py:541
  26.2 4.4 %collective-permute-start.2 = (bf16[3,64,128]{2,1,0:T(8,128)(2,1)S(1)}, bf16[3,64,128]{2,1,0:T(8,128)(2,1)S(1)}, u32[]{:S(2)}, u32[]{:S(2)}) collective-permute-start(bf16[3,64,128]{2,1,0:T(8,128)(2,1)S(1)} %pad_maximum_fusion.refs_1_), channel_id=1, source_target_pairs={{8,0},{9,1},{10,2},{11,3},{5,4},{4,5},{7,6},{6,7},{0,8},{1,9},{2,1... | collective-permute-start | bytes 147464 | tf_op jit(solution)/shard_map/ppermute | solution.py:541
  27.7 3.4 %collective-permute-start.4 = (bf16[3,64,128]{2,1,0:T(8,128)(2,1)S(1)}, bf16[3,64,128]{2,1,0:T(8,128)(2,1)S(1)}, u32[]{:S(2)}, u32[]{:S(2)}) collective-permute-start(bf16[3,64,128]{2,1,0:T(8,128)(2,1)S(1)} %pad_maximum_fusion.refs_1_), channel_id=1, source_target_pairs={{4,0},{0,4},{5,1},{1,5},{6,2},{2,6},{7,3},{3,7},{12,8},{8,12},{13,... | collective-permute-start | bytes 147464 | tf_op jit(solution)/shard_map/ppermute | solution.py:551
  30.6 1.2 %collective-permute-start.6 = (bf16[3,64,128]{2,1,0:T(8,128)(2,1)S(1)}, bf16[3,64,128]{2,1,0:T(8,128)(2,1)S(1)}, u32[]{:S(2)}, u32[]{:S(2)}) collective-permute-start(bf16[3,64,128]{2,1,0:T(8,128)(2,1)S(1)} %collective-permute-done.3.refs_3_), channel_id=1, source_target_pairs={{4,0},{0,4},{5,1},{1,5},{6,2},{2,6},{7,3},{3,7},{12,8},{8,12},{13,... | collective-permute-start | bytes 147464 | tf_op jit(solution)/shard_map/ppermute | solution.py:551
  30.6 1.4 %collective-permute-start.5 = (bf16[3,64,128]{2,1,0:T(8,128)(2,1)S(1)}, bf16[3,64,128]{2,1,0:T(8,128)(2,1)S(1)}, u32[]{:S(2)}, u32[]{:S(2)}) collective-permute-start(bf16[3,64,128]{2,1,0:T(8,128)(2,1)S(1)} %collective-permute-done.2.refs_2_), channel_id=1, source_target_pairs={{4,0},{0,4},{5,1},{1,5},{6,2},{2,6},{7,3},{3,7},{12,8},{8,12},{13,... | collective-permute-start | bytes 147464 | tf_op jit(solution)/shard_map/ppermute | solution.py:551
  33.4 5.5 %collective-permute-start.8 = (bf16[64,128]{1,0:T(8,128)(2,1)S(1)}, bf16[64,128]{1,0:T(8,128)(2,1)S(1)}, u32[]{:S(2)}, u32[]{:S(2)}) collective-permute-start(bf16[64,128]{1,0:T(8,128)(2,1)S(1)} %get-tuple-element.43.refs_7_), channel_id=1, source_target_pairs={{3,0},{2,1},{1,2},{0,3},{28,4},{29,5},{30,6},{31,7},{11,8},{10,9},... | collective-permute-start | bytes 49160 | tf_op jit(solution)/shard_map/ppermute | solution.py:541
  35.4 3.7 %collective-permute-start.7 = (bf16[64,128]{1,0:T(8,128)(2,1)S(1)}, bf16[64,128]{1,0:T(8,128)(2,1)S(1)}, u32[]{:S(2)}, u32[]{:S(2)}) collective-permute-start(bf16[64,128]{1,0:T(8,128)(2,1)S(1)} %get-tuple-element.43.refs_7_), channel_id=1, source_target_pairs={{1,0},{0,1},{3,2},{2,3},{12,4},{13,5},{14,6},{15,7},{9,8},{8,9},{1... | collective-permute-start | bytes 49160 | tf_op jit(solution)/shard_map/ppermute | solution.py:541
  39.2 5.1 %collective-permute-start.10 = (bf16[3,64,128]{2,1,0:T(8,128)(2,1)S(1)}, bf16[3,64,128]{2,1,0:T(8,128)(2,1)S(1)}, u32[]{:S(2)}, u32[]{:S(2)}) collective-permute-start(bf16[3,64,128]{2,1,0:T(8,128)(2,1)S(1)} %pad_maximum_fusion.1.refs_1_), channel_id=1, source_target_pairs={{24,0},{25,1},{26,2},{27,3},{7,4},{6,5},{5,6},{4,7},{16,8},{17,9},... | collective-permute-start | bytes 147464 | tf_op jit(solution)/shard_map/ppermute | solution.py:541
  41.1 4.1 %collective-permute-start.9 = (bf16[3,64,128]{2,1,0:T(8,128)(2,1)S(1)}, bf16[3,64,128]{2,1,0:T(8,128)(2,1)S(1)}, u32[]{:S(2)}, u32[]{:S(2)}) collective-permute-start(bf16[3,64,128]{2,1,0:T(8,128)(2,1)S(1)} %pad_maximum_fusion.1.refs_1_), channel_id=1, source_target_pairs={{8,0},{9,1},{10,2},{11,3},{5,4},{4,5},{7,6},{6,7},{0,8},{1,9},{2,1... | collective-permute-start | bytes 147464 | tf_op jit(solution)/shard_map/ppermute | solution.py:541
  41.8 3.4 %collective-permute-start.11 = (bf16[3,64,128]{2,1,0:T(8,128)(2,1)S(1)}, bf16[3,64,128]{2,1,0:T(8,128)(2,1)S(1)}, u32[]{:S(2)}, u32[]{:S(2)}) collective-permute-start(bf16[3,64,128]{2,1,0:T(8,128)(2,1)S(1)} %pad_maximum_fusion.1.refs_1_), channel_id=1, source_target_pairs={{4,0},{0,4},{5,1},{1,5},{6,2},{2,6},{7,3},{3,7},{12,8},{8,12},{13,... | collective-permute-start | bytes 147464 | tf_op jit(solution)/shard_map/ppermute | solution.py:551
  44.2 1.2 %collective-permute-start.13 = (bf16[3,64,128]{2,1,0:T(8,128)(2,1)S(1)}, bf16[3,64,128]{2,1,0:T(8,128)(2,1)S(1)}, u32[]{:S(2)}, u32[]{:S(2)}) collective-permute-start(bf16[3,64,128]{2,1,0:T(8,128)(2,1)S(1)} %collective-permute-done.10.refs_3_), channel_id=1, source_target_pairs={{4,0},{0,4},{5,1},{1,5},{6,2},{2,6},{7,3},{3,7},{12,8},{8,12},{13,... | collective-permute-start | bytes 147464 | tf_op jit(solution)/shard_map/ppermute | solution.py:551
  45.2 1.2 %collective-permute-start.12 = (bf16[3,64,128]{2,1,0:T(8,128)(2,1)S(1)}, bf16[3,64,128]{2,1,0:T(8,128)(2,1)S(1)}, u32[]{:S(2)}, u32[]{:S(2)}) collective-permute-start(bf16[3,64,128]{2,1,0:T(8,128)(2,1)S(1)} %collective-permute-done.9.refs_2_), channel_id=1, source_target_pairs={{4,0},{0,4},{5,1},{1,5},{6,2},{2,6},{7,3},{3,7},{12,8},{8,12},{13,... | collective-permute-start | bytes 147464 | tf_op jit(solution)/shard_map/ppermute | solution.py:551

commit v5 on v4

--- a/solution.py
+++ b/solution.py
@@ -34,6 +34,7 @@
     -0.007028386239784362,
 )
 VMEM_LIMIT = 24 * 1024 * 1024
+GROUP = 4
 FETCH_LIMIT = 60 * 1024 * 1024
 NT = (((1,), (1,)), ((), ()))
 NN = (((1,), (0,)), ((), ()))
@@ -118,19 +119,19 @@
             for oy in self.sides:
                 place = (moved("gx", ox) * self.sizes["gy"] + moved("gy", oy)) * self.sizes["gz"]
                 found.append(place + moved("gz", oz))
-        return jnp.stack(found).astype(jnp.int32)
-
-    def brought_place(self, places_ref, side, pair):
-        return places_ref[side * len(self.brought) + pair]
-
-    def global_place(self, places_ref, tile, side):
+        return [jnp.asarray(place, jnp.int32) for place in found]
+
+    def brought_place(self, places, side, pair):
+        return places[side * len(self.brought) + pair]
+
+    def global_place(self, places, tile, side):
         start = len(self.sides) * len(self.brought) + 2
-        return places_ref[start + tile * len(self.sides) + side]
-
-    def staged_place(self, places_ref, tile):
+        return places[start + tile * len(self.sides) + side]
+
+    def staged_place(self, places, tile):
         start = len(self.sides) * len(self.brought)
         x, z = divmod(tile, self.depth)
-        return matched(x, places_ref[start]) * self.depth + matched(z, places_ref[start + 1])
+        return matched(x, places[start]) * self.depth + matched(z, places[start + 1])
 
     def offset(self, tile, side):
         ox, oz = self.tiles[tile]
@@ -162,25 +163,38 @@
     return poly(COS_TERMS, square), -(arg * poly(SIN_TERMS, square))
 
 
-def first_kernel(plan, nrefs, places_ref, *refs):
-    far_refs, refs = refs[:nrefs], refs[nrefs:]
-    (cols_ref, table_ref, embed_ref, mix_ref), refs = refs[:4], refs[4:]
-    rows_ref, basis_ref, layer_ref, vector_ref, mixing_ref, pair_ref, block_ref = refs
+def first_kernel(plan, nrefs, places, *refs):
+    far_refs, fetched, refs = refs[:nrefs], refs[nrefs : nrefs + 8], refs[nrefs + 8 :]
+    rows_ref, basis_ref, layer_ref, vector_ref, mixing_ref, cols_ref, table_ref, *refs = refs
+    kept, (pair_ref, block_ref, embed_ref, radial_ref, sems) = refs[:6], refs[6:]
+    mix_ref = kept[0]
     slots, nbasis, nspec = plan.slots, plan.nbasis, plan.nspec
-    cols = [cols_ref[:, axis : axis + 1] for axis in range(3)]
-    species = lax.broadcasted_iota(jnp.int32, (nbasis * nspec, plan.width), 0) % nspec
-    hot = []
+    copies = begin(zip(fetched, (embed_ref, radial_ref, *kept)), sems)
 
     def put(place, block):
         block_ref[place] = block
 
     if not plan.small:
-        scatter(plan, places_ref, far_refs, put)
+        scatter(plan, places, far_refs, put)
+
+    def block_of(tile, side):
+        if plan.small:
+            return far_refs[0][plan.global_place(places, tile, side)]
+        return block_ref[tile * len(plan.sides) + side]
+
+    rows = block_of(0, 0)
+    held = jnp.concatenate([rows, rows], axis=0).T[:slots]
+    kind = held[:, 3:4]
+    lane = lax.broadcasted_iota(jnp.int32, held.shape, 1)
+    live = kind >= 0.0
+    held = jnp.where((lane == 0) & ~live, -FAR, held)
+    held = jnp.where(lane == 3, live.astype(F32), held)
+    cols_ref[...] = held
+    cols = [held[:, axis : axis + 1] for axis in range(3)]
+    species = lax.broadcasted_iota(jnp.int32, (nbasis * nspec, plan.width), 0) % nspec
+    hot, gathered = [], None
     for tile in range(len(plan.tiles)):
-        if plan.small:
-            blocks = [far_refs[0][plan.global_place(places_ref, tile, s)] for s in range(len(plan.sides))]
-        else:
-            blocks = [block_ref[tile * len(plan.sides) + s] for s in range(len(plan.sides))]
+        blocks = [block_of(tile, side) for side in range(len(plan.sides))]
         placed = side_by_side(plan, blocks) + tile_shift(plan, tile)
         rows_ref[tile] = placed
         rows = [placed[k : k + 1] for k in range(4)]
@@ -203,8 +217,22 @@
             pair_ref[n, :slots, lanes] = packed
             for k in range(3):
                 pair_ref[n, (k + 1) * slots : (k + 2) * slots, lanes] = units[k] * packed
-    hot = jnp.concatenate(hot, axis=1)
-    gathered = dot(pair_ref[...].reshape(nbasis * 4 * slots, plan.far), hot, NT)
+        if tile % GROUP == GROUP - 1 or tile == len(plan.tiles) - 1:
+            lanes = slice((tile // GROUP) * GROUP * plan.width, (tile + 1) * plan.width)
+            taken = pair_ref[:, :, lanes].reshape(nbasis * 4 * slots, -1)
+            part = dot(taken, jnp.concatenate(hot, axis=1), NT)
+            gathered = part if gathered is None else gathered + part
+            hot = []
+    for copy in copies:
+        copy.wait()
+    embed = embed_ref[...]
+    for g in range(2):
+        for n in range(nbasis):
+            row = radial_ref[g, n : n + 1]
+            weighted = row * embed.astype(F32)
+            table_ref[g, n * nspec : (n + 1) * nspec] = weighted.astype(BF16)
+    own_species = lax.broadcasted_iota(jnp.int32, (slots, nspec), 1)
+    own_hot = (kind.astype(jnp.int32) == own_species).astype(F32).astype(BF16)
     gathered = gathered.reshape(nbasis, 4 * slots, nbasis * nspec)
     group = lax.broadcasted_iota(jnp.int32, gathered.shape[1:], 1) // nspec
     counted = jnp.zeros(gathered.shape[1:], F32)
@@ -218,7 +246,7 @@
     invariants = jnp.concatenate([scalar.astype(BF16), norm.astype(BF16)], axis=1)
     mixing = dot(invariants, mix_ref[...], NT)
     mixing_ref[...] = mixing
-    layer = (embed_ref[...] + mixing * sigmoid(mixing)).astype(BF16)
+    layer = (dot(own_hot, embed) + mixing * sigmoid(mixing)).astype(BF16)
     layer_ref[...] = layer
 
 
@@ -226,11 +254,11 @@
     return 1.0 / (1.0 + jnp.exp(-value))
 
 
-def scatter(plan, places_ref, far_refs, put):
+def scatter(plan, places, far_refs, put):
     for side in range(len(plan.sides)):
         for pair, (second, first) in enumerate(plan.brought):
             block = far_refs[side * plan.wide + second][first]
-            put(plan.brought_place(places_ref, side, pair), block)
+            put(plan.brought_place(places, side, pair), block)
 
 
 def side_by_side(plan, blocks):
@@ -251,21 +279,21 @@
     return shift
 
 
-def gather_far(plan, places_ref, far_refs, all_ref):
+def gather_far(plan, places, far_refs, all_ref):
     def put(place, block):
         start = pl.multiple_of(place * plan.slots, plan.slots)
         all_ref[pl.ds(start, plan.slots)] = block
 
-    scatter(plan, places_ref, far_refs, put)
-
-
-def second_kernel(plan, nrefs, places_ref, *refs):
+    scatter(plan, places, far_refs, put)
+
+
+def second_kernel(plan, nrefs, places, *refs):
     far_refs, refs = refs[:nrefs], refs[nrefs:]
     (layer_ref, basis_ref, cols_ref, radial_ref, mix_ref), refs = refs[:5], refs[5:]
     (hidden_ref, out_ref, one_ref), refs = refs[:3], refs[3:]
     adjoint_ref, features_ref, before_ref, own_ref, all_ref = refs
     slots, nbasis = plan.slots, plan.nbasis
-    gather_far(plan, places_ref, far_refs, all_ref)
+    gather_far(plan, places, far_refs, all_ref)
     summed = dot(basis_ref[...].reshape(nbasis * slots, plan.far), all_ref[...])
     message = jnp.zeros((slots, summed.shape[1]), F32)
     for n in range(nbasis):
@@ -287,7 +315,8 @@
     adjoint_ref[...] = dot(back.astype(BF16), mix_ref[...]).astype(BF16)
 
 
-def slope_kernel(plan, rows_ref, cols_ref, layer_ref, again_ref, apart_ref, slope_ref, radial_ref, turned_ref):
+def slope_kernel(plan, rows_ref, cols_ref, layer_ref, *refs):
+    again_ref, apart_ref, slope_ref, radial_ref, turned_ref = refs
     again_ref[...] = layer_ref[...]
     cols = [cols_ref[:, axis : axis + 1] for axis in range(3)]
     for tile in range(len(plan.tiles)):
@@ -320,7 +349,7 @@
             turned_ref[n, :, lanes] = scale * slope - square * factor
 
 
-def energy_kernel(plan, nrefs, places_ref, *refs):
+def energy_kernel(plan, nrefs, places, *refs):
     far_refs, refs = refs[:nrefs], refs[nrefs:]
     (adjoint_ref, slope_ref, radial_ref, cols_ref, layer_ref), refs = refs[:5], refs[5:]
     (before_ref, out_ref, one_ref, kept_ref), refs = refs[:4], refs[4:]
@@ -334,7 +363,7 @@
     energy = dot_exact(one_ref[...], layer_ref[...].astype(F32), NT)
     energy = energy + dot_exact(out_ref[...], before * sigmoid(before), NT)
     energy_ref[...] = energy * live_row
-    gather_far(plan, places_ref, far_refs, all_ref)
+    gather_far(plan, places, far_refs, all_ref)
     adjoint = adjoint_ref[...].astype(F32) * MSG_SCALE
     weighted = jnp.concatenate(
         [(adjoint * radial_ref[n : n + 1]).astype(BF16) for n in range(nbasis)], axis=0
@@ -348,14 +377,14 @@
         pair_ref[:, lanes] = total
 
 
-def force_kernel(plan, nrefs, places_ref, *refs):
+def force_kernel(plan, nrefs, places, *refs):
     far_refs, refs = refs[:nrefs], refs[nrefs:]
     (own_ref, basis_ref, pair_ref, rows_ref), refs = refs[:4], refs[4:]
     (apart_ref, slope_ref, factor_ref, turned_ref), refs = refs[:4], refs[4:]
     (radial_ref, mixing_ref, mix_ref, vector_ref, table_ref), refs = refs[:5], refs[5:]
     out_ref, all_ref = refs
     slots, nbasis, nspec, width = plan.slots, plan.nbasis, plan.nspec, plan.width
-    gather_far(plan, places_ref, far_refs, all_ref)
+    gather_far(plan, places, far_refs, all_ref)
     summed = dot(basis_ref[...].reshape(nbasis * slots, plan.far), all_ref[...])
     adjoint = jnp.zeros((slots, summed.shape[1]), F32)
     for n in range(nbasis):
@@ -417,22 +446,23 @@
             others = [jnp.zeros_like(mine)] * (len(plan.sides) - 1)
             pulled = pulled - jnp.concatenate([mine] + others, axis=1)
         if not plan.small:
-            out_ref[plan.staged_place(places_ref, tile)] = pulled
+            out_ref[plan.staged_place(places, tile)] = pulled
             continue
         for side in range(len(plan.sides)):
-            place = plan.global_place(places_ref, tile, side)
+            place = plan.global_place(places, tile, side)
             out_ref[place, :3] = jnp.where(side_of == side, pulled, 0.0)
 
 
-def brought_in(pairs, sems):
+def begin(pairs, sems):
     copies = [pltpu.make_async_copy(*pair, sems.at[m]) for m, pair in enumerate(pairs)]
     for copy in copies:
         copy.start()
-    for copy in copies:
+    return copies
+
+
+def prepare_kernel(plan, counts_ref, place_hbm, kind_hbm, sent_ref, place_ref, kind_ref, sems):
+    for copy in begin([(place_hbm, place_ref), (kind_hbm, kind_ref)], sems):
         copy.wait()
-
-
-def live_rows(plan, counts_ref, place_ref, kind_ref):
     live = lax.broadcasted_iota(jnp.int32, (1, plan.slots), 1) < counts_ref[0]
     rows = [
         jnp.where(live, place_ref[0], FAR),
@@ -441,12 +471,7 @@
         jnp.where(live, kind_ref[...], -1).astype(F32),
     ]
     rows = jnp.concatenate(rows, axis=0)
-    return jnp.concatenate([rows, rows], axis=1)
-
-
-def prepare_kernel(plan, counts_ref, place_hbm, kind_hbm, sent_ref, place_ref, kind_ref, sems):
-    brought_in([(place_hbm, place_ref), (kind_hbm, kind_ref)], sems)
-    rows = live_rows(plan, counts_ref, place_ref, kind_ref)
+    rows = jnp.concatenate([rows, rows], axis=1)
     for copy in range(sent_ref.shape[0]):
         sent_ref[copy] = rows
 
@@ -458,30 +483,6 @@
     total = total[:, : plan.slots] + total[:, plan.slots :]
     for k in range(3):
         force_ref[k] = -total[k : k + 1]
-
-
-def own_kernel(plan, counts_ref, *refs):
-    fetched, weights, (cols_ref, table_ref, own_ref) = refs[:4], refs[4:10], refs[10:13]
-    kept, local_refs, sems = refs[13:19], refs[19:-1], refs[-1]
-    slots, nspec = plan.slots, plan.nspec
-    brought_in([*zip(fetched, local_refs), *zip(weights, kept)], sems)
-    place_ref, kind_ref, embed_ref, radial_ref = local_refs
-    rows = live_rows(plan, counts_ref, place_ref, kind_ref)
-    cols = jnp.concatenate([rows, rows], axis=0).T[:slots]
-    kind = cols[:, 3:4]
-    lane = lax.broadcasted_iota(jnp.int32, cols.shape, 1)
-    live = kind >= 0.0
-    cols = jnp.where((lane == 0) & ~live, -FAR, cols)
-    cols_ref[...] = jnp.where(lane == 3, live.astype(F32), cols)
-    species = lax.broadcasted_iota(jnp.int32, (slots, nspec), 1)
-    hot = (kind.astype(jnp.int32) == species).astype(F32).astype(BF16)
-    embed = embed_ref[...]
-    own_ref[...] = dot(hot, embed)
-    embed = embed.astype(F32)
-    for g in range(2):
-        for n in range(plan.nbasis):
-            row = radial_ref[g, n : n + 1]
-            table_ref[g, n * nspec : (n + 1) * nspec] = (row * embed).astype(BF16)
 
 
 VMEM_SPEC = pl.BlockSpec(memory_space=pltpu.VMEM)
@@ -512,11 +513,11 @@
     return got[0] if single else got
 
 
-def call(kernel, plan, far, places, operands, outs, scratch, flops):
+def call(kernel, plan, far, operands, outs, scratch, flops, **options):
     def body(plan, *refs):
-        kernel(plan, len(far), *refs)
-
-    return simple_call(body, plan, [places, *far, *operands], outs, 1, scratch, flops)
+        kernel(plan, len(far), plan.places(), *refs)
+
+    return simple_call(body, plan, [*far, *operands], outs, 0, scratch, flops, **options)
 
 
 def swaps(count):
@@ -610,45 +611,35 @@
             near=True,
             fetched=len(given),
         )
-        places = plan.places()
         far_sent = [everywhere(sent)] if plan.small else neighbours(plan, sent[0])
-        weights = [radial_two, read_out[None], read_one[None], mix_one, mix_two, read_hidden]
-        given = given + [embed, radial_one]
-        cols, table, own_embed, radial_two, out_row, one_row, mix_one, mix_two, read_hidden = simple_call(
-            own_kernel,
-            plan,
-            [count, *given, *weights],
-            [
-                ((slots, 8), F32),
-                ((2, nbasis * nspec, channels), BF16),
-                ((slots, channels), F32),
-            ]
-            + [(weight.shape, weight.dtype) for weight in weights],
-            1,
-            [(array.shape, array.dtype) for array in given],
-            near=True,
-            fetched=len(given) + len(weights),
-        )
         pair_flops = 100 * slots * plan.far
-        rows, basis, layer, vector, mixing = call(
+        weights = [mix_one, radial_two, read_out[None], read_one[None], mix_two, read_hidden]
+        rows, basis, layer, vector, mixing, cols, table, *weights = call(
             first_kernel,
             plan,
             far_sent,
-            places,
-            [cols, table, own_embed, mix_one],
+            [embed, radial_one, *weights],
             [
                 ((len(plan.tiles), 4, plan.width), F32),
                 ((nbasis, slots, plan.far), BF16),
                 ((slots, channels), BF16),
                 ((3 * slots, channels), F32),
                 ((slots, channels), F32),
-            ],
+                ((slots, 8), F32),
+                ((2, nbasis * nspec, channels), BF16),
+            ]
+            + [(weight.shape, weight.dtype) for weight in weights],
             [
                 ((nbasis, 4 * slots, plan.far), BF16),
                 ((len(plan.tiles) * len(plan.sides), 4, 2 * slots), F32),
+                (embed.shape, BF16),
+                (radial_one.shape, F32),
             ],
             pair_flops,
+            near=True,
+            fetched=2 + len(weights),
         )
+        mix_one, radial_two, out_row, one_row, mix_two, read_hidden = weights
         again, apart, slope, factor, turned = simple_call(
             slope_kernel,
             plan,
@@ -663,7 +654,6 @@
             second_kernel,
             plan,
             far_layer,
-            places,
             [layer, basis, cols, radial_two, mix_two, read_hidden, out_row, one_row],
             [
                 ((slots, channels), BF16),
@@ -678,7 +668,6 @@
             energy_kernel,
             plan,
             far_layer,
-            places,
             [adjoint, slope, radial_two, cols, layer, before, out_row, one_row, kept],
             [
                 ((slots, channels), BF16),
@@ -694,7 +683,6 @@
             force_kernel,
             plan,
             far_adjoint,
-            places,
             [own_adjoint, basis, pair, rows, apart, slope, factor, turned]
             + [radial_two, mixing, mix_one, vector, table],
             [((plan.ndev, 4, plan.width) if plan.small else (len(plan.tiles), 3, plan.width), F32)],

time: 60.1 us -> 59.4 us (0.988)
  blocking collectives: 10.1 us -> 24.8 us
  starting transfers between devices: 15.7 us -> 8.42 us
  waiting for transfers between devices: 19.8 us -> 14.4 us
  Pallas kernels: 12.7 us -> 10.1 us
    all_to_all x1 -> x2, blocking collectives: 10.1 us -> 24.8 us  [everywhere(): return lax.all_to_all(copies, AXES, 0, 0, tiled=True)]
    all_to_all x1 -> x0, starting transfers between devices: 7.3 us -> none  [everywhere(): return lax.all_to_all(copies, AXES, 0, 0, tiled=True)]
    all_to_all x1 -> x0, waiting for transfers between devices: 5.91 us -> none  [everywhere(): return lax.all_to_all(copies, AXES, 0, 0, tiled=True)]
    pallas_call x8 -> x7, Pallas kernels: 12.7 us -> 10.1 us  [simple_call(): pl.pallas_call(body, out_shape=shapes, in_specs=[SMEM_SPEC] * scalars + [...]
  transfers between devices with their start and end apart: 15 -> 14, of which waited for: 11 -> 10; matrix products, arithmetic and copies ran while one was open for 0% -> 0% of each run, Pallas kernels for 7% -> 4%
where the time goes in v5:
time: 59.4 us; the launch traced here: 59.1 us
  blocking collectives  24.8 us (42%)
  waiting for transfers between devices  14.4 us (24%)
  Pallas kernels  10.1 us (17%)
  starting transfers between devices  8.42 us (14%)
  between operations  1.33 us (2%)
    all_to_all x2, blocking collectives, everywhere(): return lax.all_to_all(copies, AXES, 0, 0, tiled=True)  24.8 us
    ppermute x8, waiting for transfers between devices, brought(): got.append(lax.ppermute(block, AXES, pairs))  12.3 us
    pallas_call x7, Pallas kernels, simple_call(): pl.pallas_call(body, out_shape=shapes, in_specs=[SMEM_SPEC] * scalars + [...  10.1 us
    ppermute x8, starting transfers between devices, brought(): got.append(lax.ppermute(block, AXES, pairs))  7.9 us
    ppermute x6, waiting for transfers between devices, along(): lax.ppermute(block, axis, [(source, i) for i, source in enumerate(sources)])  2.11 us
  transfers between devices with their start and end apart: 14, of which 10 were waited for; matrix products, arithmetic and copies ran while one was open for 0% of the time, Pallas kernels for 4%

profile of v5, /device:TPU:0, one launch (start us, length us, event | category | flops | bytes accessed | tf_op | source)
XLA Modules:
  0.0 59.1 jit_solution(9838139129838326783)
XLA Ops:
  1.3 0.8 %shard_map.130 = f32[32,4,128]{2,1,0:T(4,128)S(1)} custom-call(s32[1]{0:T(128)} %bitcast.18.refs_0_, f32[3,1,64]{2,1,0:T(1,128)} %bitcast.25, s32[1,64]{1,0:T(1,128)} %bitcast.27), custom_call_target="tpu_custom_call" | custom-call | flops 1048576 | bytes 1048576 | tf_op jit(solution)/shard_map/pallas_call | solution.py:501
  2.1 14.7 %all_to_all.10.refs_0_ = f32[32,4,128]{2,1,0:T(4,128)} all-to-all(f32[32,4,128]{2,1,0:T(4,128)S(1)} %shard_map.130), channel_id=1, replica_groups=mesh['gx'=4,'gy'=2,'gz'=4] {'gx','gy','gz'}, dimensions={0} | all-to-all | bytes 131072 | tf_op jit(solution)/shard_map/all_to_all | solution.py:565
  16.8 3.4 %shard_map.131 = (f32[9,4,128]{2,1,0:T(4,128)S(1)}, bf16[4,64,1152]{2,1,0:T(8,128)(2,1)S(1)}, bf16[64,128]{1,0:T(8,128)(2,1)S(1)}, f32[192,128]{1,0:T(8,128)S(1)...) custom-call(f32[32,4,128]{2,1,0:T(4,128)} %all_to_all.10.refs_0_, ...), custom_call_target="tpu_custom_call" | custom-call | flops 7372800 | bytes 1048576 | tf_op jit(solution)/shard_map/pallas_call | solution.py:501
  20.2 0.9 %collective-permute-start.1 = (bf16[64,128]{1,0:T(8,128)(2,1)S(1)}, bf16[64,128]{1,0:T(8,128)(2,1)S(1)}, u32[]{:S(2)}, u32[]{:S(2)}) collective-permute-start(bf16[64,128]{1,0:T(8,128)(2,1)S(1)} %get-tuple-element.31.refs_2_.refs_6_.refs_10_), channel_id=1, source_target_pairs={{3,0},{2,1},{1,2},{0,3},{28,4},{29,5},{30,6},{31,7},{11,8},{10,9},... | collective-permute-start | bytes 49160 | tf_op jit(solution)/shard_map/ppermute | solution.py:542
  21.0 0.2 collective-permute-start
  21.2 1.2 %shard_map.132 = (bf16[64,128]{1,0:T(8,128)(2,1)S(1)}, f32[3,64,1152]{2,1,0:T(8,128)S(1)}, f32[4,64,1152]{2,1,0:T(8,128)S(1)}, f32[4,64,1152]{2,1,0:T(8,128)S(1)}, f32[4,64,1152]{2,1,0:T(8,128)S(1)}) custom-call(f32[9,4,128]{2,1,0:T(4,128)S(1)} %get-tuple-element.29.refs_0_.refs_9_, f32[64,8]{1,0:T(8,128)S(1)} %get-tuple-element.30.refs_1_.refs_8_.refs_9_, ...), custom_call_target="tpu_custom_call" | custom-call | flops 7372800 | bytes 1048576 | tf_op jit(solution)/shard_map/pallas_call | solution.py:501
  22.5 3.3 %collective-permute-done.1 = bf16[64,128]{1,0:T(8,128)(2,1)S(1)} collective-permute-done((bf16[64,128]{1,0:T(8,128)(2,1)S(1)}, bf16[64,128]{1,0:T(8,128)(2,1)S(1)}, u32[]{:S(2)}, u32[]{:S(2)}) %collective-permute-start.1) | collective-permute-done | bytes 16416 | tf_op jit(solution)/shard_map/ppermute | solution.py:542
  25.8 0.0 collective-permute-done
  25.8 0.7 %collective-permute-start.3 = (bf16[3,64,128]{2,1,0:T(8,128)(2,1)S(1)}, bf16[3,64,128]{2,1,0:T(8,128)(2,1)S(1)}, u32[]{:S(2)}, u32[]{:S(2)}) collective-permute-start(bf16[3,64,128]{2,1,0:T(8,128)(2,1)S(1)} %pad_maximum_fusion.refs_0_), channel_id=1, source_target_pairs={{24,0},{25,1},{26,2},{27,3},{7,4},{6,5},{5,6},{4,7},{16,8},{17,9},... | collective-permute-start | bytes 147464 | tf_op jit(solution)/shard_map/ppermute | solution.py:542
  26.5 1.5 %collective-permute-start.2 = (bf16[3,64,128]{2,1,0:T(8,128)(2,1)S(1)}, bf16[3,64,128]{2,1,0:T(8,128)(2,1)S(1)}, u32[]{:S(2)}, u32[]{:S(2)}) collective-permute-start(bf16[3,64,128]{2,1,0:T(8,128)(2,1)S(1)} %pad_maximum_fusion.refs_0_), channel_id=1, source_target_pairs={{8,0},{9,1},{10,2},{11,3},{5,4},{4,5},{7,6},{6,7},{0,8},{1,9},{2,1... | collective-permute-start | bytes 147464 | tf_op jit(solution)/shard_map/ppermute | solution.py:542
  28.0 0.0 collective-permute-start.4
  28.0 2.9 %collective-permute-done.3.refs_2_ = bf16[3,64,128]{2,1,0:T(8,128)(2,1)S(1)} collective-permute-done((bf16[3,64,128]{2,1,0:T(8,128)(2,1)S(1)}, bf16[3,64,128]{2,1,0:T(8,128)(2,1)S(1)}, u32[]{:S(2)}, u32[]{:S(2)}) %collective-permute-start.3) | collective-permute-done | bytes 49184 | tf_op jit(solution)/shard_map/ppermute | solution.py:542
  30.8 0.0 collective-permute-start.6
  30.8 0.0 collective-permute-done.2.refs_1_
  30.8 0.5 collective-permute-start.5
  31.3 0.0 collective-permute-done.4.refs_3_
  31.3 0.7 %collective-permute-done.6.refs_5_ = bf16[3,64,128]{2,1,0:T(8,128)(2,1)S(1)} collective-permute-done((bf16[3,64,128]{2,1,0:T(8,128)(2,1)S(1)}, bf16[3,64,128]{2,1,0:T(8,128)(2,1)S(1)}, u32[]{:S(2)}, u32[]{:S(2)}) %collective-permute-start.6) | collective-permute-done | bytes 49184 | tf_op jit(solution)/shard_map/ppermute | solution.py:552
  32.1 0.2 collective-permute-done.5.refs_4_
  32.2 0.9 %shard_map.133 = (bf16[64,128]{1,0:T(8,128)(2,1)S(1)}, bf16[64,128]{1,0:T(8,128)(2,1)S(1)}, f32[64,16]{1,0:T(8,128)S(1)}, f32[64,128]{1,0:T(8,128)S(1)}) custom-call(bf16[3,64,128]{2,1,0:T(8,128)(2,1)S(1)} %pad_maximum_fusion.refs_0_, bf16[3,64,128]{2,1,0:T(8,128)(2,1)S(1)} %collective-permute-done.2.refs_1_, ...), custom_call_target="tpu_custom_call" | custom-call | flops 7372800 | bytes 1048576 | tf_op jit(solution)/shard_map/pallas_call | solution.py:501
  33.1 2.0 %collective-permute-start.8 = (bf16[64,128]{1,0:T(8,128)(2,1)S(1)}, bf16[64,128]{1,0:T(8,128)(2,1)S(1)}, u32[]{:S(2)}, u32[]{:S(2)}) collective-permute-start(bf16[64,128]{1,0:T(8,128)(2,1)S(1)} %get-tuple-element.39.refs_6_), channel_id=1, source_target_pairs={{3,0},{2,1},{1,2},{0,3},{28,4},{29,5},{30,6},{31,7},{11,8},{10,9},... | collective-permute-start | bytes 49160 | tf_op jit(solution)/shard_map/ppermute | solution.py:542
  35.1 0.0 collective-permute-start.7
  35.1 1.0 %shard_map.134 = (bf16[64,128]{1,0:T(8,128)(2,1)S(1)}, f32[64,1152]{1,0:T(8,128)S(1)}, f32[1,64]{1,0:T(1,128)}, bf16[64,128]{1,0:T(8,128)(2,1)}) custom-call(bf16[3,64,128]{2,1,0:T(8,128)(2,1)S(1)} %pad_maximum_fusion.refs_0_, bf16[3,64,128]{2,1,0:T(8,128)(2,1)S(1)} %collective-permute-done.2.refs_1_, ...), custom_call_target="tpu_custom_call" | custom-call | flops 7372800 | bytes 1048576 | tf_op jit(solution)/shard_map/pallas_call | solution.py:501
  36.1 2.5 %collective-permute-done.8 = bf16[64,128]{1,0:T(8,128)(2,1)S(1)} collective-permute-done((bf16[64,128]{1,0:T(8,128)(2,1)S(1)}, bf16[64,128]{1,0:T(8,128)(2,1)S(1)}, u32[]{:S(2)}, u32[]{:S(2)}) %collective-permute-start.8) | collective-permute-done | bytes 16416 | tf_op jit(solution)/shard_map/ppermute | solution.py:542
  38.6 0.2 collective-permute-done.7
  38.9 1.9 %collective-permute-start.10 = (bf16[3,64,128]{2,1,0:T(8,128)(2,1)S(1)}, bf16[3,64,128]{2,1,0:T(8,128)(2,1)S(1)}, u32[]{:S(2)}, u32[]{:S(2)}) collective-permute-start(bf16[3,64,128]{2,1,0:T(8,128)(2,1)S(1)} %pad_maximum_fusion.1.refs_0_), channel_id=1, source_target_pairs={{24,0},{25,1},{26,2},{27,3},{7,4},{6,5},{5,6},{4,7},{16,8},{17,9},... | collective-permute-start | bytes 147464 | tf_op jit(solution)/shard_map/ppermute | solution.py:542
  40.8 0.7 %collective-permute-start.9 = (bf16[3,64,128]{2,1,0:T(8,128)(2,1)S(1)}, bf16[3,64,128]{2,1,0:T(8,128)(2,1)S(1)}, u32[]{:S(2)}, u32[]{:S(2)}) collective-permute-start(bf16[3,64,128]{2,1,0:T(8,128)(2,1)S(1)} %pad_maximum_fusion.1.refs_0_), channel_id=1, source_target_pairs={{8,0},{9,1},{10,2},{11,3},{5,4},{4,5},{7,6},{6,7},{0,8},{1,9},{2,1... | collective-permute-start | bytes 147464 | tf_op jit(solution)/shard_map/ppermute | solution.py:542
  41.5 0.0 collective-permute-start.11
  41.5 2.5 %collective-permute-done.10.refs_2_ = bf16[3,64,128]{2,1,0:T(8,128)(2,1)S(1)} collective-permute-done((bf16[3,64,128]{2,1,0:T(8,128)(2,1)S(1)}, bf16[3,64,128]{2,1,0:T(8,128)(2,1)S(1)}, u32[]{:S(2)}, u32[]{:S(2)}) %collective-permute-start.10) | collective-permute-done | bytes 49184 | tf_op jit(solution)/shard_map/ppermute | solution.py:542
  43.9 0.0 collective-permute-start.13
  43.9 1.0 %collective-permute-done.9.refs_1_ = bf16[3,64,128]{2,1,0:T(8,128)(2,1)S(1)} collective-permute-done((bf16[3,64,128]{2,1,0:T(8,128)(2,1)S(1)}, bf16[3,64,128]{2,1,0:T(8,128)(2,1)S(1)}, u32[]{:S(2)}, u32[]{:S(2)}) %collective-permute-start.9) | collective-permute-done | bytes 49184 | tf_op jit(solution)/shard_map/ppermute | solution.py:542
  44.9 0.0 collective-permute-start.12
  44.9 0.0 collective-permute-done.11.refs_3_
  44.9 0.3 collective-permute-done.13.refs_5_
  45.2 1.0 %collective-permute-done.12.refs_4_ = bf16[3,64,128]{2,1,0:T(8,128)(2,1)S(1)} collective-permute-done((bf16[3,64,128]{2,1,0:T(8,128)(2,1)S(1)}, bf16[3,64,128]{2,1,0:T(8,128)(2,1)S(1)}, u32[]{:S(2)}, u32[]{:S(2)}) %collective-permute-start.12) | collective-permute-done | bytes 49184 | tf_op jit(solution)/shard_map/ppermute | solution.py:552
  46.1 2.1 %shard_map.135 = f32[32,4,128]{2,1,0:T(4,128)S(1)} custom-call(bf16[3,64,128]{2,1,0:T(8,128)(2,1)S(1)} %pad_maximum_fusion.1.refs_0_, bf16[3,64,128]{2,1,0:T(8,128)(2,1)S(1)} %collective-permute-done.9.refs_1_, bf16[3,64,128]{2,1,0:T(8,128)(2,1)S(1)} %collective-permute-done.10.refs_2_, bf16[3,64,128]{2,1,0:T(8,128)(2,1)S(1)} %collective-permute-done.11.refs_3_, ...), custom_call_target="tpu_custom_call" | custom-call | flops 7372800 | bytes 1048576 | tf_op jit(solution)/shard_map/pallas_call | solution.py:501
  48.3 10.1 %all_to_all.11.refs_0_ = f32[32,4,128]{2,1,0:T(4,128)S(1)} all-to-all(f32[32,4,128]{2,1,0:T(4,128)S(1)} %shard_map.135), channel_id=1, replica_groups=mesh['gx'=4,'gy'=2,'gz'=4] {'gx','gy','gz'}, dimensions={0} | all-to-all | bytes 131072 | tf_op jit(solution)/shard_map/all_to_all | solution.py:565
  58.4 0.7 %shard_map.136 = f32[3,1,64]{2,1,0:T(1,128)} custom-call(f32[32,4,128]{2,1,0:T(4,128)S(1)} %all_to_all.11.refs_0_), custom_call_target="tpu_custom_call" | custom-call | flops 1048576 | bytes 1048576 | tf_op jit(solution)/shard_map/pallas_call | solution.py:501
  (2 shorter events, 0.0 us)
Async XLA Ops:
  20.2 5.6 %collective-permute-start.1 = (bf16[64,128]{1,0:T(8,128)(2,1)S(1)}, bf16[64,128]{1,0:T(8,128)(2,1)S(1)}, u32[]{:S(2)}, u32[]{:S(2)}) collective-permute-start(bf16[64,128]{1,0:T(8,128)(2,1)S(1)} %get-tuple-element.31.refs_2_.refs_6_.refs_10_), channel_id=1, source_target_pairs={{3,0},{2,1},{1,2},{0,3},{28,4},{29,5},{30,6},{31,7},{11,8},{10,9},... | collective-permute-start | bytes 49160 | tf_op jit(solution)/shard_map/ppermute | solution.py:542
  21.0 4.7 %collective-permute-start = (bf16[64,128]{1,0:T(8,128)(2,1)S(1)}, bf16[64,128]{1,0:T(8,128)(2,1)S(1)}, u32[]{:S(2)}, u32[]{:S(2)}) collective-permute-start(bf16[64,128]{1,0:T(8,128)(2,1)S(1)} %get-tuple-element.31.refs_2_.refs_6_.refs_10_), channel_id=1, source_target_pairs={{1,0},{0,1},{3,2},{2,3},{12,4},{13,5},{14,6},{15,7},{9,8},{8,9},{1... | collective-permute-start | bytes 49160 | tf_op jit(solution)/shard_map/ppermute | solution.py:542
  25.8 5.1 %collective-permute-start.3 = (bf16[3,64,128]{2,1,0:T(8,128)(2,1)S(1)}, bf16[3,64,128]{2,1,0:T(8,128)(2,1)S(1)}, u32[]{:S(2)}, u32[]{:S(2)}) collective-permute-start(bf16[3,64,128]{2,1,0:T(8,128)(2,1)S(1)} %pad_maximum_fusion.refs_0_), channel_id=1, source_target_pairs={{24,0},{25,1},{26,2},{27,3},{7,4},{6,5},{5,6},{4,7},{16,8},{17,9},... | collective-permute-start | bytes 147464 | tf_op jit(solution)/shard_map/ppermute | solution.py:542
  26.5 4.4 %collective-permute-start.2 = (bf16[3,64,128]{2,1,0:T(8,128)(2,1)S(1)}, bf16[3,64,128]{2,1,0:T(8,128)(2,1)S(1)}, u32[]{:S(2)}, u32[]{:S(2)}) collective-permute-start(bf16[3,64,128]{2,1,0:T(8,128)(2,1)S(1)} %pad_maximum_fusion.refs_0_), channel_id=1, source_target_pairs={{8,0},{9,1},{10,2},{11,3},{5,4},{4,5},{7,6},{6,7},{0,8},{1,9},{2,1... | collective-permute-start | bytes 147464 | tf_op jit(solution)/shard_map/ppermute | solution.py:542
  28.0 3.4 %collective-permute-start.4 = (bf16[3,64,128]{2,1,0:T(8,128)(2,1)S(1)}, bf16[3,64,128]{2,1,0:T(8,128)(2,1)S(1)}, u32[]{:S(2)}, u32[]{:S(2)}) collective-permute-start(bf16[3,64,128]{2,1,0:T(8,128)(2,1)S(1)} %pad_maximum_fusion.refs_0_), channel_id=1, source_target_pairs={{4,0},{0,4},{5,1},{1,5},{6,2},{2,6},{7,3},{3,7},{12,8},{8,12},{13,... | collective-permute-start | bytes 147464 | tf_op jit(solution)/shard_map/ppermute | solution.py:552
  30.8 1.2 %collective-permute-start.6 = (bf16[3,64,128]{2,1,0:T(8,128)(2,1)S(1)}, bf16[3,64,128]{2,1,0:T(8,128)(2,1)S(1)}, u32[]{:S(2)}, u32[]{:S(2)}) collective-permute-start(bf16[3,64,128]{2,1,0:T(8,128)(2,1)S(1)} %collective-permute-done.3.refs_2_), channel_id=1, source_target_pairs={{4,0},{0,4},{5,1},{1,5},{6,2},{2,6},{7,3},{3,7},{12,8},{8,12},{13,... | collective-permute-start | bytes 147464 | tf_op jit(solution)/shard_map/ppermute | solution.py:552
  30.8 1.4 %collective-permute-start.5 = (bf16[3,64,128]{2,1,0:T(8,128)(2,1)S(1)}, bf16[3,64,128]{2,1,0:T(8,128)(2,1)S(1)}, u32[]{:S(2)}, u32[]{:S(2)}) collective-permute-start(bf16[3,64,128]{2,1,0:T(8,128)(2,1)S(1)} %collective-permute-done.2.refs_1_), channel_id=1, source_target_pairs={{4,0},{0,4},{5,1},{1,5},{6,2},{2,6},{7,3},{3,7},{12,8},{8,12},{13,... | collective-permute-start | bytes 147464 | tf_op jit(solution)/shard_map/ppermute | solution.py:552
  33.1 5.5 %collective-permute-start.8 = (bf16[64,128]{1,0:T(8,128)(2,1)S(1)}, bf16[64,128]{1,0:T(8,128)(2,1)S(1)}, u32[]{:S(2)}, u32[]{:S(2)}) collective-permute-start(bf16[64,128]{1,0:T(8,128)(2,1)S(1)} %get-tuple-element.39.refs_6_), channel_id=1, source_target_pairs={{3,0},{2,1},{1,2},{0,3},{28,4},{29,5},{30,6},{31,7},{11,8},{10,9},... | collective-permute-start | bytes 49160 | tf_op jit(solution)/shard_map/ppermute | solution.py:542
  35.1 3.7 %collective-permute-start.7 = (bf16[64,128]{1,0:T(8,128)(2,1)S(1)}, bf16[64,128]{1,0:T(8,128)(2,1)S(1)}, u32[]{:S(2)}, u32[]{:S(2)}) collective-permute-start(bf16[64,128]{1,0:T(8,128)(2,1)S(1)} %get-tuple-element.39.refs_6_), channel_id=1, source_target_pairs={{1,0},{0,1},{3,2},{2,3},{12,4},{13,5},{14,6},{15,7},{9,8},{8,9},{1... | collective-permute-start | bytes 49160 | tf_op jit(solution)/shard_map/ppermute | solution.py:542
  38.9 5.1 %collective-permute-start.10 = (bf16[3,64,128]{2,1,0:T(8,128)(2,1)S(1)}, bf16[3,64,128]{2,1,0:T(8,128)(2,1)S(1)}, u32[]{:S(2)}, u32[]{:S(2)}) collective-permute-start(bf16[3,64,128]{2,1,0:T(8,128)(2,1)S(1)} %pad_maximum_fusion.1.refs_0_), channel_id=1, source_target_pairs={{24,0},{25,1},{26,2},{27,3},{7,4},{6,5},{5,6},{4,7},{16,8},{17,9},... | collective-permute-start | bytes 147464 | tf_op jit(solution)/shard_map/ppermute | solution.py:542
  40.8 4.1 %collective-permute-start.9 = (bf16[3,64,128]{2,1,0:T(8,128)(2,1)S(1)}, bf16[3,64,128]{2,1,0:T(8,128)(2,1)S(1)}, u32[]{:S(2)}, u32[]{:S(2)}) collective-permute-start(bf16[3,64,128]{2,1,0:T(8,128)(2,1)S(1)} %pad_maximum_fusion.1.refs_0_), channel_id=1, source_target_pairs={{8,0},{9,1},{10,2},{11,3},{5,4},{4,5},{7,6},{6,7},{0,8},{1,9},{2,1... | collective-permute-start | bytes 147464 | tf_op jit(solution)/shard_map/ppermute | solution.py:542
  41.5 3.4 %collective-permute-start.11 = (bf16[3,64,128]{2,1,0:T(8,128)(2,1)S(1)}, bf16[3,64,128]{2,1,0:T(8,128)(2,1)S(1)}, u32[]{:S(2)}, u32[]{:S(2)}) collective-permute-start(bf16[3,64,128]{2,1,0:T(8,128)(2,1)S(1)} %pad_maximum_fusion.1.refs_0_), channel_id=1, source_target_pairs={{4,0},{0,4},{5,1},{1,5},{6,2},{2,6},{7,3},{3,7},{12,8},{8,12},{13,... | collective-permute-start | bytes 147464 | tf_op jit(solution)/shard_map/ppermute | solution.py:552
  43.9 1.2 %collective-permute-start.13 = (bf16[3,64,128]{2,1,0:T(8,128)(2,1)S(1)}, bf16[3,64,128]{2,1,0:T(8,128)(2,1)S(1)}, u32[]{:S(2)}, u32[]{:S(2)}) collective-permute-start(bf16[3,64,128]{2,1,0:T(8,128)(2,1)S(1)} %collective-permute-done.10.refs_2_), channel_id=1, source_target_pairs={{4,0},{0,4},{5,1},{1,5},{6,2},{2,6},{7,3},{3,7},{12,8},{8,12},{13,... | collective-permute-start | bytes 147464 | tf_op jit(solution)/shard_map/ppermute | solution.py:552
  44.9 1.2 %collective-permute-start.12 = (bf16[3,64,128]{2,1,0:T(8,128)(2,1)S(1)}, bf16[3,64,128]{2,1,0:T(8,128)(2,1)S(1)}, u32[]{:S(2)}, u32[]{:S(2)}) collective-permute-start(bf16[3,64,128]{2,1,0:T(8,128)(2,1)S(1)} %collective-permute-done.9.refs_1_), channel_id=1, source_target_pairs={{4,0},{0,4},{5,1},{1,5},{6,2},{2,6},{7,3},{3,7},{12,8},{8,12},{13,... | collective-permute-start | bytes 147464 | tf_op jit(solution)/shard_map/ppermute | solution.py:552

commit v6 on v5

--- a/solution.py
+++ b/solution.py
@@ -34,7 +34,6 @@
     -0.007028386239784362,
 )
 VMEM_LIMIT = 24 * 1024 * 1024
-GROUP = 4
 FETCH_LIMIT = 60 * 1024 * 1024
 NT = (((1,), (1,)), ((), ()))
 NN = (((1,), (0,)), ((), ()))
@@ -95,38 +94,36 @@
         self.small = self.ndev <= 64 and len(self.sides) == 2
         self.wrapped = [self.sizes[axis] == 2 for axis in AXES]
 
-    def places(self):
+    def global_id(self, offset):
+        place = 0
+        for axis, step in zip(AXES, offset):
+            count = self.sizes[axis]
+            place = place * count + lax.rem(lax.axis_index(axis) + (step + count), count)
+        return place
+
+    def places(self, column_known=False):
         index = {axis: lax.axis_index(axis) for axis in AXES}
 
         def parity(axis):
             return lax.rem(index[axis], 2) if paired(self.sizes[axis]) else jnp.int32(0)
 
-        def moved(axis, step):
-            return lax.rem(index[axis] + (step + self.sizes[axis]), self.sizes[axis])
-
         turns = parity("gx"), parity("gz")
-        core = lax.rem(index["gy"], 2) if self.mixed else jnp.int32(0)
+        mixed = self.mixed and not column_known
+        core = lax.rem(index["gy"], 2) if mixed else jnp.int32(0)
         found = []
         for side in range(len(self.sides)):
-            x_first = core if side == 0 or not self.mixed else 1 - core
+            x_first = core if side == 0 or not mixed else 1 - core
             for second, first in self.brought:
-                plain = matched(second, turns[0]) * self.depth + matched(first, turns[1])
+                row = first if column_known else matched(first, turns[1])
+                plain = matched(second, turns[0]) * self.depth + row
                 crossed = matched(first, turns[0]) * self.depth + matched(second, turns[1])
-                tile = jnp.where(x_first == 1, crossed, plain) if self.mixed else plain
+                tile = jnp.where(x_first == 1, crossed, plain) if mixed else plain
                 found.append(tile * len(self.sides) + side)
         found += turns
-        for ox, oz in self.tiles:
-            for oy in self.sides:
-                place = (moved("gx", ox) * self.sizes["gy"] + moved("gy", oy)) * self.sizes["gz"]
-                found.append(place + moved("gz", oz))
         return [jnp.asarray(place, jnp.int32) for place in found]
 
     def brought_place(self, places, side, pair):
         return places[side * len(self.brought) + pair]
-
-    def global_place(self, places, tile, side):
-        start = len(self.sides) * len(self.brought) + 2
-        return places[start + tile * len(self.sides) + side]
 
     def staged_place(self, places, tile):
         start = len(self.sides) * len(self.brought)
@@ -164,12 +161,10 @@
 
 
 def first_kernel(plan, nrefs, places, *refs):
-    far_refs, fetched, refs = refs[:nrefs], refs[nrefs : nrefs + 8], refs[nrefs + 8 :]
-    rows_ref, basis_ref, layer_ref, vector_ref, mixing_ref, cols_ref, table_ref, *refs = refs
-    kept, (pair_ref, block_ref, embed_ref, radial_ref, sems) = refs[:6], refs[6:]
-    mix_ref = kept[0]
+    far_refs, refs = refs[:nrefs], refs[nrefs:]
+    (table_ref, embed_ref, mix_ref), refs = refs[:3], refs[3:]
+    rows_ref, basis_ref, layer_ref, vector_ref, mixing_ref, cols_ref, pair_ref, block_ref = refs
     slots, nbasis, nspec = plan.slots, plan.nbasis, plan.nspec
-    copies = begin(zip(fetched, (embed_ref, radial_ref, *kept)), sems)
 
     def put(place, block):
         block_ref[place] = block
@@ -177,77 +172,81 @@
     if not plan.small:
         scatter(plan, places, far_refs, put)
 
-    def block_of(tile, side):
+    def block_of(tile, side, up):
         if plan.small:
-            return far_refs[0][plan.global_place(places, tile, side)]
+            x, y, z = plan.offset(tile, side)
+            return far_refs[0][plan.global_id((x, y, z + up))]
         return block_ref[tile * len(plan.sides) + side]
 
-    rows = block_of(0, 0)
-    held = jnp.concatenate([rows, rows], axis=0).T[:slots]
-    kind = held[:, 3:4]
-    lane = lax.broadcasted_iota(jnp.int32, held.shape, 1)
-    live = kind >= 0.0
-    held = jnp.where((lane == 0) & ~live, -FAR, held)
-    held = jnp.where(lane == 3, live.astype(F32), held)
-    cols_ref[...] = held
-    cols = [held[:, axis : axis + 1] for axis in range(3)]
     species = lax.broadcasted_iota(jnp.int32, (nbasis * nspec, plan.width), 0) % nspec
-    hot, gathered = [], None
-    for tile in range(len(plan.tiles)):
-        blocks = [block_of(tile, side) for side in range(len(plan.sides))]
-        placed = side_by_side(plan, blocks) + tile_shift(plan, tile)
-        rows_ref[tile] = placed
-        rows = [placed[k : k + 1] for k in range(4)]
-        hot.append((rows[3].astype(jnp.int32) == species).astype(F32).astype(BF16))
-        parts = separations(plan, rows, cols)
-        dist_sq, inverse = distance(plan, parts, tile)
-        sine, cosine = waves(dist_sq, inverse)
-        fade = jnp.maximum(1.0 - dist_sq * (1.0 / CUT_SQUARE), 0.0)
-        radial = fade * fade * inverse
-        units = [(part * (inverse * ROOT_THREE)).astype(BF16) for part in parts]
-        before, now = None, sine * radial
-        lanes = slice(tile * plan.width, (tile + 1) * plan.width)
-        for n in range(nbasis):
-            if n == 1:
-                before, now = now, 2.0 * cosine * now
-            elif n > 1:
-                before, now = now, 2.0 * cosine * now - before
-            packed = now.astype(BF16)
-            basis_ref[n, :, lanes] = packed
-            pair_ref[n, :slots, lanes] = packed
-            for k in range(3):
-                pair_ref[n, (k + 1) * slots : (k + 2) * slots, lanes] = units[k] * packed
-        if tile % GROUP == GROUP - 1 or tile == len(plan.tiles) - 1:
-            lanes = slice((tile // GROUP) * GROUP * plan.width, (tile + 1) * plan.width)
-            taken = pair_ref[:, :, lanes].reshape(nbasis * 4 * slots, -1)
-            part = dot(taken, jnp.concatenate(hot, axis=1), NT)
-            gathered = part if gathered is None else gathered + part
-            hot = []
-    for copy in copies:
-        copy.wait()
-    embed = embed_ref[...]
-    for g in range(2):
-        for n in range(nbasis):
-            row = radial_ref[g, n : n + 1]
-            weighted = row * embed.astype(F32)
-            table_ref[g, n * nspec : (n + 1) * nspec] = weighted.astype(BF16)
-    own_species = lax.broadcasted_iota(jnp.int32, (slots, nspec), 1)
-    own_hot = (kind.astype(jnp.int32) == own_species).astype(F32).astype(BF16)
-    gathered = gathered.reshape(nbasis, 4 * slots, nbasis * nspec)
-    group = lax.broadcasted_iota(jnp.int32, gathered.shape[1:], 1) // nspec
-    counted = jnp.zeros(gathered.shape[1:], F32)
-    for n in range(nbasis):
-        counted = jnp.where(group == n, gathered[n], counted)
-    scalar = MSG_SCALE * split_dot(counted[:slots], table_ref[0])
-    vector = MSG_SCALE * split_dot(counted[slots:], table_ref[1])
-    vector_ref[...] = vector
-    squares = vector * vector
-    norm = squares[:slots] + squares[slots : 2 * slots] + squares[2 * slots :]
+    shifts = [tile_shift(plan, tile) for tile in range(len(plan.tiles))]
+    own, counted = [], []
+    for which in range(layer_ref.shape[0]):
+        up = offsets_of(plan.sizes["gz"])[which]
+        held = block_of(0, 0, up)
+        held = jnp.concatenate([held, held], axis=0).T[:slots]
+        kind = held[:, 3:4]
+        own.append(kind)
+        lane = lax.broadcasted_iota(jnp.int32, held.shape, 1)
+        live = kind >= 0.0
+        held = jnp.where((lane == 0) & ~live, -FAR, held)
+        if which == 0:
+            cols_ref[...] = jnp.where(lane == 3, live.astype(F32), held)
+        cols = [held[:, axis : axis + 1] for axis in range(3)]
+        hot = []
+        for tile in range(len(plan.tiles)):
+            blocks = [block_of(tile, side, up) for side in range(len(plan.sides))]
+            placed = side_by_side(plan, blocks) + shifts[tile]
+            if which == 0:
+                rows_ref[tile] = placed
+            rows = [placed[k : k + 1] for k in range(4)]
+            hot.append((rows[3].astype(jnp.int32) == species).astype(F32).astype(BF16))
+            parts = separations(plan, rows, cols)
+            dist_sq, inverse = distance(plan, parts, tile)
+            sine, cosine = waves(dist_sq, inverse)
+            fade = jnp.maximum(1.0 - dist_sq * (1.0 / CUT_SQUARE), 0.0)
+            radial = fade * fade * inverse
+            units = [(part * (inverse * ROOT_THREE)).astype(BF16) for part in parts]
+            before, now = None, sine * radial
+            double = 2.0 * cosine
+            lanes = slice(tile * plan.width, (tile + 1) * plan.width)
+            for n in range(nbasis):
+                if n == 1:
+                    before, now = now, double * now
+                elif n > 1:
+                    before, now = now, double * now - before
+                packed = now.astype(BF16)
+                if which == 0:
+                    basis_ref[n, :, lanes] = packed
+                pair_ref[which, n, :slots, lanes] = packed
+                for k in range(3):
+                    pair_ref[which, n, (k + 1) * slots : (k + 2) * slots, lanes] = units[k] * packed
+        hot = jnp.concatenate(hot, axis=1)
+        gathered = dot(pair_ref[which].reshape(nbasis * 4 * slots, plan.far), hot, NT)
+        gathered = gathered.reshape(nbasis, 4 * slots, nbasis * nspec)
+        group = lax.broadcasted_iota(jnp.int32, gathered.shape[1:], 1) // nspec
+        total = gathered[0]
+        for n in range(1, nbasis):
+            total = jnp.where(group == n, gathered[n], total)
+        counted.append(total)
+    scalar = split_dot(jnp.concatenate([total[:slots] for total in counted], axis=0), table_ref[0])
+    scalar = MSG_SCALE * scalar
+    norm = None
+    for k in range(3):
+        rows = slice((k + 1) * slots, (k + 2) * slots)
+        vector = split_dot(jnp.concatenate([total[rows] for total in counted], axis=0), table_ref[1])
+        vector = MSG_SCALE * vector
+        vector_ref[k * slots : (k + 1) * slots] = vector[:slots]
+        norm = vector * vector if k == 0 else norm + vector * vector
     invariants = jnp.concatenate([scalar.astype(BF16), norm.astype(BF16)], axis=1)
     mixing = dot(invariants, mix_ref[...], NT)
-    mixing_ref[...] = mixing
-    layer = (dot(own_hot, embed) + mixing * sigmoid(mixing)).astype(BF16)
-    layer_ref[...] = layer
+    mixing_ref[...] = mixing[:slots]
+    kind = jnp.concatenate(own, axis=0)
+    own_species = lax.broadcasted_iota(jnp.int32, (kind.shape[0], nspec), 1)
+    own_hot = (kind.astype(jnp.int32) == own_species).astype(F32).astype(BF16)
+    layer = (dot(own_hot, embed_ref[...]) + mixing * sigmoid(mixing)).astype(BF16)
+    for which in range(layer_ref.shape[0]):
+        layer_ref[which] = layer[which * slots : (which + 1) * slots]
 
 
 def sigmoid(value):
@@ -301,7 +300,7 @@
     rounded = (MSG_SCALE * message).astype(BF16)
     mixing = dot(rounded, mix_ref[...], NT)
     gate = sigmoid(mixing)
-    layer = layer_ref[...].astype(F32)
+    layer = layer_ref[0].astype(F32)
     features = (layer + mixing * gate).astype(BF16)
     features_ref[...] = features
     before = dot(features, hidden_ref[...], NT)
@@ -360,7 +359,7 @@
     before = before_ref[...]
     live = jnp.where(lax.broadcasted_iota(jnp.int32, (slots, 8), 1) == 0, cols_ref[:, 3:4], 0.0)
     live_row = dot(jnp.ones((1, 8), BF16), live.astype(BF16), NT)
-    energy = dot_exact(one_ref[...], layer_ref[...].astype(F32), NT)
+    energy = dot_exact(one_ref[...], layer_ref[0].astype(F32), NT)
     energy = energy + dot_exact(out_ref[...], before * sigmoid(before), NT)
     energy_ref[...] = energy * live_row
     gather_far(plan, places, far_refs, all_ref)
@@ -449,7 +448,7 @@
             out_ref[plan.staged_place(places, tile)] = pulled
             continue
         for side in range(len(plan.sides)):
-            place = plan.global_place(places, tile, side)
+            place = plan.global_id(plan.offset(tile, side))
             out_ref[place, :3] = jnp.where(side_of == side, pulled, 0.0)
 
 
@@ -460,8 +459,11 @@
     return copies
 
 
-def prepare_kernel(plan, counts_ref, place_hbm, kind_hbm, sent_ref, place_ref, kind_ref, sems):
-    for copy in begin([(place_hbm, place_ref), (kind_hbm, kind_ref)], sems):
+def prepare_kernel(plan, counts_ref, *refs):
+    fetched, sent_ref, table_ref, refs = refs[:10], refs[10], refs[11], refs[12:]
+    kept, (place_ref, kind_ref, radial_ref, sems) = refs[:7], refs[7:]
+    copies = begin(zip(fetched, (place_ref, kind_ref, radial_ref, *kept)), sems)
+    for copy in copies[:2]:
         copy.wait()
     live = lax.broadcasted_iota(jnp.int32, (1, plan.slots), 1) < counts_ref[0]
     rows = [
@@ -474,6 +476,13 @@
     rows = jnp.concatenate([rows, rows], axis=1)
     for copy in range(sent_ref.shape[0]):
         sent_ref[copy] = rows
+    for copy in copies[2:]:
+        copy.wait()
+    embed, nspec = kept[0][...].astype(F32), plan.nspec
+    for g in range(2):
+        for n in range(plan.nbasis):
+            weighted = radial_ref[g, n : n + 1] * embed
+            table_ref[g, n * nspec : (n + 1) * nspec] = weighted.astype(BF16)
 
 
 def sum_kernel(plan, parts_ref, force_ref):
@@ -513,9 +522,9 @@
     return got[0] if single else got
 
 
-def call(kernel, plan, far, operands, outs, scratch, flops, **options):
+def call(kernel, plan, far, operands, outs, scratch, flops, column_known=False, **options):
     def body(plan, *refs):
-        kernel(plan, len(far), plan.places(), *refs)
+        kernel(plan, len(far), plan.places(column_known), *refs)
 
     return simple_call(body, plan, [*far, *operands], outs, 0, scratch, flops, **options)
 
@@ -530,13 +539,13 @@
     return [[(i + o) % count for i in range(count)] for o in offsets_of(count)[1:]]
 
 
-def brought(plan, block, second):
+def brought(plan, block, second, mixed):
     sizes, sources = plan.sizes, {axis: swaps(plan.sizes[axis]) for axis in AXES}
     got = []
     for m in range(len(sources["gx" if second else "gz"])):
         pairs = []
         for x, y, z in itertools.product(*(range(sizes[axis]) for axis in AXES)):
-            along_x = second != (plan.mixed and y % 2 == 1)
+            along_x = second != (mixed and y % 2 == 1)
             source = (sources["gx"][m][x], y, z) if along_x else (x, y, sources["gz"][m][z])
             pairs.append((flat(sizes, *source), flat(sizes, x, y, z)))
         got.append(lax.ppermute(block, AXES, pairs))
@@ -555,8 +564,14 @@
 
 
 def neighbours(plan, block, again=None):
-    column = jnp.stack([block if again is None else again] + brought(plan, block, False))
-    columns = [column] + brought(plan, column, True)
+    column = jnp.stack([block if again is None else again] + brought(plan, block, False, plan.mixed))
+    return from_columns(plan, column, plan.mixed)
+
+
+def from_columns(plan, column, mixed, again=None):
+    columns = [column] + brought(plan, column, True, mixed)
+    if again is not None:
+        columns[0] = again
     swapped = [[column] + along(column, "gy") for column in columns]
     return [column[side] for side in range(len(plan.sides)) for column in swapped]
 
@@ -599,47 +614,45 @@
         slots, channels = positions.shape[-1], embed.shape[1]
         nbasis, nspec = radial_two.shape[0], embed.shape[0]
         plan = Plan(mesh, slots, nbasis, nspec)
-        count = counts.reshape(1)
-        given = [positions[0, 0, 0].reshape(3, 1, slots), species.reshape(1, slots)]
-        sent = simple_call(
+        given = [positions[0, 0, 0].reshape(3, 1, slots), species.reshape(1, slots), radial_one]
+        weights = [embed, mix_one, radial_two, read_out[None], read_one[None], mix_two, read_hidden]
+        sent, table, *weights = simple_call(
             prepare_kernel,
             plan,
-            [count, *given],
-            ((plan.ndev if plan.small else 1, 4, 2 * slots), F32),
+            [counts.reshape(1), *given, *weights],
+            [
+                ((plan.ndev if plan.small else 1, 4, 2 * slots), F32),
+                ((2, nbasis * nspec, channels), BF16),
+            ]
+            + [(weight.shape, weight.dtype) for weight in weights],
             1,
             [(array.shape, array.dtype) for array in given],
             near=True,
-            fetched=len(given),
+            fetched=len(given) + len(weights),
         )
+        embed, mix_one, radial_two, out_row, one_row, mix_two, read_hidden = weights
         far_sent = [everywhere(sent)] if plan.small else neighbours(plan, sent[0])
         pair_flops = 100 * slots * plan.far
-        weights = [mix_one, radial_two, read_out[None], read_one[None], mix_two, read_hidden]
-        rows, basis, layer, vector, mixing, cols, table, *weights = call(
+        known = plan.depth if plan.small else 1
+        rows, basis, layer, vector, mixing, cols = call(
             first_kernel,
             plan,
             far_sent,
-            [embed, radial_one, *weights],
+            [table, embed, mix_one],
             [
                 ((len(plan.tiles), 4, plan.width), F32),
                 ((nbasis, slots, plan.far), BF16),
-                ((slots, channels), BF16),
+                ((known, slots, channels), BF16),
                 ((3 * slots, channels), F32),
                 ((slots, channels), F32),
                 ((slots, 8), F32),
-                ((2, nbasis * nspec, channels), BF16),
-            ]
-            + [(weight.shape, weight.dtype) for weight in weights],
+            ],
             [
-                ((nbasis, 4 * slots, plan.far), BF16),
+                ((known, nbasis, 4 * slots, plan.far), BF16),
                 ((len(plan.tiles) * len(plan.sides), 4, 2 * slots), F32),
-                (embed.shape, BF16),
-                (radial_one.shape, F32),
             ],
             pair_flops,
-            near=True,
-            fetched=2 + len(weights),
         )
-        mix_one, radial_two, out_row, one_row, mix_two, read_hidden = weights
         again, apart, slope, factor, turned = simple_call(
             slope_kernel,
             plan,
@@ -648,7 +661,10 @@
             + [((count, slots, plan.far), F32) for count in (3, nbasis, nbasis, nbasis)],
             flops=pair_flops,
         )
-        far_layer = neighbours(plan, layer, again)
+        if plan.small:
+            far_layer = from_columns(plan, layer, False, again)
+        else:
+            far_layer = neighbours(plan, layer[0], again[0])
         far_scratch = ((plan.far, channels), BF16)
         adjoint, kept, before, own_adjoint = call(
             second_kernel,
@@ -663,6 +679,7 @@
             ],
             [far_scratch],
             pair_flops,
+            plan.small,
         )
         again, pair, energy, features = call(
             energy_kernel,
@@ -677,6 +694,7 @@
             ],
             [far_scratch],
             pair_flops,
+            plan.small,
         )
         far_adjoint = neighbours(plan, adjoint, again)
         pulls = call(

time: 59.4 us -> 54.5 us (0.918)
  waiting for transfers between devices: 14.4 us -> 10.6 us
  starting transfers between devices: 8.42 us -> 6.4 us
  Pallas kernels: 10.1 us -> 11.1 us
    ppermute x8 -> x6, waiting for transfers between devices: 12.3 us -> 8.48 us  [brought(): got.append(lax.ppermute(block, AXES, pairs))]
    ppermute x8 -> x6, starting transfers between devices: 7.9 us -> 5.81 us  [brought(): got.append(lax.ppermute(block, AXES, pairs))]
    pallas_call x7, Pallas kernels: 10.1 us -> 11.1 us  [simple_call(): pl.pallas_call(body, out_shape=shapes, in_specs=[SMEM_SPEC] * scalars + [...]
  transfers between devices with their start and end apart: 14 -> 12, of which waited for: 10 -> 8; matrix products, arithmetic and copies ran while one was open for 0% -> 0% of each run, Pallas kernels for 4% -> 4%
where the time goes in v6:
time: 54.5 us; the launch traced here: 54.3 us
  blocking collectives  24.8 us (46%)
  Pallas kernels  11.1 us (20%)
  waiting for transfers between devices  10.6 us (19%)
  starting transfers between devices  6.4 us (12%)
  between operations  1.34 us (2%)
    all_to_all x2, blocking collectives, everywhere(): return lax.all_to_all(copies, AXES, 0, 0, tiled=True)  24.8 us
    pallas_call x7, Pallas kernels, simple_call(): pl.pallas_call(body, out_shape=shapes, in_specs=[SMEM_SPEC] * scalars + [...  11.1 us
    ppermute x6, waiting for transfers between devices, brought(): got.append(lax.ppermute(block, AXES, pairs))  8.48 us
    ppermute x6, starting transfers between devices, brought(): got.append(lax.ppermute(block, AXES, pairs))  5.81 us
    ppermute x6, waiting for transfers between devices, along(): lax.ppermute(block, axis, [(source, i) for i, source in enumerate(sources)])  2.11 us
  transfers between devices with their start and end apart: 12, of which 8 were waited for; matrix products, arithmetic and copies ran while one was open for 0% of the time, Pallas kernels for 4%

profile of v6, /device:TPU:0, one launch (start us, length us, event | category | flops | bytes accessed | tf_op | source)
XLA Modules:
  0.0 54.3 jit_solution(6702072955442896344)
XLA Ops:
  1.3 1.0 %shard_map.130 = (f32[32,4,128]{2,1,0:T(4,128)S(1)}, bf16[2,32,128]{2,1,0:T(8,128)(2,1)S(1)}, bf16[8,128]{1,0:T(8,128)(2,1)S(1)}, bf16[128,256]{1,0:T(8,128)(2,1...) custom-call(s32[1]{0:T(128)} %bitcast.15.refs_0_, ...), custom_call_target="tpu_custom_call" | custom-call | flops 1048576 | bytes 1048576 | tf_op jit(solution)/shard_map/pallas_call | solution.py:510
  2.3 14.6 %all_to_all.10.refs_0_ = f32[32,4,128]{2,1,0:T(4,128)S(1)} all-to-all(f32[32,4,128]{2,1,0:T(4,128)S(1)} %get-tuple-element.31), channel_id=1, replica_groups=mesh['gx'=4,'gy'=2,'gz'=4] {'gx','gy','gz'}, dimensions={0} | all-to-all | bytes 131072 | tf_op jit(solution)/shard_map/all_to_all | solution.py:580
  16.9 4.2 %shard_map.131 = (f32[9,4,128]{2,1,0:T(4,128)S(1)}, bf16[4,64,1152]{2,1,0:T(8,128)(2,1)S(1)}, bf16[3,64,128]{2,1,0:T(8,128)(2,1)S(1)}, f32[192,128]{1,0:T(8,128)...) custom-call(f32[32,4,128]{2,1,0:T(4,128)S(1)} %all_to_all.10.refs_0_, ...), custom_call_target="tpu_custom_call" | custom-call | flops 7372800 | bytes 1048576 | tf_op jit(solution)/shard_map/pallas_call | solution.py:510
  21.1 0.7 %collective-permute-start.1 = (bf16[3,64,128]{2,1,0:T(8,128)(2,1)S(1)}, bf16[3,64,128]{2,1,0:T(8,128)(2,1)S(1)}, u32[]{:S(2)}, u32[]{:S(2)}) collective-permute-start(bf16[3,64,128]{2,1,0:T(8,128)(2,1)S(1)} %get-tuple-element.37.refs_2_.refs_6_.refs_10_), channel_id=1, source_target_pairs={{24,0},{25,1},{26,2},{27,3},{28,4},{29,5},{30,6},{31,7},{16,8},{17... | collective-permute-start | bytes 147464 | tf_op jit(solution)/shard_map/ppermute | solution.py:551
  21.8 1.5 %collective-permute-start = (bf16[3,64,128]{2,1,0:T(8,128)(2,1)S(1)}, bf16[3,64,128]{2,1,0:T(8,128)(2,1)S(1)}, u32[]{:S(2)}, u32[]{:S(2)}) collective-permute-start(bf16[3,64,128]{2,1,0:T(8,128)(2,1)S(1)} %get-tuple-element.37.refs_2_.refs_6_.refs_10_), channel_id=1, source_target_pairs={{8,0},{9,1},{10,2},{11,3},{12,4},{13,5},{14,6},{15,7},{0,8},{1,9},... | collective-permute-start | bytes 147464 | tf_op jit(solution)/shard_map/ppermute | solution.py:551
  23.3 1.2 %shard_map.132 = (bf16[3,64,128]{2,1,0:T(8,128)(2,1)S(1)}, f32[3,64,1152]{2,1,0:T(8,128)S(1)}, f32[4,64,1152]{2,1,0:T(8,128)S(1)}, f32[4,64,1152]{2,1,0:T(8,128)S(1)}, f32[4,64,1152]{2,1,0:T(8,128)S(1)}) custom-call(f32[9,4,128]{2,1,0:T(4,128)S(1)} %get-tuple-element.35.refs_0_.refs_9_, f32[64,8]{1,0:T(8,128)S(1)} %get-tuple-element.36.refs_1_.refs_8_.refs_9_, ...), custom_call_target="tpu_custom_call" | custom-call | flops 7372800 | bytes 1048576 | tf_op jit(solution)/shard_map/pallas_call | solution.py:510
  24.5 0.1 collective-permute-start.2
  24.6 1.5 %collective-permute-done.1.refs_2_ = bf16[3,64,128]{2,1,0:T(8,128)(2,1)S(1)} collective-permute-done((bf16[3,64,128]{2,1,0:T(8,128)(2,1)S(1)}, bf16[3,64,128]{2,1,0:T(8,128)(2,1)S(1)}, u32[]{:S(2)}, u32[]{:S(2)}) %collective-permute-start.1) | collective-permute-done | bytes 49184 | tf_op jit(solution)/shard_map/ppermute | solution.py:551
  26.2 0.0 collective-permute-start.4
  26.2 0.0 collective-permute-done.refs_1_
  26.2 0.5 collective-permute-start.3
  26.7 0.0 collective-permute-done.2.refs_3_
  26.7 0.7 %collective-permute-done.4.refs_5_ = bf16[3,64,128]{2,1,0:T(8,128)(2,1)S(1)} collective-permute-done((bf16[3,64,128]{2,1,0:T(8,128)(2,1)S(1)}, bf16[3,64,128]{2,1,0:T(8,128)(2,1)S(1)}, u32[]{:S(2)}, u32[]{:S(2)}) %collective-permute-start.4) | collective-permute-done | bytes 49184 | tf_op jit(solution)/shard_map/ppermute | solution.py:561
  27.4 0.2 collective-permute-done.3.refs_4_
  27.6 0.8 %shard_map.133 = (bf16[64,128]{1,0:T(8,128)(2,1)S(1)}, bf16[64,128]{1,0:T(8,128)(2,1)S(1)}, f32[64,16]{1,0:T(8,128)S(1)}, f32[64,128]{1,0:T(8,128)S(1)}) custom-call(bf16[3,64,128]{2,1,0:T(8,128)(2,1)S(1)} %get-tuple-element.38.refs_0_, bf16[3,64,128]{2,1,0:T(8,128)(2,1)S(1)} %collective-permute-done.refs_1_, ...), custom_call_target="tpu_custom_call" | custom-call | flops 7372800 | bytes 1048576 | tf_op jit(solution)/shard_map/pallas_call | solution.py:510
  28.4 0.8 %collective-permute-start.6 = (bf16[64,128]{1,0:T(8,128)(2,1)S(1)}, bf16[64,128]{1,0:T(8,128)(2,1)S(1)}, u32[]{:S(2)}, u32[]{:S(2)}) collective-permute-start(bf16[64,128]{1,0:T(8,128)(2,1)S(1)} %get-tuple-element.45.refs_6_), channel_id=1, source_target_pairs={{3,0},{2,1},{1,2},{0,3},{28,4},{29,5},{30,6},{31,7},{11,8},{10,9},... | collective-permute-start | bytes 49160 | tf_op jit(solution)/shard_map/ppermute | solution.py:551
  29.2 0.2 collective-permute-start.5
  29.4 1.0 %shard_map.134 = (bf16[64,128]{1,0:T(8,128)(2,1)S(1)}, f32[64,1152]{1,0:T(8,128)S(1)}, f32[1,64]{1,0:T(1,128)}, bf16[64,128]{1,0:T(8,128)(2,1)}) custom-call(bf16[3,64,128]{2,1,0:T(8,128)(2,1)S(1)} %get-tuple-element.38.refs_0_, bf16[3,64,128]{2,1,0:T(8,128)(2,1)S(1)} %collective-permute-done.refs_1_, ...), custom_call_target="tpu_custom_call" | custom-call | flops 7372800 | bytes 1048576 | tf_op jit(solution)/shard_map/pallas_call | solution.py:510
  30.5 3.5 %collective-permute-done.6 = bf16[64,128]{1,0:T(8,128)(2,1)S(1)} collective-permute-done((bf16[64,128]{1,0:T(8,128)(2,1)S(1)}, bf16[64,128]{1,0:T(8,128)(2,1)S(1)}, u32[]{:S(2)}, u32[]{:S(2)}) %collective-permute-start.6) | collective-permute-done | bytes 16416 | tf_op jit(solution)/shard_map/ppermute | solution.py:551
  34.0 0.0 collective-permute-done.5
  34.0 1.9 %collective-permute-start.8 = (bf16[3,64,128]{2,1,0:T(8,128)(2,1)S(1)}, bf16[3,64,128]{2,1,0:T(8,128)(2,1)S(1)}, u32[]{:S(2)}, u32[]{:S(2)}) collective-permute-start(bf16[3,64,128]{2,1,0:T(8,128)(2,1)S(1)} %pad_maximum_fusion.refs_0_), channel_id=1, source_target_pairs={{24,0},{25,1},{26,2},{27,3},{7,4},{6,5},{5,6},{4,7},{16,8},{17,9},... | collective-permute-start | bytes 147464 | tf_op jit(solution)/shard_map/ppermute | solution.py:551
  35.9 0.7 %collective-permute-start.7 = (bf16[3,64,128]{2,1,0:T(8,128)(2,1)S(1)}, bf16[3,64,128]{2,1,0:T(8,128)(2,1)S(1)}, u32[]{:S(2)}, u32[]{:S(2)}) collective-permute-start(bf16[3,64,128]{2,1,0:T(8,128)(2,1)S(1)} %pad_maximum_fusion.refs_0_), channel_id=1, source_target_pairs={{8,0},{9,1},{10,2},{11,3},{5,4},{4,5},{7,6},{6,7},{0,8},{1,9},{2,1... | collective-permute-start | bytes 147464 | tf_op jit(solution)/shard_map/ppermute | solution.py:551
  36.6 0.0 collective-permute-start.9
  36.6 2.5 %collective-permute-done.8.refs_2_ = bf16[3,64,128]{2,1,0:T(8,128)(2,1)S(1)} collective-permute-done((bf16[3,64,128]{2,1,0:T(8,128)(2,1)S(1)}, bf16[3,64,128]{2,1,0:T(8,128)(2,1)S(1)}, u32[]{:S(2)}, u32[]{:S(2)}) %collective-permute-start.8) | collective-permute-done | bytes 49184 | tf_op jit(solution)/shard_map/ppermute | solution.py:551
  39.0 0.0 collective-permute-start.11
  39.0 1.0 %collective-permute-done.7.refs_1_ = bf16[3,64,128]{2,1,0:T(8,128)(2,1)S(1)} collective-permute-done((bf16[3,64,128]{2,1,0:T(8,128)(2,1)S(1)}, bf16[3,64,128]{2,1,0:T(8,128)(2,1)S(1)}, u32[]{:S(2)}, u32[]{:S(2)}) %collective-permute-start.7) | collective-permute-done | bytes 49184 | tf_op jit(solution)/shard_map/ppermute | solution.py:551
  40.0 0.0 collective-permute-start.10
  40.0 0.0 collective-permute-done.9.refs_3_
  40.0 0.3 collective-permute-done.11.refs_5_
  40.3 1.0 %collective-permute-done.10.refs_4_ = bf16[3,64,128]{2,1,0:T(8,128)(2,1)S(1)} collective-permute-done((bf16[3,64,128]{2,1,0:T(8,128)(2,1)S(1)}, bf16[3,64,128]{2,1,0:T(8,128)(2,1)S(1)}, u32[]{:S(2)}, u32[]{:S(2)}) %collective-permute-start.10) | collective-permute-done | bytes 49184 | tf_op jit(solution)/shard_map/ppermute | solution.py:561
  41.2 2.2 %shard_map.135 = f32[32,4,128]{2,1,0:T(4,128)S(1)} custom-call(bf16[3,64,128]{2,1,0:T(8,128)(2,1)S(1)} %pad_maximum_fusion.refs_0_, bf16[3,64,128]{2,1,0:T(8,128)(2,1)S(1)} %collective-permute-done.7.refs_1_, bf16[3,64,128]{2,1,0:T(8,128)(2,1)S(1)} %collective-permute-done.8.refs_2_, bf16[3,64,128]{2,1,0:T(8,128)(2,1)S(1)} %collective-permute-done.9.refs_3_, ...), custom_call_target="tpu_custom_call" | custom-call | flops 7372800 | bytes 1048576 | tf_op jit(solution)/shard_map/pallas_call | solution.py:510
  43.4 10.2 %all_to_all.11.refs_0_ = f32[32,4,128]{2,1,0:T(4,128)S(1)} all-to-all(f32[32,4,128]{2,1,0:T(4,128)S(1)} %shard_map.135), channel_id=1, replica_groups=mesh['gx'=4,'gy'=2,'gz'=4] {'gx','gy','gz'}, dimensions={0} | all-to-all | bytes 131072 | tf_op jit(solution)/shard_map/all_to_all | solution.py:580
  53.6 0.7 %shard_map.136 = f32[3,1,64]{2,1,0:T(1,128)} custom-call(f32[32,4,128]{2,1,0:T(4,128)S(1)} %all_to_all.11.refs_0_), custom_call_target="tpu_custom_call" | custom-call | flops 1048576 | bytes 1048576 | tf_op jit(solution)/shard_map/pallas_call | solution.py:510
  (1 shorter events, 0.0 us)
Async XLA Ops:
  21.1 5.1 %collective-permute-start.1 = (bf16[3,64,128]{2,1,0:T(8,128)(2,1)S(1)}, bf16[3,64,128]{2,1,0:T(8,128)(2,1)S(1)}, u32[]{:S(2)}, u32[]{:S(2)}) collective-permute-start(bf16[3,64,128]{2,1,0:T(8,128)(2,1)S(1)} %get-tuple-element.37.refs_2_.refs_6_.refs_10_), channel_id=1, source_target_pairs={{24,0},{25,1},{26,2},{27,3},{28,4},{29,5},{30,6},{31,7},{16,8},{17... | collective-permute-start | bytes 147464 | tf_op jit(solution)/shard_map/ppermute | solution.py:551
  21.8 4.4 %collective-permute-start = (bf16[3,64,128]{2,1,0:T(8,128)(2,1)S(1)}, bf16[3,64,128]{2,1,0:T(8,128)(2,1)S(1)}, u32[]{:S(2)}, u32[]{:S(2)}) collective-permute-start(bf16[3,64,128]{2,1,0:T(8,128)(2,1)S(1)} %get-tuple-element.37.refs_2_.refs_6_.refs_10_), channel_id=1, source_target_pairs={{8,0},{9,1},{10,2},{11,3},{12,4},{13,5},{14,6},{15,7},{0,8},{1,9},... | collective-permute-start | bytes 147464 | tf_op jit(solution)/shard_map/ppermute | solution.py:551
  24.5 2.1 %collective-permute-start.2 = (bf16[3,64,128]{2,1,0:T(8,128)(2,1)S(1)}, bf16[3,64,128]{2,1,0:T(8,128)(2,1)S(1)}, u32[]{:S(2)}, u32[]{:S(2)}) collective-permute-start(bf16[3,64,128]{2,1,0:T(8,128)(2,1)S(1)} %get-tuple-element.38.refs_0_), channel_id=1, source_target_pairs={{4,0},{0,4},{5,1},{1,5},{6,2},{2,6},{7,3},{3,7},{12,8},{8,12},{13,... | collective-permute-start | bytes 147464 | tf_op jit(solution)/shard_map/ppermute | solution.py:561
  26.2 1.2 %collective-permute-start.4 = (bf16[3,64,128]{2,1,0:T(8,128)(2,1)S(1)}, bf16[3,64,128]{2,1,0:T(8,128)(2,1)S(1)}, u32[]{:S(2)}, u32[]{:S(2)}) collective-permute-start(bf16[3,64,128]{2,1,0:T(8,128)(2,1)S(1)} %collective-permute-done.1.refs_2_), channel_id=1, source_target_pairs={{4,0},{0,4},{5,1},{1,5},{6,2},{2,6},{7,3},{3,7},{12,8},{8,12},{13,... | collective-permute-start | bytes 147464 | tf_op jit(solution)/shard_map/ppermute | solution.py:561
  26.2 1.4 %collective-permute-start.3 = (bf16[3,64,128]{2,1,0:T(8,128)(2,1)S(1)}, bf16[3,64,128]{2,1,0:T(8,128)(2,1)S(1)}, u32[]{:S(2)}, u32[]{:S(2)}) collective-permute-start(bf16[3,64,128]{2,1,0:T(8,128)(2,1)S(1)} %collective-permute-done.refs_1_), channel_id=1, source_target_pairs={{4,0},{0,4},{5,1},{1,5},{6,2},{2,6},{7,3},{3,7},{12,8},{8,12},{13,... | collective-permute-start | bytes 147464 | tf_op jit(solution)/shard_map/ppermute | solution.py:561
  28.4 5.5 %collective-permute-start.6 = (bf16[64,128]{1,0:T(8,128)(2,1)S(1)}, bf16[64,128]{1,0:T(8,128)(2,1)S(1)}, u32[]{:S(2)}, u32[]{:S(2)}) collective-permute-start(bf16[64,128]{1,0:T(8,128)(2,1)S(1)} %get-tuple-element.45.refs_6_), channel_id=1, source_target_pairs={{3,0},{2,1},{1,2},{0,3},{28,4},{29,5},{30,6},{31,7},{11,8},{10,9},... | collective-permute-start | bytes 49160 | tf_op jit(solution)/shard_map/ppermute | solution.py:551
  29.2 4.7 %collective-permute-start.5 = (bf16[64,128]{1,0:T(8,128)(2,1)S(1)}, bf16[64,128]{1,0:T(8,128)(2,1)S(1)}, u32[]{:S(2)}, u32[]{:S(2)}) collective-permute-start(bf16[64,128]{1,0:T(8,128)(2,1)S(1)} %get-tuple-element.45.refs_6_), channel_id=1, source_target_pairs={{1,0},{0,1},{3,2},{2,3},{12,4},{13,5},{14,6},{15,7},{9,8},{8,9},{1... | collective-permute-start | bytes 49160 | tf_op jit(solution)/shard_map/ppermute | solution.py:551
  34.0 5.1 %collective-permute-start.8 = (bf16[3,64,128]{2,1,0:T(8,128)(2,1)S(1)}, bf16[3,64,128]{2,1,0:T(8,128)(2,1)S(1)}, u32[]{:S(2)}, u32[]{:S(2)}) collective-permute-start(bf16[3,64,128]{2,1,0:T(8,128)(2,1)S(1)} %pad_maximum_fusion.refs_0_), channel_id=1, source_target_pairs={{24,0},{25,1},{26,2},{27,3},{7,4},{6,5},{5,6},{4,7},{16,8},{17,9},... | collective-permute-start | bytes 147464 | tf_op jit(solution)/shard_map/ppermute | solution.py:551
  35.9 4.1 %collective-permute-start.7 = (bf16[3,64,128]{2,1,0:T(8,128)(2,1)S(1)}, bf16[3,64,128]{2,1,0:T(8,128)(2,1)S(1)}, u32[]{:S(2)}, u32[]{:S(2)}) collective-permute-start(bf16[3,64,128]{2,1,0:T(8,128)(2,1)S(1)} %pad_maximum_fusion.refs_0_), channel_id=1, source_target_pairs={{8,0},{9,1},{10,2},{11,3},{5,4},{4,5},{7,6},{6,7},{0,8},{1,9},{2,1... | collective-permute-start | bytes 147464 | tf_op jit(solution)/shard_map/ppermute | solution.py:551
  36.6 3.4 %collective-permute-start.9 = (bf16[3,64,128]{2,1,0:T(8,128)(2,1)S(1)}, bf16[3,64,128]{2,1,0:T(8,128)(2,1)S(1)}, u32[]{:S(2)}, u32[]{:S(2)}) collective-permute-start(bf16[3,64,128]{2,1,0:T(8,128)(2,1)S(1)} %pad_maximum_fusion.refs_0_), channel_id=1, source_target_pairs={{4,0},{0,4},{5,1},{1,5},{6,2},{2,6},{7,3},{3,7},{12,8},{8,12},{13,... | collective-permute-start | bytes 147464 | tf_op jit(solution)/shard_map/ppermute | solution.py:561
  39.0 1.2 %collective-permute-start.11 = (bf16[3,64,128]{2,1,0:T(8,128)(2,1)S(1)}, bf16[3,64,128]{2,1,0:T(8,128)(2,1)S(1)}, u32[]{:S(2)}, u32[]{:S(2)}) collective-permute-start(bf16[3,64,128]{2,1,0:T(8,128)(2,1)S(1)} %collective-permute-done.8.refs_2_), channel_id=1, source_target_pairs={{4,0},{0,4},{5,1},{1,5},{6,2},{2,6},{7,3},{3,7},{12,8},{8,12},{13,... | collective-permute-start | bytes 147464 | tf_op jit(solution)/shard_map/ppermute | solution.py:561
  40.0 1.2 %collective-permute-start.10 = (bf16[3,64,128]{2,1,0:T(8,128)(2,1)S(1)}, bf16[3,64,128]{2,1,0:T(8,128)(2,1)S(1)}, u32[]{:S(2)}, u32[]{:S(2)}) collective-permute-start(bf16[3,64,128]{2,1,0:T(8,128)(2,1)S(1)} %collective-permute-done.7.refs_1_), channel_id=1, source_target_pairs={{4,0},{0,4},{5,1},{1,5},{6,2},{2,6},{7,3},{3,7},{12,8},{8,12},{13,... | collective-permute-start | bytes 147464 | tf_op jit(solution)/shard_map/ppermute | solution.py:561

commit v7 on v6

--- a/solution.py
+++ b/solution.py
@@ -92,6 +92,12 @@
         self.brought = list(itertools.product(range(self.wide), range(self.depth)))
         self.mixed = self.depth == self.wide and self.sizes["gy"] % 2 == 0
         self.small = self.ndev <= 64 and len(self.sides) == 2
+        near = offsets_of(self.sizes["gz"])
+        self.column = list(near) if self.small else [0]
+        for step in [a + b for a in near for b in near] if self.small else []:
+            if all((step - known) % self.sizes["gz"] for known in self.column):
+                self.column.append(step)
+        self.known = self.depth if self.small else 1
         self.wrapped = [self.sizes[axis] == 2 for axis in AXES]
 
     def global_id(self, offset):
@@ -101,23 +107,24 @@
             place = place * count + lax.rem(lax.axis_index(axis) + (step + count), count)
         return place
 
-    def places(self, column_known=False):
+    def column_place(self, step):
+        return [(step - known) % self.sizes["gz"] == 0 for known in self.column].index(True)
+
+    def places(self):
         index = {axis: lax.axis_index(axis) for axis in AXES}
 
         def parity(axis):
             return lax.rem(index[axis], 2) if paired(self.sizes[axis]) else jnp.int32(0)
 
         turns = parity("gx"), parity("gz")
-        mixed = self.mixed and not column_known
-        core = lax.rem(index["gy"], 2) if mixed else jnp.int32(0)
+        core = lax.rem(index["gy"], 2) if self.mixed else jnp.int32(0)
         found = []
         for side in range(len(self.sides)):
-            x_first = core if side == 0 or not mixed else 1 - core
+            x_first = core if side == 0 or not self.mixed else 1 - core
             for second, first in self.brought:
-                row = first if column_known else matched(first, turns[1])
-                plain = matched(second, turns[0]) * self.depth + row
+                plain = matched(second, turns[0]) * self.depth + matched(first, turns[1])
                 crossed = matched(first, turns[0]) * self.depth + matched(second, turns[1])
-                tile = jnp.where(x_first == 1, crossed, plain) if mixed else plain
+                tile = jnp.where(x_first == 1, crossed, plain) if self.mixed else plain
                 found.append(tile * len(self.sides) + side)
         found += turns
         return [jnp.asarray(place, jnp.int32) for place in found]
@@ -181,8 +188,7 @@
     species = lax.broadcasted_iota(jnp.int32, (nbasis * nspec, plan.width), 0) % nspec
     shifts = [tile_shift(plan, tile) for tile in range(len(plan.tiles))]
     own, counted = [], []
-    for which in range(layer_ref.shape[0]):
-        up = offsets_of(plan.sizes["gz"])[which]
+    for which, up in enumerate(plan.column):
         held = block_of(0, 0, up)
         held = jnp.concatenate([held, held], axis=0).T[:slots]
         kind = held[:, 3:4]
@@ -190,8 +196,8 @@
         lane = lax.broadcasted_iota(jnp.int32, held.shape, 1)
         live = kind >= 0.0
         held = jnp.where((lane == 0) & ~live, -FAR, held)
-        if which == 0:
-            cols_ref[...] = jnp.where(lane == 3, live.astype(F32), held)
+        if which < plan.known:
+            cols_ref[which] = jnp.where(lane == 3, live.astype(F32), held)
         cols = [held[:, axis : axis + 1] for axis in range(3)]
         hot = []
         for tile in range(len(plan.tiles)):
@@ -216,8 +222,8 @@
                 elif n > 1:
                     before, now = now, double * now - before
                 packed = now.astype(BF16)
-                if which == 0:
-                    basis_ref[n, :, lanes] = packed
+                if which < plan.known:
+                    basis_ref[which, n, :, lanes] = packed
                 pair_ref[which, n, :slots, lanes] = packed
                 for k in range(3):
                     pair_ref[which, n, (k + 1) * slots : (k + 2) * slots, lanes] = units[k] * packed
@@ -253,11 +259,17 @@
     return 1.0 / (1.0 + jnp.exp(-value))
 
 
-def scatter(plan, places, far_refs, put):
+def scatter(plan, places, far_refs, put, up=0):
     for side in range(len(plan.sides)):
         for pair, (second, first) in enumerate(plan.brought):
-            block = far_refs[side * plan.wide + second][first]
-            put(plan.brought_place(places, side, pair), block)
+            column = far_refs[side * plan.wide + second]
+            if not plan.small:
+                put(plan.brought_place(places, side, pair), column[first])
+                continue
+            turn = places[len(plan.sides) * len(plan.brought)]
+            tile = matched(second, turn) * plan.depth + first
+            step = offsets_of(plan.sizes["gz"])[first] + up
+            put(tile * len(plan.sides) + side, column[plan.column_place(step)])
 
 
 def side_by_side(plan, blocks):
@@ -278,46 +290,51 @@
     return shift
 
 
-def gather_far(plan, places, far_refs, all_ref):
+def gather_far(plan, places, far_refs, all_ref, up=0):
     def put(place, block):
         start = pl.multiple_of(place * plan.slots, plan.slots)
         all_ref[pl.ds(start, plan.slots)] = block
 
-    scatter(plan, places, far_refs, put)
+    scatter(plan, places, far_refs, put, up)
 
 
 def second_kernel(plan, nrefs, places, *refs):
     far_refs, refs = refs[:nrefs], refs[nrefs:]
     (layer_ref, basis_ref, cols_ref, radial_ref, mix_ref), refs = refs[:5], refs[5:]
     (hidden_ref, out_ref, one_ref), refs = refs[:3], refs[3:]
-    adjoint_ref, features_ref, before_ref, own_ref, all_ref = refs
-    slots, nbasis = plan.slots, plan.nbasis
-    gather_far(plan, places, far_refs, all_ref)
-    summed = dot(basis_ref[...].reshape(nbasis * slots, plan.far), all_ref[...])
-    message = jnp.zeros((slots, summed.shape[1]), F32)
-    for n in range(nbasis):
-        message = message + summed[n * slots : (n + 1) * slots] * radial_ref[n : n + 1]
-    rounded = (MSG_SCALE * message).astype(BF16)
-    mixing = dot(rounded, mix_ref[...], NT)
+    adjoint_ref, features_ref, before_ref, own_ref, own_far_ref, all_ref = refs
+    slots, nbasis, known = plan.slots, plan.nbasis, plan.known
+    messages = []
+    for which in range(known):
+        target = own_far_ref if which == 0 else all_ref.at[which - 1]
+        gather_far(plan, places, far_refs, target, plan.column[which])
+        summed = dot(basis_ref[which].reshape(nbasis * slots, plan.far), target[...])
+        message = summed[:slots] * radial_ref[0:1]
+        for n in range(1, nbasis):
+            message = message + summed[n * slots : (n + 1) * slots] * radial_ref[n : n + 1]
+        messages.append((MSG_SCALE * message).astype(BF16))
+    mixing = dot(jnp.concatenate(messages, axis=0), mix_ref[...], NT)
     gate = sigmoid(mixing)
-    layer = layer_ref[0].astype(F32)
+    layer = layer_ref[:known].reshape(known * slots, -1).astype(F32)
     features = (layer + mixing * gate).astype(BF16)
-    features_ref[...] = features
+    features_ref[...] = features[:slots]
     before = dot(features, hidden_ref[...], NT)
+    before_ref[...] = before[:slots]
     open_hidden = sigmoid(before)
-    live = cols_ref[:, 3:4]
-    before_ref[...] = before
+    live = cols_ref[...].reshape(known * slots, 8)[:, 3:4]
     slope = out_ref[...] * (open_hidden * (1.0 + before * (1.0 - open_hidden))) * live
     from_hidden = dot(slope.astype(BF16), hidden_ref[...])
-    own_ref[...] = from_hidden + one_ref[...] * live
+    own_ref[...] = from_hidden[:slots] + one_ref[...] * live[:slots]
     back = from_hidden * (gate * (1.0 + mixing * (1.0 - gate)))
-    adjoint_ref[...] = dot(back.astype(BF16), mix_ref[...]).astype(BF16)
+    adjoint = dot(back.astype(BF16), mix_ref[...]).astype(BF16)
+    for which in range(known):
+        adjoint_ref[which] = adjoint[which * slots : (which + 1) * slots]
 
 
 def slope_kernel(plan, rows_ref, cols_ref, layer_ref, *refs):
     again_ref, apart_ref, slope_ref, radial_ref, turned_ref = refs
     again_ref[...] = layer_ref[...]
-    cols = [cols_ref[:, axis : axis + 1] for axis in range(3)]
+    cols = [cols_ref[0, :, axis : axis + 1] for axis in range(3)]
     for tile in range(len(plan.tiles)):
         lanes = slice(tile * plan.width, (tile + 1) * plan.width)
         parts = separations(plan, [rows_ref[tile, k : k + 1] for k in range(3)], cols)
@@ -348,22 +365,20 @@
             turned_ref[n, :, lanes] = scale * slope - square * factor
 
 
-def energy_kernel(plan, nrefs, places, *refs):
-    far_refs, refs = refs[:nrefs], refs[nrefs:]
-    (adjoint_ref, slope_ref, radial_ref, cols_ref, layer_ref), refs = refs[:5], refs[5:]
+def energy_kernel(plan, *refs):
+    (all_ref, adjoint_ref, slope_ref, radial_ref, cols_ref, layer_ref), refs = refs[:6], refs[6:]
     (before_ref, out_ref, one_ref, kept_ref), refs = refs[:4], refs[4:]
-    again_ref, pair_ref, energy_ref, features_ref, all_ref = refs
+    again_ref, pair_ref, energy_ref, features_ref = refs
     slots, nbasis = plan.slots, plan.nbasis
     again_ref[...] = adjoint_ref[...]
     features_ref[...] = kept_ref[...]
     before = before_ref[...]
-    live = jnp.where(lax.broadcasted_iota(jnp.int32, (slots, 8), 1) == 0, cols_ref[:, 3:4], 0.0)
+    live = jnp.where(lax.broadcasted_iota(jnp.int32, (slots, 8), 1) == 0, cols_ref[0, :, 3:4], 0.0)
     live_row = dot(jnp.ones((1, 8), BF16), live.astype(BF16), NT)
     energy = dot_exact(one_ref[...], layer_ref[0].astype(F32), NT)
     energy = energy + dot_exact(out_ref[...], before * sigmoid(before), NT)
     energy_ref[...] = energy * live_row
-    gather_far(plan, places, far_refs, all_ref)
-    adjoint = adjoint_ref[...].astype(F32) * MSG_SCALE
+    adjoint = adjoint_ref[0].astype(F32) * MSG_SCALE
     weighted = jnp.concatenate(
         [(adjoint * radial_ref[n : n + 1]).astype(BF16) for n in range(nbasis)], axis=0
     )
@@ -384,7 +399,7 @@
     out_ref, all_ref = refs
     slots, nbasis, nspec, width = plan.slots, plan.nbasis, plan.nspec, plan.width
     gather_far(plan, places, far_refs, all_ref)
-    summed = dot(basis_ref[...].reshape(nbasis * slots, plan.far), all_ref[...])
+    summed = dot(basis_ref[0].reshape(nbasis * slots, plan.far), all_ref[...])
     adjoint = jnp.zeros((slots, summed.shape[1]), F32)
     for n in range(nbasis):
         adjoint = adjoint + summed[n * slots : (n + 1) * slots] * radial_ref[n : n + 1]
@@ -522,9 +537,9 @@
     return got[0] if single else got
 
 
-def call(kernel, plan, far, operands, outs, scratch, flops, column_known=False, **options):
+def call(kernel, plan, far, operands, outs, scratch, flops, **options):
     def body(plan, *refs):
-        kernel(plan, len(far), plan.places(column_known), *refs)
+        kernel(plan, len(far), plan.places(), *refs)
 
     return simple_call(body, plan, [*far, *operands], outs, 0, scratch, flops, **options)
 
@@ -633,7 +648,6 @@
         embed, mix_one, radial_two, out_row, one_row, mix_two, read_hidden = weights
         far_sent = [everywhere(sent)] if plan.small else neighbours(plan, sent[0])
         pair_flops = 100 * slots * plan.far
-        known = plan.depth if plan.small else 1
         rows, basis, layer, vector, mixing, cols = call(
             first_kernel,
             plan,
@@ -641,14 +655,14 @@
             [table, embed, mix_one],
             [
                 ((len(plan.tiles), 4, plan.width), F32),
-                ((nbasis, slots, plan.far), BF16),
-                ((known, slots, channels), BF16),
+                ((plan.known, nbasis, slots, plan.far), BF16),
+                ((len(plan.column), slots, channels), BF16),
                 ((3 * slots, channels), F32),
                 ((slots, channels), F32),
-                ((slots, 8), F32),
+                ((plan.known, slots, 8), F32),
             ],
             [
-                ((known, nbasis, 4 * slots, plan.far), BF16),
+                ((len(plan.column), nbasis, 4 * slots, plan.far), BF16),
                 ((len(plan.tiles) * len(plan.sides), 4, 2 * slots), F32),
             ],
             pair_flops,
@@ -666,37 +680,37 @@
         else:
             far_layer = neighbours(plan, layer[0], again[0])
         far_scratch = ((plan.far, channels), BF16)
-        adjoint, kept, before, own_adjoint = call(
+        adjoint, kept, before, own_adjoint, own_far = call(
             second_kernel,
             plan,
             far_layer,
             [layer, basis, cols, radial_two, mix_two, read_hidden, out_row, one_row],
             [
-                ((slots, channels), BF16),
+                ((plan.known, slots, channels), BF16),
                 ((slots, channels), BF16),
                 ((slots, read_hidden.shape[0]), F32),
                 ((slots, channels), F32),
+                far_scratch,
             ],
-            [far_scratch],
+            [((max(plan.known - 1, 1), plan.far, channels), BF16)],
             pair_flops,
-            plan.small,
         )
-        again, pair, energy, features = call(
+        again, pair, energy, features = simple_call(
             energy_kernel,
             plan,
-            far_layer,
-            [adjoint, slope, radial_two, cols, layer, before, out_row, one_row, kept],
+            [own_far, adjoint, slope, radial_two, cols, layer, before, out_row, one_row, kept],
             [
-                ((slots, channels), BF16),
+                (adjoint.shape, BF16),
                 ((slots, plan.far), F32),
                 ((1, slots), F32),
                 ((slots, channels), BF16),
             ],
-            [far_scratch],
-            pair_flops,
-            plan.small,
+            flops=pair_flops,
         )
-        far_adjoint = neighbours(plan, adjoint, again)
+        if plan.small:
+            far_adjoint = from_columns(plan, adjoint, False, again)
+        else:
+            far_adjoint = neighbours(plan, adjoint[0], again[0])
         pulls = call(
             force_kernel,
             plan,

time: 54.5 us -> 49.4 us (0.906)
  waiting for transfers between devices: 10.6 us -> 6.41 us
  Pallas kernels: 11.1 us -> 12.4 us
  starting transfers between devices: 6.4 us -> 5.18 us
  blocking collectives: 24.8 us -> 23.9 us
    ppermute x6 -> x4, waiting for transfers between devices: 8.48 us -> 4.26 us  [brought(): got.append(lax.ppermute(block, AXES, pairs))]
    pallas_call x7, Pallas kernels: 11.1 us -> 12.4 us  [simple_call(): pl.pallas_call(body, out_shape=shapes, in_specs=[SMEM_SPEC] * scalars + [...]
    ppermute x6 -> x4, starting transfers between devices: 5.81 us -> 4.76 us  [brought(): got.append(lax.ppermute(block, AXES, pairs))]
    all_to_all x2, blocking collectives: 24.8 us -> 23.9 us  [everywhere(): return lax.all_to_all(copies, AXES, 0, 0, tiled=True)]
  transfers between devices with their start and end apart: 12 -> 10, of which waited for: 8 -> 8; matrix products, arithmetic and copies ran while one was open for 0% -> 0% of each run, Pallas kernels for 4% -> 5%
where the time goes in v7:
time: 49.4 us; the launch traced here: 49.2 us
  blocking collectives  23.9 us (48%)
  Pallas kernels  12.4 us (25%)
  waiting for transfers between devices  6.41 us (13%)
  starting transfers between devices  5.18 us (10%)
  between operations  1.33 us (3%)
    all_to_all x2, blocking collectives, everywhere(): return lax.all_to_all(copies, AXES, 0, 0, tiled=True)  23.9 us
    pallas_call x7, Pallas kernels, simple_call(): pl.pallas_call(body, out_shape=shapes, in_specs=[SMEM_SPEC] * scalars + [...  12.4 us
    ppermute x4, starting transfers between devices, brought(): got.append(lax.ppermute(block, AXES, pairs))  4.76 us
    ppermute x4, waiting for transfers between devices, brought(): got.append(lax.ppermute(block, AXES, pairs))  4.26 us
    ppermute x6, waiting for transfers between devices, along(): lax.ppermute(block, axis, [(source, i) for i, source in enumerate(sources)])  2.15 us
  transfers between devices with their start and end apart: 10, of which 8 were waited for; matrix products, arithmetic and copies ran while one was open for 0% of the time, Pallas kernels for 5%

profile of v7, /device:TPU:0, one launch (start us, length us, event | category | flops | bytes accessed | tf_op | source)
XLA Modules:
  0.0 49.2 jit_solution(11552105462603266780)
XLA Ops:
  1.3 1.0 %shard_map.130 = (f32[32,4,128]{2,1,0:T(4,128)S(1)}, bf16[2,32,128]{2,1,0:T(8,128)(2,1)S(1)}, bf16[8,128]{1,0:T(8,128)(2,1)S(1)}, bf16[128,256]{1,0:T(8,128)(2,1...) custom-call(s32[1]{0:T(128)} %bitcast.12.refs_0_, ...), custom_call_target="tpu_custom_call" | custom-call | flops 1048576 | bytes 1048576 | tf_op jit(solution)/shard_map/pallas_call | solution.py:525
  2.3 14.6 %all_to_all.10.refs_0_ = f32[32,4,128]{2,1,0:T(4,128)S(1)} all-to-all(f32[32,4,128]{2,1,0:T(4,128)S(1)} %get-tuple-element.32), channel_id=1, replica_groups=mesh['gx'=4,'gy'=2,'gz'=4] {'gx','gy','gz'}, dimensions={0} | all-to-all | bytes 131072 | tf_op jit(solution)/shard_map/all_to_all | solution.py:595
  16.9 5.2 %shard_map.131 = (f32[9,4,128]{2,1,0:T(4,128)S(1)}, bf16[3,4,64,1152]{3,2,1,0:T(8,128)(2,1)S(1)}, bf16[4,64,128]{2,1,0:T(8,128)(2,1)S(1)}, f32[192,128]{1,0:T(8,...) custom-call(f32[32,4,128]{2,1,0:T(4,128)S(1)} %all_to_all.10.refs_0_, ...), custom_call_target="tpu_custom_call" | custom-call | flops 7372800 | bytes 1048576 | tf_op jit(solution)/shard_map/pallas_call | solution.py:525
  22.1 0.7 %collective-permute-start.1 = (bf16[4,64,128]{2,1,0:T(8,128)(2,1)S(1)}, bf16[4,64,128]{2,1,0:T(8,128)(2,1)S(1)}, u32[]{:S(2)}, u32[]{:S(2)}) collective-permute-start(bf16[4,64,128]{2,1,0:T(8,128)(2,1)S(1)} %get-tuple-element.38.refs_2_.refs_6_.refs_5_), channel_id=1, source_target_pairs={{24,0},{25,1},{26,2},{27,3},{28,4},{29,5},{30,6},{31,7},{16,8},{17... | collective-permute-start | bytes 196616 | tf_op jit(solution)/shard_map/ppermute | solution.py:566
  22.8 1.5 %collective-permute-start = (bf16[4,64,128]{2,1,0:T(8,128)(2,1)S(1)}, bf16[4,64,128]{2,1,0:T(8,128)(2,1)S(1)}, u32[]{:S(2)}, u32[]{:S(2)}) collective-permute-start(bf16[4,64,128]{2,1,0:T(8,128)(2,1)S(1)} %get-tuple-element.38.refs_2_.refs_6_.refs_5_), channel_id=1, source_target_pairs={{8,0},{9,1},{10,2},{11,3},{12,4},{13,5},{14,6},{15,7},{0,8},{1,9},... | collective-permute-start | bytes 196616 | tf_op jit(solution)/shard_map/ppermute | solution.py:566
  24.3 1.2 %shard_map.132 = (bf16[4,64,128]{2,1,0:T(8,128)(2,1)S(1)}, f32[3,64,1152]{2,1,0:T(8,128)S(1)}, f32[4,64,1152]{2,1,0:T(8,128)S(1)}, f32[4,64,1152]{2,1,0:T(8,128)S(1)}, f32[4,64,1152]{2,1,0:T(8,128)S(1)}) custom-call(f32[9,4,128]{2,1,0:T(4,128)S(1)} %get-tuple-element.36.refs_0_.refs_9_, f32[3,64,8]{2,1,0:T(8,128)S(1)} %get-tuple-element.37.refs_1_.refs_8_.refs_4_, ...), custom_call_target="tpu_custom_call" | custom-call | flops 7372800 | bytes 1048576 | tf_op jit(solution)/shard_map/pallas_call | solution.py:525
  25.5 0.1 collective-permute-start.2
  25.6 1.8 %collective-permute-done.1.refs_2_ = bf16[4,64,128]{2,1,0:T(8,128)(2,1)S(1)} collective-permute-done((bf16[4,64,128]{2,1,0:T(8,128)(2,1)S(1)}, bf16[4,64,128]{2,1,0:T(8,128)(2,1)S(1)}, u32[]{:S(2)}, u32[]{:S(2)}) %collective-permute-start.1) | collective-permute-done | bytes 65568 | tf_op jit(solution)/shard_map/ppermute | solution.py:566
  27.3 0.0 collective-permute-start.4
  27.3 0.2 collective-permute-done.refs_1_
  27.5 0.3 collective-permute-start.3
  27.9 0.0 collective-permute-done.2.refs_3_
  27.9 0.7 %collective-permute-done.4.refs_5_ = bf16[4,64,128]{2,1,0:T(8,128)(2,1)S(1)} collective-permute-done((bf16[4,64,128]{2,1,0:T(8,128)(2,1)S(1)}, bf16[4,64,128]{2,1,0:T(8,128)(2,1)S(1)}, u32[]{:S(2)}, u32[]{:S(2)}) %collective-permute-start.4) | collective-permute-done | bytes 65568 | tf_op jit(solution)/shard_map/ppermute | solution.py:576
  28.6 0.2 collective-permute-done.3.refs_4_
  28.8 1.2 %shard_map.133 = (bf16[3,64,128]{2,1,0:T(8,128)(2,1)S(1)}, bf16[64,128]{1,0:T(8,128)(2,1)S(1)}, f32[64,16]{1,0:T(8,128)S(1)}, f32[64,128]{1,0:T(8,128)S(1)}, bf16[1152,128]{1,0:T(8,128)(2,1)S(1)}) custom-call(bf16[4,64,128]{2,1,0:T(8,128)(2,1)S(1)} %get-tuple-element.39.refs_0_, bf16[4,64,128]{2,1,0:T(8,128)(2,1)S(1)} %collective-permute-done.refs_1_, ...), custom_call_target="tpu_custom_call" | custom-call | flops 7372800 | bytes 1048576 | tf_op jit(solution)/shard_map/pallas_call | solution.py:525
  30.0 1.8 %collective-permute-start.6 = (bf16[3,64,128]{2,1,0:T(8,128)(2,1)S(1)}, bf16[3,64,128]{2,1,0:T(8,128)(2,1)S(1)}, u32[]{:S(2)}, u32[]{:S(2)}) collective-permute-start(bf16[3,64,128]{2,1,0:T(8,128)(2,1)S(1)} %get-tuple-element.47.refs_1_), channel_id=1, source_target_pairs={{24,0},{25,1},{26,2},{27,3},{28,4},{29,5},{30,6},{31,7},{16,8},{17... | collective-permute-start | bytes 147464 | tf_op jit(solution)/shard_map/ppermute | solution.py:566
  31.8 0.7 %collective-permute-start.5 = (bf16[3,64,128]{2,1,0:T(8,128)(2,1)S(1)}, bf16[3,64,128]{2,1,0:T(8,128)(2,1)S(1)}, u32[]{:S(2)}, u32[]{:S(2)}) collective-permute-start(bf16[3,64,128]{2,1,0:T(8,128)(2,1)S(1)} %get-tuple-element.47.refs_1_), channel_id=1, source_target_pairs={{8,0},{9,1},{10,2},{11,3},{12,4},{13,5},{14,6},{15,7},{0,8},{1,9},... | collective-permute-start | bytes 147464 | tf_op jit(solution)/shard_map/ppermute | solution.py:566
  32.5 1.0 %shard_map.134 = (bf16[3,64,128]{2,1,0:T(8,128)(2,1)S(1)}, f32[64,1152]{1,0:T(8,128)S(1)}, f32[1,64]{1,0:T(1,128)}, bf16[64,128]{1,0:T(8,128)(2,1)}) custom-call(bf16[1152,128]{1,0:T(8,128)(2,1)S(1)} %get-tuple-element.46.refs_0_, bf16[3,64,128]{2,1,0:T(8,128)(2,1)S(1)} %get-tuple-element.47.refs_1_, f32[4,64,1152]{2,1,0:T(8,128)S(1)} %get-tuple-element.48.refs_2_.refs_11_, ...), custom_call_target="tpu_custom_call" | custom-call | flops 7372800 | bytes 1048576 | tf_op jit(solution)/shard_map/pallas_call | solution.py:525
  33.5 0.0 collective-permute-start.7
  33.5 1.8 %collective-permute-done.6.refs_2_ = bf16[3,64,128]{2,1,0:T(8,128)(2,1)S(1)} collective-permute-done((bf16[3,64,128]{2,1,0:T(8,128)(2,1)S(1)}, bf16[3,64,128]{2,1,0:T(8,128)(2,1)S(1)}, u32[]{:S(2)}, u32[]{:S(2)}) %collective-permute-start.6) | collective-permute-done | bytes 49184 | tf_op jit(solution)/shard_map/ppermute | solution.py:566
  35.3 0.0 collective-permute-start.9
  35.3 0.5 %collective-permute-done.5.refs_1_ = bf16[3,64,128]{2,1,0:T(8,128)(2,1)S(1)} collective-permute-done((bf16[3,64,128]{2,1,0:T(8,128)(2,1)S(1)}, bf16[3,64,128]{2,1,0:T(8,128)(2,1)S(1)}, u32[]{:S(2)}, u32[]{:S(2)}) %collective-permute-start.5) | collective-permute-done | bytes 49184 | tf_op jit(solution)/shard_map/ppermute | solution.py:566
  35.9 0.0 collective-permute-start.8
  35.9 0.0 collective-permute-done.7.refs_3_
  35.9 0.7 %collective-permute-done.9.refs_5_ = bf16[3,64,128]{2,1,0:T(8,128)(2,1)S(1)} collective-permute-done((bf16[3,64,128]{2,1,0:T(8,128)(2,1)S(1)}, bf16[3,64,128]{2,1,0:T(8,128)(2,1)S(1)}, u32[]{:S(2)}, u32[]{:S(2)}) %collective-permute-start.9) | collective-permute-done | bytes 49184 | tf_op jit(solution)/shard_map/ppermute | solution.py:576
  36.6 0.5 %collective-permute-done.8.refs_4_ = bf16[3,64,128]{2,1,0:T(8,128)(2,1)S(1)} collective-permute-done((bf16[3,64,128]{2,1,0:T(8,128)(2,1)S(1)}, bf16[3,64,128]{2,1,0:T(8,128)(2,1)S(1)}, u32[]{:S(2)}, u32[]{:S(2)}) %collective-permute-start.8) | collective-permute-done | bytes 49184 | tf_op jit(solution)/shard_map/ppermute | solution.py:576
  37.1 2.1 %shard_map.135 = f32[32,4,128]{2,1,0:T(4,128)S(1)} custom-call(bf16[3,64,128]{2,1,0:T(8,128)(2,1)S(1)} %get-tuple-element.51.refs_0_, bf16[3,64,128]{2,1,0:T(8,128)(2,1)S(1)} %collective-permute-done.5.refs_1_, bf16[3,64,128]{2,1,0:T(8,128)(2,1)S(1)} %collective-permute-done.6.refs_2_, bf16[3,64,128]{2,1,0:T(8,128)(2,1)S(1)} %collective-permute-done.7.refs_3_, ...), custom_call_target="tpu_custom_call" | custom-call | flops 7372800 | bytes 1048576 | tf_op jit(solution)/shard_map/pallas_call | solution.py:525
  39.2 9.3 %all_to_all.11.refs_0_ = f32[32,4,128]{2,1,0:T(4,128)S(1)} all-to-all(f32[32,4,128]{2,1,0:T(4,128)S(1)} %shard_map.135), channel_id=1, replica_groups=mesh['gx'=4,'gy'=2,'gz'=4] {'gx','gy','gz'}, dimensions={0} | all-to-all | bytes 131072 | tf_op jit(solution)/shard_map/all_to_all | solution.py:595
  48.5 0.7 %shard_map.136 = f32[3,1,64]{2,1,0:T(1,128)} custom-call(f32[32,4,128]{2,1,0:T(4,128)S(1)} %all_to_all.11.refs_0_), custom_call_target="tpu_custom_call" | custom-call | flops 1048576 | bytes 1048576 | tf_op jit(solution)/shard_map/pallas_call | solution.py:525
Async XLA Ops:
  22.1 5.3 %collective-permute-start.1 = (bf16[4,64,128]{2,1,0:T(8,128)(2,1)S(1)}, bf16[4,64,128]{2,1,0:T(8,128)(2,1)S(1)}, u32[]{:S(2)}, u32[]{:S(2)}) collective-permute-start(bf16[4,64,128]{2,1,0:T(8,128)(2,1)S(1)} %get-tuple-element.38.refs_2_.refs_6_.refs_5_), channel_id=1, source_target_pairs={{24,0},{25,1},{26,2},{27,3},{28,4},{29,5},{30,6},{31,7},{16,8},{17... | collective-permute-start | bytes 196616 | tf_op jit(solution)/shard_map/ppermute | solution.py:566
  22.8 4.8 %collective-permute-start = (bf16[4,64,128]{2,1,0:T(8,128)(2,1)S(1)}, bf16[4,64,128]{2,1,0:T(8,128)(2,1)S(1)}, u32[]{:S(2)}, u32[]{:S(2)}) collective-permute-start(bf16[4,64,128]{2,1,0:T(8,128)(2,1)S(1)} %get-tuple-element.38.refs_2_.refs_6_.refs_5_), channel_id=1, source_target_pairs={{8,0},{9,1},{10,2},{11,3},{12,4},{13,5},{14,6},{15,7},{0,8},{1,9},... | collective-permute-start | bytes 196616 | tf_op jit(solution)/shard_map/ppermute | solution.py:566
  25.5 2.4 %collective-permute-start.2 = (bf16[4,64,128]{2,1,0:T(8,128)(2,1)S(1)}, bf16[4,64,128]{2,1,0:T(8,128)(2,1)S(1)}, u32[]{:S(2)}, u32[]{:S(2)}) collective-permute-start(bf16[4,64,128]{2,1,0:T(8,128)(2,1)S(1)} %get-tuple-element.39.refs_0_), channel_id=1, source_target_pairs={{4,0},{0,4},{5,1},{1,5},{6,2},{2,6},{7,3},{3,7},{12,8},{8,12},{13,... | collective-permute-start | bytes 196616 | tf_op jit(solution)/shard_map/ppermute | solution.py:576
  27.3 1.3 %collective-permute-start.4 = (bf16[4,64,128]{2,1,0:T(8,128)(2,1)S(1)}, bf16[4,64,128]{2,1,0:T(8,128)(2,1)S(1)}, u32[]{:S(2)}, u32[]{:S(2)}) collective-permute-start(bf16[4,64,128]{2,1,0:T(8,128)(2,1)S(1)} %collective-permute-done.1.refs_2_), channel_id=1, source_target_pairs={{4,0},{0,4},{5,1},{1,5},{6,2},{2,6},{7,3},{3,7},{12,8},{8,12},{13,... | collective-permute-start | bytes 196616 | tf_op jit(solution)/shard_map/ppermute | solution.py:576
  27.5 1.3 %collective-permute-start.3 = (bf16[4,64,128]{2,1,0:T(8,128)(2,1)S(1)}, bf16[4,64,128]{2,1,0:T(8,128)(2,1)S(1)}, u32[]{:S(2)}, u32[]{:S(2)}) collective-permute-start(bf16[4,64,128]{2,1,0:T(8,128)(2,1)S(1)} %collective-permute-done.refs_1_), channel_id=1, source_target_pairs={{4,0},{0,4},{5,1},{1,5},{6,2},{2,6},{7,3},{3,7},{12,8},{8,12},{13,... | collective-permute-start | bytes 196616 | tf_op jit(solution)/shard_map/ppermute | solution.py:576
  30.0 5.4 %collective-permute-start.6 = (bf16[3,64,128]{2,1,0:T(8,128)(2,1)S(1)}, bf16[3,64,128]{2,1,0:T(8,128)(2,1)S(1)}, u32[]{:S(2)}, u32[]{:S(2)}) collective-permute-start(bf16[3,64,128]{2,1,0:T(8,128)(2,1)S(1)} %get-tuple-element.47.refs_1_), channel_id=1, source_target_pairs={{24,0},{25,1},{26,2},{27,3},{28,4},{29,5},{30,6},{31,7},{16,8},{17... | collective-permute-start | bytes 147464 | tf_op jit(solution)/shard_map/ppermute | solution.py:566
  31.8 4.1 %collective-permute-start.5 = (bf16[3,64,128]{2,1,0:T(8,128)(2,1)S(1)}, bf16[3,64,128]{2,1,0:T(8,128)(2,1)S(1)}, u32[]{:S(2)}, u32[]{:S(2)}) collective-permute-start(bf16[3,64,128]{2,1,0:T(8,128)(2,1)S(1)} %get-tuple-element.47.refs_1_), channel_id=1, source_target_pairs={{8,0},{9,1},{10,2},{11,3},{12,4},{13,5},{14,6},{15,7},{0,8},{1,9},... | collective-permute-start | bytes 147464 | tf_op jit(solution)/shard_map/ppermute | solution.py:566
  33.5 2.3 %collective-permute-start.7 = (bf16[3,64,128]{2,1,0:T(8,128)(2,1)S(1)}, bf16[3,64,128]{2,1,0:T(8,128)(2,1)S(1)}, u32[]{:S(2)}, u32[]{:S(2)}) collective-permute-start(bf16[3,64,128]{2,1,0:T(8,128)(2,1)S(1)} %get-tuple-element.51.refs_0_), channel_id=1, source_target_pairs={{4,0},{0,4},{5,1},{1,5},{6,2},{2,6},{7,3},{3,7},{12,8},{8,12},{13,... | collective-permute-start | bytes 147464 | tf_op jit(solution)/shard_map/ppermute | solution.py:576
  35.3 1.2 %collective-permute-start.9 = (bf16[3,64,128]{2,1,0:T(8,128)(2,1)S(1)}, bf16[3,64,128]{2,1,0:T(8,128)(2,1)S(1)}, u32[]{:S(2)}, u32[]{:S(2)}) collective-permute-start(bf16[3,64,128]{2,1,0:T(8,128)(2,1)S(1)} %collective-permute-done.6.refs_2_), channel_id=1, source_target_pairs={{4,0},{0,4},{5,1},{1,5},{6,2},{2,6},{7,3},{3,7},{12,8},{8,12},{13,... | collective-permute-start | bytes 147464 | tf_op jit(solution)/shard_map/ppermute | solution.py:576
  35.9 1.2 %collective-permute-start.8 = (bf16[3,64,128]{2,1,0:T(8,128)(2,1)S(1)}, bf16[3,64,128]{2,1,0:T(8,128)(2,1)S(1)}, u32[]{:S(2)}, u32[]{:S(2)}) collective-permute-start(bf16[3,64,128]{2,1,0:T(8,128)(2,1)S(1)} %collective-permute-done.5.refs_1_), channel_id=1, source_target_pairs={{4,0},{0,4},{5,1},{1,5},{6,2},{2,6},{7,3},{3,7},{12,8},{8,12},{13,... | collective-permute-start | bytes 147464 | tf_op jit(solution)/shard_map/ppermute | solution.py:576

commit v8 on v7

--- a/solution.py
+++ b/solution.py
@@ -18,20 +18,18 @@
 F32 = jnp.float32
 BF16 = jnp.bfloat16
 COS_TERMS = (
-    0.9999999997799041,
-    -4.934802137078749,
-    4.058709159554242,
-    -1.335212003029471,
-    0.23493731372678894,
-    -0.024396324214549327,
+    0.9999999532476085,
+    -4.934792830619644,
+    4.058411352862619,
+    -1.3318765680811142,
+    0.2196896110983216,
 )
 SIN_TERMS = (
-    3.14159265353629,
-    -5.167712764624453,
-    2.550163318944743,
-    -0.5992521977996564,
-    0.08205040170151112,
-    -0.007028386239784362,
+    3.1415926401307073,
+    -5.167710083507891,
+    2.550077523214631,
+    -0.5982912856208596,
+    0.07765766030668693,
 )
 VMEM_LIMIT = 24 * 1024 * 1024
 FETCH_LIMIT = 60 * 1024 * 1024
@@ -99,6 +97,9 @@
                 self.column.append(step)
         self.known = self.depth if self.small else 1
         self.wrapped = [self.sizes[axis] == 2 for axis in AXES]
+        self.plain = [k for k in range(3) if not self.wrapped[k]]
+        self.folded = [k for k in range(3) if self.wrapped[k]]
+        self.kinds = 2 + len(self.folded)
 
     def global_id(self, offset):
         place = 0
@@ -142,18 +143,22 @@
         return (ox, self.sides[side], oz)
 
 
-def separations(plan, rows, cols):
+def scaled(terms, factor):
+    return [factor * term for term in terms]
+
+
+def separations(plan, rows, cols, side=CELL_SIDE):
     parts = []
     for axis in range(3):
         diff = rows[axis] - cols[axis]
         if plan.wrapped[axis]:
-            diff = jnp.where(diff > CELL_SIDE, diff - 2.0 * CELL_SIDE, diff)
+            diff = jnp.where(diff > side, diff - 2.0 * side, diff)
         parts.append(diff)
     return parts
 
 
-def distance(plan, parts, tile):
-    dist_sq = parts[0] * parts[0] + parts[1] * parts[1] + parts[2] * parts[2] + SOFTEN
+def distance(plan, parts, tile, soften=SOFTEN):
+    dist_sq = parts[0] * parts[0] + parts[1] * parts[1] + parts[2] * parts[2] + soften
     if tile == 0:
         row = lax.broadcasted_iota(jnp.int32, dist_sq.shape, 0)
         col = lax.broadcasted_iota(jnp.int32, dist_sq.shape, 1)
@@ -169,7 +174,7 @@
 
 def first_kernel(plan, nrefs, places, *refs):
     far_refs, refs = refs[:nrefs], refs[nrefs:]
-    (table_ref, embed_ref, mix_ref), refs = refs[:3], refs[3:]
+    (table_ref, wide_ref, embed_ref, mix_ref), refs = refs[:4], refs[4:]
     rows_ref, basis_ref, layer_ref, vector_ref, mixing_ref, cols_ref, pair_ref, block_ref = refs
     slots, nbasis, nspec = plan.slots, plan.nbasis, plan.nspec
 
@@ -187,7 +192,7 @@
 
     species = lax.broadcasted_iota(jnp.int32, (nbasis * nspec, plan.width), 0) % nspec
     shifts = [tile_shift(plan, tile) for tile in range(len(plan.tiles))]
-    own, counted = [], []
+    own, counted, places_of = [], [], []
     for which, up in enumerate(plan.column):
         held = block_of(0, 0, up)
         held = jnp.concatenate([held, held], axis=0).T[:slots]
@@ -198,23 +203,31 @@
         held = jnp.where((lane == 0) & ~live, -FAR, held)
         if which < plan.known:
             cols_ref[which] = jnp.where(lane == 3, live.astype(F32), held)
-        cols = [held[:, axis : axis + 1] for axis in range(3)]
+        cols = [held[:, axis : axis + 1] * (1.0 / CELL_SIDE) for axis in range(3)]
+        places_of.append(cols)
         hot = []
         for tile in range(len(plan.tiles)):
             blocks = [block_of(tile, side, up) for side in range(len(plan.sides))]
             placed = side_by_side(plan, blocks) + shifts[tile]
             if which == 0:
                 rows_ref[tile] = placed
-            rows = [placed[k : k + 1] for k in range(4)]
-            hot.append((rows[3].astype(jnp.int32) == species).astype(F32).astype(BF16))
-            parts = separations(plan, rows, cols)
-            dist_sq, inverse = distance(plan, parts, tile)
-            sine, cosine = waves(dist_sq, inverse)
-            fade = jnp.maximum(1.0 - dist_sq * (1.0 / CUT_SQUARE), 0.0)
-            radial = fade * fade * inverse
-            units = [(part * (inverse * ROOT_THREE)).astype(BF16) for part in parts]
-            before, now = None, sine * radial
-            double = 2.0 * cosine
+            is_kind = placed[3:4].astype(jnp.int32) == species
+            placed = placed * (1.0 / CELL_SIDE)
+            high = placed.astype(BF16).astype(F32)
+            low = placed - high
+            columns = [jnp.where(is_kind, 1.0, 0.0)]
+            for k in plan.plain:
+                columns += [jnp.where(is_kind, part[k : k + 1], 0.0) for part in (high, low)]
+            hot.append(jnp.concatenate([column.astype(BF16) for column in columns], axis=0))
+            parts = separations(plan, [placed[k : k + 1] for k in range(3)], cols, 1.0)
+            dist_sq, inverse = distance(plan, parts, tile, SOFTEN / CUT_SQUARE)
+            turn = jnp.minimum(dist_sq * inverse - 0.5, 0.5)
+            square = turn * turn
+            double = turn * poly(scaled(SIN_TERMS, -2.0), square)
+            fade = jnp.maximum(1.0 - dist_sq, 0.0)
+            before, now = None, poly(scaled(COS_TERMS, 1.0 / CELL_SIDE), square) * (fade * fade * inverse)
+            scale = inverse * ROOT_THREE
+            units = [scale.astype(BF16)] + [(scale * parts[k]).astype(BF16) for k in plan.folded]
             lanes = slice(tile * plan.width, (tile + 1) * plan.width)
             for n in range(nbasis):
                 if n == 1:
@@ -225,23 +238,31 @@
                 if which < plan.known:
                     basis_ref[which, n, :, lanes] = packed
                 pair_ref[which, n, :slots, lanes] = packed
-                for k in range(3):
-                    pair_ref[which, n, (k + 1) * slots : (k + 2) * slots, lanes] = units[k] * packed
+                for m, unit in enumerate(units):
+                    pair_ref[which, n, (m + 1) * slots : (m + 2) * slots, lanes] = unit * packed
         hot = jnp.concatenate(hot, axis=1)
-        gathered = dot(pair_ref[which].reshape(nbasis * 4 * slots, plan.far), hot, NT)
-        gathered = gathered.reshape(nbasis, 4 * slots, nbasis * nspec)
-        group = lax.broadcasted_iota(jnp.int32, gathered.shape[1:], 1) // nspec
+        gathered = dot(pair_ref[which].reshape(nbasis * plan.kinds * slots, plan.far), hot, NT)
+        gathered = gathered.reshape(nbasis, plan.kinds * slots, hot.shape[0])
+        group = lax.broadcasted_iota(jnp.int32, gathered.shape[1:], 1) % (nbasis * nspec) // nspec
         total = gathered[0]
         for n in range(1, nbasis):
             total = jnp.where(group == n, gathered[n], total)
         counted.append(total)
-    scalar = split_dot(jnp.concatenate([total[:slots] for total in counted], axis=0), table_ref[0])
-    scalar = MSG_SCALE * scalar
+    scalar = jnp.concatenate([total[:slots, : nbasis * nspec] for total in counted], axis=0)
+    scalar = MSG_SCALE * split_dot(scalar, table_ref[0])
+    moved = jnp.concatenate([total[slots : 2 * slots] for total in counted], axis=0)
+    moved = MSG_SCALE * split_dot(moved, wide_ref[...])
+    channels = layer_ref.shape[2]
     norm = None
     for k in range(3):
-        rows = slice((k + 1) * slots, (k + 2) * slots)
-        vector = split_dot(jnp.concatenate([total[rows] for total in counted], axis=0), table_ref[1])
-        vector = MSG_SCALE * vector
+        if k in plan.plain:
+            start = (plan.plain.index(k) + 1) * channels
+            place = jnp.concatenate([cols[k] for cols in places_of], axis=0)
+            vector = moved[:, start : start + channels] - place * moved[:, :channels]
+        else:
+            start = (plan.folded.index(k) + 2) * slots
+            vector = [total[start : start + slots, : nbasis * nspec] for total in counted]
+            vector = MSG_SCALE * split_dot(jnp.concatenate(vector, axis=0), table_ref[1])
         vector_ref[k * slots : (k + 1) * slots] = vector[:slots]
         norm = vector * vector if k == 0 else norm + vector * vector
     invariants = jnp.concatenate([scalar.astype(BF16), norm.astype(BF16)], axis=1)
@@ -475,7 +496,7 @@
 
 
 def prepare_kernel(plan, counts_ref, *refs):
-    fetched, sent_ref, table_ref, refs = refs[:10], refs[10], refs[11], refs[12:]
+    fetched, (sent_ref, table_ref, wide_ref), refs = refs[:10], refs[10:13], refs[13:]
     kept, (place_ref, kind_ref, radial_ref, sems) = refs[:7], refs[7:]
     copies = begin(zip(fetched, (place_ref, kind_ref, radial_ref, *kept)), sems)
     for copy in copies[:2]:
@@ -498,6 +519,11 @@
         for n in range(plan.nbasis):
             weighted = radial_ref[g, n : n + 1] * embed
             table_ref[g, n * nspec : (n + 1) * nspec] = weighted.astype(BF16)
+    wide_ref[...] = jnp.zeros_like(wide_ref)
+    count, channels = table_ref.shape[1:]
+    for m in range(1 + 2 * len(plan.plain)):
+        start = (m + 1) // 2 * channels
+        wide_ref[m * count : (m + 1) * count, start : start + channels] = table_ref[1]
 
 
 def sum_kernel(plan, parts_ref, force_ref):
@@ -631,13 +657,14 @@
         plan = Plan(mesh, slots, nbasis, nspec)
         given = [positions[0, 0, 0].reshape(3, 1, slots), species.reshape(1, slots), radial_one]
         weights = [embed, mix_one, radial_two, read_out[None], read_one[None], mix_two, read_hidden]
-        sent, table, *weights = simple_call(
+        sent, table, wide, *weights = simple_call(
             prepare_kernel,
             plan,
             [counts.reshape(1), *given, *weights],
             [
                 ((plan.ndev if plan.small else 1, 4, 2 * slots), F32),
                 ((2, nbasis * nspec, channels), BF16),
+                (((1 + 2 * len(plan.plain)) * nbasis * nspec, (1 + len(plan.plain)) * channels), BF16),
             ]
             + [(weight.shape, weight.dtype) for weight in weights],
             1,
@@ -652,7 +679,7 @@
             first_kernel,
             plan,
             far_sent,
-            [table, embed, mix_one],
+            [table, wide, embed, mix_one],
             [
                 ((len(plan.tiles), 4, plan.width), F32),
                 ((plan.known, nbasis, slots, plan.far), BF16),
@@ -662,7 +689,7 @@
                 ((plan.known, slots, 8), F32),
             ],
             [
-                ((len(plan.column), nbasis, 4 * slots, plan.far), BF16),
+                ((len(plan.column), nbasis, plan.kinds * slots, plan.far), BF16),
                 ((len(plan.tiles) * len(plan.sides), 4, 2 * slots), F32),
             ],
             pair_flops,

time: 49.4 us -> 48.7 us (0.986)
  Pallas kernels: 12.4 us -> 11.6 us
    pallas_call x7, Pallas kernels: 12.4 us -> 11.6 us  [simple_call(): pl.pallas_call(body, out_shape=shapes, in_specs=[SMEM_SPEC] * scalars + [...]
where the time goes in v8:
time: 48.7 us; the launch traced here: 48.5 us
  blocking collectives  23.9 us (49%)
  Pallas kernels  11.6 us (24%)
  waiting for transfers between devices  6.47 us (13%)
  starting transfers between devices  5.16 us (11%)
  between operations  1.33 us (3%)
    all_to_all x2, blocking collectives, everywhere(): return lax.all_to_all(copies, AXES, 0, 0, tiled=True)  23.9 us
    pallas_call x7, Pallas kernels, simple_call(): pl.pallas_call(body, out_shape=shapes, in_specs=[SMEM_SPEC] * scalars + [...  11.6 us
    ppermute x4, starting transfers between devices, brought(): got.append(lax.ppermute(block, AXES, pairs))  4.75 us
    ppermute x4, waiting for transfers between devices, brought(): got.append(lax.ppermute(block, AXES, pairs))  4.32 us
    ppermute x6, waiting for transfers between devices, along(): lax.ppermute(block, axis, [(source, i) for i, source in enumerate(sources)])  2.15 us
  transfers between devices with their start and end apart: 10, of which 8 were waited for; matrix products, arithmetic and copies ran while one was open for 0% of the time, Pallas kernels for 5%

profile of v8, /device:TPU:0, one launch (start us, length us, event | category | flops | bytes accessed | tf_op | source)
XLA Modules:
  0.0 48.5 jit_solution(3984736218142178965)
XLA Ops:
  1.3 1.0 %shard_map.130 = (f32[32,4,128]{2,1,0:T(4,128)S(1)}, bf16[2,32,128]{2,1,0:T(8,128)(2,1)S(1)}, bf16[160,384]{1,0:T(8,128)(2,1)S(1)}, bf16[8,128]{1,0:T(8,128)(2,1...) custom-call(s32[1]{0:T(128)} %bitcast.12.refs_0_, ...), custom_call_target="tpu_custom_call" | custom-call | flops 1048576 | bytes 1048576 | tf_op jit(solution)/shard_map/pallas_call | solution.py:551
  2.3 14.6 %all_to_all.10.refs_0_ = f32[32,4,128]{2,1,0:T(4,128)S(1)} all-to-all(f32[32,4,128]{2,1,0:T(4,128)S(1)} %get-tuple-element.33), channel_id=1, replica_groups=mesh['gx'=4,'gy'=2,'gz'=4] {'gx','gy','gz'}, dimensions={0} | all-to-all | bytes 131072 | tf_op jit(solution)/shard_map/all_to_all | solution.py:621
  16.9 4.4 %shard_map.131 = (f32[9,4,128]{2,1,0:T(4,128)S(1)}, bf16[3,4,64,1152]{3,2,1,0:T(8,128)(2,1)S(1)}, bf16[4,64,128]{2,1,0:T(8,128)(2,1)S(1)}, f32[192,128]{1,0:T(8,...) custom-call(f32[32,4,128]{2,1,0:T(4,128)S(1)} %all_to_all.10.refs_0_, ...), custom_call_target="tpu_custom_call" | custom-call | flops 7372800 | bytes 1048576 | tf_op jit(solution)/shard_map/pallas_call | solution.py:551
  21.4 0.7 %collective-permute-start.1 = (bf16[4,64,128]{2,1,0:T(8,128)(2,1)S(1)}, bf16[4,64,128]{2,1,0:T(8,128)(2,1)S(1)}, u32[]{:S(2)}, u32[]{:S(2)}) collective-permute-start(bf16[4,64,128]{2,1,0:T(8,128)(2,1)S(1)} %get-tuple-element.40.refs_2_.refs_6_.refs_5_), channel_id=1, source_target_pairs={{24,0},{25,1},{26,2},{27,3},{28,4},{29,5},{30,6},{31,7},{16,8},{17... | collective-permute-start | bytes 196616 | tf_op jit(solution)/shard_map/ppermute | solution.py:592
  22.0 1.5 %collective-permute-start = (bf16[4,64,128]{2,1,0:T(8,128)(2,1)S(1)}, bf16[4,64,128]{2,1,0:T(8,128)(2,1)S(1)}, u32[]{:S(2)}, u32[]{:S(2)}) collective-permute-start(bf16[4,64,128]{2,1,0:T(8,128)(2,1)S(1)} %get-tuple-element.40.refs_2_.refs_6_.refs_5_), channel_id=1, source_target_pairs={{8,0},{9,1},{10,2},{11,3},{12,4},{13,5},{14,6},{15,7},{0,8},{1,9},... | collective-permute-start | bytes 196616 | tf_op jit(solution)/shard_map/ppermute | solution.py:592
  23.6 1.2 %shard_map.132 = (bf16[4,64,128]{2,1,0:T(8,128)(2,1)S(1)}, f32[3,64,1152]{2,1,0:T(8,128)S(1)}, f32[4,64,1152]{2,1,0:T(8,128)S(1)}, f32[4,64,1152]{2,1,0:T(8,128)S(1)}, f32[4,64,1152]{2,1,0:T(8,128)S(1)}) custom-call(f32[9,4,128]{2,1,0:T(4,128)S(1)} %get-tuple-element.38.refs_0_.refs_9_, f32[3,64,8]{2,1,0:T(8,128)S(1)} %get-tuple-element.39.refs_1_.refs_8_.refs_4_, ...), custom_call_target="tpu_custom_call" | custom-call | flops 7372800 | bytes 1048576 | tf_op jit(solution)/shard_map/pallas_call | solution.py:551
  24.7 0.1 collective-permute-start.2
  24.8 1.8 %collective-permute-done.1.refs_2_ = bf16[4,64,128]{2,1,0:T(8,128)(2,1)S(1)} collective-permute-done((bf16[4,64,128]{2,1,0:T(8,128)(2,1)S(1)}, bf16[4,64,128]{2,1,0:T(8,128)(2,1)S(1)}, u32[]{:S(2)}, u32[]{:S(2)}) %collective-permute-start.1) | collective-permute-done | bytes 65568 | tf_op jit(solution)/shard_map/ppermute | solution.py:592
  26.6 0.0 collective-permute-start.4
  26.6 0.2 collective-permute-done.refs_1_
  26.8 0.3 collective-permute-start.3
  27.1 0.0 collective-permute-done.2.refs_3_
  27.1 0.7 %collective-permute-done.4.refs_5_ = bf16[4,64,128]{2,1,0:T(8,128)(2,1)S(1)} collective-permute-done((bf16[4,64,128]{2,1,0:T(8,128)(2,1)S(1)}, bf16[4,64,128]{2,1,0:T(8,128)(2,1)S(1)}, u32[]{:S(2)}, u32[]{:S(2)}) %collective-permute-start.4) | collective-permute-done | bytes 65568 | tf_op jit(solution)/shard_map/ppermute | solution.py:602
  27.9 0.2 collective-permute-done.3.refs_4_
  28.1 1.2 %shard_map.133 = (bf16[3,64,128]{2,1,0:T(8,128)(2,1)S(1)}, bf16[64,128]{1,0:T(8,128)(2,1)S(1)}, f32[64,16]{1,0:T(8,128)S(1)}, f32[64,128]{1,0:T(8,128)S(1)}, bf16[1152,128]{1,0:T(8,128)(2,1)S(1)}) custom-call(bf16[4,64,128]{2,1,0:T(8,128)(2,1)S(1)} %get-tuple-element.41.refs_0_, bf16[4,64,128]{2,1,0:T(8,128)(2,1)S(1)} %collective-permute-done.refs_1_, ...), custom_call_target="tpu_custom_call" | custom-call | flops 7372800 | bytes 1048576 | tf_op jit(solution)/shard_map/pallas_call | solution.py:551
  29.2 1.8 %collective-permute-start.6 = (bf16[3,64,128]{2,1,0:T(8,128)(2,1)S(1)}, bf16[3,64,128]{2,1,0:T(8,128)(2,1)S(1)}, u32[]{:S(2)}, u32[]{:S(2)}) collective-permute-start(bf16[3,64,128]{2,1,0:T(8,128)(2,1)S(1)} %get-tuple-element.49.refs_1_), channel_id=1, source_target_pairs={{24,0},{25,1},{26,2},{27,3},{28,4},{29,5},{30,6},{31,7},{16,8},{17... | collective-permute-start | bytes 147464 | tf_op jit(solution)/shard_map/ppermute | solution.py:592
  31.1 0.7 %collective-permute-start.5 = (bf16[3,64,128]{2,1,0:T(8,128)(2,1)S(1)}, bf16[3,64,128]{2,1,0:T(8,128)(2,1)S(1)}, u32[]{:S(2)}, u32[]{:S(2)}) collective-permute-start(bf16[3,64,128]{2,1,0:T(8,128)(2,1)S(1)} %get-tuple-element.49.refs_1_), channel_id=1, source_target_pairs={{8,0},{9,1},{10,2},{11,3},{12,4},{13,5},{14,6},{15,7},{0,8},{1,9},... | collective-permute-start | bytes 147464 | tf_op jit(solution)/shard_map/ppermute | solution.py:592
  31.8 1.0 %shard_map.134 = (bf16[3,64,128]{2,1,0:T(8,128)(2,1)S(1)}, f32[64,1152]{1,0:T(8,128)S(1)}, f32[1,64]{1,0:T(1,128)}, bf16[64,128]{1,0:T(8,128)(2,1)}) custom-call(bf16[1152,128]{1,0:T(8,128)(2,1)S(1)} %get-tuple-element.48.refs_0_, bf16[3,64,128]{2,1,0:T(8,128)(2,1)S(1)} %get-tuple-element.49.refs_1_, f32[4,64,1152]{2,1,0:T(8,128)S(1)} %get-tuple-element.50.refs_2_.refs_11_, ...), custom_call_target="tpu_custom_call" | custom-call | flops 7372800 | bytes 1048576 | tf_op jit(solution)/shard_map/pallas_call | solution.py:551
  32.8 0.0 collective-permute-start.7
  32.8 1.8 %collective-permute-done.6.refs_2_ = bf16[3,64,128]{2,1,0:T(8,128)(2,1)S(1)} collective-permute-done((bf16[3,64,128]{2,1,0:T(8,128)(2,1)S(1)}, bf16[3,64,128]{2,1,0:T(8,128)(2,1)S(1)}, u32[]{:S(2)}, u32[]{:S(2)}) %collective-permute-start.6) | collective-permute-done | bytes 49184 | tf_op jit(solution)/shard_map/ppermute | solution.py:592
  34.6 0.0 collective-permute-start.9
  34.6 0.5 %collective-permute-done.5.refs_1_ = bf16[3,64,128]{2,1,0:T(8,128)(2,1)S(1)} collective-permute-done((bf16[3,64,128]{2,1,0:T(8,128)(2,1)S(1)}, bf16[3,64,128]{2,1,0:T(8,128)(2,1)S(1)}, u32[]{:S(2)}, u32[]{:S(2)}) %collective-permute-start.5) | collective-permute-done | bytes 49184 | tf_op jit(solution)/shard_map/ppermute | solution.py:592
  35.2 0.0 collective-permute-start.8
  35.2 0.0 collective-permute-done.7.refs_3_
  35.2 0.7 %collective-permute-done.9.refs_5_ = bf16[3,64,128]{2,1,0:T(8,128)(2,1)S(1)} collective-permute-done((bf16[3,64,128]{2,1,0:T(8,128)(2,1)S(1)}, bf16[3,64,128]{2,1,0:T(8,128)(2,1)S(1)}, u32[]{:S(2)}, u32[]{:S(2)}) %collective-permute-start.9) | collective-permute-done | bytes 49184 | tf_op jit(solution)/shard_map/ppermute | solution.py:602
  35.9 0.5 %collective-permute-done.8.refs_4_ = bf16[3,64,128]{2,1,0:T(8,128)(2,1)S(1)} collective-permute-done((bf16[3,64,128]{2,1,0:T(8,128)(2,1)S(1)}, bf16[3,64,128]{2,1,0:T(8,128)(2,1)S(1)}, u32[]{:S(2)}, u32[]{:S(2)}) %collective-permute-start.8) | collective-permute-done | bytes 49184 | tf_op jit(solution)/shard_map/ppermute | solution.py:602
  36.4 2.1 %shard_map.135 = f32[32,4,128]{2,1,0:T(4,128)S(1)} custom-call(bf16[3,64,128]{2,1,0:T(8,128)(2,1)S(1)} %get-tuple-element.53.refs_0_, bf16[3,64,128]{2,1,0:T(8,128)(2,1)S(1)} %collective-permute-done.5.refs_1_, bf16[3,64,128]{2,1,0:T(8,128)(2,1)S(1)} %collective-permute-done.6.refs_2_, bf16[3,64,128]{2,1,0:T(8,128)(2,1)S(1)} %collective-permute-done.7.refs_3_, ...), custom_call_target="tpu_custom_call" | custom-call | flops 7372800 | bytes 1048576 | tf_op jit(solution)/shard_map/pallas_call | solution.py:551
  38.5 9.3 %all_to_all.11.refs_0_ = f32[32,4,128]{2,1,0:T(4,128)S(1)} all-to-all(f32[32,4,128]{2,1,0:T(4,128)S(1)} %shard_map.135), channel_id=1, replica_groups=mesh['gx'=4,'gy'=2,'gz'=4] {'gx','gy','gz'}, dimensions={0} | all-to-all | bytes 131072 | tf_op jit(solution)/shard_map/all_to_all | solution.py:621
  47.8 0.7 %shard_map.136 = f32[3,1,64]{2,1,0:T(1,128)} custom-call(f32[32,4,128]{2,1,0:T(4,128)S(1)} %all_to_all.11.refs_0_), custom_call_target="tpu_custom_call" | custom-call | flops 1048576 | bytes 1048576 | tf_op jit(solution)/shard_map/pallas_call | solution.py:551
Async XLA Ops:
  21.4 5.3 %collective-permute-start.1 = (bf16[4,64,128]{2,1,0:T(8,128)(2,1)S(1)}, bf16[4,64,128]{2,1,0:T(8,128)(2,1)S(1)}, u32[]{:S(2)}, u32[]{:S(2)}) collective-permute-start(bf16[4,64,128]{2,1,0:T(8,128)(2,1)S(1)} %get-tuple-element.40.refs_2_.refs_6_.refs_5_), channel_id=1, source_target_pairs={{24,0},{25,1},{26,2},{27,3},{28,4},{29,5},{30,6},{31,7},{16,8},{17... | collective-permute-start | bytes 196616 | tf_op jit(solution)/shard_map/ppermute | solution.py:592
  22.0 4.8 %collective-permute-start = (bf16[4,64,128]{2,1,0:T(8,128)(2,1)S(1)}, bf16[4,64,128]{2,1,0:T(8,128)(2,1)S(1)}, u32[]{:S(2)}, u32[]{:S(2)}) collective-permute-start(bf16[4,64,128]{2,1,0:T(8,128)(2,1)S(1)} %get-tuple-element.40.refs_2_.refs_6_.refs_5_), channel_id=1, source_target_pairs={{8,0},{9,1},{10,2},{11,3},{12,4},{13,5},{14,6},{15,7},{0,8},{1,9},... | collective-permute-start | bytes 196616 | tf_op jit(solution)/shard_map/ppermute | solution.py:592
  24.7 2.4 %collective-permute-start.2 = (bf16[4,64,128]{2,1,0:T(8,128)(2,1)S(1)}, bf16[4,64,128]{2,1,0:T(8,128)(2,1)S(1)}, u32[]{:S(2)}, u32[]{:S(2)}) collective-permute-start(bf16[4,64,128]{2,1,0:T(8,128)(2,1)S(1)} %get-tuple-element.41.refs_0_), channel_id=1, source_target_pairs={{4,0},{0,4},{5,1},{1,5},{6,2},{2,6},{7,3},{3,7},{12,8},{8,12},{13,... | collective-permute-start | bytes 196616 | tf_op jit(solution)/shard_map/ppermute | solution.py:602
  26.6 1.3 %collective-permute-start.4 = (bf16[4,64,128]{2,1,0:T(8,128)(2,1)S(1)}, bf16[4,64,128]{2,1,0:T(8,128)(2,1)S(1)}, u32[]{:S(2)}, u32[]{:S(2)}) collective-permute-start(bf16[4,64,128]{2,1,0:T(8,128)(2,1)S(1)} %collective-permute-done.1.refs_2_), channel_id=1, source_target_pairs={{4,0},{0,4},{5,1},{1,5},{6,2},{2,6},{7,3},{3,7},{12,8},{8,12},{13,... | collective-permute-start | bytes 196616 | tf_op jit(solution)/shard_map/ppermute | solution.py:602
  26.8 1.3 %collective-permute-start.3 = (bf16[4,64,128]{2,1,0:T(8,128)(2,1)S(1)}, bf16[4,64,128]{2,1,0:T(8,128)(2,1)S(1)}, u32[]{:S(2)}, u32[]{:S(2)}) collective-permute-start(bf16[4,64,128]{2,1,0:T(8,128)(2,1)S(1)} %collective-permute-done.refs_1_), channel_id=1, source_target_pairs={{4,0},{0,4},{5,1},{1,5},{6,2},{2,6},{7,3},{3,7},{12,8},{8,12},{13,... | collective-permute-start | bytes 196616 | tf_op jit(solution)/shard_map/ppermute | solution.py:602
  29.2 5.4 %collective-permute-start.6 = (bf16[3,64,128]{2,1,0:T(8,128)(2,1)S(1)}, bf16[3,64,128]{2,1,0:T(8,128)(2,1)S(1)}, u32[]{:S(2)}, u32[]{:S(2)}) collective-permute-start(bf16[3,64,128]{2,1,0:T(8,128)(2,1)S(1)} %get-tuple-element.49.refs_1_), channel_id=1, source_target_pairs={{24,0},{25,1},{26,2},{27,3},{28,4},{29,5},{30,6},{31,7},{16,8},{17... | collective-permute-start | bytes 147464 | tf_op jit(solution)/shard_map/ppermute | solution.py:592
  31.1 4.1 %collective-permute-start.5 = (bf16[3,64,128]{2,1,0:T(8,128)(2,1)S(1)}, bf16[3,64,128]{2,1,0:T(8,128)(2,1)S(1)}, u32[]{:S(2)}, u32[]{:S(2)}) collective-permute-start(bf16[3,64,128]{2,1,0:T(8,128)(2,1)S(1)} %get-tuple-element.49.refs_1_), channel_id=1, source_target_pairs={{8,0},{9,1},{10,2},{11,3},{12,4},{13,5},{14,6},{15,7},{0,8},{1,9},... | collective-permute-start | bytes 147464 | tf_op jit(solution)/shard_map/ppermute | solution.py:592
  32.8 2.3 %collective-permute-start.7 = (bf16[3,64,128]{2,1,0:T(8,128)(2,1)S(1)}, bf16[3,64,128]{2,1,0:T(8,128)(2,1)S(1)}, u32[]{:S(2)}, u32[]{:S(2)}) collective-permute-start(bf16[3,64,128]{2,1,0:T(8,128)(2,1)S(1)} %get-tuple-element.53.refs_0_), channel_id=1, source_target_pairs={{4,0},{0,4},{5,1},{1,5},{6,2},{2,6},{7,3},{3,7},{12,8},{8,12},{13,... | collective-permute-start | bytes 147464 | tf_op jit(solution)/shard_map/ppermute | solution.py:602
  34.6 1.2 %collective-permute-start.9 = (bf16[3,64,128]{2,1,0:T(8,128)(2,1)S(1)}, bf16[3,64,128]{2,1,0:T(8,128)(2,1)S(1)}, u32[]{:S(2)}, u32[]{:S(2)}) collective-permute-start(bf16[3,64,128]{2,1,0:T(8,128)(2,1)S(1)} %collective-permute-done.6.refs_2_), channel_id=1, source_target_pairs={{4,0},{0,4},{5,1},{1,5},{6,2},{2,6},{7,3},{3,7},{12,8},{8,12},{13,... | collective-permute-start | bytes 147464 | tf_op jit(solution)/shard_map/ppermute | solution.py:602
  35.2 1.2 %collective-permute-start.8 = (bf16[3,64,128]{2,1,0:T(8,128)(2,1)S(1)}, bf16[3,64,128]{2,1,0:T(8,128)(2,1)S(1)}, u32[]{:S(2)}, u32[]{:S(2)}) collective-permute-start(bf16[3,64,128]{2,1,0:T(8,128)(2,1)S(1)} %collective-permute-done.5.refs_1_), channel_id=1, source_target_pairs={{4,0},{0,4},{5,1},{1,5},{6,2},{2,6},{7,3},{3,7},{12,8},{8,12},{13,... | collective-permute-start | bytes 147464 | tf_op jit(solution)/shard_map/ppermute | solution.py:602

commit v9 on v8

--- a/solution.py
+++ b/solution.py
@@ -90,12 +90,9 @@
         self.brought = list(itertools.product(range(self.wide), range(self.depth)))
         self.mixed = self.depth == self.wide and self.sizes["gy"] % 2 == 0
         self.small = self.ndev <= 64 and len(self.sides) == 2
-        near = offsets_of(self.sizes["gz"])
-        self.column = list(near) if self.small else [0]
-        for step in [a + b for a in near for b in near] if self.small else []:
-            if all((step - known) % self.sizes["gz"] for known in self.column):
-                self.column.append(step)
+        self.columns, self.column = [self.reach(axis) if self.small else [0] for axis in ("gx", "gz")]
         self.known = self.depth if self.small else 1
+        self.targets = self.tiles if self.small else self.tiles[:1]
         self.wrapped = [self.sizes[axis] == 2 for axis in AXES]
         self.plain = [k for k in range(3) if not self.wrapped[k]]
         self.folded = [k for k in range(3) if self.wrapped[k]]
@@ -108,8 +105,19 @@
             place = place * count + lax.rem(lax.axis_index(axis) + (step + count), count)
         return place
 
-    def column_place(self, step):
-        return [(step - known) % self.sizes["gz"] == 0 for known in self.column].index(True)
+    def reach(self, axis):
+        near, count = offsets_of(self.sizes[axis]), self.sizes[axis]
+        steps = list(near)
+        for step in [a + b for a in near for b in near]:
+            if all((step - other) % count for other in steps):
+                steps.append(step)
+        return steps
+
+    def held(self, x, z):
+        found = []
+        for step, steps, axis in ((x, self.columns, "gx"), (z, self.column, "gz")):
+            found.append([(step - other) % self.sizes[axis] == 0 for other in steps].index(True))
+        return found[0] * len(self.column) + found[1]
 
     def places(self):
         index = {axis: lax.axis_index(axis) for axis in AXES}
@@ -172,6 +180,37 @@
     return poly(COS_TERMS, square), -(arg * poly(SIN_TERMS, square))
 
 
+def global_block(plan, far_ref, tile, side, target):
+    x, y, z = plan.offset(tile, side)
+    return far_ref[plan.global_id((x + target[0], y, z + target[1]))]
+
+
+def own_columns(plan, block):
+    held = jnp.concatenate([block, block], axis=0).T[: plan.slots]
+    kind = held[:, 3:4]
+    lane = lax.broadcasted_iota(jnp.int32, held.shape, 1)
+    live = kind >= 0.0
+    held = jnp.where((lane == 0) & ~live, -FAR, held)
+    return jnp.where(lane == 3, live.astype(F32), held), kind
+
+
+def scaled_columns(held):
+    return [held[:, axis : axis + 1] * (1.0 / CELL_SIDE) for axis in range(3)]
+
+
+def basis_of(plan, placed, cols, tile):
+    parts = separations(plan, [placed[k : k + 1] for k in range(3)], cols, 1.0)
+    dist_sq, inverse = distance(plan, parts, tile, SOFTEN / CUT_SQUARE)
+    turn = jnp.minimum(dist_sq * inverse - 0.5, 0.5)
+    square = turn * turn
+    double = turn * poly(scaled(SIN_TERMS, -2.0), square)
+    fade = jnp.maximum(1.0 - dist_sq, 0.0)
+    basis = [poly(scaled(COS_TERMS, 1.0 / CELL_SIDE), square) * (fade * fade * inverse)]
+    for n in range(1, plan.nbasis):
+        basis.append(double * basis[-1] if n == 1 else double * basis[-1] - basis[-2])
+    return parts, inverse, basis
+
+
 def first_kernel(plan, nrefs, places, *refs):
     far_refs, refs = refs[:nrefs], refs[nrefs:]
     (table_ref, wide_ref, embed_ref, mix_ref), refs = refs[:4], refs[4:]
@@ -186,24 +225,18 @@
 
     def block_of(tile, side, up):
         if plan.small:
-            x, y, z = plan.offset(tile, side)
-            return far_refs[0][plan.global_id((x, y, z + up))]
+            return global_block(plan, far_refs[0], tile, side, (0, up))
         return block_ref[tile * len(plan.sides) + side]
 
     species = lax.broadcasted_iota(jnp.int32, (nbasis * nspec, plan.width), 0) % nspec
     shifts = [tile_shift(plan, tile) for tile in range(len(plan.tiles))]
     own, counted, places_of = [], [], []
     for which, up in enumerate(plan.column):
-        held = block_of(0, 0, up)
-        held = jnp.concatenate([held, held], axis=0).T[:slots]
-        kind = held[:, 3:4]
+        held, kind = own_columns(plan, block_of(0, 0, up))
         own.append(kind)
-        lane = lax.broadcasted_iota(jnp.int32, held.shape, 1)
-        live = kind >= 0.0
-        held = jnp.where((lane == 0) & ~live, -FAR, held)
         if which < plan.known:
-            cols_ref[which] = jnp.where(lane == 3, live.astype(F32), held)
-        cols = [held[:, axis : axis + 1] * (1.0 / CELL_SIDE) for axis in range(3)]
+            cols_ref[which] = held
+        cols = scaled_columns(held)
         places_of.append(cols)
         hot = []
         for tile in range(len(plan.tiles)):
@@ -219,22 +252,12 @@
             for k in plan.plain:
                 columns += [jnp.where(is_kind, part[k : k + 1], 0.0) for part in (high, low)]
             hot.append(jnp.concatenate([column.astype(BF16) for column in columns], axis=0))
-            parts = separations(plan, [placed[k : k + 1] for k in range(3)], cols, 1.0)
-            dist_sq, inverse = distance(plan, parts, tile, SOFTEN / CUT_SQUARE)
-            turn = jnp.minimum(dist_sq * inverse - 0.5, 0.5)
-            square = turn * turn
-            double = turn * poly(scaled(SIN_TERMS, -2.0), square)
-            fade = jnp.maximum(1.0 - dist_sq, 0.0)
-            before, now = None, poly(scaled(COS_TERMS, 1.0 / CELL_SIDE), square) * (fade * fade * inverse)
+            parts, inverse, basis = basis_of(plan, placed, cols, tile)
             scale = inverse * ROOT_THREE
             units = [scale.astype(BF16)] + [(scale * parts[k]).astype(BF16) for k in plan.folded]
             lanes = slice(tile * plan.width, (tile + 1) * plan.width)
             for n in range(nbasis):
-                if n == 1:
-                    before, now = now, double * now
-                elif n > 1:
-                    before, now = now, double * now - before
-                packed = now.astype(BF16)
+                packed = basis[n].astype(BF16)
                 if which < plan.known:
                     basis_ref[which, n, :, lanes] = packed
                 pair_ref[which, n, :slots, lanes] = packed
@@ -280,17 +303,28 @@
     return 1.0 / (1.0 + jnp.exp(-value))
 
 
-def scatter(plan, places, far_refs, put, up=0):
+def scatter(plan, places, far_refs, put):
     for side in range(len(plan.sides)):
         for pair, (second, first) in enumerate(plan.brought):
-            column = far_refs[side * plan.wide + second]
-            if not plan.small:
-                put(plan.brought_place(places, side, pair), column[first])
-                continue
-            turn = places[len(plan.sides) * len(plan.brought)]
-            tile = matched(second, turn) * plan.depth + first
-            step = offsets_of(plan.sizes["gz"])[first] + up
-            put(tile * len(plan.sides) + side, column[plan.column_place(step)])
+            put(plan.brought_place(places, side, pair), far_refs[side * plan.wide + second][first])
+
+
+def scatter_held(plan, places, far_refs, put):
+    turn = places[len(plan.sides) * len(plan.brought)]
+    for side in range(len(plan.sides)):
+        for m in range(len(plan.columns)):
+            x = matched(m, turn) if m < plan.wide else m
+            for z in range(len(plan.column)):
+                place = (x * len(plan.column) + z) * len(plan.sides) + side
+                put(place, far_refs[side * len(plan.columns) + m][z])
+
+
+def far_blocks(plan, block_ref, target):
+    blocks = []
+    for x, z in plan.tiles:
+        place = plan.held(x + target[0], z + target[1]) * len(plan.sides)
+        blocks += [block_ref[place + side] for side in range(len(plan.sides))]
+    return jnp.concatenate(blocks, axis=0)
 
 
 def side_by_side(plan, blocks):
@@ -311,38 +345,53 @@
     return shift
 
 
-def gather_far(plan, places, far_refs, all_ref, up=0):
+def gather_far(plan, places, far_refs, all_ref):
     def put(place, block):
         start = pl.multiple_of(place * plan.slots, plan.slots)
         all_ref[pl.ds(start, plan.slots)] = block
 
-    scatter(plan, places, far_refs, put, up)
+    scatter(plan, places, far_refs, put)
 
 
 def second_kernel(plan, nrefs, places, *refs):
     far_refs, refs = refs[:nrefs], refs[nrefs:]
-    (layer_ref, basis_ref, cols_ref, radial_ref, mix_ref), refs = refs[:5], refs[5:]
+    (layer_ref, basis_ref, cols_ref, more_ref, more_cols_ref, radial_ref, mix_ref), refs = refs[:7], refs[7:]
     (hidden_ref, out_ref, one_ref), refs = refs[:3], refs[3:]
-    adjoint_ref, features_ref, before_ref, own_ref, own_far_ref, all_ref = refs
-    slots, nbasis, known = plan.slots, plan.nbasis, plan.known
-    messages = []
-    for which in range(known):
-        target = own_far_ref if which == 0 else all_ref.at[which - 1]
-        gather_far(plan, places, far_refs, target, plan.column[which])
-        summed = dot(basis_ref[which].reshape(nbasis * slots, plan.far), target[...])
+    adjoint_ref, features_ref, before_ref, own_ref, own_far_ref, block_ref = refs
+    slots, nbasis, known = plan.slots, plan.nbasis, len(plan.targets)
+
+    def put(place, block):
+        block_ref[place] = block
+
+    (scatter_held if plan.small else scatter)(plan, places, far_refs, put)
+    messages, layers, lives = [], [], []
+    for which, target in enumerate(plan.targets):
+        if plan.small:
+            far = far_blocks(plan, block_ref, target)
+            layers.append(block_ref[plan.held(*target) * len(plan.sides)])
+        else:
+            far = block_ref[...].reshape(plan.far, -1)
+            layers.append(layer_ref[0])
+        first = which < plan.known
+        held_ref, held_cols_ref = (basis_ref, cols_ref) if first else (more_ref, more_cols_ref)
+        place = which if first else which - plan.known
+        lives.append(held_cols_ref[place, :, 3:4])
+        if which == 0:
+            own_far_ref[...] = far
+        summed = dot(held_ref[place].reshape(nbasis * slots, plan.far), far)
         message = summed[:slots] * radial_ref[0:1]
         for n in range(1, nbasis):
             message = message + summed[n * slots : (n + 1) * slots] * radial_ref[n : n + 1]
         messages.append((MSG_SCALE * message).astype(BF16))
     mixing = dot(jnp.concatenate(messages, axis=0), mix_ref[...], NT)
     gate = sigmoid(mixing)
-    layer = layer_ref[:known].reshape(known * slots, -1).astype(F32)
+    layer = jnp.concatenate(layers, axis=0).astype(F32)
     features = (layer + mixing * gate).astype(BF16)
     features_ref[...] = features[:slots]
     before = dot(features, hidden_ref[...], NT)
     before_ref[...] = before[:slots]
     open_hidden = sigmoid(before)
-    live = cols_ref[...].reshape(known * slots, 8)[:, 3:4]
+    live = jnp.concatenate(lives, axis=0)
     slope = out_ref[...] * (open_hidden * (1.0 + before * (1.0 - open_hidden))) * live
     from_hidden = dot(slope.astype(BF16), hidden_ref[...])
     own_ref[...] = from_hidden[:slots] + one_ref[...] * live[:slots]
@@ -352,9 +401,20 @@
         adjoint_ref[which] = adjoint[which * slots : (which + 1) * slots]
 
 
-def slope_kernel(plan, rows_ref, cols_ref, layer_ref, *refs):
-    again_ref, apart_ref, slope_ref, radial_ref, turned_ref = refs
+def slope_kernel(plan, nrefs, places, *refs):
+    far_refs, (rows_ref, cols_ref, layer_ref), refs = refs[:nrefs], refs[nrefs : nrefs + 3], refs[nrefs + 3 :]
+    again_ref, apart_ref, slope_ref, radial_ref, turned_ref, more_ref, more_cols_ref = refs
     again_ref[...] = layer_ref[...]
+    for which, target in enumerate(plan.targets[plan.known :]):
+        held, _ = own_columns(plan, global_block(plan, far_refs[0], 0, 0, target))
+        more_cols_ref[which] = held
+        for tile in range(len(plan.tiles)):
+            lanes = slice(tile * plan.width, (tile + 1) * plan.width)
+            blocks = [global_block(plan, far_refs[0], tile, s, target) for s in range(len(plan.sides))]
+            placed = (side_by_side(plan, blocks) + tile_shift(plan, tile)) * (1.0 / CELL_SIDE)
+            basis = basis_of(plan, placed, scaled_columns(held), tile)[2]
+            for n in range(plan.nbasis):
+                more_ref[which, n, :, lanes] = basis[n].astype(BF16)
     cols = [cols_ref[0, :, axis : axis + 1] for axis in range(3)]
     for tile in range(len(plan.tiles)):
         lanes = slice(tile * plan.width, (tile + 1) * plan.width)
@@ -391,7 +451,7 @@
     (before_ref, out_ref, one_ref, kept_ref), refs = refs[:4], refs[4:]
     again_ref, pair_ref, energy_ref, features_ref = refs
     slots, nbasis = plan.slots, plan.nbasis
-    again_ref[...] = adjoint_ref[...]
+    again_ref[...] = adjoint_ref[:1]
     features_ref[...] = kept_ref[...]
     before = before_ref[...]
     live = jnp.where(lax.broadcasted_iota(jnp.int32, (slots, 8), 1) == 0, cols_ref[0, :, 3:4], 0.0)
@@ -419,7 +479,11 @@
     (radial_ref, mixing_ref, mix_ref, vector_ref, table_ref), refs = refs[:5], refs[5:]
     out_ref, all_ref = refs
     slots, nbasis, nspec, width = plan.slots, plan.nbasis, plan.nspec, plan.width
-    gather_far(plan, places, far_refs, all_ref)
+    if plan.small:
+        far = [far_refs[side][tile] for tile in range(len(plan.tiles)) for side in range(len(plan.sides))]
+        all_ref[...] = jnp.concatenate(far, axis=0)
+    else:
+        gather_far(plan, places, far_refs, all_ref)
     summed = dot(basis_ref[0].reshape(nbasis * slots, plan.far), all_ref[...])
     adjoint = jnp.zeros((slots, summed.shape[1]), F32)
     for n in range(nbasis):
@@ -611,6 +675,9 @@
 
 def from_columns(plan, column, mixed, again=None):
     columns = [column] + brought(plan, column, True, mixed)
+    count = plan.sizes["gx"]
+    for step in plan.columns[plan.wide :]:
+        columns.append(lax.ppermute(column, "gx", [((i + step) % count, i) for i in range(count)]))
     if again is not None:
         columns[0] = again
     swapped = [[column] + along(column, "gy") for column in columns]
@@ -694,32 +761,38 @@
             ],
             pair_flops,
         )
-        again, apart, slope, factor, turned = simple_call(
+        more = max(len(plan.targets) - plan.known, 1)
+        again, apart, slope, factor, turned, more_basis, more_cols = call(
             slope_kernel,
             plan,
+            far_sent[:1],
             [rows, cols, layer],
             [(layer.shape, BF16)]
-            + [((count, slots, plan.far), F32) for count in (3, nbasis, nbasis, nbasis)],
-            flops=pair_flops,
+            + [((count, slots, plan.far), F32) for count in (3, nbasis, nbasis, nbasis)]
+            + [((more, nbasis, slots, plan.far), BF16), ((more, slots, 8), F32)],
+            [],
+            pair_flops,
         )
         if plan.small:
             far_layer = from_columns(plan, layer, False, again)
         else:
             far_layer = neighbours(plan, layer[0], again[0])
         far_scratch = ((plan.far, channels), BF16)
+        held = len(plan.columns) * len(plan.column) if plan.small else len(plan.tiles)
+        held = held * len(plan.sides)
         adjoint, kept, before, own_adjoint, own_far = call(
             second_kernel,
             plan,
             far_layer,
-            [layer, basis, cols, radial_two, mix_two, read_hidden, out_row, one_row],
+            [layer, basis, cols, more_basis, more_cols, radial_two, mix_two, read_hidden, out_row, one_row],
             [
-                ((plan.known, slots, channels), BF16),
+                ((len(plan.targets), slots, channels), BF16),
                 ((slots, channels), BF16),
                 ((slots, read_hidden.shape[0]), F32),
                 ((slots, channels), F32),
                 far_scratch,
             ],
-            [((max(plan.known - 1, 1), plan.far, channels), BF16)],
+            [((held, slots, channels), BF16)],
             pair_flops,
         )
         again, pair, energy, features = simple_call(
@@ -727,7 +800,7 @@
             plan,
             [own_far, adjoint, slope, radial_two, cols, layer, before, out_row, one_row, kept],
             [
-                (adjoint.shape, BF16),
+                ((1, slots, channels), BF16),
                 ((slots, plan.far), F32),
                 ((1, slots), F32),
                 ((slots, channels), BF16),
@@ -735,7 +808,7 @@
             flops=pair_flops,
         )
         if plan.small:
-            far_adjoint = from_columns(plan, adjoint, False, again)
+            far_adjoint = [adjoint] + along(adjoint, "gy")
         else:
             far_adjoint = neighbours(plan, adjoint[0], again[0])
         pulls = call(

time: 48.7 us -> 46.9 us (0.963)
  waiting for transfers between devices: 6.47 us -> 0.91 us
  Pallas kernels: 11.6 us -> 15.6 us
    ppermute x4 -> x2, waiting for transfers between devices: 4.32 us -> 0.01 us  [brought(): got.append(lax.ppermute(block, AXES, pairs))]
    pallas_call x7, Pallas kernels: 11.6 us -> 15.6 us  [simple_call(): pl.pallas_call(body, out_shape=shapes, in_specs=[SMEM_SPEC] * scalars + [...]
    ppermute x4 -> x2, starting transfers between devices: 4.75 us -> 2.81 us  [brought(): got.append(lax.ppermute(block, AXES, pairs))]
    ppermute x6 -> x5, waiting for transfers between devices: 2.15 us -> 0.9 us  [along(): lax.ppermute(block, axis, [(source, i) for i, source in enumerate(sources)])]
    ppermute x6 -> x5, starting transfers between devices: 0.41 us -> 1.49 us  [along(): lax.ppermute(block, axis, [(source, i) for i, source in enumerate(sources)])]
    ppermute x0 -> x1, starting transfers between devices: none -> 0.74 us  [from_columns(): lax.ppermute(column, 'gx', [((i + step) % count, i) for i in range(count)])]
  transfers between devices with their start and end apart: 10 -> 8, of which waited for: 8 -> 4; matrix products, arithmetic and copies ran while one was open for 0% -> 0% of each run, Pallas kernels for 5% -> 11%
where the time goes in v9:
time: 46.9 us; the launch traced here: 46.6 us
  blocking collectives  23.8 us (51%)
  Pallas kernels  15.6 us (33%)
  starting transfers between devices  5.04 us (11%)
  between operations  1.33 us (3%)
  waiting for transfers between devices  0.91 us (2%)
    all_to_all x2, blocking collectives, everywhere(): return lax.all_to_all(copies, AXES, 0, 0, tiled=True)  23.8 us
    pallas_call x7, Pallas kernels, simple_call(): pl.pallas_call(body, out_shape=shapes, in_specs=[SMEM_SPEC] * scalars + [...  15.6 us
    ppermute x2, starting transfers between devices, brought(): got.append(lax.ppermute(block, AXES, pairs))  2.81 us
    ppermute x5, starting transfers between devices, along(): lax.ppermute(block, axis, [(source, i) for i, source in enumerate(sources)])  1.49 us
  transfers between devices with their start and end apart: 8, of which 4 were waited for; matrix products, arithmetic and copies ran while one was open for 0% of the time, Pallas kernels for 11%

profile of v9, /device:TPU:0, one launch (start us, length us, event | category | flops | bytes accessed | tf_op | source)
XLA Modules:
  0.0 46.6 jit_solution(8172041478322169639)
XLA Ops:
  1.3 1.0 %shard_map.130 = (f32[32,4,128]{2,1,0:T(4,128)S(1)}, bf16[2,32,128]{2,1,0:T(8,128)(2,1)S(1)}, bf16[160,384]{1,0:T(8,128)(2,1)S(1)}, bf16[8,128]{1,0:T(8,128)(2,1...) custom-call(s32[1]{0:T(128)} %bitcast.12.refs_0_, ...), custom_call_target="tpu_custom_call" | custom-call | flops 1048576 | bytes 1048576 | tf_op jit(solution)/shard_map/pallas_call | solution.py:615
  2.3 14.6 %all_to_all.10.refs_0_ = f32[32,4,128]{2,1,0:T(4,128)S(1)} all-to-all(f32[32,4,128]{2,1,0:T(4,128)S(1)} %get-tuple-element.34), channel_id=1, replica_groups=mesh['gx'=4,'gy'=2,'gz'=4] {'gx','gy','gz'}, dimensions={0} | all-to-all | bytes 131072 | tf_op jit(solution)/shard_map/all_to_all | solution.py:688
  16.9 4.4 %shard_map.131 = (f32[9,4,128]{2,1,0:T(4,128)S(1)}, bf16[3,4,64,1152]{3,2,1,0:T(8,128)(2,1)S(1)}, bf16[4,64,128]{2,1,0:T(8,128)(2,1)S(1)}, f32[192,128]{1,0:T(8,...) custom-call(f32[32,4,128]{2,1,0:T(4,128)S(1)} %all_to_all.10.refs_0_, ...), custom_call_target="tpu_custom_call" | custom-call | flops 7372800 | bytes 1048576 | tf_op jit(solution)/shard_map/pallas_call | solution.py:615
  21.3 0.7 %collective-permute-start.2 = (bf16[4,64,128]{2,1,0:T(8,128)(2,1)S(1)}, bf16[4,64,128]{2,1,0:T(8,128)(2,1)S(1)}, u32[]{:S(2)}, u32[]{:S(2)}) collective-permute-start(bf16[4,64,128]{2,1,0:T(8,128)(2,1)S(1)} %get-tuple-element.41.refs_3_.refs_8_.refs_5_), channel_id=1, source_target_pairs={{16,0},{24,8},{0,16},{8,24},{17,1},{25,9},{1,17},{9,25},{18,2},{26... | collective-permute-start | bytes 196616 | tf_op jit(solution)/shard_map/ppermute | solution.py:680
  22.1 1.4 %collective-permute-start.1 = (bf16[4,64,128]{2,1,0:T(8,128)(2,1)S(1)}, bf16[4,64,128]{2,1,0:T(8,128)(2,1)S(1)}, u32[]{:S(2)}, u32[]{:S(2)}) collective-permute-start(bf16[4,64,128]{2,1,0:T(8,128)(2,1)S(1)} %get-tuple-element.41.refs_3_.refs_8_.refs_5_), channel_id=1, source_target_pairs={{24,0},{25,1},{26,2},{27,3},{28,4},{29,5},{30,6},{31,7},{16,8},{17... | collective-permute-start | bytes 196616 | tf_op jit(solution)/shard_map/ppermute | solution.py:656
  23.5 1.4 %collective-permute-start = (bf16[4,64,128]{2,1,0:T(8,128)(2,1)S(1)}, bf16[4,64,128]{2,1,0:T(8,128)(2,1)S(1)}, u32[]{:S(2)}, u32[]{:S(2)}) collective-permute-start(bf16[4,64,128]{2,1,0:T(8,128)(2,1)S(1)} %get-tuple-element.41.refs_3_.refs_8_.refs_5_), channel_id=1, source_target_pairs={{8,0},{9,1},{10,2},{11,3},{12,4},{13,5},{14,6},{15,7},{0,8},{1,9},... | collective-permute-start | bytes 196616 | tf_op jit(solution)/shard_map/ppermute | solution.py:656
  24.9 4.1 %shard_map.132 = (bf16[4,64,128]{2,1,0:T(8,128)(2,1)S(1)}, f32[3,64,1152]{2,1,0:T(8,128)S(1)}, f32[4,64,1152]{2,1,0:T(8,128)S(1)}, f32[4,64,1152]{2,1,0:T(8,128)...) custom-call(f32[32,4,128]{2,1,0:T(4,128)S(1)} %all_to_all.10.refs_0_, ...), custom_call_target="tpu_custom_call" | custom-call | flops 7372800 | bytes 1048576 | tf_op jit(solution)/shard_map/pallas_call | solution.py:615
  29.0 0.1 collective-permute-start.3
  29.1 0.0 collective-permute-done.2.refs_3_
  29.1 0.5 %collective-permute-start.6 = (bf16[4,64,128]{2,1,0:T(8,128)(2,1)S(1)}, bf16[4,64,128]{2,1,0:T(8,128)(2,1)S(1)}, u32[]{:S(2)}, u32[]{:S(2)}) collective-permute-start(bf16[4,64,128]{2,1,0:T(8,128)(2,1)S(1)} %collective-permute-done.2.refs_3_), channel_id=1, source_target_pairs={{4,0},{0,4},{5,1},{1,5},{6,2},{2,6},{7,3},{3,7},{12,8},{8,12},{13,... | collective-permute-start | bytes 196616 | tf_op jit(solution)/shard_map/ppermute | solution.py:666
  29.6 0.0 collective-permute-done.1.refs_2_
  29.6 0.1 collective-permute-start.5
  29.7 0.0 collective-permute-done.refs_1_
  29.7 0.4 collective-permute-start.4
  30.1 0.2 collective-permute-done.3.refs_4_
  30.4 0.2 collective-permute-done.6.refs_7_
  30.5 0.4 collective-permute-done.5.refs_6_
  30.9 0.2 collective-permute-done.4.refs_5_
  31.0 2.1 %shard_map.133 = (bf16[9,64,128]{2,1,0:T(8,128)(2,1)S(1)}, bf16[64,128]{1,0:T(8,128)(2,1)S(1)}, f32[64,16]{1,0:T(8,128)S(1)}, f32[64,128]{1,0:T(8,128)S(1)}, bf16[1152,128]{1,0:T(8,128)(2,1)S(1)}) custom-call(bf16[4,64,128]{2,1,0:T(8,128)(2,1)S(1)} %get-tuple-element.42.refs_0_, bf16[4,64,128]{2,1,0:T(8,128)(2,1)S(1)} %collective-permute-done.refs_1_, ...), custom_call_target="tpu_custom_call" | custom-call | flops 7372800 | bytes 1048576 | tf_op jit(solution)/shard_map/pallas_call | solution.py:615
  33.2 0.4 collective-permute-start.7
  33.6 1.0 %shard_map.134 = (bf16[1,64,128]{2,1,0:T(8,128)(2,1)}, f32[64,1152]{1,0:T(8,128)S(1)}, f32[1,64]{1,0:T(1,128)}, bf16[64,128]{1,0:T(8,128)(2,1)}) custom-call(bf16[1152,128]{1,0:T(8,128)(2,1)S(1)} %get-tuple-element.53.refs_0_, bf16[9,64,128]{2,1,0:T(8,128)(2,1)S(1)} %get-tuple-element.51.refs_1_.refs_0_, ...), custom_call_target="tpu_custom_call" | custom-call | flops 7372800 | bytes 1048576 | tf_op jit(solution)/shard_map/pallas_call | solution.py:615
  34.6 0.0 collective-permute-done.7.refs_1_
  34.6 2.2 %shard_map.135 = f32[32,4,128]{2,1,0:T(4,128)S(1)} custom-call(bf16[9,64,128]{2,1,0:T(8,128)(2,1)S(1)} %get-tuple-element.51.refs_1_.refs_0_, bf16[9,64,128]{2,1,0:T(8,128)(2,1)S(1)} %collective-permute-done.7.refs_1_, f32[64,128]{1,0:T(8,128)S(1)} %get-tuple-element.52.refs_2_, bf16[3,4,64,1152]{3,2,1,0:T(8,128)(2,1)S(1)} %get-tuple-element.43.refs_9_.refs_3_, ...), custom_call_target="tpu_custom_call" | custom-call | flops 7372800 | bytes 1048576 | tf_op jit(solution)/shard_map/pallas_call | solution.py:615
  36.8 9.2 %all_to_all.11.refs_0_ = f32[32,4,128]{2,1,0:T(4,128)S(1)} all-to-all(f32[32,4,128]{2,1,0:T(4,128)S(1)} %shard_map.135), channel_id=1, replica_groups=mesh['gx'=4,'gy'=2,'gz'=4] {'gx','gy','gz'}, dimensions={0} | all-to-all | bytes 131072 | tf_op jit(solution)/shard_map/all_to_all | solution.py:688
  46.0 0.7 %shard_map.136 = f32[3,1,64]{2,1,0:T(1,128)} custom-call(f32[32,4,128]{2,1,0:T(4,128)S(1)} %all_to_all.11.refs_0_), custom_call_target="tpu_custom_call" | custom-call | flops 1048576 | bytes 1048576 | tf_op jit(solution)/shard_map/pallas_call | solution.py:615
Async XLA Ops:
  21.3 7.8 %collective-permute-start.2 = (bf16[4,64,128]{2,1,0:T(8,128)(2,1)S(1)}, bf16[4,64,128]{2,1,0:T(8,128)(2,1)S(1)}, u32[]{:S(2)}, u32[]{:S(2)}) collective-permute-start(bf16[4,64,128]{2,1,0:T(8,128)(2,1)S(1)} %get-tuple-element.41.refs_3_.refs_8_.refs_5_), channel_id=1, source_target_pairs={{16,0},{24,8},{0,16},{8,24},{17,1},{25,9},{1,17},{9,25},{18,2},{26... | collective-permute-start | bytes 196616 | tf_op jit(solution)/shard_map/ppermute | solution.py:680
  22.1 7.5 %collective-permute-start.1 = (bf16[4,64,128]{2,1,0:T(8,128)(2,1)S(1)}, bf16[4,64,128]{2,1,0:T(8,128)(2,1)S(1)}, u32[]{:S(2)}, u32[]{:S(2)}) collective-permute-start(bf16[4,64,128]{2,1,0:T(8,128)(2,1)S(1)} %get-tuple-element.41.refs_3_.refs_8_.refs_5_), channel_id=1, source_target_pairs={{24,0},{25,1},{26,2},{27,3},{28,4},{29,5},{30,6},{31,7},{16,8},{17... | collective-permute-start | bytes 196616 | tf_op jit(solution)/shard_map/ppermute | solution.py:656
  23.5 6.2 %collective-permute-start = (bf16[4,64,128]{2,1,0:T(8,128)(2,1)S(1)}, bf16[4,64,128]{2,1,0:T(8,128)(2,1)S(1)}, u32[]{:S(2)}, u32[]{:S(2)}) collective-permute-start(bf16[4,64,128]{2,1,0:T(8,128)(2,1)S(1)} %get-tuple-element.41.refs_3_.refs_8_.refs_5_), channel_id=1, source_target_pairs={{8,0},{9,1},{10,2},{11,3},{12,4},{13,5},{14,6},{15,7},{0,8},{1,9},... | collective-permute-start | bytes 196616 | tf_op jit(solution)/shard_map/ppermute | solution.py:656
  29.0 1.3 %collective-permute-start.3 = (bf16[4,64,128]{2,1,0:T(8,128)(2,1)S(1)}, bf16[4,64,128]{2,1,0:T(8,128)(2,1)S(1)}, u32[]{:S(2)}, u32[]{:S(2)}) collective-permute-start(bf16[4,64,128]{2,1,0:T(8,128)(2,1)S(1)} %get-tuple-element.42.refs_0_), channel_id=1, source_target_pairs={{4,0},{0,4},{5,1},{1,5},{6,2},{2,6},{7,3},{3,7},{12,8},{8,12},{13,... | collective-permute-start | bytes 196616 | tf_op jit(solution)/shard_map/ppermute | solution.py:666
  29.1 1.4 %collective-permute-start.6 = (bf16[4,64,128]{2,1,0:T(8,128)(2,1)S(1)}, bf16[4,64,128]{2,1,0:T(8,128)(2,1)S(1)}, u32[]{:S(2)}, u32[]{:S(2)}) collective-permute-start(bf16[4,64,128]{2,1,0:T(8,128)(2,1)S(1)} %collective-permute-done.2.refs_3_), channel_id=1, source_target_pairs={{4,0},{0,4},{5,1},{1,5},{6,2},{2,6},{7,3},{3,7},{12,8},{8,12},{13,... | collective-permute-start | bytes 196616 | tf_op jit(solution)/shard_map/ppermute | solution.py:666
  29.6 1.3 %collective-permute-start.5 = (bf16[4,64,128]{2,1,0:T(8,128)(2,1)S(1)}, bf16[4,64,128]{2,1,0:T(8,128)(2,1)S(1)}, u32[]{:S(2)}, u32[]{:S(2)}) collective-permute-start(bf16[4,64,128]{2,1,0:T(8,128)(2,1)S(1)} %collective-permute-done.1.refs_2_), channel_id=1, source_target_pairs={{4,0},{0,4},{5,1},{1,5},{6,2},{2,6},{7,3},{3,7},{12,8},{8,12},{13,... | collective-permute-start | bytes 196616 | tf_op jit(solution)/shard_map/ppermute | solution.py:666
  29.7 1.3 %collective-permute-start.4 = (bf16[4,64,128]{2,1,0:T(8,128)(2,1)S(1)}, bf16[4,64,128]{2,1,0:T(8,128)(2,1)S(1)}, u32[]{:S(2)}, u32[]{:S(2)}) collective-permute-start(bf16[4,64,128]{2,1,0:T(8,128)(2,1)S(1)} %collective-permute-done.refs_1_), channel_id=1, source_target_pairs={{4,0},{0,4},{5,1},{1,5},{6,2},{2,6},{7,3},{3,7},{12,8},{8,12},{13,... | collective-permute-start | bytes 196616 | tf_op jit(solution)/shard_map/ppermute | solution.py:666
  33.2 1.4 %collective-permute-start.7 = (bf16[9,64,128]{2,1,0:T(8,128)(2,1)S(1)}, bf16[9,64,128]{2,1,0:T(8,128)(2,1)S(1)}, u32[]{:S(2)}, u32[]{:S(2)}) collective-permute-start(bf16[9,64,128]{2,1,0:T(8,128)(2,1)S(1)} %get-tuple-element.51.refs_1_.refs_0_), channel_id=1, source_target_pairs={{4,0},{0,4},{5,1},{1,5},{6,2},{2,6},{7,3},{3,7},{12,8},{8,12},{13,... | collective-permute-start | bytes 442376 | tf_op jit(solution)/shard_map/ppermute | solution.py:666

commit v10 on v9

--- a/solution.py
+++ b/solution.py
@@ -401,20 +401,24 @@
         adjoint_ref[which] = adjoint[which * slots : (which + 1) * slots]
 
 
-def slope_kernel(plan, nrefs, places, *refs):
-    far_refs, (rows_ref, cols_ref, layer_ref), refs = refs[:nrefs], refs[nrefs : nrefs + 3], refs[nrefs + 3 :]
-    again_ref, apart_ref, slope_ref, radial_ref, turned_ref, more_ref, more_cols_ref = refs
+def basis_kernel(plan, nrefs, places, *refs):
+    far_ref, (layer_ref, again_ref, more_ref, more_cols_ref) = refs[0], refs[nrefs:]
     again_ref[...] = layer_ref[...]
     for which, target in enumerate(plan.targets[plan.known :]):
-        held, _ = own_columns(plan, global_block(plan, far_refs[0], 0, 0, target))
+        held, _ = own_columns(plan, global_block(plan, far_ref, 0, 0, target))
         more_cols_ref[which] = held
         for tile in range(len(plan.tiles)):
             lanes = slice(tile * plan.width, (tile + 1) * plan.width)
-            blocks = [global_block(plan, far_refs[0], tile, s, target) for s in range(len(plan.sides))]
+            blocks = [global_block(plan, far_ref, tile, s, target) for s in range(len(plan.sides))]
             placed = (side_by_side(plan, blocks) + tile_shift(plan, tile)) * (1.0 / CELL_SIDE)
             basis = basis_of(plan, placed, scaled_columns(held), tile)[2]
             for n in range(plan.nbasis):
                 more_ref[which, n, :, lanes] = basis[n].astype(BF16)
+
+
+def slope_kernel(plan, rows_ref, cols_ref, one_ref, *refs):
+    kept_ref, apart_ref, slope_ref, radial_ref, turned_ref = refs
+    kept_ref[...] = one_ref[...]
     cols = [cols_ref[0, :, axis : axis + 1] for axis in range(3)]
     for tile in range(len(plan.tiles)):
         lanes = slice(tile * plan.width, (tile + 1) * plan.width)
@@ -481,10 +485,11 @@
     slots, nbasis, nspec, width = plan.slots, plan.nbasis, plan.nspec, plan.width
     if plan.small:
         far = [far_refs[side][tile] for tile in range(len(plan.tiles)) for side in range(len(plan.sides))]
-        all_ref[...] = jnp.concatenate(far, axis=0)
+        far = jnp.concatenate(far, axis=0)
     else:
         gather_far(plan, places, far_refs, all_ref)
-    summed = dot(basis_ref[0].reshape(nbasis * slots, plan.far), all_ref[...])
+        far = all_ref[...]
+    summed = dot(basis_ref[0].reshape(nbasis * slots, plan.far), far)
     adjoint = jnp.zeros((slots, summed.shape[1]), F32)
     for n in range(nbasis):
         adjoint = adjoint + summed[n * slots : (n + 1) * slots] * radial_ref[n : n + 1]
@@ -762,16 +767,26 @@
             pair_flops,
         )
         more = max(len(plan.targets) - plan.known, 1)
-        again, apart, slope, factor, turned, more_basis, more_cols = call(
+        again, more_basis, more_cols = call(
+            basis_kernel,
+            plan,
+            far_sent[:1],
+            [layer],
+            [
+                (layer.shape, BF16),
+                ((more, nbasis, slots, plan.far), BF16),
+                ((more, slots, 8), F32),
+            ],
+            [],
+            pair_flops,
+        )
+        one_row, apart, slope, factor, turned = simple_call(
             slope_kernel,
             plan,
-            far_sent[:1],
-            [rows, cols, layer],
-            [(layer.shape, BF16)]
-            + [((count, slots, plan.far), F32) for count in (3, nbasis, nbasis, nbasis)]
-            + [((more, nbasis, slots, plan.far), BF16), ((more, slots, 8), F32)],
-            [],
-            pair_flops,
+            [rows, cols, one_row],
+            [(one_row.shape, F32)]
+            + [((count, slots, plan.far), F32) for count in (3, nbasis, nbasis, nbasis)],
+            flops=pair_flops,
         )
         if plan.small:
             far_layer = from_columns(plan, layer, False, again)

time: 46.9 us -> 46.3 us (0.987)
  waiting for transfers between devices: 0.91 us -> 0.28 us
    ppermute x5, waiting for transfers between devices: 0.9 us -> 0.27 us  [along(): lax.ppermute(block, axis, [(source, i) for i, source in enumerate(sources)])]
    pallas_call x7 -> x8, Pallas kernels: 15.6 us -> 15.8 us  [simple_call(): pl.pallas_call(body, out_shape=shapes, in_specs=[SMEM_SPEC] * scalars + [...]
  transfers between devices with their start and end apart: 8 -> 8, of which waited for: 4 -> 1; matrix products, arithmetic and copies ran while one was open for 0% -> 0% of each run, Pallas kernels for 11% -> 12%
where the time goes in v10:
time: 46.3 us; the launch traced here: 46.1 us
  blocking collectives  23.8 us (51%)
  Pallas kernels  15.8 us (34%)
  starting transfers between devices  4.78 us (10%)
  between operations  1.37 us (3%)
    all_to_all x2, blocking collectives, everywhere(): return lax.all_to_all(copies, AXES, 0, 0, tiled=True)  23.8 us
    pallas_call x8, Pallas kernels, simple_call(): pl.pallas_call(body, out_shape=shapes, in_specs=[SMEM_SPEC] * scalars + [...  15.8 us
    ppermute x2, starting transfers between devices, brought(): got.append(lax.ppermute(block, AXES, pairs))  2.81 us
    ppermute x5, starting transfers between devices, along(): lax.ppermute(block, axis, [(source, i) for i, source in enumerate(sources)])  1.22 us
  transfers between devices with their start and end apart: 8, of which 1 were waited for; matrix products, arithmetic and copies ran while one was open for 0% of the time, Pallas kernels for 12%

profile of v10, /device:TPU:0, one launch (start us, length us, event | category | flops | bytes accessed | tf_op | source)
XLA Modules:
  0.0 46.1 jit_solution(16200403709393254218)
XLA Ops:
  1.3 1.0 %shard_map.130 = (f32[32,4,128]{2,1,0:T(4,128)S(1)}, bf16[2,32,128]{2,1,0:T(8,128)(2,1)S(1)}, bf16[160,384]{1,0:T(8,128)(2,1)S(1)}, bf16[8,128]{1,0:T(8,128)(2,1...) custom-call(s32[1]{0:T(128)} %bitcast.12.refs_0_, ...), custom_call_target="tpu_custom_call" | custom-call | flops 1048576 | bytes 1048576 | tf_op jit(solution)/shard_map/pallas_call | solution.py:620
  2.3 14.6 %all_to_all.10.refs_0_ = f32[32,4,128]{2,1,0:T(4,128)S(1)} all-to-all(f32[32,4,128]{2,1,0:T(4,128)S(1)} %get-tuple-element.35), channel_id=1, replica_groups=mesh['gx'=4,'gy'=2,'gz'=4] {'gx','gy','gz'}, dimensions={0} | all-to-all | bytes 131072 | tf_op jit(solution)/shard_map/all_to_all | solution.py:693
  16.9 4.4 %shard_map.131 = (f32[9,4,128]{2,1,0:T(4,128)S(1)}, bf16[3,4,64,1152]{3,2,1,0:T(8,128)(2,1)S(1)}, bf16[4,64,128]{2,1,0:T(8,128)(2,1)S(1)}, f32[192,128]{1,0:T(8,...) custom-call(f32[32,4,128]{2,1,0:T(4,128)S(1)} %all_to_all.10.refs_0_, ...), custom_call_target="tpu_custom_call" | custom-call | flops 7372800 | bytes 1048576 | tf_op jit(solution)/shard_map/pallas_call | solution.py:620
  21.3 0.7 %collective-permute-start.2 = (bf16[4,64,128]{2,1,0:T(8,128)(2,1)S(1)}, bf16[4,64,128]{2,1,0:T(8,128)(2,1)S(1)}, u32[]{:S(2)}, u32[]{:S(2)}) collective-permute-start(bf16[4,64,128]{2,1,0:T(8,128)(2,1)S(1)} %get-tuple-element.40.refs_1_.refs_8_.refs_5_), channel_id=1, source_target_pairs={{16,0},{24,8},{0,16},{8,24},{17,1},{25,9},{1,17},{9,25},{18,2},{26... | collective-permute-start | bytes 196616 | tf_op jit(solution)/shard_map/ppermute | solution.py:685
  22.1 1.4 %collective-permute-start.1 = (bf16[4,64,128]{2,1,0:T(8,128)(2,1)S(1)}, bf16[4,64,128]{2,1,0:T(8,128)(2,1)S(1)}, u32[]{:S(2)}, u32[]{:S(2)}) collective-permute-start(bf16[4,64,128]{2,1,0:T(8,128)(2,1)S(1)} %get-tuple-element.40.refs_1_.refs_8_.refs_5_), channel_id=1, source_target_pairs={{24,0},{25,1},{26,2},{27,3},{28,4},{29,5},{30,6},{31,7},{16,8},{17... | collective-permute-start | bytes 196616 | tf_op jit(solution)/shard_map/ppermute | solution.py:661
  23.5 1.4 %collective-permute-start = (bf16[4,64,128]{2,1,0:T(8,128)(2,1)S(1)}, bf16[4,64,128]{2,1,0:T(8,128)(2,1)S(1)}, u32[]{:S(2)}, u32[]{:S(2)}) collective-permute-start(bf16[4,64,128]{2,1,0:T(8,128)(2,1)S(1)} %get-tuple-element.40.refs_1_.refs_8_.refs_5_), channel_id=1, source_target_pairs={{8,0},{9,1},{10,2},{11,3},{12,4},{13,5},{14,6},{15,7},{0,8},{1,9},... | collective-permute-start | bytes 196616 | tf_op jit(solution)/shard_map/ppermute | solution.py:661
  24.9 3.3 %shard_map.132 = (bf16[4,64,128]{2,1,0:T(8,128)(2,1)S(1)}, bf16[6,4,64,1152]{3,2,1,0:T(8,128)(2,1)S(1)}, f32[6,64,8]{2,1,0:T(8,128)S(1)}) custom-call(f32[32,4,128]{2,1,0:T(4,128)S(1)} %all_to_all.10.refs_0_, bf16[4,64,128]{2,1,0:T(8,128)(2,1)S(1)} %get-tuple-element.40.refs_1_.refs_8_.refs_5_), custom_call_target="tpu_custom_call" | custom-call | flops 7372800 | bytes 1048576 | tf_op jit(solution)/shard_map/pallas_call | solution.py:620
  28.2 0.1 collective-permute-start.3
  28.3 0.0 collective-permute-done.2.refs_3_
  28.3 0.5 %collective-permute-start.6 = (bf16[4,64,128]{2,1,0:T(8,128)(2,1)S(1)}, bf16[4,64,128]{2,1,0:T(8,128)(2,1)S(1)}, u32[]{:S(2)}, u32[]{:S(2)}) collective-permute-start(bf16[4,64,128]{2,1,0:T(8,128)(2,1)S(1)} %collective-permute-done.2.refs_3_), channel_id=1, source_target_pairs={{4,0},{0,4},{5,1},{1,5},{6,2},{2,6},{7,3},{3,7},{12,8},{8,12},{13,... | collective-permute-start | bytes 196616 | tf_op jit(solution)/shard_map/ppermute | solution.py:671
  28.8 0.0 collective-permute-done.1.refs_2_
  28.8 0.1 collective-permute-start.5
  28.9 0.0 collective-permute-done.refs_1_
  28.9 0.4 collective-permute-start.4
  29.3 1.2 %shard_map.133 = (f32[1,128]{1,0:T(1,128)S(1)}, f32[3,64,1152]{2,1,0:T(8,128)S(1)}, f32[4,64,1152]{2,1,0:T(8,128)S(1)}, f32[4,64,1152]{2,1,0:T(8,128)S(1)}, f32[4,64,1152]{2,1,0:T(8,128)S(1)}) custom-call(f32[9,4,128]{2,1,0:T(4,128)S(1)} %get-tuple-element.50.refs_0_.refs_5_, f32[3,64,8]{2,1,0:T(8,128)S(1)} %get-tuple-element.43.refs_1_.refs_10_.refs_4_, ...), custom_call_target="tpu_custom_call" | custom-call | flops 7372800 | bytes 1048576 | tf_op jit(solution)/shard_map/pallas_call | solution.py:620
  30.5 0.0 collective-permute-done.3.refs_4_
  30.5 0.0 collective-permute-done.6.refs_7_
  30.5 0.0 collective-permute-done.5.refs_6_
  30.5 0.0 collective-permute-done.4.refs_5_
  30.5 2.1 %shard_map.134 = (bf16[9,64,128]{2,1,0:T(8,128)(2,1)S(1)}, bf16[64,128]{1,0:T(8,128)(2,1)S(1)}, f32[64,16]{1,0:T(8,128)S(1)}, f32[64,128]{1,0:T(8,128)S(1)}, bf16[1152,128]{1,0:T(8,128)(2,1)S(1)}) custom-call(bf16[4,64,128]{2,1,0:T(8,128)(2,1)S(1)} %get-tuple-element.41.refs_0_, bf16[4,64,128]{2,1,0:T(8,128)(2,1)S(1)} %collective-permute-done.refs_1_, ...), custom_call_target="tpu_custom_call" | custom-call | flops 7372800 | bytes 1048576 | tf_op jit(solution)/shard_map/pallas_call | solution.py:620
  32.6 0.2 collective-permute-start.7
  32.8 1.0 %shard_map.135 = (bf16[1,64,128]{2,1,0:T(8,128)(2,1)}, f32[64,1152]{1,0:T(8,128)S(1)}, f32[1,64]{1,0:T(1,128)}, bf16[64,128]{1,0:T(8,128)(2,1)}) custom-call(bf16[1152,128]{1,0:T(8,128)(2,1)S(1)} %get-tuple-element.55.refs_0_, bf16[9,64,128]{2,1,0:T(8,128)(2,1)S(1)} %get-tuple-element.53.refs_1_.refs_0_, ...), custom_call_target="tpu_custom_call" | custom-call | flops 7372800 | bytes 1048576 | tf_op jit(solution)/shard_map/pallas_call | solution.py:620
  33.8 0.3 collective-permute-done.7.refs_1_
  34.1 2.1 %shard_map.136 = f32[32,4,128]{2,1,0:T(4,128)S(1)} custom-call(bf16[9,64,128]{2,1,0:T(8,128)(2,1)S(1)} %get-tuple-element.53.refs_1_.refs_0_, bf16[9,64,128]{2,1,0:T(8,128)(2,1)S(1)} %collective-permute-done.7.refs_1_, f32[64,128]{1,0:T(8,128)S(1)} %get-tuple-element.54.refs_2_, bf16[3,4,64,1152]{3,2,1,0:T(8,128)(2,1)S(1)} %get-tuple-element.42.refs_9_.refs_3_, ...), custom_call_target="tpu_custom_call" | custom-call | flops 7372800 | bytes 1048576 | tf_op jit(solution)/shard_map/pallas_call | solution.py:620
  36.2 9.2 %all_to_all.11.refs_0_ = f32[32,4,128]{2,1,0:T(4,128)S(1)} all-to-all(f32[32,4,128]{2,1,0:T(4,128)S(1)} %shard_map.136), channel_id=1, replica_groups=mesh['gx'=4,'gy'=2,'gz'=4] {'gx','gy','gz'}, dimensions={0} | all-to-all | bytes 131072 | tf_op jit(solution)/shard_map/all_to_all | solution.py:693
  45.4 0.7 %shard_map.137 = f32[3,1,64]{2,1,0:T(1,128)} custom-call(f32[32,4,128]{2,1,0:T(4,128)S(1)} %all_to_all.11.refs_0_), custom_call_target="tpu_custom_call" | custom-call | flops 1048576 | bytes 1048576 | tf_op jit(solution)/shard_map/pallas_call | solution.py:620
Async XLA Ops:
  21.3 6.9 %collective-permute-start.2 = (bf16[4,64,128]{2,1,0:T(8,128)(2,1)S(1)}, bf16[4,64,128]{2,1,0:T(8,128)(2,1)S(1)}, u32[]{:S(2)}, u32[]{:S(2)}) collective-permute-start(bf16[4,64,128]{2,1,0:T(8,128)(2,1)S(1)} %get-tuple-element.40.refs_1_.refs_8_.refs_5_), channel_id=1, source_target_pairs={{16,0},{24,8},{0,16},{8,24},{17,1},{25,9},{1,17},{9,25},{18,2},{26... | collective-permute-start | bytes 196616 | tf_op jit(solution)/shard_map/ppermute | solution.py:685
  22.1 6.7 %collective-permute-start.1 = (bf16[4,64,128]{2,1,0:T(8,128)(2,1)S(1)}, bf16[4,64,128]{2,1,0:T(8,128)(2,1)S(1)}, u32[]{:S(2)}, u32[]{:S(2)}) collective-permute-start(bf16[4,64,128]{2,1,0:T(8,128)(2,1)S(1)} %get-tuple-element.40.refs_1_.refs_8_.refs_5_), channel_id=1, source_target_pairs={{24,0},{25,1},{26,2},{27,3},{28,4},{29,5},{30,6},{31,7},{16,8},{17... | collective-permute-start | bytes 196616 | tf_op jit(solution)/shard_map/ppermute | solution.py:661
  23.5 5.3 %collective-permute-start = (bf16[4,64,128]{2,1,0:T(8,128)(2,1)S(1)}, bf16[4,64,128]{2,1,0:T(8,128)(2,1)S(1)}, u32[]{:S(2)}, u32[]{:S(2)}) collective-permute-start(bf16[4,64,128]{2,1,0:T(8,128)(2,1)S(1)} %get-tuple-element.40.refs_1_.refs_8_.refs_5_), channel_id=1, source_target_pairs={{8,0},{9,1},{10,2},{11,3},{12,4},{13,5},{14,6},{15,7},{0,8},{1,9},... | collective-permute-start | bytes 196616 | tf_op jit(solution)/shard_map/ppermute | solution.py:661
  28.2 2.3 %collective-permute-start.3 = (bf16[4,64,128]{2,1,0:T(8,128)(2,1)S(1)}, bf16[4,64,128]{2,1,0:T(8,128)(2,1)S(1)}, u32[]{:S(2)}, u32[]{:S(2)}) collective-permute-start(bf16[4,64,128]{2,1,0:T(8,128)(2,1)S(1)} %get-tuple-element.41.refs_0_), channel_id=1, source_target_pairs={{4,0},{0,4},{5,1},{1,5},{6,2},{2,6},{7,3},{3,7},{12,8},{8,12},{13,... | collective-permute-start | bytes 196616 | tf_op jit(solution)/shard_map/ppermute | solution.py:671
  28.3 2.2 %collective-permute-start.6 = (bf16[4,64,128]{2,1,0:T(8,128)(2,1)S(1)}, bf16[4,64,128]{2,1,0:T(8,128)(2,1)S(1)}, u32[]{:S(2)}, u32[]{:S(2)}) collective-permute-start(bf16[4,64,128]{2,1,0:T(8,128)(2,1)S(1)} %collective-permute-done.2.refs_3_), channel_id=1, source_target_pairs={{4,0},{0,4},{5,1},{1,5},{6,2},{2,6},{7,3},{3,7},{12,8},{8,12},{13,... | collective-permute-start | bytes 196616 | tf_op jit(solution)/shard_map/ppermute | solution.py:671
  28.8 1.7 %collective-permute-start.5 = (bf16[4,64,128]{2,1,0:T(8,128)(2,1)S(1)}, bf16[4,64,128]{2,1,0:T(8,128)(2,1)S(1)}, u32[]{:S(2)}, u32[]{:S(2)}) collective-permute-start(bf16[4,64,128]{2,1,0:T(8,128)(2,1)S(1)} %collective-permute-done.1.refs_2_), channel_id=1, source_target_pairs={{4,0},{0,4},{5,1},{1,5},{6,2},{2,6},{7,3},{3,7},{12,8},{8,12},{13,... | collective-permute-start | bytes 196616 | tf_op jit(solution)/shard_map/ppermute | solution.py:671
  28.9 1.6 %collective-permute-start.4 = (bf16[4,64,128]{2,1,0:T(8,128)(2,1)S(1)}, bf16[4,64,128]{2,1,0:T(8,128)(2,1)S(1)}, u32[]{:S(2)}, u32[]{:S(2)}) collective-permute-start(bf16[4,64,128]{2,1,0:T(8,128)(2,1)S(1)} %collective-permute-done.refs_1_), channel_id=1, source_target_pairs={{4,0},{0,4},{5,1},{1,5},{6,2},{2,6},{7,3},{3,7},{12,8},{8,12},{13,... | collective-permute-start | bytes 196616 | tf_op jit(solution)/shard_map/ppermute | solution.py:671
  32.6 1.4 %collective-permute-start.7 = (bf16[9,64,128]{2,1,0:T(8,128)(2,1)S(1)}, bf16[9,64,128]{2,1,0:T(8,128)(2,1)S(1)}, u32[]{:S(2)}, u32[]{:S(2)}) collective-permute-start(bf16[9,64,128]{2,1,0:T(8,128)(2,1)S(1)} %get-tuple-element.53.refs_1_.refs_0_), channel_id=1, source_target_pairs={{4,0},{0,4},{5,1},{1,5},{6,2},{2,6},{7,3},{3,7},{12,8},{8,12},{13,... | collective-permute-start | bytes 442376 | tf_op jit(solution)/shard_map/ppermute | solution.py:671

commit v11 on v10

--- a/solution.py
+++ b/solution.py
@@ -316,7 +316,7 @@
             x = matched(m, turn) if m < plan.wide else m
             for z in range(len(plan.column)):
                 place = (x * len(plan.column) + z) * len(plan.sides) + side
-                put(place, far_refs[side * len(plan.columns) + m][z])
+                put(place, far_refs[m][z] if side == 0 else far_refs[len(plan.columns)][m, z])
 
 
 def far_blocks(plan, block_ref, target):
@@ -678,15 +678,18 @@
     return from_columns(plan, column, plan.mixed)
 
 
-def from_columns(plan, column, mixed, again=None):
+def from_columns(plan, column, mixed):
     columns = [column] + brought(plan, column, True, mixed)
+    swapped = [[column] + along(column, "gy") for column in columns]
+    return [column[side] for side in range(len(plan.sides)) for column in swapped]
+
+
+def held_columns(plan, column, again):
     count = plan.sizes["gx"]
+    columns = brought(plan, column, True, False)
     for step in plan.columns[plan.wide :]:
         columns.append(lax.ppermute(column, "gx", [((i + step) % count, i) for i in range(count)]))
-    if again is not None:
-        columns[0] = again
-    swapped = [[column] + along(column, "gy") for column in columns]
-    return [column[side] for side in range(len(plan.sides)) for column in swapped]
+    return [column, *columns] + along(jnp.stack([again, *columns]), "gy")
 
 
 def everywhere(copies):
@@ -789,7 +792,7 @@
             flops=pair_flops,
         )
         if plan.small:
-            far_layer = from_columns(plan, layer, False, again)
+            far_layer = held_columns(plan, layer, again)
         else:
             far_layer = neighbours(plan, layer[0], again[0])
         far_scratch = ((plan.far, channels), BF16)

time: 46.3 us -> 45.6 us (0.985)
  starting transfers between devices: 4.78 us -> 3.86 us
    ppermute x5 -> x2, starting transfers between devices: 1.22 us -> 0.31 us  [along(): lax.ppermute(block, axis, [(source, i) for i, source in enumerate(sources)])]
  transfers between devices with their start and end apart: 8 -> 5, of which waited for: 1 -> 2; matrix products, arithmetic and copies ran while one was open for 0% -> 0% of each run, Pallas kernels for 12% -> 12%
where the time goes in v11:
time: 45.6 us; the launch traced here: 45.4 us
  blocking collectives  23.8 us (52%)
  Pallas kernels  15.8 us (35%)
  starting transfers between devices  3.86 us (8%)
  between operations  1.36 us (3%)
  waiting for transfers between devices  0.52 us (1%)
    all_to_all x2, blocking collectives, everywhere(): return lax.all_to_all(copies, AXES, 0, 0, tiled=True)  23.8 us
    pallas_call x8, Pallas kernels, simple_call(): pl.pallas_call(body, out_shape=shapes, in_specs=[SMEM_SPEC] * scalars + [...  15.8 us
    ppermute x2, starting transfers between devices, brought(): got.append(lax.ppermute(block, AXES, pairs))  2.81 us
  transfers between devices with their start and end apart: 5, of which 2 were waited for; matrix products, arithmetic and copies ran while one was open for 0% of the time, Pallas kernels for 12%

profile of v11, /device:TPU:0, one launch (start us, length us, event | category | flops | bytes accessed | tf_op | source)
XLA Modules:
  0.0 45.4 jit_solution(14119435707452063348)
XLA Ops:
  1.3 1.0 %shard_map.130 = (f32[32,4,128]{2,1,0:T(4,128)S(1)}, bf16[2,32,128]{2,1,0:T(8,128)(2,1)S(1)}, bf16[160,384]{1,0:T(8,128)(2,1)S(1)}, bf16[8,128]{1,0:T(8,128)(2,1...) custom-call(s32[1]{0:T(128)} %bitcast.16.refs_0_, ...), custom_call_target="tpu_custom_call" | custom-call | flops 1048576 | bytes 1048576 | tf_op jit(solution)/shard_map/pallas_call | solution.py:620
  2.3 14.6 %all_to_all.10.refs_0_ = f32[32,4,128]{2,1,0:T(4,128)S(1)} all-to-all(f32[32,4,128]{2,1,0:T(4,128)S(1)} %get-tuple-element.35), channel_id=1, replica_groups=mesh['gx'=4,'gy'=2,'gz'=4] {'gx','gy','gz'}, dimensions={0} | all-to-all | bytes 131072 | tf_op jit(solution)/shard_map/all_to_all | solution.py:696
  16.9 4.4 %shard_map.131 = (f32[9,4,128]{2,1,0:T(4,128)S(1)}, bf16[3,4,64,1152]{3,2,1,0:T(8,128)(2,1)S(1)}, bf16[4,64,128]{2,1,0:T(8,128)(2,1)S(1)}, f32[192,128]{1,0:T(8,...) custom-call(f32[32,4,128]{2,1,0:T(4,128)S(1)} %all_to_all.10.refs_0_, ...), custom_call_target="tpu_custom_call" | custom-call | flops 7372800 | bytes 1048576 | tf_op jit(solution)/shard_map/pallas_call | solution.py:620
  21.3 0.7 %collective-permute-start.2 = (bf16[4,64,128]{2,1,0:T(8,128)(2,1)S(1)}, bf16[4,64,128]{2,1,0:T(8,128)(2,1)S(1)}, u32[]{:S(2)}, u32[]{:S(2)}) collective-permute-start(bf16[4,64,128]{2,1,0:T(8,128)(2,1)S(1)} %get-tuple-element.40.refs_1_.refs_0_.refs_5_), channel_id=1, source_target_pairs={{16,0},{24,8},{0,16},{8,24},{17,1},{25,9},{1,17},{9,25},{18,2},{26... | collective-permute-start | bytes 196616 | tf_op jit(solution)/shard_map/ppermute | solution.py:691
  22.1 1.4 %collective-permute-start.1 = (bf16[4,64,128]{2,1,0:T(8,128)(2,1)S(1)}, bf16[4,64,128]{2,1,0:T(8,128)(2,1)S(1)}, u32[]{:S(2)}, u32[]{:S(2)}) collective-permute-start(bf16[4,64,128]{2,1,0:T(8,128)(2,1)S(1)} %get-tuple-element.40.refs_1_.refs_0_.refs_5_), channel_id=1, source_target_pairs={{24,0},{25,1},{26,2},{27,3},{28,4},{29,5},{30,6},{31,7},{16,8},{17... | collective-permute-start | bytes 196616 | tf_op jit(solution)/shard_map/ppermute | solution.py:661
  23.5 1.4 %collective-permute-start = (bf16[4,64,128]{2,1,0:T(8,128)(2,1)S(1)}, bf16[4,64,128]{2,1,0:T(8,128)(2,1)S(1)}, u32[]{:S(2)}, u32[]{:S(2)}) collective-permute-start(bf16[4,64,128]{2,1,0:T(8,128)(2,1)S(1)} %get-tuple-element.40.refs_1_.refs_0_.refs_5_), channel_id=1, source_target_pairs={{8,0},{9,1},{10,2},{11,3},{12,4},{13,5},{14,6},{15,7},{0,8},{1,9},... | collective-permute-start | bytes 196616 | tf_op jit(solution)/shard_map/ppermute | solution.py:661
  24.9 3.3 %shard_map.132 = (bf16[4,64,128]{2,1,0:T(8,128)(2,1)S(1)}, bf16[6,4,64,1152]{3,2,1,0:T(8,128)(2,1)S(1)}, f32[6,64,8]{2,1,0:T(8,128)S(1)}) custom-call(f32[32,4,128]{2,1,0:T(4,128)S(1)} %all_to_all.10.refs_0_, bf16[4,64,128]{2,1,0:T(8,128)(2,1)S(1)} %get-tuple-element.40.refs_1_.refs_0_.refs_5_), custom_call_target="tpu_custom_call" | custom-call | flops 7372800 | bytes 1048576 | tf_op jit(solution)/shard_map/pallas_call | solution.py:620
  28.2 0.0 collective-permute-done.2.refs_3_
  28.2 0.0 collective-permute-done.1.refs_2_
  28.2 0.0 collective-permute-done.refs_1_
  28.3 0.1 collective-permute-start.3
  28.3 1.2 %shard_map.133 = (f32[1,128]{1,0:T(1,128)S(1)}, f32[3,64,1152]{2,1,0:T(8,128)S(1)}, f32[4,64,1152]{2,1,0:T(8,128)S(1)}, f32[4,64,1152]{2,1,0:T(8,128)S(1)}, f32[4,64,1152]{2,1,0:T(8,128)S(1)}) custom-call(f32[9,4,128]{2,1,0:T(4,128)S(1)} %get-tuple-element.50.refs_0_.refs_5_, f32[3,64,8]{2,1,0:T(8,128)S(1)} %get-tuple-element.43.refs_1_.refs_7_.refs_4_, ...), custom_call_target="tpu_custom_call" | custom-call | flops 7372800 | bytes 1048576 | tf_op jit(solution)/shard_map/pallas_call | solution.py:620
  29.5 0.3 collective-permute-done.3.refs_4_
  29.9 2.1 %shard_map.134 = (bf16[9,64,128]{2,1,0:T(8,128)(2,1)S(1)}, bf16[64,128]{1,0:T(8,128)(2,1)S(1)}, f32[64,16]{1,0:T(8,128)S(1)}, f32[64,128]{1,0:T(8,128)S(1)}, bf16[1152,128]{1,0:T(8,128)(2,1)S(1)}) custom-call(bf16[4,64,128]{2,1,0:T(8,128)(2,1)S(1)} %get-tuple-element.40.refs_1_.refs_0_.refs_5_, bf16[4,64,128]{2,1,0:T(8,128)(2,1)S(1)} %collective-permute-done.refs_1_, ...), custom_call_target="tpu_custom_call" | custom-call | flops 7372800 | bytes 1048576 | tf_op jit(solution)/shard_map/pallas_call | solution.py:620
  32.0 0.2 collective-permute-start.4
  32.2 1.0 %shard_map.135 = (bf16[1,64,128]{2,1,0:T(8,128)(2,1)}, f32[64,1152]{1,0:T(8,128)S(1)}, f32[1,64]{1,0:T(1,128)}, bf16[64,128]{1,0:T(8,128)(2,1)}) custom-call(bf16[1152,128]{1,0:T(8,128)(2,1)S(1)} %get-tuple-element.55.refs_0_, bf16[9,64,128]{2,1,0:T(8,128)(2,1)S(1)} %get-tuple-element.53.refs_1_.refs_0_, ...), custom_call_target="tpu_custom_call" | custom-call | flops 7372800 | bytes 1048576 | tf_op jit(solution)/shard_map/pallas_call | solution.py:620
  33.3 0.2 collective-permute-done.4.refs_1_
  33.4 2.1 %shard_map.136 = f32[32,4,128]{2,1,0:T(4,128)S(1)} custom-call(bf16[9,64,128]{2,1,0:T(8,128)(2,1)S(1)} %get-tuple-element.53.refs_1_.refs_0_, bf16[9,64,128]{2,1,0:T(8,128)(2,1)S(1)} %collective-permute-done.4.refs_1_, f32[64,128]{1,0:T(8,128)S(1)} %get-tuple-element.54.refs_2_, bf16[3,4,64,1152]{3,2,1,0:T(8,128)(2,1)S(1)} %get-tuple-element.42.refs_6_.refs_3_, ...), custom_call_target="tpu_custom_call" | custom-call | flops 7372800 | bytes 1048576 | tf_op jit(solution)/shard_map/pallas_call | solution.py:620
  35.6 9.2 %all_to_all.11.refs_0_ = f32[32,4,128]{2,1,0:T(4,128)S(1)} all-to-all(f32[32,4,128]{2,1,0:T(4,128)S(1)} %shard_map.136), channel_id=1, replica_groups=mesh['gx'=4,'gy'=2,'gz'=4] {'gx','gy','gz'}, dimensions={0} | all-to-all | bytes 131072 | tf_op jit(solution)/shard_map/all_to_all | solution.py:696
  44.7 0.7 %shard_map.137 = f32[3,1,64]{2,1,0:T(1,128)} custom-call(f32[32,4,128]{2,1,0:T(4,128)S(1)} %all_to_all.11.refs_0_), custom_call_target="tpu_custom_call" | custom-call | flops 1048576 | bytes 1048576 | tf_op jit(solution)/shard_map/pallas_call | solution.py:620
  (1 shorter events, 0.0 us)
Async XLA Ops:
  21.3 6.9 %collective-permute-start.2 = (bf16[4,64,128]{2,1,0:T(8,128)(2,1)S(1)}, bf16[4,64,128]{2,1,0:T(8,128)(2,1)S(1)}, u32[]{:S(2)}, u32[]{:S(2)}) collective-permute-start(bf16[4,64,128]{2,1,0:T(8,128)(2,1)S(1)} %get-tuple-element.40.refs_1_.refs_0_.refs_5_), channel_id=1, source_target_pairs={{16,0},{24,8},{0,16},{8,24},{17,1},{25,9},{1,17},{9,25},{18,2},{26... | collective-permute-start | bytes 196616 | tf_op jit(solution)/shard_map/ppermute | solution.py:691
  22.1 6.1 %collective-permute-start.1 = (bf16[4,64,128]{2,1,0:T(8,128)(2,1)S(1)}, bf16[4,64,128]{2,1,0:T(8,128)(2,1)S(1)}, u32[]{:S(2)}, u32[]{:S(2)}) collective-permute-start(bf16[4,64,128]{2,1,0:T(8,128)(2,1)S(1)} %get-tuple-element.40.refs_1_.refs_0_.refs_5_), channel_id=1, source_target_pairs={{24,0},{25,1},{26,2},{27,3},{28,4},{29,5},{30,6},{31,7},{16,8},{17... | collective-permute-start | bytes 196616 | tf_op jit(solution)/shard_map/ppermute | solution.py:661
  23.5 4.7 %collective-permute-start = (bf16[4,64,128]{2,1,0:T(8,128)(2,1)S(1)}, bf16[4,64,128]{2,1,0:T(8,128)(2,1)S(1)}, u32[]{:S(2)}, u32[]{:S(2)}) collective-permute-start(bf16[4,64,128]{2,1,0:T(8,128)(2,1)S(1)} %get-tuple-element.40.refs_1_.refs_0_.refs_5_), channel_id=1, source_target_pairs={{8,0},{9,1},{10,2},{11,3},{12,4},{13,5},{14,6},{15,7},{0,8},{1,9},... | collective-permute-start | bytes 196616 | tf_op jit(solution)/shard_map/ppermute | solution.py:661
  28.3 1.6 %collective-permute-start.3 = (bf16[4,4,64,128]{3,2,1,0:T(8,128)(2,1)S(1)}, bf16[4,4,64,128]{3,2,1,0:T(8,128)(2,1)S(1)}, u32[]{:S(2)}, u32[]{:S(2)}) collective-permute-start(bf16[4,4,64,128]{3,2,1,0:T(8,128)(2,1)S(1)} %pad_maximum_fusion), channel_id=1, source_target_pairs={{4,0},{0,4},{5,1},{1,5},{6,2},{2,6},{7,3},{3,7},{12,8},{8,12},{13,... | collective-permute-start | bytes 786440 | tf_op jit(solution)/shard_map/ppermute | solution.py:671
  32.0 1.4 %collective-permute-start.4 = (bf16[9,64,128]{2,1,0:T(8,128)(2,1)S(1)}, bf16[9,64,128]{2,1,0:T(8,128)(2,1)S(1)}, u32[]{:S(2)}, u32[]{:S(2)}) collective-permute-start(bf16[9,64,128]{2,1,0:T(8,128)(2,1)S(1)} %get-tuple-element.53.refs_1_.refs_0_), channel_id=1, source_target_pairs={{4,0},{0,4},{5,1},{1,5},{6,2},{2,6},{7,3},{3,7},{12,8},{8,12},{13,... | collective-permute-start | bytes 442376 | tf_op jit(solution)/shard_map/ppermute | solution.py:671

commit v12 on v11

--- a/solution.py
+++ b/solution.py
@@ -565,8 +565,8 @@
 
 
 def prepare_kernel(plan, counts_ref, *refs):
-    fetched, (sent_ref, table_ref, wide_ref), refs = refs[:10], refs[10:13], refs[13:]
-    kept, (place_ref, kind_ref, radial_ref, sems) = refs[:7], refs[7:]
+    embed_ref, fetched, (sent_ref, table_ref, wide_ref, again_ref) = refs[0], refs[1:10], refs[10:14]
+    kept, (place_ref, kind_ref, radial_ref, sems) = refs[14:20], refs[20:]
     copies = begin(zip(fetched, (place_ref, kind_ref, radial_ref, *kept)), sems)
     for copy in copies[:2]:
         copy.wait()
@@ -583,11 +583,11 @@
         sent_ref[copy] = rows
     for copy in copies[2:]:
         copy.wait()
-    embed, nspec = kept[0][...].astype(F32), plan.nspec
+    again_ref[...] = embed_ref[...]
+    embed = embed_ref[...].astype(F32)
     for g in range(2):
-        for n in range(plan.nbasis):
-            weighted = radial_ref[g, n : n + 1] * embed
-            table_ref[g, n * nspec : (n + 1) * nspec] = weighted.astype(BF16)
+        weighted = [radial_ref[g, n : n + 1] * embed for n in range(plan.nbasis)]
+        table_ref[g] = jnp.concatenate(weighted, axis=0).astype(BF16)
     wide_ref[...] = jnp.zeros_like(wide_ref)
     count, channels = table_ref.shape[1:]
     for m in range(1 + 2 * len(plan.plain)):
@@ -731,15 +731,16 @@
         nbasis, nspec = radial_two.shape[0], embed.shape[0]
         plan = Plan(mesh, slots, nbasis, nspec)
         given = [positions[0, 0, 0].reshape(3, 1, slots), species.reshape(1, slots), radial_one]
-        weights = [embed, mix_one, radial_two, read_out[None], read_one[None], mix_two, read_hidden]
-        sent, table, wide, *weights = simple_call(
+        weights = [mix_one, radial_two, read_out[None], read_one[None], mix_two, read_hidden]
+        sent, table, wide, embed, *weights = simple_call(
             prepare_kernel,
             plan,
-            [counts.reshape(1), *given, *weights],
+            [counts.reshape(1), embed, *given, *weights],
             [
                 ((plan.ndev if plan.small else 1, 4, 2 * slots), F32),
                 ((2, nbasis * nspec, channels), BF16),
                 (((1 + 2 * len(plan.plain)) * nbasis * nspec, (1 + len(plan.plain)) * channels), BF16),
+                (embed.shape, BF16),
             ]
             + [(weight.shape, weight.dtype) for weight in weights],
             1,
@@ -747,7 +748,7 @@
             near=True,
             fetched=len(given) + len(weights),
         )
-        embed, mix_one, radial_two, out_row, one_row, mix_two, read_hidden = weights
+        mix_one, radial_two, out_row, one_row, mix_two, read_hidden = weights
         far_sent = [everywhere(sent)] if plan.small else neighbours(plan, sent[0])
         pair_flops = 100 * slots * plan.far
         rows, basis, layer, vector, mixing, cols = call(

time: 45.6 us -> 46.3 us (1.015)
  Pallas kernels: 15.8 us -> 16.5 us
    pallas_call x8, Pallas kernels: 15.8 us -> 16.5 us  [simple_call(): pl.pallas_call(body, out_shape=shapes, in_specs=[SMEM_SPEC] * scalars + [...]
where the time goes in v12:
time: 46.3 us; the launch traced here: 46.1 us
  blocking collectives  23.8 us (51%)
  Pallas kernels  16.5 us (36%)
  starting transfers between devices  3.86 us (8%)
  between operations  1.36 us (3%)
  waiting for transfers between devices  0.52 us (1%)
    all_to_all x2, blocking collectives, everywhere(): return lax.all_to_all(copies, AXES, 0, 0, tiled=True)  23.8 us
    pallas_call x8, Pallas kernels, simple_call(): pl.pallas_call(body, out_shape=shapes, in_specs=[SMEM_SPEC] * scalars + [...  16.5 us
    ppermute x2, starting transfers between devices, brought(): got.append(lax.ppermute(block, AXES, pairs))  2.82 us
  transfers between devices with their start and end apart: 5, of which 2 were waited for; matrix products, arithmetic and copies ran while one was open for 0% of the time, Pallas kernels for 12%

profile of v12, /device:TPU:0, one launch (start us, length us, event | category | flops | bytes accessed | tf_op | source)
XLA Modules:
  0.0 46.1 jit_solution(511180118356891141)
XLA Ops:
  1.3 1.7 %shard_map.130 = (f32[32,4,128]{2,1,0:T(4,128)S(1)}, bf16[2,32,128]{2,1,0:T(8,128)(2,1)S(1)}, bf16[160,384]{1,0:T(8,128)(2,1)S(1)}, bf16[8,128]{1,0:T(8,128)(2,1...) custom-call(s32[1]{0:T(128)} %bitcast.16.refs_0_, ...), custom_call_target="tpu_custom_call" | custom-call | flops 1048576 | bytes 1048576 | tf_op jit(solution)/shard_map/pallas_call | solution.py:620
  3.0 14.6 %all_to_all.10.refs_0_ = f32[32,4,128]{2,1,0:T(4,128)S(1)} all-to-all(f32[32,4,128]{2,1,0:T(4,128)S(1)} %get-tuple-element.35), channel_id=1, replica_groups=mesh['gx'=4,'gy'=2,'gz'=4] {'gx','gy','gz'}, dimensions={0} | all-to-all | bytes 131072 | tf_op jit(solution)/shard_map/all_to_all | solution.py:696
  17.6 4.4 %shard_map.131 = (f32[9,4,128]{2,1,0:T(4,128)S(1)}, bf16[3,4,64,1152]{3,2,1,0:T(8,128)(2,1)S(1)}, bf16[4,64,128]{2,1,0:T(8,128)(2,1)S(1)}, f32[192,128]{1,0:T(8,...) custom-call(f32[32,4,128]{2,1,0:T(4,128)S(1)} %all_to_all.10.refs_0_, ...), custom_call_target="tpu_custom_call" | custom-call | flops 7372800 | bytes 1048576 | tf_op jit(solution)/shard_map/pallas_call | solution.py:620
  22.0 0.7 %collective-permute-start.2 = (bf16[4,64,128]{2,1,0:T(8,128)(2,1)S(1)}, bf16[4,64,128]{2,1,0:T(8,128)(2,1)S(1)}, u32[]{:S(2)}, u32[]{:S(2)}) collective-permute-start(bf16[4,64,128]{2,1,0:T(8,128)(2,1)S(1)} %get-tuple-element.40.refs_1_.refs_0_.refs_5_), channel_id=1, source_target_pairs={{16,0},{24,8},{0,16},{8,24},{17,1},{25,9},{1,17},{9,25},{18,2},{26... | collective-permute-start | bytes 196616 | tf_op jit(solution)/shard_map/ppermute | solution.py:691
  22.7 1.4 %collective-permute-start.1 = (bf16[4,64,128]{2,1,0:T(8,128)(2,1)S(1)}, bf16[4,64,128]{2,1,0:T(8,128)(2,1)S(1)}, u32[]{:S(2)}, u32[]{:S(2)}) collective-permute-start(bf16[4,64,128]{2,1,0:T(8,128)(2,1)S(1)} %get-tuple-element.40.refs_1_.refs_0_.refs_5_), channel_id=1, source_target_pairs={{24,0},{25,1},{26,2},{27,3},{28,4},{29,5},{30,6},{31,7},{16,8},{17... | collective-permute-start | bytes 196616 | tf_op jit(solution)/shard_map/ppermute | solution.py:661
  24.2 1.4 %collective-permute-start = (bf16[4,64,128]{2,1,0:T(8,128)(2,1)S(1)}, bf16[4,64,128]{2,1,0:T(8,128)(2,1)S(1)}, u32[]{:S(2)}, u32[]{:S(2)}) collective-permute-start(bf16[4,64,128]{2,1,0:T(8,128)(2,1)S(1)} %get-tuple-element.40.refs_1_.refs_0_.refs_5_), channel_id=1, source_target_pairs={{8,0},{9,1},{10,2},{11,3},{12,4},{13,5},{14,6},{15,7},{0,8},{1,9},... | collective-permute-start | bytes 196616 | tf_op jit(solution)/shard_map/ppermute | solution.py:661
  25.5 3.3 %shard_map.132 = (bf16[4,64,128]{2,1,0:T(8,128)(2,1)S(1)}, bf16[6,4,64,1152]{3,2,1,0:T(8,128)(2,1)S(1)}, f32[6,64,8]{2,1,0:T(8,128)S(1)}) custom-call(f32[32,4,128]{2,1,0:T(4,128)S(1)} %all_to_all.10.refs_0_, bf16[4,64,128]{2,1,0:T(8,128)(2,1)S(1)} %get-tuple-element.40.refs_1_.refs_0_.refs_5_), custom_call_target="tpu_custom_call" | custom-call | flops 7372800 | bytes 1048576 | tf_op jit(solution)/shard_map/pallas_call | solution.py:620
  28.8 0.0 collective-permute-done.2.refs_3_
  28.9 0.0 collective-permute-done.1.refs_2_
  28.9 0.0 collective-permute-done.refs_1_
  28.9 0.1 collective-permute-start.3
  29.0 1.2 %shard_map.133 = (f32[1,128]{1,0:T(1,128)S(1)}, f32[3,64,1152]{2,1,0:T(8,128)S(1)}, f32[4,64,1152]{2,1,0:T(8,128)S(1)}, f32[4,64,1152]{2,1,0:T(8,128)S(1)}, f32[4,64,1152]{2,1,0:T(8,128)S(1)}) custom-call(f32[9,4,128]{2,1,0:T(4,128)S(1)} %get-tuple-element.50.refs_0_.refs_5_, f32[3,64,8]{2,1,0:T(8,128)S(1)} %get-tuple-element.43.refs_1_.refs_7_.refs_4_, ...), custom_call_target="tpu_custom_call" | custom-call | flops 7372800 | bytes 1048576 | tf_op jit(solution)/shard_map/pallas_call | solution.py:620
  30.2 0.3 collective-permute-done.3.refs_4_
  30.5 2.1 %shard_map.134 = (bf16[9,64,128]{2,1,0:T(8,128)(2,1)S(1)}, bf16[64,128]{1,0:T(8,128)(2,1)S(1)}, f32[64,16]{1,0:T(8,128)S(1)}, f32[64,128]{1,0:T(8,128)S(1)}, bf16[1152,128]{1,0:T(8,128)(2,1)S(1)}) custom-call(bf16[4,64,128]{2,1,0:T(8,128)(2,1)S(1)} %get-tuple-element.40.refs_1_.refs_0_.refs_5_, bf16[4,64,128]{2,1,0:T(8,128)(2,1)S(1)} %collective-permute-done.refs_1_, ...), custom_call_target="tpu_custom_call" | custom-call | flops 7372800 | bytes 1048576 | tf_op jit(solution)/shard_map/pallas_call | solution.py:620
  32.7 0.2 collective-permute-start.4
  32.9 1.0 %shard_map.135 = (bf16[1,64,128]{2,1,0:T(8,128)(2,1)}, f32[64,1152]{1,0:T(8,128)S(1)}, f32[1,64]{1,0:T(1,128)}, bf16[64,128]{1,0:T(8,128)(2,1)}) custom-call(bf16[1152,128]{1,0:T(8,128)(2,1)S(1)} %get-tuple-element.55.refs_0_, bf16[9,64,128]{2,1,0:T(8,128)(2,1)S(1)} %get-tuple-element.53.refs_1_.refs_0_, ...), custom_call_target="tpu_custom_call" | custom-call | flops 7372800 | bytes 1048576 | tf_op jit(solution)/shard_map/pallas_call | solution.py:620
  33.9 0.2 collective-permute-done.4.refs_1_
  34.1 2.1 %shard_map.136 = f32[32,4,128]{2,1,0:T(4,128)S(1)} custom-call(bf16[9,64,128]{2,1,0:T(8,128)(2,1)S(1)} %get-tuple-element.53.refs_1_.refs_0_, bf16[9,64,128]{2,1,0:T(8,128)(2,1)S(1)} %collective-permute-done.4.refs_1_, f32[64,128]{1,0:T(8,128)S(1)} %get-tuple-element.54.refs_2_, bf16[3,4,64,1152]{3,2,1,0:T(8,128)(2,1)S(1)} %get-tuple-element.42.refs_6_.refs_3_, ...), custom_call_target="tpu_custom_call" | custom-call | flops 7372800 | bytes 1048576 | tf_op jit(solution)/shard_map/pallas_call | solution.py:620
  36.2 9.2 %all_to_all.11.refs_0_ = f32[32,4,128]{2,1,0:T(4,128)S(1)} all-to-all(f32[32,4,128]{2,1,0:T(4,128)S(1)} %shard_map.136), channel_id=1, replica_groups=mesh['gx'=4,'gy'=2,'gz'=4] {'gx','gy','gz'}, dimensions={0} | all-to-all | bytes 131072 | tf_op jit(solution)/shard_map/all_to_all | solution.py:696
  45.4 0.7 %shard_map.137 = f32[3,1,64]{2,1,0:T(1,128)} custom-call(f32[32,4,128]{2,1,0:T(4,128)S(1)} %all_to_all.11.refs_0_), custom_call_target="tpu_custom_call" | custom-call | flops 1048576 | bytes 1048576 | tf_op jit(solution)/shard_map/pallas_call | solution.py:620
  (1 shorter events, 0.0 us)
Async XLA Ops:
  22.0 6.9 %collective-permute-start.2 = (bf16[4,64,128]{2,1,0:T(8,128)(2,1)S(1)}, bf16[4,64,128]{2,1,0:T(8,128)(2,1)S(1)}, u32[]{:S(2)}, u32[]{:S(2)}) collective-permute-start(bf16[4,64,128]{2,1,0:T(8,128)(2,1)S(1)} %get-tuple-element.40.refs_1_.refs_0_.refs_5_), channel_id=1, source_target_pairs={{16,0},{24,8},{0,16},{8,24},{17,1},{25,9},{1,17},{9,25},{18,2},{26... | collective-permute-start | bytes 196616 | tf_op jit(solution)/shard_map/ppermute | solution.py:691
  22.7 6.1 %collective-permute-start.1 = (bf16[4,64,128]{2,1,0:T(8,128)(2,1)S(1)}, bf16[4,64,128]{2,1,0:T(8,128)(2,1)S(1)}, u32[]{:S(2)}, u32[]{:S(2)}) collective-permute-start(bf16[4,64,128]{2,1,0:T(8,128)(2,1)S(1)} %get-tuple-element.40.refs_1_.refs_0_.refs_5_), channel_id=1, source_target_pairs={{24,0},{25,1},{26,2},{27,3},{28,4},{29,5},{30,6},{31,7},{16,8},{17... | collective-permute-start | bytes 196616 | tf_op jit(solution)/shard_map/ppermute | solution.py:661
  24.2 4.7 %collective-permute-start = (bf16[4,64,128]{2,1,0:T(8,128)(2,1)S(1)}, bf16[4,64,128]{2,1,0:T(8,128)(2,1)S(1)}, u32[]{:S(2)}, u32[]{:S(2)}) collective-permute-start(bf16[4,64,128]{2,1,0:T(8,128)(2,1)S(1)} %get-tuple-element.40.refs_1_.refs_0_.refs_5_), channel_id=1, source_target_pairs={{8,0},{9,1},{10,2},{11,3},{12,4},{13,5},{14,6},{15,7},{0,8},{1,9},... | collective-permute-start | bytes 196616 | tf_op jit(solution)/shard_map/ppermute | solution.py:661
  28.9 1.6 %collective-permute-start.3 = (bf16[4,4,64,128]{3,2,1,0:T(8,128)(2,1)S(1)}, bf16[4,4,64,128]{3,2,1,0:T(8,128)(2,1)S(1)}, u32[]{:S(2)}, u32[]{:S(2)}) collective-permute-start(bf16[4,4,64,128]{3,2,1,0:T(8,128)(2,1)S(1)} %pad_maximum_fusion), channel_id=1, source_target_pairs={{4,0},{0,4},{5,1},{1,5},{6,2},{2,6},{7,3},{3,7},{12,8},{8,12},{13,... | collective-permute-start | bytes 786440 | tf_op jit(solution)/shard_map/ppermute | solution.py:671
  32.7 1.4 %collective-permute-start.4 = (bf16[9,64,128]{2,1,0:T(8,128)(2,1)S(1)}, bf16[9,64,128]{2,1,0:T(8,128)(2,1)S(1)}, u32[]{:S(2)}, u32[]{:S(2)}) collective-permute-start(bf16[9,64,128]{2,1,0:T(8,128)(2,1)S(1)} %get-tuple-element.53.refs_1_.refs_0_), channel_id=1, source_target_pairs={{4,0},{0,4},{5,1},{1,5},{6,2},{2,6},{7,3},{3,7},{12,8},{8,12},{13,... | collective-permute-start | bytes 442376 | tf_op jit(solution)/shard_map/ppermute | solution.py:671

commit v13 on v11

--- a/solution.py
+++ b/solution.py
@@ -568,6 +568,7 @@
     fetched, (sent_ref, table_ref, wide_ref), refs = refs[:10], refs[10:13], refs[13:]
     kept, (place_ref, kind_ref, radial_ref, sems) = refs[:7], refs[7:]
     copies = begin(zip(fetched, (place_ref, kind_ref, radial_ref, *kept)), sems)
+    wide_ref[...] = jnp.zeros_like(wide_ref)
     for copy in copies[:2]:
         copy.wait()
     live = lax.broadcasted_iota(jnp.int32, (1, plan.slots), 1) < counts_ref[0]
@@ -581,18 +582,19 @@
     rows = jnp.concatenate([rows, rows], axis=1)
     for copy in range(sent_ref.shape[0]):
         sent_ref[copy] = rows
-    for copy in copies[2:]:
+    for copy in copies[2:4]:
         copy.wait()
     embed, nspec = kept[0][...].astype(F32), plan.nspec
     for g in range(2):
         for n in range(plan.nbasis):
             weighted = radial_ref[g, n : n + 1] * embed
             table_ref[g, n * nspec : (n + 1) * nspec] = weighted.astype(BF16)
-    wide_ref[...] = jnp.zeros_like(wide_ref)
     count, channels = table_ref.shape[1:]
     for m in range(1 + 2 * len(plan.plain)):
         start = (m + 1) // 2 * channels
         wide_ref[m * count : (m + 1) * count, start : start + channels] = table_ref[1]
+    for copy in copies[4:]:
+        copy.wait()
 
 
 def sum_kernel(plan, parts_ref, force_ref):

time: 45.6 us -> 45.6 us (level)
  no operation moved by 1% of the time
where the time goes in v13:
time: 45.6 us; the launch traced here: 45.4 us
  blocking collectives  23.8 us (52%)
  Pallas kernels  15.8 us (35%)
  starting transfers between devices  3.86 us (8%)
  between operations  1.36 us (3%)
  waiting for transfers between devices  0.52 us (1%)
    all_to_all x2, blocking collectives, everywhere(): return lax.all_to_all(copies, AXES, 0, 0, tiled=True)  23.8 us
    pallas_call x8, Pallas kernels, simple_call(): pl.pallas_call(body, out_shape=shapes, in_specs=[SMEM_SPEC] * scalars + [...  15.8 us
    ppermute x2, starting transfers between devices, brought(): got.append(lax.ppermute(block, AXES, pairs))  2.81 us
  transfers between devices with their start and end apart: 5, of which 2 were waited for; matrix products, arithmetic and copies ran while one was open for 0% of the time, Pallas kernels for 12%

profile of v13, /device:TPU:0, one launch (start us, length us, event | category | flops | bytes accessed | tf_op | source)
XLA Modules:
  0.0 45.4 jit_solution(16685223401080280603)
XLA Ops:
  1.3 1.0 %shard_map.130 = (f32[32,4,128]{2,1,0:T(4,128)S(1)}, bf16[2,32,128]{2,1,0:T(8,128)(2,1)S(1)}, bf16[160,384]{1,0:T(8,128)(2,1)S(1)}, bf16[8,128]{1,0:T(8,128)(2,1...) custom-call(s32[1]{0:T(128)} %bitcast.16.refs_0_, ...), custom_call_target="tpu_custom_call" | custom-call | flops 1048576 | bytes 1048576 | tf_op jit(solution)/shard_map/pallas_call | solution.py:622
  2.3 14.6 %all_to_all.10.refs_0_ = f32[32,4,128]{2,1,0:T(4,128)S(1)} all-to-all(f32[32,4,128]{2,1,0:T(4,128)S(1)} %get-tuple-element.35), channel_id=1, replica_groups=mesh['gx'=4,'gy'=2,'gz'=4] {'gx','gy','gz'}, dimensions={0} | all-to-all | bytes 131072 | tf_op jit(solution)/shard_map/all_to_all | solution.py:698
  16.9 4.4 %shard_map.131 = (f32[9,4,128]{2,1,0:T(4,128)S(1)}, bf16[3,4,64,1152]{3,2,1,0:T(8,128)(2,1)S(1)}, bf16[4,64,128]{2,1,0:T(8,128)(2,1)S(1)}, f32[192,128]{1,0:T(8,...) custom-call(f32[32,4,128]{2,1,0:T(4,128)S(1)} %all_to_all.10.refs_0_, ...), custom_call_target="tpu_custom_call" | custom-call | flops 7372800 | bytes 1048576 | tf_op jit(solution)/shard_map/pallas_call | solution.py:622
  21.3 0.7 %collective-permute-start.2 = (bf16[4,64,128]{2,1,0:T(8,128)(2,1)S(1)}, bf16[4,64,128]{2,1,0:T(8,128)(2,1)S(1)}, u32[]{:S(2)}, u32[]{:S(2)}) collective-permute-start(bf16[4,64,128]{2,1,0:T(8,128)(2,1)S(1)} %get-tuple-element.40.refs_1_.refs_0_.refs_5_), channel_id=1, source_target_pairs={{16,0},{24,8},{0,16},{8,24},{17,1},{25,9},{1,17},{9,25},{18,2},{26... | collective-permute-start | bytes 196616 | tf_op jit(solution)/shard_map/ppermute | solution.py:693
  22.0 1.4 %collective-permute-start.1 = (bf16[4,64,128]{2,1,0:T(8,128)(2,1)S(1)}, bf16[4,64,128]{2,1,0:T(8,128)(2,1)S(1)}, u32[]{:S(2)}, u32[]{:S(2)}) collective-permute-start(bf16[4,64,128]{2,1,0:T(8,128)(2,1)S(1)} %get-tuple-element.40.refs_1_.refs_0_.refs_5_), channel_id=1, source_target_pairs={{24,0},{25,1},{26,2},{27,3},{28,4},{29,5},{30,6},{31,7},{16,8},{17... | collective-permute-start | bytes 196616 | tf_op jit(solution)/shard_map/ppermute | solution.py:663
  23.5 1.4 %collective-permute-start = (bf16[4,64,128]{2,1,0:T(8,128)(2,1)S(1)}, bf16[4,64,128]{2,1,0:T(8,128)(2,1)S(1)}, u32[]{:S(2)}, u32[]{:S(2)}) collective-permute-start(bf16[4,64,128]{2,1,0:T(8,128)(2,1)S(1)} %get-tuple-element.40.refs_1_.refs_0_.refs_5_), channel_id=1, source_target_pairs={{8,0},{9,1},{10,2},{11,3},{12,4},{13,5},{14,6},{15,7},{0,8},{1,9},... | collective-permute-start | bytes 196616 | tf_op jit(solution)/shard_map/ppermute | solution.py:663
  24.9 3.3 %shard_map.132 = (bf16[4,64,128]{2,1,0:T(8,128)(2,1)S(1)}, bf16[6,4,64,1152]{3,2,1,0:T(8,128)(2,1)S(1)}, f32[6,64,8]{2,1,0:T(8,128)S(1)}) custom-call(f32[32,4,128]{2,1,0:T(4,128)S(1)} %all_to_all.10.refs_0_, bf16[4,64,128]{2,1,0:T(8,128)(2,1)S(1)} %get-tuple-element.40.refs_1_.refs_0_.refs_5_), custom_call_target="tpu_custom_call" | custom-call | flops 7372800 | bytes 1048576 | tf_op jit(solution)/shard_map/pallas_call | solution.py:622
  28.2 0.0 collective-permute-done.2.refs_3_
  28.2 0.0 collective-permute-done.1.refs_2_
  28.2 0.0 collective-permute-done.refs_1_
  28.2 0.1 collective-permute-start.3
  28.3 1.2 %shard_map.133 = (f32[1,128]{1,0:T(1,128)S(1)}, f32[3,64,1152]{2,1,0:T(8,128)S(1)}, f32[4,64,1152]{2,1,0:T(8,128)S(1)}, f32[4,64,1152]{2,1,0:T(8,128)S(1)}, f32[4,64,1152]{2,1,0:T(8,128)S(1)}) custom-call(f32[9,4,128]{2,1,0:T(4,128)S(1)} %get-tuple-element.50.refs_0_.refs_5_, f32[3,64,8]{2,1,0:T(8,128)S(1)} %get-tuple-element.43.refs_1_.refs_7_.refs_4_, ...), custom_call_target="tpu_custom_call" | custom-call | flops 7372800 | bytes 1048576 | tf_op jit(solution)/shard_map/pallas_call | solution.py:622
  29.5 0.3 collective-permute-done.3.refs_4_
  29.8 2.1 %shard_map.134 = (bf16[9,64,128]{2,1,0:T(8,128)(2,1)S(1)}, bf16[64,128]{1,0:T(8,128)(2,1)S(1)}, f32[64,16]{1,0:T(8,128)S(1)}, f32[64,128]{1,0:T(8,128)S(1)}, bf16[1152,128]{1,0:T(8,128)(2,1)S(1)}) custom-call(bf16[4,64,128]{2,1,0:T(8,128)(2,1)S(1)} %get-tuple-element.40.refs_1_.refs_0_.refs_5_, bf16[4,64,128]{2,1,0:T(8,128)(2,1)S(1)} %collective-permute-done.refs_1_, ...), custom_call_target="tpu_custom_call" | custom-call | flops 7372800 | bytes 1048576 | tf_op jit(solution)/shard_map/pallas_call | solution.py:622
  32.0 0.2 collective-permute-start.4
  32.2 1.0 %shard_map.135 = (bf16[1,64,128]{2,1,0:T(8,128)(2,1)}, f32[64,1152]{1,0:T(8,128)S(1)}, f32[1,64]{1,0:T(1,128)}, bf16[64,128]{1,0:T(8,128)(2,1)}) custom-call(bf16[1152,128]{1,0:T(8,128)(2,1)S(1)} %get-tuple-element.55.refs_0_, bf16[9,64,128]{2,1,0:T(8,128)(2,1)S(1)} %get-tuple-element.53.refs_1_.refs_0_, ...), custom_call_target="tpu_custom_call" | custom-call | flops 7372800 | bytes 1048576 | tf_op jit(solution)/shard_map/pallas_call | solution.py:622
  33.2 0.2 collective-permute-done.4.refs_1_
  33.4 2.1 %shard_map.136 = f32[32,4,128]{2,1,0:T(4,128)S(1)} custom-call(bf16[9,64,128]{2,1,0:T(8,128)(2,1)S(1)} %get-tuple-element.53.refs_1_.refs_0_, bf16[9,64,128]{2,1,0:T(8,128)(2,1)S(1)} %collective-permute-done.4.refs_1_, f32[64,128]{1,0:T(8,128)S(1)} %get-tuple-element.54.refs_2_, bf16[3,4,64,1152]{3,2,1,0:T(8,128)(2,1)S(1)} %get-tuple-element.42.refs_6_.refs_3_, ...), custom_call_target="tpu_custom_call" | custom-call | flops 7372800 | bytes 1048576 | tf_op jit(solution)/shard_map/pallas_call | solution.py:622
  35.5 9.2 %all_to_all.11.refs_0_ = f32[32,4,128]{2,1,0:T(4,128)S(1)} all-to-all(f32[32,4,128]{2,1,0:T(4,128)S(1)} %shard_map.136), channel_id=1, replica_groups=mesh['gx'=4,'gy'=2,'gz'=4] {'gx','gy','gz'}, dimensions={0} | all-to-all | bytes 131072 | tf_op jit(solution)/shard_map/all_to_all | solution.py:698
  44.7 0.7 %shard_map.137 = f32[3,1,64]{2,1,0:T(1,128)} custom-call(f32[32,4,128]{2,1,0:T(4,128)S(1)} %all_to_all.11.refs_0_), custom_call_target="tpu_custom_call" | custom-call | flops 1048576 | bytes 1048576 | tf_op jit(solution)/shard_map/pallas_call | solution.py:622
  (1 shorter events, 0.0 us)
Async XLA Ops:
  21.3 6.9 %collective-permute-start.2 = (bf16[4,64,128]{2,1,0:T(8,128)(2,1)S(1)}, bf16[4,64,128]{2,1,0:T(8,128)(2,1)S(1)}, u32[]{:S(2)}, u32[]{:S(2)}) collective-permute-start(bf16[4,64,128]{2,1,0:T(8,128)(2,1)S(1)} %get-tuple-element.40.refs_1_.refs_0_.refs_5_), channel_id=1, source_target_pairs={{16,0},{24,8},{0,16},{8,24},{17,1},{25,9},{1,17},{9,25},{18,2},{26... | collective-permute-start | bytes 196616 | tf_op jit(solution)/shard_map/ppermute | solution.py:693
  22.0 6.1 %collective-permute-start.1 = (bf16[4,64,128]{2,1,0:T(8,128)(2,1)S(1)}, bf16[4,64,128]{2,1,0:T(8,128)(2,1)S(1)}, u32[]{:S(2)}, u32[]{:S(2)}) collective-permute-start(bf16[4,64,128]{2,1,0:T(8,128)(2,1)S(1)} %get-tuple-element.40.refs_1_.refs_0_.refs_5_), channel_id=1, source_target_pairs={{24,0},{25,1},{26,2},{27,3},{28,4},{29,5},{30,6},{31,7},{16,8},{17... | collective-permute-start | bytes 196616 | tf_op jit(solution)/shard_map/ppermute | solution.py:663
  23.5 4.7 %collective-permute-start = (bf16[4,64,128]{2,1,0:T(8,128)(2,1)S(1)}, bf16[4,64,128]{2,1,0:T(8,128)(2,1)S(1)}, u32[]{:S(2)}, u32[]{:S(2)}) collective-permute-start(bf16[4,64,128]{2,1,0:T(8,128)(2,1)S(1)} %get-tuple-element.40.refs_1_.refs_0_.refs_5_), channel_id=1, source_target_pairs={{8,0},{9,1},{10,2},{11,3},{12,4},{13,5},{14,6},{15,7},{0,8},{1,9},... | collective-permute-start | bytes 196616 | tf_op jit(solution)/shard_map/ppermute | solution.py:663
  28.2 1.6 %collective-permute-start.3 = (bf16[4,4,64,128]{3,2,1,0:T(8,128)(2,1)S(1)}, bf16[4,4,64,128]{3,2,1,0:T(8,128)(2,1)S(1)}, u32[]{:S(2)}, u32[]{:S(2)}) collective-permute-start(bf16[4,4,64,128]{3,2,1,0:T(8,128)(2,1)S(1)} %pad_maximum_fusion), channel_id=1, source_target_pairs={{4,0},{0,4},{5,1},{1,5},{6,2},{2,6},{7,3},{3,7},{12,8},{8,12},{13,... | collective-permute-start | bytes 786440 | tf_op jit(solution)/shard_map/ppermute | solution.py:673
  32.0 1.4 %collective-permute-start.4 = (bf16[9,64,128]{2,1,0:T(8,128)(2,1)S(1)}, bf16[9,64,128]{2,1,0:T(8,128)(2,1)S(1)}, u32[]{:S(2)}, u32[]{:S(2)}) collective-permute-start(bf16[9,64,128]{2,1,0:T(8,128)(2,1)S(1)} %get-tuple-element.53.refs_1_.refs_0_), channel_id=1, source_target_pairs={{4,0},{0,4},{5,1},{1,5},{6,2},{2,6},{7,3},{3,7},{12,8},{8,12},{13,... | collective-permute-start | bytes 442376 | tf_op jit(solution)/shard_map/ppermute | solution.py:673
